TPU v7x, 256 devices: a whole 4x4x8 slice. The times are simulated.
256 devices in a mesh: tm: 32 (over z, y), chan: 8 (over x, core).
Axes of the slice: x: 4, y: 4, z: 8, core: 2. Of those that a mesh axis runs over, the one named last changes fastest.
Arguments:
- observed_real: float32 [4096, 4096], P(('tm', 'chan')), may hold values from -6 to 6
- observed_imag: float32 [4096, 4096], P(('tm', 'chan')), may hold values from -6 to 6
- weights: float32 [4096, 4096], P(('tm', 'chan')), may hold values from 0.15 to 162
- taps: float32 [16, 8192], replicated, may hold values from -0.5 to 2
Outputs:
- solution: float32 [4096, 8192], P('tm', 'chan')
- residual: float32 [4096, 8192], P('tm', 'chan')
All inputs are finite; a program needn't handle non-finite values.
Results may differ from a plain program's by a relative error of at most 0.00019.
Values sent between devices are 32-bit elements; how exact they have to be, the bound alone decides.
No kernel may reach another device: no remote copies, remote signals or barrier semaphores. Data moves between devices by JAX's collectives and lax.ppermute only.
A program may use at most 64 MiB of HBM per device.

v0:
```python
import math

import jax
import jax.numpy as jnp
from jax import lax
from jax.sharding import PartitionSpec as P

ITERS = 2


RIDGE = 0.25
HIGHEST = lax.Precision.HIGHEST


def passed_along(block, axis, distance):
    devices = range(lax.axis_size(axis))
    route = [(i - distance, i) for i in devices if i - distance in devices]
    return lax.ppermute(block, axis, route)


def dft_tables(frame_len):
    inner_size = frame_len // 8
    inner_steps = jnp.arange(inner_size, dtype=jnp.int32)
    phase = inner_steps[:, None] * inner_steps[None, :] % inner_size
    angle = phase.astype(jnp.float32) * (2.0 * math.pi / inner_size)
    outer_steps = jnp.arange(8, dtype=jnp.int32)
    twist = (outer_steps[:, None] * inner_steps[None, :]).astype(jnp.float32) * (
        2.0 * math.pi / frame_len
    )
    low_bins = jnp.arange(4, dtype=jnp.int32)
    small_phase = low_bins[:, None] * outer_steps[None, :] % 8
    small_angle = small_phase.astype(jnp.float32) * (2.0 * math.pi / 8.0)
    return (
        jnp.cos(angle),
        jnp.sin(angle),
        jnp.cos(twist),
        jnp.sin(twist),
        jnp.cos(small_angle),
        jnp.sin(small_angle),
    )


def transform(frames, tables):
    big_cos, big_sin, twist_cos, twist_sin, small_cos, small_sin = tables
    count = frames.shape[0]
    inner_size = big_cos.shape[0]
    grid = jnp.swapaxes(frames.reshape(count, inner_size, 8), 1, 2).reshape(count * 8, inner_size)
    real_one = jnp.dot(grid, big_cos, precision=HIGHEST).reshape(count, 8, inner_size)
    imag_one = -jnp.dot(grid, big_sin, precision=HIGHEST).reshape(count, 8, inner_size)
    real_two = real_one * twist_cos + imag_one * twist_sin
    imag_two = imag_one * twist_cos - real_one * twist_sin
    real_out = jnp.einsum("kn,fnj->fkj", small_cos, real_two, precision=HIGHEST) + jnp.einsum(
        "kn,fnj->fkj", small_sin, imag_two, precision=HIGHEST
    )
    imag_out = jnp.einsum("kn,fnj->fkj", small_cos, imag_two, precision=HIGHEST) - jnp.einsum(
        "kn,fnj->fkj", small_sin, real_two, precision=HIGHEST
    )
    scale = 1.0 / math.sqrt(4 * inner_size)
    return (
        real_out.reshape(count, 4 * inner_size) * scale,
        imag_out.reshape(count, 4 * inner_size) * scale,
    )


def filter_samples(block, local_taps):
    count = block.shape[0]
    reach = local_taps.shape[0] - 1
    before = passed_along(block[count - reach :], "tm", 1)
    longer = jnp.concatenate([before, block], 0)
    total = jnp.zeros_like(block)
    for tap in range(reach + 1):
        total = total + local_taps[tap] * longer[reach - tap : reach - tap + count]
    return total


def unfilter_samples(block, local_taps):
    count = block.shape[0]
    reach = local_taps.shape[0] - 1
    after = passed_along(block[:reach], "tm", -1)
    longer = jnp.concatenate([block, after], 0)
    total = jnp.zeros_like(block)
    for tap in range(reach + 1):
        total = total + local_taps[tap] * longer[tap : tap + count]
    return total


def to_samples(frames):
    return lax.all_to_all(frames, "chan", split_axis=1, concat_axis=0, tiled=True)


def squares(vector):
    return lax.psum(jnp.sum(vector * vector), ("tm", "chan"))


def curving(direction, image):
    return lax.psum(jnp.sum(direction * image), ("tm", "chan"))


def solve(operator, right_side, rounds):
    solution = jnp.zeros_like(right_side)
    residual = right_side
    direction = right_side
    norm_now = squares(residual)
    for step in range(rounds):
        image = operator(direction)
        alpha = norm_now / curving(direction, image)
        solution = solution + alpha * direction
        residual = residual - alpha * image
        norm_next = squares(residual)
        direction = residual + norm_next / norm_now * direction
        norm_now = norm_next
    return (solution, residual)


def local(observed_real, observed_imag, weights, taps):
    frame_len = taps.shape[1]
    tables = dft_tables(frame_len)
    count = weights.shape[0]

    def channelize(frames):
        return transform(frames, tables)

    _, pullback = jax.vjp(channelize, jnp.zeros((count, frame_len), jnp.float32))

    def back_project(real_part, imag_part):
        return pullback((weights * real_part, weights * imag_part))[0]

    seed_frames = back_project(observed_real, observed_imag)
    width = frame_len // lax.axis_size("chan")
    local_taps = lax.dynamic_slice_in_dim(taps, lax.axis_index("chan") * width, width, 1)

    def operator(block):
        gathered = lax.all_to_all(
            filter_samples(block, local_taps), "chan", split_axis=0, concat_axis=1, tiled=True
        )
        spectrum_real, spectrum_imag = channelize(gathered)
        returned = to_samples(back_project(spectrum_real, spectrum_imag))
        return unfilter_samples(returned, local_taps) + RIDGE * block

    right_side = unfilter_samples(to_samples(seed_frames), local_taps)
    solution, residual = solve(operator, right_side, ITERS)
    return (solution, residual)


def solution(mesh):
    placed = (P(("tm", "chan"), None), P(("tm", "chan"), None), P(("tm", "chan"), None), P())
    return jax.shard_map(
        local,
        mesh=mesh,
        in_specs=placed,
        out_specs=(P("tm", "chan"), P("tm", "chan")),
        check_vma=False,
    )
```

profile of v0, /device:TPU:1, one launch (start us, length us, event | category | flops | bytes accessed | tf_op | source)
XLA Modules:
  0.0 588.0 jit_solution(10124287840407107597)
XLA Ops:
  0.8 1.2 multiply_multiply_fusion.4
  2.1 0.7 fusion.334
  2.8 0.7 fusion.338
  3.7 0.7 fusion.33
  4.4 0.7 fusion.32
  5.1 27.7 %fusion.22 = f32[128,1024]{1,0:T(8,128)S(1)} fusion(f32[16,8,1024]{2,1,0:T(8,128)S(1)} %fusion.33, f32[16,8,1024]{2,1,0:T(8,128)S(1)} %fusion.32, f32[8,1024]{1,0:T(8,128)S(1)} %get-tuple-element.33, f32[8,1024]{1,0:T(8,128)S(1)} %get-tuple-element.34), kind=kOutput, calls=%fused_computation.91 | convolution fusion | flops 1625817088 | bytes 1638400 | tf_op jit(solution)/shard_map/transpose(jvp())/dot_general | solution.py:49
  32.8 19.4 %fusion.41 = f32[16,8,1024]{2,1,0:T(8,128)S(1)} fusion(f32[128,1024]{1,0:T(8,128)S(1)} %fusion.22, f32[16,8,1024]{2,1,0:T(8,128)S(1)} %fusion.33, f32[16,8,1024]{2,1,0:T(8,128)S(1)} %fusion.32, f32[8,1024]{1,0:T(8,128)S(1)} %get-tuple-element.33, f32[8,1024]{1,0:T(8,128)S(1)} %get-tuple-element.34), kind=kOutput, calls=%fused_computation.108 | convolution fusion | flops 1625948160 | bytes 2162688 | tf_op jit(solution)/shard_map/transpose(jvp())/dot_general | solution.py:48
  52.2 2.7 copy.23
  55.0 3.5 copy.24
  58.5 6.6 %all-to-all-start = ((f32[16,8,1024]{2,0,1:T(8,128)}), f32[16,8,1024]{2,0,1:T(8,128)S(1)}, u32[]{:S(2)}, u32[]{:S(2)}) async-start(f32[16,8,1024]{2,0,1:T(8,128)} %copy.24), calls=%async_computation | async-start | bytes 1048576 | tf_op jit(solution)/shard_map/all_to_all | solution.py:88
  65.1 9.5 %all-to-all-done = f32[16,8,1024]{2,0,1:T(8,128)S(1)} async-done(((f32[16,8,1024]{2,0,1:T(8,128)}), f32[16,8,1024]{2,0,1:T(8,128)S(1)}, u32[]{:S(2)}, u32[]{:S(2)}) %all-to-all-start) | async-done | bytes 524320 | tf_op jit(solution)/shard_map/all_to_all | solution.py:88
  74.6 1.3 collective-permute-start
  75.9 1.5 constant_dynamic-slice_fusion
  77.4 2.2 collective-permute-done
  79.6 1.3 fusion.243
  80.9 2.3 collective-permute-start.1
  83.3 1.3 collective-permute-done.1
  84.6 0.9 fusion.200
  85.5 14.8 %all_to_all.89 = f32[8,16,1024]{2,1,0:T(8,128)S(1)} all-to-all(f32[8,16,1024]{2,1,0:T(8,128)S(1)} %bitcast.200), channel_id=1, replica_groups=mesh['tm'=32,'chan'=8] {'chan'}, dimensions={0} | all-to-all | bytes 1048576 | tf_op jit(solution)/shard_map/all_to_all | solution.py:133
  100.3 2.6 copy.25
  102.9 3.0 copy.26
  105.8 18.3 %fusion.5 = f32[16,8,1024]{2,1,0:T(8,128)S(1)} fusion(f32[16,1024,8]{1,2,0:T(8,128)S(1)} %copy.26), kind=kOutput, calls=%fused_computation.8 | convolution fusion | flops 1625292800 | bytes 1048576 | tf_op jit(solution)/shard_map/dot_general | solution.py:48
  124.1 18.5 %fusion.56 = f32[16,8,1024]{2,1,0:T(8,128)S(1)} fusion(f32[16,1024,8]{1,2,0:T(8,128)S(1)} %copy.26), kind=kOutput, calls=%fused_computation.113 | convolution fusion | flops 1625423872 | bytes 1048576 | tf_op jit(solution)/shard_map/dot_general | solution.py:49
  143.9 0.7 fusion.64
  144.8 0.7 fusion.65
  145.8 0.7 fusion.328
  146.5 0.7 fusion.332
  147.4 0.7 fusion.35
  148.1 0.7 fusion.34
  148.8 19.5 %fusion.19 = f32[128,1024]{1,0:T(8,128)S(1)} fusion(f32[16,8,1024]{2,1,0:T(8,128)S(1)} %fusion.35, f32[16,8,1024]{2,1,0:T(8,128)S(1)} %fusion.34, f32[8,1024]{1,0:T(8,128)S(1)} %get-tuple-element.33, f32[8,1024]{1,0:T(8,128)S(1)} %get-tuple-element.34), kind=kOutput, calls=%fused_computation.90 | convolution fusion | flops 1625817088 | bytes 1638400 | tf_op jit(solution)/shard_map/transpose(jvp())/dot_general | solution.py:49
  168.3 19.2 %fusion.47 = f32[16,8,1024]{2,1,0:T(8,128)S(1)} fusion(f32[128,1024]{1,0:T(8,128)S(1)} %fusion.19, f32[16,8,1024]{2,1,0:T(8,128)S(1)} %fusion.35, f32[16,8,1024]{2,1,0:T(8,128)S(1)} %fusion.34, f32[8,1024]{1,0:T(8,128)S(1)} %get-tuple-element.33, f32[8,1024]{1,0:T(8,128)S(1)} %get-tuple-element.34), kind=kOutput, calls=%fused_computation.110 | convolution fusion | flops 1625948160 | bytes 2162688 | tf_op jit(solution)/shard_map/transpose(jvp())/dot_general | solution.py:48
  187.5 2.7 copy.27
  190.3 2.8 copy.28
  193.0 12.8 %all_to_all.90 = f32[16,8,1024]{2,0,1:T(8,128)S(1)} all-to-all(f32[16,8,1024]{2,0,1:T(8,128)S(1)} %copy.28), channel_id=1, replica_groups=mesh['tm'=32,'chan'=8] {'chan'}, dimensions={1} | all-to-all | bytes 1048576 | tf_op jit(solution)/shard_map/all_to_all | solution.py:88
  205.8 1.3 collective-permute-start.2
  207.1 4.3 collective-permute-done.2
  211.5 2.0 multiply_reduce_fusion.2
  213.5 84.7 %all-reduce = (f32[]{:T(128)}, f32[]{:T(128)}) all-reduce(f32[]{:T(128)} %get-tuple-element.3, f32[]{:T(128)} %get-tuple-element.2), channel_id=1, replica_groups=mesh['tm'=32,'chan'=8] {'tm','chan'}, use_global_device_ids=true, to_apply=%region_1.2 | all-reduce | flops 2 | bytes 16 | tf_op jit(solution)/shard_map/psum | solution.py:92
  299.5 0.7 multiply_reduce_fusion.1
  300.2 72.9 %psum.30 = f32[]{:T(128)} all-reduce(f32[]{:T(128)} %multiply_reduce_fusion.1), channel_id=1, replica_groups=mesh['tm'=32,'chan'=8] {'tm','chan'}, use_global_device_ids=true, to_apply=%region_5.6 | all-reduce | flops 1 | bytes 8 | tf_op jit(solution)/shard_map/psum | solution.py:92
  374.6 2.2 collective-permute-start.3
  376.8 1.3 collective-permute-done.3
  378.1 0.9 fusion.113
  379.0 13.7 %all_to_all.91 = f32[8,16,1024]{2,1,0:T(8,128)S(1)} all-to-all(f32[8,16,1024]{2,1,0:T(8,128)S(1)} %bitcast.201), channel_id=1, replica_groups=mesh['tm'=32,'chan'=8] {'chan'}, dimensions={0} | all-to-all | bytes 1048576 | tf_op jit(solution)/shard_map/all_to_all | solution.py:133
  392.6 2.6 copy.29
  395.2 3.0 copy.30
  398.2 18.3 %fusion.3 = f32[16,8,1024]{2,1,0:T(8,128)S(1)} fusion(f32[16,1024,8]{1,2,0:T(8,128)S(1)} %copy.30), kind=kOutput, calls=%fused_computation.6 | convolution fusion | flops 1625292800 | bytes 1048576 | tf_op jit(solution)/shard_map/dot_general | solution.py:48
  416.5 18.7 %fusion.59 = f32[16,8,1024]{2,1,0:T(8,128)S(1)} fusion(f32[16,1024,8]{1,2,0:T(8,128)S(1)} %copy.30), kind=kOutput, calls=%fused_computation.114 | convolution fusion | flops 1625423872 | bytes 1048576 | tf_op jit(solution)/shard_map/dot_general | solution.py:49
  436.5 0.7 fusion.62
  437.3 0.7 fusion.63
  438.4 0.7 fusion.322
  439.1 0.7 fusion.326
  439.9 0.7 fusion.37
  440.6 0.7 fusion.36
  441.3 19.3 %fusion.17 = f32[128,1024]{1,0:T(8,128)S(1)} fusion(f32[16,8,1024]{2,1,0:T(8,128)S(1)} %fusion.37, f32[16,8,1024]{2,1,0:T(8,128)S(1)} %fusion.36, f32[8,1024]{1,0:T(8,128)S(1)} %get-tuple-element.33, f32[8,1024]{1,0:T(8,128)S(1)} %get-tuple-element.34), kind=kOutput, calls=%fused_computation.89 | convolution fusion | flops 1625817088 | bytes 1638400 | tf_op jit(solution)/shard_map/transpose(jvp())/dot_general | solution.py:49
  460.7 19.1 %fusion.53 = f32[16,8,1024]{2,1,0:T(8,128)S(1)} fusion(f32[128,1024]{1,0:T(8,128)S(1)} %fusion.17, f32[16,8,1024]{2,1,0:T(8,128)S(1)} %fusion.37, f32[16,8,1024]{2,1,0:T(8,128)S(1)} %fusion.36, f32[8,1024]{1,0:T(8,128)S(1)} %get-tuple-element.33, f32[8,1024]{1,0:T(8,128)S(1)} %get-tuple-element.34), kind=kOutput, calls=%fused_computation.112 | convolution fusion | flops 1625948160 | bytes 2162688 | tf_op jit(solution)/shard_map/transpose(jvp())/dot_general | solution.py:48
  479.7 2.7 copy.31
  482.4 2.8 copy.32
  485.2 12.8 %all_to_all.92 = f32[16,8,1024]{2,0,1:T(8,128)S(1)} all-to-all(f32[16,8,1024]{2,0,1:T(8,128)S(1)} %copy.32), channel_id=1, replica_groups=mesh['tm'=32,'chan'=8] {'chan'}, dimensions={1} | all-to-all | bytes 1048576 | tf_op jit(solution)/shard_map/all_to_all | solution.py:88
  498.0 1.3 collective-permute-start.4
  499.3 4.3 collective-permute-done.4
  503.7 2.0 multiply_reduce_fusion
  505.6 79.4 %psum.31 = f32[]{:T(128)} all-reduce(f32[]{:T(128)} %get-tuple-element.6), channel_id=1, replica_groups=mesh['tm'=32,'chan'=8] {'tm','chan'}, use_global_device_ids=true, to_apply=%region_7.8 | all-reduce | flops 1 | bytes 8 | tf_op jit(solution)/shard_map/psum | solution.py:96
  586.4 1.2 multiply_subtract_fusion
  (25 shorter events, 4.7 us)
Async XLA Ops:
  58.5 16.1 %all-to-all-start = ((f32[16,8,1024]{2,0,1:T(8,128)}), f32[16,8,1024]{2,0,1:T(8,128)S(1)}, u32[]{:S(2)}, u32[]{:S(2)}) async-start(f32[16,8,1024]{2,0,1:T(8,128)} %copy.24), calls=%async_computation | async-start | bytes 1048576 | tf_op jit(solution)/shard_map/all_to_all | solution.py:88
  74.6 5.0 collective-permute-start
  80.9 3.7 collective-permute-start.1
  142.6 3.0 copy-start
  205.8 5.6 collective-permute-start.2
  374.6 3.5 collective-permute-start.3
  498.0 5.6 collective-permute-start.4
where the time goes:
time: 598 us; the launch traced here: 588 us
  blocking collectives  291 us (49%)
  matrix products  211 us (35%)
  local copies, waits for them, and re-layouts  31.5 us (5%)
  waiting for transfers between devices  23 us (4%)
  starting transfers between devices  15 us (3%)
  other arithmetic  10.4 us (2%)
    psum x2, blocking collectives, squares(): return lax.psum(jnp.sum(vector * vector), ('tm', 'chan'))  158 us
    dot_general x5, matrix products, transform(): jnp.dot(grid, big_sin, precision=HIGHEST).reshape(count, 8, inner_size)  104 us
    dot_general x5, matrix products, transform(): jnp.dot(grid, big_cos, precision=HIGHEST).reshape(count, 8, inner_size)  94.3 us
    psum x1, blocking collectives, curving(): return lax.psum(jnp.sum(direction * image), ('tm', 'chan'))  79.4 us
    all_to_all x2, blocking collectives, operator(): lax.all_to_all(filter_samples(block, local_taps), 'chan', split_axis=0, c...  28.5 us
    all_to_all x2, blocking collectives, to_samples(): lax.all_to_all(frames, 'chan', split_axis=1, concat_axis=0, tiled=True)  25.6 us
    ppermute x5, waiting for transfers between devices, passed_along(): return lax.ppermute(block, axis, route)  13.5 us
  transfers between devices with their start and end apart: 6, of which 6 were waited for; matrix products, arithmetic and copies ran while one was open for 0% of the time, Pallas kernels for 0%

commit v1 on v0

v1 whole, which is shorter than its diff:
```python
import functools
import math

import jax
import jax.numpy as jnp
import numpy as np
from jax import lax
from jax.experimental import pallas as pl
from jax.experimental.pallas import tpu as pltpu
from jax.sharding import PartitionSpec as P

RIDGE = 0.25
ROWS = 64
LANES = 128
CHUNK = 4
F32 = jnp.float32
BF16 = jnp.bfloat16
AXES = ("tm", "chan")
VMEM_BYTES = 40 * 1024 * 1024


def params():
    return pltpu.CompilerParams(vmem_limit_bytes=VMEM_BYTES)


def halves(table):
    high = table.astype(np.float32).astype(jnp.bfloat16)
    low = (table - high.astype(np.float64)).astype(np.float32).astype(jnp.bfloat16)
    return high, low


def dft_tables():
    n1 = np.arange(ROWS)
    n2 = np.arange(LANES)
    k1 = np.arange(ROWS)
    k2 = (2 * np.arange(32)[None, :] + np.arange(2)[:, None]).reshape(-1)
    first = 2.0 * np.pi * (n1[:, None] * k1[None, :] % ROWS) / ROWS
    back_rows = np.concatenate([np.cos(first), -np.sin(first)], 1)
    second = 2.0 * np.pi * (k2[:, None] * n2[None, :] % LANES) / LANES
    scale = 1.0 / math.sqrt(ROWS * ROWS)
    cos = (np.cos(second) * scale).reshape(2, 32, LANES)
    sin = (np.sin(second) * scale).reshape(2, 32, LANES)
    from_real = np.concatenate([cos, sin], 2)
    from_imag = np.concatenate([-sin, cos], 2)
    back_lanes = np.stack([from_real, from_imag], 1).reshape(LANES, 2 * LANES)
    rows_high, rows_low = halves(back_rows)
    lanes_high, lanes_low = halves(back_lanes)
    twist = 2.0 * np.pi * k1[:, None] * n2[None, :] / (ROWS * LANES)
    return (
        np.concatenate([rows_high.T, rows_high.T, rows_low.T], 1),
        np.concatenate([lanes_high.T, lanes_high.T, lanes_low.T], 0),
        np.concatenate([lanes_high, lanes_high, lanes_low], 0),
        np.concatenate([rows_high, rows_high, rows_low], 1),
        np.stack([np.cos(twist), np.sin(twist)]).astype(np.float32),
    )


def split(value):
    high = value.astype(BF16)
    low = (value - high.astype(F32)).astype(BF16)
    return high, low


def dot(left, right):
    return jnp.dot(left, right, preferred_element_type=F32)


def forward_chunk(frames, ahead_rows, ahead_lanes, cos, sin):
    high, low = split(jnp.concatenate(frames, 1))
    mixed = dot(ahead_rows, jnp.concatenate([high, low, high], 0))
    turned = []
    for f in range(len(frames)):
        real = mixed[:ROWS, f * LANES : (f + 1) * LANES]
        imag = mixed[ROWS:, f * LANES : (f + 1) * LANES]
        turned.append(jnp.concatenate([real * cos + imag * sin, imag * cos - real * sin], 1))
    high, low = split(jnp.concatenate(turned, 0))
    return dot(jnp.concatenate([high, low, high], 1), ahead_lanes)


def backward_chunk(spectra, back_lanes, back_rows, cos, sin):
    high, low = split(spectra)
    mixed = dot(jnp.concatenate([high, low, high], 1), back_lanes)
    turned = []
    for f in range(spectra.shape[0] // ROWS):
        real = mixed[f * ROWS : (f + 1) * ROWS, :LANES]
        imag = mixed[f * ROWS : (f + 1) * ROWS, LANES:]
        turned.append(jnp.concatenate([real * cos - imag * sin, real * sin + imag * cos], 0))
    high, low = split(jnp.concatenate(turned, 1))
    return dot(back_rows, jnp.concatenate([high, low, high], 0))


def turn_pair(block):
    flipped = block.T
    low_half = flipped[:ROWS]
    high_half = flipped[ROWS:]
    left = lax.broadcasted_iota(jnp.int32, (ROWS, LANES), 1) < ROWS
    return (
        jnp.where(left, low_half, pltpu.roll(high_half, ROWS, 1)),
        jnp.where(left, pltpu.roll(low_half, ROWS, 1), high_half),
    )


def seed_kernel(real_ref, imag_ref, weights_ref, back_lanes_ref, back_rows_ref, twist_ref, out_ref, held):
    count = real_ref.shape[0]
    for j in range(32):
        columns = slice(j * LANES, (j + 1) * LANES)
        weights = weights_ref[:, columns]
        held[pl.ds(j, count, stride=ROWS), :] = weights * real_ref[:, columns]
        held[pl.ds(32 + j, count, stride=ROWS), :] = weights * imag_ref[:, columns]
    cos = twist_ref[0]
    sin = twist_ref[1]
    for start in range(0, count, CHUNK):
        spectra = []
        for f in range(start, start + CHUNK, 2):
            spectra += turn_pair(held[f * ROWS : (f + 2) * ROWS, :])
        frames = backward_chunk(
            jnp.concatenate(spectra, 0), back_lanes_ref[...], back_rows_ref[...], cos, sin
        )
        for f in range(CHUNK):
            out_ref[start + f] = frames[:, f * LANES : (f + 1) * LANES]


def arrange_kernel(weights_ref, taps_ref, weights_out, taps_out, held):
    count = weights_ref.shape[0]
    for j in range(32):
        weights = weights_ref[:, j * LANES : (j + 1) * LANES]
        held[pl.ds(j, count, stride=ROWS), :] = weights
        held[pl.ds(32 + j, count, stride=ROWS), :] = weights
    for f in range(0, count, 2):
        first, second = turn_pair(held[f * ROWS : (f + 2) * ROWS, :])
        weights_out[f] = first
        weights_out[f + 1] = second
    for n1 in range(ROWS):
        taps_out[pl.ds(n1, taps_ref.shape[0], stride=ROWS), :] = taps_ref[
            :, n1 * LANES : (n1 + 1) * LANES
        ]


def weighted_sum(taps, values):
    total = taps[0] * values[0]
    for tap, value in zip(taps[1:], values[1:]):
        total = total + tap * value
    return total


def back_filter(rows, taps, before_ref, here_ref, after_ref, keep):
    reach = len(taps) - 1
    count = here_ref.shape[0]
    frames = [before_ref[t, rows, :] for t in range(count - reach, count)]
    frames += [here_ref[t, rows, :] for t in range(count)]
    frames += [after_ref[t, rows, :] for t in range(reach)]
    result = []
    for at in range(reach + count):
        total = weighted_sum(taps, frames[at : at + reach + 1])
        result.append(total * keep if at < reach else total)
    return result


def ahead_filter(taps, frames):
    reach = len(taps) - 1
    return [
        weighted_sum(taps, [frames[at + reach - tap] for tap in range(reach + 1)])
        for at in range(len(frames) - reach)
    ]


def first_kernel(
    keep_ref, before_ref, here_ref, after_ref, taps_ref, weights_ref,
    ahead_rows_ref, ahead_lanes_ref, back_lanes_ref, back_rows_ref, twist_ref,
    out_ref, side_ref, filtered,
):
    count = here_ref.shape[0]
    keep = keep_ref[0]

    @pl.loop(0, ROWS // 8)
    def _(group):
        rows = pl.ds(pl.multiple_of(group * 8, 8), 8)
        taps = [taps_ref[p, rows, :] for p in range(taps_ref.shape[0])]
        side = back_filter(rows, taps, before_ref, here_ref, after_ref, keep)
        for at, value in enumerate(side):
            side_ref[at, rows, :] = value
        for at, value in enumerate(ahead_filter(taps, side)):
            filtered[at, rows, :] = value

    cos = twist_ref[0]
    sin = twist_ref[1]
    for start in range(0, count, CHUNK):
        spectra = forward_chunk(
            [filtered[start + f] for f in range(CHUNK)], ahead_rows_ref[...], ahead_lanes_ref[...], cos, sin
        )
        weights = weights_ref[start : start + CHUNK].reshape(CHUNK * ROWS, LANES)
        frames = backward_chunk(spectra * weights, back_lanes_ref[...], back_rows_ref[...], cos, sin)
        for f in range(CHUNK):
            out_ref[start + f] = frames[:, f * LANES : (f + 1) * LANES]


def second_kernel(
    keep_ref, before_ref, here_ref, after_ref, side_ref, taps_ref, weights_ref,
    ahead_rows_ref, ahead_lanes_ref, back_lanes_ref, back_rows_ref, twist_ref,
    out_ref, filtered, sums,
):
    count = here_ref.shape[0]
    keep = keep_ref[0]
    reach = taps_ref.shape[0] - 1
    sums[...] = jnp.zeros_like(sums)

    @pl.loop(0, ROWS // 8)
    def _(group):
        rows = pl.ds(pl.multiple_of(group * 8, 8), 8)
        taps = [taps_ref[p, rows, :] for p in range(reach + 1)]
        image = back_filter(rows, taps, before_ref, here_ref, after_ref, keep)
        side = [side_ref[at, rows, :] for at in range(reach + count)]
        image = [value + RIDGE * base for value, base in zip(image, side)]
        for at, value in enumerate(ahead_filter(taps, image)):
            filtered[at, rows, :] = value
        zero = sums[0]
        first, second, third = zero, sums[1], sums[2]
        for at in range(count):
            base = side[reach + at]
            value = image[reach + at]
            out_ref[group, at] = base
            out_ref[group, count + at] = value
            first = first + base * base
            second = second + base * value
            third = third + value * value
        sums[0] = first
        sums[1] = second
        sums[2] = third

    cos = twist_ref[0]
    sin = twist_ref[1]
    power = jnp.zeros((8, LANES), F32)
    for start in range(0, count, CHUNK):
        spectra = forward_chunk(
            [filtered[start + f] for f in range(CHUNK)], ahead_rows_ref[...], ahead_lanes_ref[...], cos, sin
        )
        weights = weights_ref[start : start + CHUNK].reshape(CHUNK * ROWS, LANES)
        weighted = spectra * weights
        power = power + jnp.sum((weighted * spectra).reshape(CHUNK * ROWS // 8, 8, LANES), 0)
        frames = backward_chunk(weighted, back_lanes_ref[...], back_rows_ref[...], cos, sin)
        for f in range(CHUNK):
            for group in range(ROWS // 8):
                out_ref[group, 2 * count + start + f] = frames[
                    group * 8 : (group + 1) * 8, f * LANES : (f + 1) * LANES
                ]
    totals = [jnp.sum(value, 0, keepdims=True) for value in (sums[0], sums[1], sums[2], power)]
    totals.append(jnp.zeros((4, LANES), F32))
    totals = jnp.concatenate(totals, 0)
    for group in range(ROWS // 8):
        out_ref[group, 3 * count] = totals


def last_kernel(place_ref, moved_ref, after_ref, sums_ref, taps_ref, solution_ref, residual_ref, kept, left):
    parts, slots = moved_ref.shape[:2]
    count = (slots - 1) // 3
    reach = taps_ref.shape[0] - 1
    rows = pl.ds(pl.multiple_of(place_ref[0] * 8, 8), 8)
    sums = sums_ref[0]
    for at in range(1, sums_ref.shape[0]):
        sums = sums + sums_ref[at]
    sums = jnp.sum(sums, 1, keepdims=True)
    norm, curve, square, power = (sums[at : at + 1] for at in range(4))
    cube = power + RIDGE * square
    step = norm / curve
    next_norm = step * step * square - norm
    grown = step * square / curve
    next_step = next_norm / (step * (step * cube - grown * square))
    to_base = step + next_step * grown
    to_image = -(next_step * step)
    image_rate = -(step + next_step * grown)
    cube_rate = next_step * step
    to_base, to_image, image_rate, cube_rate = (
        jnp.broadcast_to(value, (8, LANES)) for value in (to_base, to_image, image_rate, cube_rate)
    )
    taps = [taps_ref[p, rows, :] for p in range(reach + 1)]

    def finish(part, tail):
        frames = [moved_ref[part, 2 * count + t] for t in range(count)] + tail
        for at in range(count):
            base = moved_ref[part, at]
            image = moved_ref[part, count + at]
            again = weighted_sum(taps, frames[at : at + reach + 1]) + RIDGE * image
            here = pl.ds(pl.multiple_of((part * count + at) * 8, 8), 8)
            kept[here, :] = to_base * base + to_image * image
            left[here, :] = base + image_rate * image + cube_rate * again

    @pl.loop(0, parts - 1)
    def _(part):
        finish(part, [moved_ref[part + 1, 2 * count + t] for t in range(reach)])

    finish(parts - 1, [after_ref[t] for t in range(reach)])

    for block in range(parts * count // 8):
        for n1 in range(8):
            places = pl.ds(block * 64 + n1, 8, stride=8)
            columns = slice(n1 * LANES, (n1 + 1) * LANES)
            solution_ref[block * 8 : (block + 1) * 8, columns] = kept[places, :]
            residual_ref[block * 8 : (block + 1) * 8, columns] = left[places, :]


def shape(*dims):
    return jax.ShapeDtypeStruct(dims, F32)


def vmem(number):
    return [pl.BlockSpec(memory_space=pltpu.VMEM)] * number


SMEM = pl.BlockSpec(memory_space=pltpu.SMEM)


def local(observed_real, observed_imag, weights, taps):
    ahead_rows, ahead_lanes, back_lanes, back_rows, twist = dft_tables()
    count = weights.shape[0]
    reach = taps.shape[0] - 1
    parts = lax.axis_size("chan")
    devices = lax.axis_size("tm") * parts
    blocks = shape(count, ROWS, LANES)
    position = lax.axis_index(AXES)
    keep = (position > 0).astype(F32).reshape(1)
    place = lax.axis_index("chan").astype(jnp.int32).reshape(1)
    tables = (ahead_rows, ahead_lanes, back_lanes, back_rows, twist)

    def neighbours(block):
        later = [(i, i + 1) for i in range(devices - 1)]
        earlier = [(i + 1, i) for i in range(devices - 1)]
        return lax.ppermute(block, AXES, later), lax.ppermute(block, AXES, earlier)

    seeds = pl.pallas_call(
        seed_kernel,
        out_shape=blocks,
        in_specs=vmem(6),
        out_specs=vmem(1)[0],
        scratch_shapes=[pltpu.VMEM((count * ROWS, LANES), F32)],
        compiler_params=params(),
        name="seed",
    )(observed_real, observed_imag, weights, back_lanes, back_rows, twist)
    before, after = neighbours(seeds)
    weights, taps = pl.pallas_call(
        arrange_kernel,
        out_shape=(blocks, shape((reach + 1) * ROWS, LANES)),
        in_specs=vmem(2),
        out_specs=tuple(vmem(2)),
        scratch_shapes=[pltpu.VMEM((count * ROWS, LANES), F32)],
        compiler_params=params(),
        cost_estimate=pl.CostEstimate(flops=10**7, bytes_accessed=2 * 10**6, transcendentals=0),
        name="arrange",
    )(weights, taps)
    taps = taps.reshape(reach + 1, ROWS, LANES)

    images, side = pl.pallas_call(
        first_kernel,
        out_shape=(blocks, shape(reach + count, ROWS, LANES)),
        in_specs=[SMEM] + vmem(10),
        out_specs=tuple(vmem(2)),
        scratch_shapes=[pltpu.VMEM((count, ROWS, LANES), F32)],
        compiler_params=params(),
        name="first",
    )(keep, before, seeds, after, taps, weights, *tables)
    before, after = neighbours(images)

    outgoing = pl.pallas_call(
        second_kernel,
        out_shape=shape(parts, 3 * count + 1, 8, LANES),
        in_specs=[SMEM] + vmem(11),
        out_specs=vmem(1)[0],
        scratch_shapes=[
            pltpu.VMEM((count, ROWS, LANES), F32),
            pltpu.VMEM((3, 8, LANES), F32),
        ],
        compiler_params=params(),
        name="second",
    )(keep, before, images, after, side, taps, weights, *tables)

    moved = lax.all_to_all(outgoing, "chan", split_axis=0, concat_axis=0, tiled=True)
    groups = lax.axis_size("tm")
    after = lax.ppermute(
        moved[0, 2 * count : 3 * count], "tm", [(i + 1, i) for i in range(groups - 1)]
    )
    sums = jnp.sum(moved[:, 3 * count], 0)
    sums = lax.all_to_all(
        jnp.broadcast_to(sums, (groups, 8, LANES)), "tm", split_axis=0, concat_axis=0, tiled=True
    )
    return pl.pallas_call(
        last_kernel,
        out_shape=(shape(parts * count, 8 * LANES), shape(parts * count, 8 * LANES)),
        in_specs=[SMEM] + vmem(4),
        out_specs=tuple(vmem(2)),
        scratch_shapes=[
            pltpu.VMEM((parts * count * 8, LANES), F32),
            pltpu.VMEM((parts * count * 8, LANES), F32),
        ],
        compiler_params=params(),
        name="last",
    )(place, moved, after, sums, taps)


def solution(mesh):
    placed = (P(AXES, None), P(AXES, None), P(AXES, None), P())
    return jax.shard_map(
        local,
        mesh=mesh,
        in_specs=placed,
        out_specs=(P("tm", "chan"), P("tm", "chan")),
        check_vma=False,
    )
```

time: 598 us -> 105 us (0.18); the launches traced: 588 us -> 105 us
  blocking collectives: 291 us -> 29.1 us
  matrix products: 211 us -> 0 us
  local copies, waits for them, and re-layouts: 31.5 us -> 6.12 us
  starting transfers between devices: 15 us -> 34.1 us
  Pallas kernels: 0 us -> 15.6 us
  other arithmetic: 10.4 us -> 0.01 us
    psum x3 -> x0, blocking collectives: 237 us -> none  [the longest x2 158 us: squares(): return lax.psum(jnp.sum(vector * vector), ('tm', 'chan'))]
    dot_general x30 -> x0, matrix products: 211 us -> none  [the longest x5 104 us: transform(): jnp.dot(grid, big_sin, precision=HIGHEST).reshape(count, 8, inner_size)]
    all_to_all x4 -> x1, blocking collectives: 54.1 us -> 29.1 us  [local(): lax.all_to_all(outgoing, 'chan', split_axis=0, concat_axis=0, tiled=True)]
    pallas_call x0 -> x5, Pallas kernels: none -> 15.6 us  [the longest x1 5.57 us: local(): pl.pallas_call(first_kernel, out_shape=(blocks, shape(reach + count, ROWS...]
    reshape x11 -> x0, local copies, waits for them, and re-layouts: 15.1 us -> none  [the longest x3 8.16 us: transform(): jnp.swapaxes(frames.reshape(count, inner_size, 8), 1, 2)]
    all_to_all x5 -> x0, local copies, waits for them, and re-layouts: 14.2 us -> none  [the longest x3 9.07 us: to_samples(): lax.all_to_all(frames, 'chan', split_axis=1, concat_axis=0, tiled=True)]
    all_to_all x1, starting transfers between devices: 6.64 us -> 19.3 us  [local(): lax.all_to_all(jnp.broadcast_to(sums, (groups, 8, LANES)), 'tm', split_ax...]
    ppermute x5, starting transfers between devices: 8.4 us -> 14.8 us  [the longest x2 7.07 us: neighbours(): lax.ppermute(block, AXES, earlier)]
  transfers between devices with their start and end apart: 6 -> 6, of which waited for: 6 -> 6; matrix products, arithmetic and copies ran while one was open for 0% -> 0% of each run, Pallas kernels for 0% -> 1%
where the time goes in v1:
time: 105 us
  starting transfers between devices  34.1 us (32%)
  blocking collectives  29.1 us (28%)
  waiting for transfers between devices  19 us (18%)
  Pallas kernels  15.6 us (15%)
  local copies, waits for them, and re-layouts  6.12 us (6%)
    all_to_all x1, blocking collectives, local(): lax.all_to_all(outgoing, 'chan', split_axis=0, concat_axis=0, tiled=True)  29.1 us
    all_to_all x1, starting transfers between devices, local(): lax.all_to_all(jnp.broadcast_to(sums, (groups, 8, LANES)), 'tm', split_ax...  19.3 us
    ppermute x2, waiting for transfers between devices, neighbours(): lax.ppermute(block, AXES, earlier)  7.98 us
    ppermute x2, starting transfers between devices, neighbours(): lax.ppermute(block, AXES, earlier)  7.07 us
    ppermute x2, starting transfers between devices, neighbours(): lax.ppermute(block, AXES, later)  6.42 us
    pallas_call x1, Pallas kernels, local(): pl.pallas_call(first_kernel, out_shape=(blocks, shape(reach + count, ROWS...  5.57 us
    unnamed x26, local copies, waits for them, and re-layouts  5.44 us
    pallas_call x1, Pallas kernels, local(): pl.pallas_call(second_kernel, out_shape=shape(parts, 3 * count + 1, 8, LA...  4.73 us
  transfers between devices with their start and end apart: 6, of which 6 were waited for; matrix products, arithmetic and copies ran while one was open for 0% of the time, Pallas kernels for 1%

profile of v1, /device:TPU:1, one launch (start us, length us, event | category | flops | bytes accessed | tf_op | source)
XLA Modules:
  0.0 104.7 jit_solution(5836117679593391076)
XLA Ops:
  0.6 0.0 copy-start
  0.6 0.9 copy-done
  1.6 0.0 copy-start.2
  1.6 0.9 copy-done.2
  2.5 0.0 copy-start.5
  2.5 0.8 copy-done.5
  3.4 0.0 copy-start.8
  3.4 0.8 copy-done.8
  4.2 0.0 copy-start.11
  4.2 0.9 copy-done.11
  5.1 0.0 copy-start.12
  5.1 0.9 copy-done.12
  6.1 0.0 copy-start.3
  6.1 0.0 copy-start.7
  6.1 0.0 copy-start.1
  6.1 0.0 copy-start.4
  6.1 0.0 copy-start.6
  6.1 0.0 copy-start.9
  6.1 0.0 copy-start.10
  6.1 2.0 %seed.1.here_ref = f32[16,64,128]{2,1,0:T(8,128)S(1)} custom-call(f32[16,4096]{1,0:T(8,128)S(1)} %copy-done.11, f32[16,4096]{1,0:T(8,128)S(1)} %copy-done.12, f32[16,4096]{1,0:T(8,128)S(1)} %copy-done.2, bf16[384,256]{1,0:T(8,128)(2,1)S(1)} %copy-done, bf16[64,384]{1,0:T(8,128)(2,1)S(1)} %copy-done.8, f32[2,64,128]{2,1,0:T(8,128)S(1)} %copy-done.5), custom_call_target="tpu_custom_call" | custom-call | tf_op jit(solution)/shard_map/seed/pallas_call | solution.py:329
  8.1 5.1 %collective-permute-start.1 = (f32[16,64,128]{2,1,0:T(8,128)S(1)}, f32[16,64,128]{2,1,0:T(8,128)S(1)}, u32[]{:S(2)}, u32[]{:S(2)}) collective-permute-start(f32[16,64,128]{2,1,0:T(8,128)S(1)} %seed.1.here_ref), channel_id=1, source_target_pairs={{1,0},{2,1},{3,2},{4,3},{5,4},{6,5},{7,6},{8,7},{9,8},{10,9},{11,1... | collective-permute-start | bytes 1572872 | tf_op jit(solution)/shard_map/ppermute | solution.py:327
  13.3 1.9 %collective-permute-start = (f32[16,64,128]{2,1,0:T(8,128)S(1)}, f32[16,64,128]{2,1,0:T(8,128)}, u32[]{:S(2)}, u32[]{:S(2)}) collective-permute-start(f32[16,64,128]{2,1,0:T(8,128)S(1)} %seed.1.here_ref), channel_id=1, source_target_pairs={{0,1},{1,2},{2,3},{3,4},{4,5},{5,6},{6,7},{7,8},{8,9},{9,10},{10,1... | collective-permute-start | bytes 1572872 | tf_op jit(solution)/shard_map/ppermute | solution.py:327
  15.2 0.0 copy-done.3
  15.2 0.0 copy-done.7
  15.2 1.2 %arrange.1 = (f32[16,64,128]{2,1,0:T(8,128)S(1)}, f32[1024,128]{1,0:T(8,128)S(1)}) custom-call(f32[16,4096]{1,0:T(8,128)S(1)} %copy-done.3, f32[16,8192]{1,0:T(8,128)S(1)} %copy-done.7), custom_call_target="tpu_custom_call" | custom-call | flops 10000000 | bytes 2000000 | tf_op jit(solution)/shard_map/arrange/pallas_call | solution.py:339
  16.4 3.1 %collective-permute-done.1.after_ref = f32[16,64,128]{2,1,0:T(8,128)S(1)} collective-permute-done((f32[16,64,128]{2,1,0:T(8,128)S(1)}, f32[16,64,128]{2,1,0:T(8,128)S(1)}, u32[]{:S(2)}, u32[]{:S(2)}) %collective-permute-start.1) | collective-permute-done | bytes 524320 | tf_op jit(solution)/shard_map/ppermute | solution.py:327
  19.5 1.8 %collective-permute-done.before_ref = f32[16,64,128]{2,1,0:T(8,128)} collective-permute-done((f32[16,64,128]{2,1,0:T(8,128)S(1)}, f32[16,64,128]{2,1,0:T(8,128)}, u32[]{:S(2)}, u32[]{:S(2)}) %collective-permute-start) | collective-permute-done | bytes 524320 | tf_op jit(solution)/shard_map/ppermute | solution.py:327
  21.3 0.0 copy-done.1
  21.3 0.0 copy-done.4
  21.3 0.0 copy-done.6
  21.3 0.0 copy-done.9
  21.3 0.0 copy-done.10
  21.3 5.6 %first.1 = (f32[16,64,128]{2,1,0:T(8,128)S(1)}, f32[31,64,128]{2,1,0:T(8,128)S(1)}) custom-call(f32[1]{0:T(128)} %bitcast.1.keep_ref, f32[16,64,128]{2,1,0:T(8,128)} %collective-permute-done.before_ref, f32[16,64,128]{2,1,0:T(8,128)S(1)} %seed.1.here_ref, f32[16,64,128]{2,1,0:T(8,128)S(1)} %collective-permute-done.1.after_ref, f32[16,64,128]{2,1,0:T(8,128)S(1)} %bitcast.5, ...), custom_call_target="tpu_custom_call" | custom-call | tf_op jit(solution)/shard_map/first/pallas_call | solution.py:351
  26.9 1.9 %collective-permute-start.3 = (f32[16,64,128]{2,1,0:T(8,128)S(1)}, f32[16,64,128]{2,1,0:T(8,128)S(1)}, u32[]{:S(2)}, u32[]{:S(2)}) collective-permute-start(f32[16,64,128]{2,1,0:T(8,128)S(1)} %get-tuple-element.8.here_ref), channel_id=1, source_target_pairs={{1,0},{2,1},{3,2},{4,3},{5,4},{6,5},{7,6},{8,7},{9,8},{10,9},{11,1... | collective-permute-start | bytes 1572872 | tf_op jit(solution)/shard_map/ppermute | solution.py:327
  28.8 4.5 %collective-permute-start.2 = (f32[16,64,128]{2,1,0:T(8,128)S(1)}, f32[16,64,128]{2,1,0:T(8,128)S(1)}, u32[]{:S(2)}, u32[]{:S(2)}) collective-permute-start(f32[16,64,128]{2,1,0:T(8,128)S(1)} %get-tuple-element.8.here_ref), channel_id=1, source_target_pairs={{0,1},{1,2},{2,3},{3,4},{4,5},{5,6},{6,7},{7,8},{8,9},{9,10},{10,1... | collective-permute-start | bytes 1572872 | tf_op jit(solution)/shard_map/ppermute | solution.py:327
  33.4 4.9 %collective-permute-done.3.after_ref = f32[16,64,128]{2,1,0:T(8,128)S(1)} collective-permute-done((f32[16,64,128]{2,1,0:T(8,128)S(1)}, f32[16,64,128]{2,1,0:T(8,128)S(1)}, u32[]{:S(2)}, u32[]{:S(2)}) %collective-permute-start.3) | collective-permute-done | bytes 524320 | tf_op jit(solution)/shard_map/ppermute | solution.py:327
  38.3 1.2 %collective-permute-done.2.before_ref = f32[16,64,128]{2,1,0:T(8,128)S(1)} collective-permute-done((f32[16,64,128]{2,1,0:T(8,128)S(1)}, f32[16,64,128]{2,1,0:T(8,128)S(1)}, u32[]{:S(2)}, u32[]{:S(2)}) %collective-permute-start.2) | collective-permute-done | bytes 524320 | tf_op jit(solution)/shard_map/ppermute | solution.py:327
  39.5 4.7 %second.1 = f32[8,49,8,128]{3,2,1,0:T(8,128)S(1)} custom-call(f32[1]{0:T(128)} %bitcast.1.keep_ref, f32[16,64,128]{2,1,0:T(8,128)S(1)} %collective-permute-done.2.before_ref, f32[16,64,128]{2,1,0:T(8,128)S(1)} %get-tuple-element.8.here_ref, f32[16,64,128]{2,1,0:T(8,128)S(1)} %collective-permute-done.3.after_ref, ...), custom_call_target="tpu_custom_call" | custom-call | tf_op jit(solution)/shard_map/second/pallas_call | solution.py:362
  44.2 29.1 %all_to_all.10.moved_ref = f32[8,49,8,128]{3,2,1,0:T(8,128)S(1)} all-to-all(f32[8,49,8,128]{3,2,1,0:T(8,128)S(1)} %second.1), channel_id=1, replica_groups=mesh['tm'=32,'chan'=8] {'chan'}, dimensions={0} | all-to-all | bytes 3211264 | tf_op jit(solution)/shard_map/all_to_all | solution.py:375
  73.3 0.7 broadcast_in_dim.3
  74.0 19.3 %all-to-all-start.1 = ((f32[32,8,128]{2,1,0:T(8,128)}), f32[32,8,128]{2,1,0:T(8,128)S(1)}, u32[]{:S(2)}, u32[]{:S(2)}) async-start(f32[32,8,128]{2,1,0:T(8,128)} %broadcast_in_dim.3), calls=%async_computation.1 | async-start | bytes 262144 | tf_op jit(solution)/shard_map/all_to_all | solution.py:381
  93.2 1.3 %collective-permute-start.4 = (f32[16,8,128]{2,1,0:T(8,128)S(1)}, f32[16,8,128]{2,1,0:T(8,128)S(1)}, u32[]{:S(2)}, u32[]{:S(2)}) collective-permute-start(f32[16,8,128]{2,1,0:T(8,128)S(1)} %slice_bitcast_fusion), channel_id=1, source_target_pairs={{8,0},{16,8},{24,16},{32,24},{40,32},{48,40},{56,48},{64,56},{72,6... | collective-permute-start | bytes 196616 | tf_op jit(solution)/shard_map/ppermute | solution.py:377
  94.5 4.4 %collective-permute-done.4.after_ref = f32[16,8,128]{2,1,0:T(8,128)S(1)} collective-permute-done((f32[16,8,128]{2,1,0:T(8,128)S(1)}, f32[16,8,128]{2,1,0:T(8,128)S(1)}, u32[]{:S(2)}, u32[]{:S(2)}) %collective-permute-start.4) | collective-permute-done | bytes 65568 | tf_op jit(solution)/shard_map/ppermute | solution.py:377
  98.9 3.7 %all-to-all-done.1.sums_ref = f32[32,8,128]{2,1,0:T(8,128)S(1)} async-done(((f32[32,8,128]{2,1,0:T(8,128)}), f32[32,8,128]{2,1,0:T(8,128)S(1)}, u32[]{:S(2)}, u32[]{:S(2)}) %all-to-all-start.1) | async-done | bytes 131104 | tf_op jit(solution)/shard_map/all_to_all | solution.py:381
  102.6 2.1 %last.1 = (f32[128,1024]{1,0:T(8,128)}, f32[128,1024]{1,0:T(8,128)}) custom-call(s32[1]{0:T(128)} %bitcast.place_ref, f32[8,49,8,128]{3,2,1,0:T(8,128)S(1)} %all_to_all.10.moved_ref, f32[16,8,128]{2,1,0:T(8,128)S(1)} %collective-permute-done.4.after_ref, f32[32,8,128]{2,1,0:T(8,128)S(1)} %all-to-all-done.1.sums_ref, f32[16,64,128]{2,1,0:T(8,128)S(1)} %bitcast.7), custom_call_target="tpu_custom_call" | custom-call | tf_op jit(solution)/shard_map/last/pallas_call | solution.py:384
  (2 shorter events, 0.0 us)
Async XLA Ops:
  0.6 0.9 copy-start
  1.6 0.9 copy-start.2
  2.5 0.8 copy-start.5
  3.4 0.8 copy-start.8
  4.2 0.9 copy-start.11
  5.1 0.9 copy-start.12
  6.1 9.2 %copy-start.3 = (f32[16,4096]{1,0:T(8,128)S(1)}, f32[16,4096]{1,0:T(8,128)}, u32[]{:S(2)}) copy-start(f32[16,4096]{1,0:T(8,128)} %weights_ref.3) | copy-start | bytes 786436
  6.1 9.2 %copy-start.7 = (f32[16,8192]{1,0:T(8,128)S(1)}, f32[16,8192]{1,0:T(8,128)}, u32[]{:S(2)}) copy-start(f32[16,8192]{1,0:T(8,128)} %taps_ref.1) | copy-start | bytes 1572868
  6.1 15.3 %copy-start.1 = (bf16[384,256]{1,0:T(8,128)(2,1)S(1)}, bf16[384,256]{1,0:T(8,128)(2,1)}, u32[]{:S(2)}) copy-start(bf16[384,256]{1,0:T(8,128)(2,1)} %constant.25.clone.back_lanes_ref) | copy-start | bytes 589828
  6.1 15.3 %copy-start.4 = (bf16[768,128]{1,0:T(8,128)(2,1)S(1)}, bf16[768,128]{1,0:T(8,128)(2,1)}, u32[]{:S(2)}) copy-start(bf16[768,128]{1,0:T(8,128)(2,1)} %constant.29.clone.ahead_lanes_ref) | copy-start | bytes 589828
  6.1 15.3 %copy-start.6 = (f32[2,64,128]{2,1,0:T(8,128)S(1)}, f32[2,64,128]{2,1,0:T(8,128)}, u32[]{:S(2)}) copy-start(f32[2,64,128]{2,1,0:T(8,128)} %constant.27.clone.twist_ref) | copy-start | bytes 196612
  6.1 15.3 %copy-start.9 = (bf16[64,384]{1,0:T(8,128)(2,1)S(1)}, bf16[64,384]{1,0:T(8,128)(2,1)}, u32[]{:S(2)}) copy-start(bf16[64,384]{1,0:T(8,128)(2,1)} %constant.26.clone.back_rows_ref) | copy-start | bytes 147460
  6.1 15.3 %copy-start.10 = (bf16[128,192]{1,0:T(8,128)(2,1)S(1)}, bf16[128,192]{1,0:T(8,128)(2,1)}, u32[]{:S(2)}) copy-start(bf16[128,192]{1,0:T(8,128)(2,1)} %constant.28.clone.ahead_rows_ref) | copy-start | bytes 147460
  8.1 11.4 %collective-permute-start.1 = (f32[16,64,128]{2,1,0:T(8,128)S(1)}, f32[16,64,128]{2,1,0:T(8,128)S(1)}, u32[]{:S(2)}, u32[]{:S(2)}) collective-permute-start(f32[16,64,128]{2,1,0:T(8,128)S(1)} %seed.1.here_ref), channel_id=1, source_target_pairs={{1,0},{2,1},{3,2},{4,3},{5,4},{6,5},{7,6},{8,7},{9,8},{10,9},{11,1... | collective-permute-start | bytes 1572872 | tf_op jit(solution)/shard_map/ppermute | solution.py:327
  13.3 8.0 %collective-permute-start = (f32[16,64,128]{2,1,0:T(8,128)S(1)}, f32[16,64,128]{2,1,0:T(8,128)}, u32[]{:S(2)}, u32[]{:S(2)}) collective-permute-start(f32[16,64,128]{2,1,0:T(8,128)S(1)} %seed.1.here_ref), channel_id=1, source_target_pairs={{0,1},{1,2},{2,3},{3,4},{4,5},{5,6},{6,7},{7,8},{8,9},{9,10},{10,1... | collective-permute-start | bytes 1572872 | tf_op jit(solution)/shard_map/ppermute | solution.py:327
  26.9 11.4 %collective-permute-start.3 = (f32[16,64,128]{2,1,0:T(8,128)S(1)}, f32[16,64,128]{2,1,0:T(8,128)S(1)}, u32[]{:S(2)}, u32[]{:S(2)}) collective-permute-start(f32[16,64,128]{2,1,0:T(8,128)S(1)} %get-tuple-element.8.here_ref), channel_id=1, source_target_pairs={{1,0},{2,1},{3,2},{4,3},{5,4},{6,5},{7,6},{8,7},{9,8},{10,9},{11,1... | collective-permute-start | bytes 1572872 | tf_op jit(solution)/shard_map/ppermute | solution.py:327
  28.8 10.6 %collective-permute-start.2 = (f32[16,64,128]{2,1,0:T(8,128)S(1)}, f32[16,64,128]{2,1,0:T(8,128)S(1)}, u32[]{:S(2)}, u32[]{:S(2)}) collective-permute-start(f32[16,64,128]{2,1,0:T(8,128)S(1)} %get-tuple-element.8.here_ref), channel_id=1, source_target_pairs={{0,1},{1,2},{2,3},{3,4},{4,5},{5,6},{6,7},{7,8},{8,9},{9,10},{10,1... | collective-permute-start | bytes 1572872 | tf_op jit(solution)/shard_map/ppermute | solution.py:327
  74.0 28.6 %all-to-all-start.1 = ((f32[32,8,128]{2,1,0:T(8,128)}), f32[32,8,128]{2,1,0:T(8,128)S(1)}, u32[]{:S(2)}, u32[]{:S(2)}) async-start(f32[32,8,128]{2,1,0:T(8,128)} %broadcast_in_dim.3), calls=%async_computation.1 | async-start | bytes 262144 | tf_op jit(solution)/shard_map/all_to_all | solution.py:381
  93.2 5.7 %collective-permute-start.4 = (f32[16,8,128]{2,1,0:T(8,128)S(1)}, f32[16,8,128]{2,1,0:T(8,128)S(1)}, u32[]{:S(2)}, u32[]{:S(2)}) collective-permute-start(f32[16,8,128]{2,1,0:T(8,128)S(1)} %slice_bitcast_fusion), channel_id=1, source_target_pairs={{8,0},{16,8},{24,16},{32,24},{40,32},{48,40},{56,48},{64,56},{72,6... | collective-permute-start | bytes 196616 | tf_op jit(solution)/shard_map/ppermute | solution.py:377

commit v2 on v1

--- a/solution.py
+++ b/solution.py
@@ -19,8 +19,8 @@
 VMEM_BYTES = 40 * 1024 * 1024
 
 
-def params():
-    return pltpu.CompilerParams(vmem_limit_bytes=VMEM_BYTES)
+def params(limit=VMEM_BYTES):
+    return pltpu.CompilerParams(vmem_limit_bytes=limit)
 
 
 def halves(table):
@@ -100,8 +100,18 @@
     )
 
 
-def seed_kernel(real_ref, imag_ref, weights_ref, back_lanes_ref, back_rows_ref, twist_ref, out_ref, held):
+def seed_kernel(*refs):
+    sources, out_ref, places, held, semaphore = refs[:6], refs[6], refs[7:13], refs[13], refs[14]
+    copies = [
+        pltpu.make_async_copy(source, place, semaphore.at[at])
+        for at, (source, place) in enumerate(zip(sources, places))
+    ]
+    for copy in copies:
+        copy.start()
+    real_ref, imag_ref, weights_ref, back_lanes_ref, back_rows_ref, twist_ref = places
     count = real_ref.shape[0]
+    for copy in copies:
+        copy.wait()
     for j in range(32):
         columns = slice(j * LANES, (j + 1) * LANES)
         weights = weights_ref[:, columns]
@@ -148,11 +158,11 @@
     count = here_ref.shape[0]
     frames = [before_ref[t, rows, :] for t in range(count - reach, count)]
     frames += [here_ref[t, rows, :] for t in range(count)]
-    frames += [after_ref[t, rows, :] for t in range(reach)]
+    frames += [after_ref[t, rows, :] * keep[1] for t in range(reach)]
     result = []
     for at in range(reach + count):
         total = weighted_sum(taps, frames[at : at + reach + 1])
-        result.append(total * keep if at < reach else total)
+        result.append(total * keep[0] if at < reach else total)
     return result
 
 
@@ -170,7 +180,7 @@
     out_ref, side_ref, filtered,
 ):
     count = here_ref.shape[0]
-    keep = keep_ref[0]
+    keep = (keep_ref[0], keep_ref[1])
 
     @pl.loop(0, ROWS // 8)
     def _(group):
@@ -194,13 +204,26 @@
             out_ref[start + f] = frames[:, f * LANES : (f + 1) * LANES]
 
 
+def quarters():
+    return lax.broadcasted_iota(jnp.int32, (8, LANES), 1) // 32
+
+
+def pack(values):
+    packed = jnp.zeros((8, LANES), F32)
+    for at, value in enumerate(values):
+        value = value + pltpu.roll(value, 64, 1)
+        value = value + pltpu.roll(value, 32, 1)
+        packed = jnp.where(quarters() == at, value, packed)
+    return packed
+
+
 def second_kernel(
     keep_ref, before_ref, here_ref, after_ref, side_ref, taps_ref, weights_ref,
     ahead_rows_ref, ahead_lanes_ref, back_lanes_ref, back_rows_ref, twist_ref,
     out_ref, filtered, sums,
 ):
     count = here_ref.shape[0]
-    keep = keep_ref[0]
+    keep = (keep_ref[0], keep_ref[1])
     reach = taps_ref.shape[0] - 1
     sums[...] = jnp.zeros_like(sums)
 
@@ -213,8 +236,7 @@
         image = [value + RIDGE * base for value, base in zip(image, side)]
         for at, value in enumerate(ahead_filter(taps, image)):
             filtered[at, rows, :] = value
-        zero = sums[0]
-        first, second, third = zero, sums[1], sums[2]
+        first, second, third = sums[0], sums[1], sums[2]
         for at in range(count):
             base = side[reach + at]
             value = image[reach + at]
@@ -243,23 +265,26 @@
                 out_ref[group, 2 * count + start + f] = frames[
                     group * 8 : (group + 1) * 8, f * LANES : (f + 1) * LANES
                 ]
-    totals = [jnp.sum(value, 0, keepdims=True) for value in (sums[0], sums[1], sums[2], power)]
-    totals.append(jnp.zeros((4, LANES), F32))
-    totals = jnp.concatenate(totals, 0)
+    totals = pack([sums[0], sums[1], sums[2], power])
     for group in range(ROWS // 8):
         out_ref[group, 3 * count] = totals
 
 
-def last_kernel(place_ref, moved_ref, after_ref, sums_ref, taps_ref, solution_ref, residual_ref, kept, left):
-    parts, slots = moved_ref.shape[:2]
-    count = (slots - 1) // 3
+def last_kernel(
+    place_ref, keep_ref, moved_ref, after_ref, sums_ref, taps_ref,
+    solution_ref, residual_ref, kept, left,
+):
+    parts = moved_ref.shape[0]
+    count = (moved_ref.shape[1] - 1) // 3
     reach = taps_ref.shape[0] - 1
     rows = pl.ds(pl.multiple_of(place_ref[0] * 8, 8), 8)
-    sums = sums_ref[0]
-    for at in range(1, sums_ref.shape[0]):
-        sums = sums + sums_ref[at]
-    sums = jnp.sum(sums, 1, keepdims=True)
-    norm, curve, square, power = (sums[at : at + 1] for at in range(4))
+    sums = sums_ref[0:8]
+    for at in range(8, sums_ref.shape[0], 8):
+        sums = sums + sums_ref[at : at + 8]
+    norm, curve, square, power = (
+        jnp.sum(jnp.sum(jnp.where(quarters() == at, sums, 0.0), 1, keepdims=True), 0, keepdims=True)
+        for at in range(4)
+    )
     cube = power + RIDGE * square
     step = norm / curve
     next_norm = step * step * square - norm
@@ -288,7 +313,7 @@
     def _(part):
         finish(part, [moved_ref[part + 1, 2 * count + t] for t in range(reach)])
 
-    finish(parts - 1, [after_ref[t] for t in range(reach)])
+    finish(parts - 1, [after_ref[t] * keep_ref[0] for t in range(reach)])
 
     for block in range(parts * count // 8):
         for n1 in range(8):
@@ -316,25 +341,32 @@
     parts = lax.axis_size("chan")
     devices = lax.axis_size("tm") * parts
     blocks = shape(count, ROWS, LANES)
+    groups = lax.axis_size("tm")
     position = lax.axis_index(AXES)
-    keep = (position > 0).astype(F32).reshape(1)
+    keep = jnp.stack([position > 0, position < devices - 1]).astype(F32)
     place = lax.axis_index("chan").astype(jnp.int32).reshape(1)
+    keep_group = (lax.axis_index("tm") < groups - 1).astype(F32).reshape(1)
     tables = (ahead_rows, ahead_lanes, back_lanes, back_rows, twist)
 
     def neighbours(block):
-        later = [(i, i + 1) for i in range(devices - 1)]
-        earlier = [(i + 1, i) for i in range(devices - 1)]
+        later = [(i, (i + 1) % devices) for i in range(devices)]
+        earlier = [((i + 1) % devices, i) for i in range(devices)]
         return lax.ppermute(block, AXES, later), lax.ppermute(block, AXES, earlier)
 
+    def exchange(value, axis):
+        return lax.all_to_all(value, axis, split_axis=0, concat_axis=0, tiled=True)
+
+    seed_inputs = (observed_real, observed_imag, weights, back_lanes, back_rows, twist)
     seeds = pl.pallas_call(
         seed_kernel,
         out_shape=blocks,
-        in_specs=vmem(6),
+        in_specs=[pl.BlockSpec(memory_space=pltpu.HBM)] * 6,
         out_specs=vmem(1)[0],
-        scratch_shapes=[pltpu.VMEM((count * ROWS, LANES), F32)],
-        compiler_params=params(),
+        scratch_shapes=[pltpu.VMEM(value.shape, value.dtype) for value in seed_inputs]
+        + [pltpu.VMEM((count * ROWS, LANES), F32), pltpu.SemaphoreType.DMA((6,))],
+        compiler_params=params(62 * 1024 * 1024),
         name="seed",
-    )(observed_real, observed_imag, weights, back_lanes, back_rows, twist)
+    )(*seed_inputs)
     before, after = neighbours(seeds)
     weights, taps = pl.pallas_call(
         arrange_kernel,
@@ -372,19 +404,16 @@
         name="second",
     )(keep, before, images, after, side, taps, weights, *tables)
 
-    moved = lax.all_to_all(outgoing, "chan", split_axis=0, concat_axis=0, tiled=True)
-    groups = lax.axis_size("tm")
+    moved = exchange(outgoing, "chan")
     after = lax.ppermute(
-        moved[0, 2 * count : 3 * count], "tm", [(i + 1, i) for i in range(groups - 1)]
-    )
-    sums = jnp.sum(moved[:, 3 * count], 0)
-    sums = lax.all_to_all(
-        jnp.broadcast_to(sums, (groups, 8, LANES)), "tm", split_axis=0, concat_axis=0, tiled=True
-    )
+        moved[0, 2 * count : 3 * count], "tm", [((i + 1) % groups, i) for i in range(groups)]
+    )
+    sums = jnp.sum(moved[:, 3 * count], (0, 1))
+    sums = exchange(jnp.broadcast_to(sums, (groups, LANES)), "tm")
     return pl.pallas_call(
         last_kernel,
         out_shape=(shape(parts * count, 8 * LANES), shape(parts * count, 8 * LANES)),
-        in_specs=[SMEM] + vmem(4),
+        in_specs=[SMEM, SMEM] + vmem(4),
         out_specs=tuple(vmem(2)),
         scratch_shapes=[
             pltpu.VMEM((parts * count * 8, LANES), F32),
@@ -392,7 +421,7 @@
         ],
         compiler_params=params(),
         name="last",
-    )(place, moved, after, sums, taps)
+    )(place, keep_group, moved, after, sums, taps)
 
 
 def solution(mesh):

time: 105 us -> 95.7 us (0.911)
  starting transfers between devices: 34.1 us -> 20 us
  local copies, waits for them, and re-layouts: 6.12 us -> 1.7 us
  waiting for transfers between devices: 19 us -> 23.2 us
  blocking collectives: 29.1 us -> 32 us
  Pallas kernels: 15.6 us -> 17.7 us
    all_to_all x1, starting transfers between devices: 19.3 us -> 4 us  [exchange(): return lax.all_to_all(value, axis, split_axis=0, concat_axis=0, tiled=True)]
    ppermute x2, starting transfers between devices: 7.07 us -> 16 us  [neighbours(): lax.ppermute(block, AXES, earlier)]
    ppermute x2, starting transfers between devices: 6.42 us -> 0.01 us  [neighbours(): lax.ppermute(block, AXES, later)]
    ppermute x2, waiting for transfers between devices: 3 us -> 7.97 us  [neighbours(): lax.ppermute(block, AXES, later)]
    all_to_all x1, waiting for transfers between devices: 3.68 us -> 8.5 us  [exchange(): return lax.all_to_all(value, axis, split_axis=0, concat_axis=0, tiled=True)]
    unnamed x26 -> x16, local copies, waits for them, and re-layouts: 5.44 us -> 1.08 us
    ppermute x1, waiting for transfers between devices: 4.36 us -> 0.01 us  [local(): lax.ppermute(moved[0, 2 * count:3 * count], 'tm', [((i + 1) % groups, i)...]
    all_to_all x1, blocking collectives: 29.1 us -> 32 us  [exchange(): return lax.all_to_all(value, axis, split_axis=0, concat_axis=0, tiled=True)]
  transfers between devices with their start and end apart: 6 -> 6, of which waited for: 6 -> 5; matrix products, arithmetic and copies ran while one was open for 0% -> 1% of each run, Pallas kernels for 1% -> 1%
where the time goes in v2:
time: 95.7 us; the launch traced here: 95.5 us
  blocking collectives  32 us (33%)
  waiting for transfers between devices  23.2 us (24%)
  starting transfers between devices  20 us (21%)
  Pallas kernels  17.7 us (18%)
  local copies, waits for them, and re-layouts  1.7 us (2%)
    all_to_all x1, blocking collectives, exchange(): return lax.all_to_all(value, axis, split_axis=0, concat_axis=0, tiled=True)  32 us
    ppermute x2, starting transfers between devices, neighbours(): lax.ppermute(block, AXES, earlier)  16 us
    all_to_all x1, waiting for transfers between devices, exchange(): return lax.all_to_all(value, axis, split_axis=0, concat_axis=0, tiled=True)  8.5 us
    ppermute x2, waiting for transfers between devices, neighbours(): lax.ppermute(block, AXES, later)  7.97 us
    ppermute x2, waiting for transfers between devices, neighbours(): lax.ppermute(block, AXES, earlier)  6.68 us
    pallas_call x1, Pallas kernels, local(): pl.pallas_call(second_kernel, out_shape=shape(parts, 3 * count + 1, 8, LA...  5.31 us
    pallas_call x1, Pallas kernels, local(): pl.pallas_call(first_kernel, out_shape=(blocks, shape(reach + count, ROWS...  5.07 us
    pallas_call x1, Pallas kernels, local(): pl.pallas_call(seed_kernel, out_shape=blocks, in_specs=[pl.BlockSpec(memo...  4.15 us
  transfers between devices with their start and end apart: 6, of which 5 were waited for; matrix products, arithmetic and copies ran while one was open for 1% of the time, Pallas kernels for 1%

profile of v2, /device:TPU:1, one launch (start us, length us, event | category | flops | bytes accessed | tf_op | source)
XLA Modules:
  0.0 95.5 jit_solution(14676095545638446946)
XLA Ops:
  0.6 0.0 copy-start.4
  0.6 0.0 copy-start.6
  0.7 0.0 copy-start.1
  0.7 0.0 copy-start.3
  0.7 0.0 copy-start.7
  0.7 0.0 copy-start.2
  0.7 0.0 copy-start.5
  0.7 4.2 %seed.1.here_ref = f32[16,64,128]{2,1,0:T(8,128)} custom-call(f32[16,4096]{1,0:T(8,128)} %refs_0_.1, f32[16,4096]{1,0:T(8,128)} %refs_1_.1, f32[16,4096]{1,0:T(8,128)} %weights_ref.1, bf16[384,256]{1,0:T(8,128)(2,1)} %constant.29.clone.refs_3_.back_lanes_ref, bf16[64,384]{1,0:T(8,128)(2,1)} %constant.30.clone.refs_4_.back_rows_ref, ...), custom_call_target="tpu_custom_call" | custom-call | tf_op jit(solution)/shard_map/seed/pallas_call | solution.py:360
  4.9 3.3 %collective-permute-start.1 = (f32[16,64,128]{2,1,0:T(8,128)}, f32[16,64,128]{2,1,0:T(8,128)S(1)}, u32[]{:S(2)}, u32[]{:S(2)}) collective-permute-start(f32[16,64,128]{2,1,0:T(8,128)} %seed.1.here_ref), channel_id=1, source_target_pairs={{1,0},{2,1},{3,2},{4,3},{5,4},{6,5},{7,6},{8,7},{9,8},{10,9},{11,1... | collective-permute-start | bytes 1572872 | tf_op jit(solution)/shard_map/ppermute | solution.py:354
  8.2 0.0 collective-permute-start
  8.2 0.0 copy-done.2
  8.2 0.0 copy-done.5
  8.2 1.2 %arrange.1 = (f32[16,64,128]{2,1,0:T(8,128)S(1)}, f32[1024,128]{1,0:T(8,128)S(1)}) custom-call(f32[16,4096]{1,0:T(8,128)S(1)} %copy-done.2, f32[16,8192]{1,0:T(8,128)S(1)} %copy-done.5), custom_call_target="tpu_custom_call" | custom-call | flops 10000000 | bytes 2000000 | tf_op jit(solution)/shard_map/arrange/pallas_call | solution.py:371
  9.4 0.1 add_convert_fusion.keep_ref
  9.5 5.2 %collective-permute-done.1.after_ref = f32[16,64,128]{2,1,0:T(8,128)S(1)} collective-permute-done((f32[16,64,128]{2,1,0:T(8,128)}, f32[16,64,128]{2,1,0:T(8,128)S(1)}, u32[]{:S(2)}, u32[]{:S(2)}) %collective-permute-start.1) | collective-permute-done | bytes 524320 | tf_op jit(solution)/shard_map/ppermute | solution.py:354
  14.6 3.4 %collective-permute-done.before_ref = f32[16,64,128]{2,1,0:T(8,128)S(1)} collective-permute-done((f32[16,64,128]{2,1,0:T(8,128)}, f32[16,64,128]{2,1,0:T(8,128)S(1)}, u32[]{:S(2)}, u32[]{:S(2)}) %collective-permute-start) | collective-permute-done | bytes 524320 | tf_op jit(solution)/shard_map/ppermute | solution.py:354
  18.0 0.0 copy-done.4
  18.0 0.0 copy-done.6
  18.0 0.0 copy-done.1
  18.0 0.0 copy-done.3
  18.0 0.0 copy-done.7
  18.0 0.0 copy-start
  18.1 1.0 %copy-done = f32[16,64,128]{2,1,0:T(8,128)S(1)} copy-done((f32[16,64,128]{2,1,0:T(8,128)S(1)}, f32[16,64,128]{2,1,0:T(8,128)}, u32[]{:S(2)}) %copy-start) | copy-done | bytes 524312
  19.1 5.1 %first.1 = (f32[16,64,128]{2,1,0:T(8,128)S(1)}, f32[31,64,128]{2,1,0:T(8,128)S(1)}) custom-call(f32[2]{0:T(128)S(1)} %add_convert_fusion.keep_ref, f32[16,64,128]{2,1,0:T(8,128)S(1)} %collective-permute-done.before_ref, f32[16,64,128]{2,1,0:T(8,128)S(1)} %copy-done, f32[16,64,128]{2,1,0:T(8,128)S(1)} %collective-permute-done.1.after_ref, ...), custom_call_target="tpu_custom_call" | custom-call | tf_op jit(solution)/shard_map/first/pallas_call | solution.py:383
  24.2 12.7 %collective-permute-start.3 = (f32[16,64,128]{2,1,0:T(8,128)S(1)}, f32[16,64,128]{2,1,0:T(8,128)S(1)}, u32[]{:S(2)}, u32[]{:S(2)}) collective-permute-start(f32[16,64,128]{2,1,0:T(8,128)S(1)} %get-tuple-element.8.here_ref), channel_id=1, source_target_pairs={{1,0},{2,1},{3,2},{4,3},{5,4},{6,5},{7,6},{8,7},{9,8},{10,9},{11,1... | collective-permute-start | bytes 1572872 | tf_op jit(solution)/shard_map/ppermute | solution.py:354
  36.9 0.0 collective-permute-start.2
  36.9 1.5 %collective-permute-done.3.after_ref = f32[16,64,128]{2,1,0:T(8,128)S(1)} collective-permute-done((f32[16,64,128]{2,1,0:T(8,128)S(1)}, f32[16,64,128]{2,1,0:T(8,128)S(1)}, u32[]{:S(2)}, u32[]{:S(2)}) %collective-permute-start.3) | collective-permute-done | bytes 524320 | tf_op jit(solution)/shard_map/ppermute | solution.py:354
  38.4 4.6 %collective-permute-done.2.before_ref = f32[16,64,128]{2,1,0:T(8,128)S(1)} collective-permute-done((f32[16,64,128]{2,1,0:T(8,128)S(1)}, f32[16,64,128]{2,1,0:T(8,128)S(1)}, u32[]{:S(2)}, u32[]{:S(2)}) %collective-permute-start.2) | collective-permute-done | bytes 524320 | tf_op jit(solution)/shard_map/ppermute | solution.py:354
  43.0 5.3 %second.1 = f32[8,49,8,128]{3,2,1,0:T(8,128)S(1)} custom-call(f32[2]{0:T(128)S(1)} %add_convert_fusion.keep_ref, f32[16,64,128]{2,1,0:T(8,128)S(1)} %collective-permute-done.2.before_ref, f32[16,64,128]{2,1,0:T(8,128)S(1)} %get-tuple-element.8.here_ref, f32[16,64,128]{2,1,0:T(8,128)S(1)} %collective-permute-done.3.after_ref, ...), custom_call_target="tpu_custom_call" | custom-call | tf_op jit(solution)/shard_map/second/pallas_call | solution.py:394
  48.3 32.0 %all_to_all.13.moved_ref = f32[8,49,8,128]{3,2,1,0:T(8,128)S(1)} all-to-all(f32[8,49,8,128]{3,2,1,0:T(8,128)S(1)} %second.1), channel_id=1, replica_groups=mesh['tm'=32,'chan'=8] {'chan'}, dimensions={0} | all-to-all | bytes 3211264 | tf_op jit(solution)/shard_map/all_to_all | solution.py:357
  80.3 0.0 collective-permute-start.4
  80.3 0.6 broadcast_in_dim.3
  81.0 4.0 %all-to-all-start.1 = ((f32[32,1,128]{2,1,0:T(1,128)}), f32[32,1,128]{2,1,0:T(1,128)S(1)}, u32[]{:S(2)}, u32[]{:S(2)}) async-start(f32[32,1,128]{2,1,0:T(1,128)} %broadcast_in_dim.3), calls=%async_computation.1 | async-start | bytes 32768 | tf_op jit(solution)/shard_map/all_to_all | solution.py:357
  85.0 8.5 %all-to-all-done.1 = f32[32,1,128]{2,1,0:T(1,128)S(1)} async-done(((f32[32,1,128]{2,1,0:T(1,128)}), f32[32,1,128]{2,1,0:T(1,128)S(1)}, u32[]{:S(2)}, u32[]{:S(2)}) %all-to-all-start.1) | async-done | bytes 16416 | tf_op jit(solution)/shard_map/all_to_all | solution.py:357
  93.5 0.0 collective-permute-done.4.after_ref
  93.5 2.0 %last.1 = (f32[128,1024]{1,0:T(8,128)}, f32[128,1024]{1,0:T(8,128)}) custom-call(s32[1]{0:T(128)} %bitcast.place_ref, f32[1]{0:T(128)} %bitcast.1.keep_ref, f32[8,49,8,128]{3,2,1,0:T(8,128)S(1)} %all_to_all.13.moved_ref, f32[16,8,128]{2,1,0:T(8,128)S(1)} %collective-permute-done.4.after_ref, f32[32,128]{1,0:T(8,128)S(1)} %bitcast.11, f32[16,64,128]{2,1,0:T(8,128)S(1)} %bitcast.10), custom_call_target="tpu_custom_call" | custom-call | tf_op jit(solution)/shard_map/last/pallas_call | solution.py:413
  (2 shorter events, 0.0 us)
Async XLA Ops:
  0.6 17.4 %copy-start.4 = (f32[2,64,128]{2,1,0:T(8,128)S(1)}, f32[2,64,128]{2,1,0:T(8,128)}, u32[]{:S(2)}) copy-start(f32[2,64,128]{2,1,0:T(8,128)} %constant.31.clone.refs_5_.twist_ref) | copy-start | bytes 196612
  0.6 17.4 %copy-start.6 = (bf16[64,384]{1,0:T(8,128)(2,1)S(1)}, bf16[64,384]{1,0:T(8,128)(2,1)}, u32[]{:S(2)}) copy-start(bf16[64,384]{1,0:T(8,128)(2,1)} %constant.30.clone.refs_4_.back_rows_ref) | copy-start | bytes 147460
  0.7 17.4 %copy-start.1 = (bf16[384,256]{1,0:T(8,128)(2,1)S(1)}, bf16[384,256]{1,0:T(8,128)(2,1)}, u32[]{:S(2)}) copy-start(bf16[384,256]{1,0:T(8,128)(2,1)} %constant.29.clone.refs_3_.back_lanes_ref) | copy-start | bytes 589828
  0.7 17.4 %copy-start.3 = (bf16[768,128]{1,0:T(8,128)(2,1)S(1)}, bf16[768,128]{1,0:T(8,128)(2,1)}, u32[]{:S(2)}) copy-start(bf16[768,128]{1,0:T(8,128)(2,1)} %constant.33.clone.ahead_lanes_ref) | copy-start | bytes 589828
  0.7 17.4 %copy-start.7 = (bf16[128,192]{1,0:T(8,128)(2,1)S(1)}, bf16[128,192]{1,0:T(8,128)(2,1)}, u32[]{:S(2)}) copy-start(bf16[128,192]{1,0:T(8,128)(2,1)} %constant.32.clone.ahead_rows_ref) | copy-start | bytes 147460
  0.7 7.5 %copy-start.2 = (f32[16,4096]{1,0:T(8,128)S(1)}, f32[16,4096]{1,0:T(8,128)}, u32[]{:S(2)}) copy-start(f32[16,4096]{1,0:T(8,128)} %weights_ref.1) | copy-start | bytes 786436
  0.7 7.5 %copy-start.5 = (f32[16,8192]{1,0:T(8,128)S(1)}, f32[16,8192]{1,0:T(8,128)}, u32[]{:S(2)}) copy-start(f32[16,8192]{1,0:T(8,128)} %taps_ref.1) | copy-start | bytes 1572868
  4.9 9.8 %collective-permute-start.1 = (f32[16,64,128]{2,1,0:T(8,128)}, f32[16,64,128]{2,1,0:T(8,128)S(1)}, u32[]{:S(2)}, u32[]{:S(2)}) collective-permute-start(f32[16,64,128]{2,1,0:T(8,128)} %seed.1.here_ref), channel_id=1, source_target_pairs={{1,0},{2,1},{3,2},{4,3},{5,4},{6,5},{7,6},{8,7},{9,8},{10,9},{11,1... | collective-permute-start | bytes 1572872 | tf_op jit(solution)/shard_map/ppermute | solution.py:354
  8.2 9.8 %collective-permute-start = (f32[16,64,128]{2,1,0:T(8,128)}, f32[16,64,128]{2,1,0:T(8,128)S(1)}, u32[]{:S(2)}, u32[]{:S(2)}) collective-permute-start(f32[16,64,128]{2,1,0:T(8,128)} %seed.1.here_ref), channel_id=1, source_target_pairs={{0,1},{1,2},{2,3},{3,4},{4,5},{5,6},{6,7},{7,8},{8,9},{9,10},{10,1... | collective-permute-start | bytes 1572872 | tf_op jit(solution)/shard_map/ppermute | solution.py:354
  18.0 1.0 %copy-start = (f32[16,64,128]{2,1,0:T(8,128)S(1)}, f32[16,64,128]{2,1,0:T(8,128)}, u32[]{:S(2)}) copy-start(f32[16,64,128]{2,1,0:T(8,128)} %seed.1.here_ref) | copy-start | bytes 1572868
  24.2 14.2 %collective-permute-start.3 = (f32[16,64,128]{2,1,0:T(8,128)S(1)}, f32[16,64,128]{2,1,0:T(8,128)S(1)}, u32[]{:S(2)}, u32[]{:S(2)}) collective-permute-start(f32[16,64,128]{2,1,0:T(8,128)S(1)} %get-tuple-element.8.here_ref), channel_id=1, source_target_pairs={{1,0},{2,1},{3,2},{4,3},{5,4},{6,5},{7,6},{8,7},{9,8},{10,9},{11,1... | collective-permute-start | bytes 1572872 | tf_op jit(solution)/shard_map/ppermute | solution.py:354
  36.9 6.1 %collective-permute-start.2 = (f32[16,64,128]{2,1,0:T(8,128)S(1)}, f32[16,64,128]{2,1,0:T(8,128)S(1)}, u32[]{:S(2)}, u32[]{:S(2)}) collective-permute-start(f32[16,64,128]{2,1,0:T(8,128)S(1)} %get-tuple-element.8.here_ref), channel_id=1, source_target_pairs={{0,1},{1,2},{2,3},{3,4},{4,5},{5,6},{6,7},{7,8},{8,9},{9,10},{10,1... | collective-permute-start | bytes 1572872 | tf_op jit(solution)/shard_map/ppermute | solution.py:354
  80.3 13.2 %collective-permute-start.4 = (f32[16,8,128]{2,1,0:T(8,128)S(1)}, f32[16,8,128]{2,1,0:T(8,128)S(1)}, u32[]{:S(2)}, u32[]{:S(2)}) collective-permute-start(f32[16,8,128]{2,1,0:T(8,128)S(1)} %slice_bitcast_fusion), channel_id=1, source_target_pairs={{8,0},{16,8},{24,16},{32,24},{40,32},{48,40},{56,48},{64,56},{72,6... | collective-permute-start | bytes 196616 | tf_op jit(solution)/shard_map/ppermute | solution.py:408
  81.0 12.5 %all-to-all-start.1 = ((f32[32,1,128]{2,1,0:T(1,128)}), f32[32,1,128]{2,1,0:T(1,128)S(1)}, u32[]{:S(2)}, u32[]{:S(2)}) async-start(f32[32,1,128]{2,1,0:T(1,128)} %broadcast_in_dim.3), calls=%async_computation.1 | async-start | bytes 32768 | tf_op jit(solution)/shard_map/all_to_all | solution.py:357

commit v3 on v2

--- a/solution.py
+++ b/solution.py
@@ -153,12 +153,17 @@
     return total
 
 
-def back_filter(rows, taps, before_ref, here_ref, after_ref, keep):
+def back_filter(rows, taps, inside_ref, here_ref, across_ref, keep):
     reach = len(taps) - 1
     count = here_ref.shape[0]
-    frames = [before_ref[t, rows, :] for t in range(count - reach, count)]
+    odd = jnp.full((8, LANES), keep[2]) > 0.5
+    frames = [
+        jnp.where(odd, inside_ref[t, rows, :], across_ref[t, rows, :]) for t in range(count - reach, count)
+    ]
     frames += [here_ref[t, rows, :] for t in range(count)]
-    frames += [after_ref[t, rows, :] * keep[1] for t in range(reach)]
+    frames += [
+        jnp.where(odd, across_ref[t, rows, :], inside_ref[t, rows, :]) * keep[1] for t in range(reach)
+    ]
     result = []
     for at in range(reach + count):
         total = weighted_sum(taps, frames[at : at + reach + 1])
@@ -175,18 +180,18 @@
 
 
 def first_kernel(
-    keep_ref, before_ref, here_ref, after_ref, taps_ref, weights_ref,
+    keep_ref, inside_ref, here_ref, across_ref, taps_ref, weights_ref,
     ahead_rows_ref, ahead_lanes_ref, back_lanes_ref, back_rows_ref, twist_ref,
     out_ref, side_ref, filtered,
 ):
     count = here_ref.shape[0]
-    keep = (keep_ref[0], keep_ref[1])
+    keep = (keep_ref[0], keep_ref[1], keep_ref[2])
 
     @pl.loop(0, ROWS // 8)
     def _(group):
         rows = pl.ds(pl.multiple_of(group * 8, 8), 8)
         taps = [taps_ref[p, rows, :] for p in range(taps_ref.shape[0])]
-        side = back_filter(rows, taps, before_ref, here_ref, after_ref, keep)
+        side = back_filter(rows, taps, inside_ref, here_ref, across_ref, keep)
         for at, value in enumerate(side):
             side_ref[at, rows, :] = value
         for at, value in enumerate(ahead_filter(taps, side)):
@@ -218,12 +223,12 @@
 
 
 def second_kernel(
-    keep_ref, before_ref, here_ref, after_ref, side_ref, taps_ref, weights_ref,
+    keep_ref, inside_ref, here_ref, across_ref, side_ref, taps_ref, weights_ref,
     ahead_rows_ref, ahead_lanes_ref, back_lanes_ref, back_rows_ref, twist_ref,
     out_ref, filtered, sums,
 ):
     count = here_ref.shape[0]
-    keep = (keep_ref[0], keep_ref[1])
+    keep = (keep_ref[0], keep_ref[1], keep_ref[2])
     reach = taps_ref.shape[0] - 1
     sums[...] = jnp.zeros_like(sums)
 
@@ -231,7 +236,7 @@
     def _(group):
         rows = pl.ds(pl.multiple_of(group * 8, 8), 8)
         taps = [taps_ref[p, rows, :] for p in range(reach + 1)]
-        image = back_filter(rows, taps, before_ref, here_ref, after_ref, keep)
+        image = back_filter(rows, taps, inside_ref, here_ref, across_ref, keep)
         side = [side_ref[at, rows, :] for at in range(reach + count)]
         image = [value + RIDGE * base for value, base in zip(image, side)]
         for at, value in enumerate(ahead_filter(taps, image)):
@@ -343,15 +348,15 @@
     blocks = shape(count, ROWS, LANES)
     groups = lax.axis_size("tm")
     position = lax.axis_index(AXES)
-    keep = jnp.stack([position > 0, position < devices - 1]).astype(F32)
+    keep = jnp.stack([position > 0, position < devices - 1, position % 2 == 1]).astype(F32)
     place = lax.axis_index("chan").astype(jnp.int32).reshape(1)
     keep_group = (lax.axis_index("tm") < groups - 1).astype(F32).reshape(1)
     tables = (ahead_rows, ahead_lanes, back_lanes, back_rows, twist)
 
     def neighbours(block):
-        later = [(i, (i + 1) % devices) for i in range(devices)]
-        earlier = [((i + 1) % devices, i) for i in range(devices)]
-        return lax.ppermute(block, AXES, later), lax.ppermute(block, AXES, earlier)
+        inside = [(i, i ^ 1) for i in range(devices)]
+        across = [(i, min(max(((i + 1) ^ 1) - 1, 0), devices - 1)) for i in range(devices)]
+        return lax.ppermute(block, AXES, inside), lax.ppermute(block, AXES, across)
 
     def exchange(value, axis):
         return lax.all_to_all(value, axis, split_axis=0, concat_axis=0, tiled=True)
@@ -367,7 +372,7 @@
         compiler_params=params(62 * 1024 * 1024),
         name="seed",
     )(*seed_inputs)
-    before, after = neighbours(seeds)
+    inside, across = neighbours(seeds)
     weights, taps = pl.pallas_call(
         arrange_kernel,
         out_shape=(blocks, shape((reach + 1) * ROWS, LANES)),
@@ -388,8 +393,8 @@
         scratch_shapes=[pltpu.VMEM((count, ROWS, LANES), F32)],
         compiler_params=params(),
         name="first",
-    )(keep, before, seeds, after, taps, weights, *tables)
-    before, after = neighbours(images)
+    )(keep, inside, seeds, across, taps, weights, *tables)
+    inside, across = neighbours(images)
 
     outgoing = pl.pallas_call(
         second_kernel,
@@ -402,7 +407,7 @@
         ],
         compiler_params=params(),
         name="second",
-    )(keep, before, images, after, side, taps, weights, *tables)
+    )(keep, inside, images, across, side, taps, weights, *tables)
 
     moved = exchange(outgoing, "chan")
     after = lax.ppermute(

time: 95.7 us -> 97.3 us (1.017)
  starting transfers between devices: 20 us -> 26.2 us
  waiting for transfers between devices: 23.2 us -> 20.6 us
  blocking collectives: 32 us -> 29.7 us
    ppermute x4, starting transfers between devices: 16 us -> 8.67 us  [the longest x2 8.15 us: neighbours(): lax.ppermute(block, AXES, across)]
    ppermute x1, starting transfers between devices: 0.01 us -> 7.15 us  [local(): lax.ppermute(moved[0, 2 * count:3 * count], 'tm', [((i + 1) % groups, i)...]
    all_to_all x1, starting transfers between devices: 4 us -> 10.3 us  [exchange(): return lax.all_to_all(value, axis, split_axis=0, concat_axis=0, tiled=True)]
    ppermute x4, waiting for transfers between devices: 14.7 us -> 12.1 us  [the longest x2 12.1 us: neighbours(): lax.ppermute(block, AXES, across)]
    all_to_all x1, blocking collectives: 32 us -> 29.7 us  [exchange(): return lax.all_to_all(value, axis, split_axis=0, concat_axis=0, tiled=True)]
  transfers between devices with their start and end apart: 6 -> 6, of which waited for: 5 -> 3; matrix products, arithmetic and copies ran while one was open for 1% -> 1% of each run, Pallas kernels for 1% -> 1%
where the time goes in v3:
time: 97.3 us; the launch traced here: 97 us
  blocking collectives  29.7 us (31%)
  starting transfers between devices  26.2 us (27%)
  waiting for transfers between devices  20.6 us (21%)
  Pallas kernels  17.9 us (18%)
  local copies, waits for them, and re-layouts  1.7 us (2%)
    all_to_all x1, blocking collectives, exchange(): return lax.all_to_all(value, axis, split_axis=0, concat_axis=0, tiled=True)  29.7 us
    ppermute x2, waiting for transfers between devices, neighbours(): lax.ppermute(block, AXES, across)  12.1 us
    all_to_all x1, starting transfers between devices, exchange(): return lax.all_to_all(value, axis, split_axis=0, concat_axis=0, tiled=True)  10.3 us
    all_to_all x1, waiting for transfers between devices, exchange(): return lax.all_to_all(value, axis, split_axis=0, concat_axis=0, tiled=True)  8.5 us
    ppermute x2, starting transfers between devices, neighbours(): lax.ppermute(block, AXES, across)  8.15 us
    ppermute x1, starting transfers between devices, local(): lax.ppermute(moved[0, 2 * count:3 * count], 'tm', [((i + 1) % groups, i)...  7.15 us
    pallas_call x1, Pallas kernels, local(): pl.pallas_call(second_kernel, out_shape=shape(parts, 3 * count + 1, 8, LA...  5.36 us
    pallas_call x1, Pallas kernels, local(): pl.pallas_call(first_kernel, out_shape=(blocks, shape(reach + count, ROWS...  5.19 us
  transfers between devices with their start and end apart: 6, of which 3 were waited for; matrix products, arithmetic and copies ran while one was open for 1% of the time, Pallas kernels for 1%

profile of v3, /device:TPU:1, one launch (start us, length us, event | category | flops | bytes accessed | tf_op | source)
XLA Modules:
  0.0 97.0 jit_solution(5664933662394659403)
XLA Ops:
  0.6 0.0 copy-start.4
  0.6 0.0 copy-start.6
  0.7 0.0 copy-start.1
  0.7 0.0 copy-start.3
  0.7 0.0 copy-start.7
  0.7 0.0 copy-start.2
  0.7 0.0 copy-start.5
  0.7 4.2 %seed.1.here_ref = f32[16,64,128]{2,1,0:T(8,128)} custom-call(f32[16,4096]{1,0:T(8,128)} %refs_0_.1, f32[16,4096]{1,0:T(8,128)} %refs_1_.1, f32[16,4096]{1,0:T(8,128)} %weights_ref.1, bf16[384,256]{1,0:T(8,128)(2,1)} %constant.42.clone.refs_3_.back_lanes_ref, bf16[64,384]{1,0:T(8,128)(2,1)} %constant.43.clone.refs_4_.back_rows_ref, ...), custom_call_target="tpu_custom_call" | custom-call | tf_op jit(solution)/shard_map/seed/pallas_call | solution.py:365
  4.9 4.5 %collective-permute-start.1 = (f32[16,64,128]{2,1,0:T(8,128)}, f32[16,64,128]{2,1,0:T(8,128)S(1)}, u32[]{:S(2)}, u32[]{:S(2)}) collective-permute-start(f32[16,64,128]{2,1,0:T(8,128)} %seed.1.here_ref), channel_id=1, source_target_pairs={{0,0},{1,2},{2,1},{3,4},{4,3},{5,6},{6,5},{7,8},{8,7},{9,10},{10,9... | collective-permute-start | bytes 1572872 | tf_op jit(solution)/shard_map/ppermute | solution.py:359
  9.4 0.4 collective-permute-start
  9.8 0.0 copy-done.2
  9.8 0.0 copy-done.5
  9.8 1.2 %arrange.1 = (f32[16,64,128]{2,1,0:T(8,128)S(1)}, f32[1024,128]{1,0:T(8,128)S(1)}) custom-call(f32[16,4096]{1,0:T(8,128)S(1)} %copy-done.2, f32[16,8192]{1,0:T(8,128)S(1)} %copy-done.5), custom_call_target="tpu_custom_call" | custom-call | flops 10000000 | bytes 2000000 | tf_op jit(solution)/shard_map/arrange/pallas_call | solution.py:376
  11.0 0.1 add_convert_fusion.keep_ref
  11.1 5.4 %collective-permute-done.1.across_ref = f32[16,64,128]{2,1,0:T(8,128)S(1)} collective-permute-done((f32[16,64,128]{2,1,0:T(8,128)}, f32[16,64,128]{2,1,0:T(8,128)S(1)}, u32[]{:S(2)}, u32[]{:S(2)}) %collective-permute-start.1) | collective-permute-done | bytes 524320 | tf_op jit(solution)/shard_map/ppermute | solution.py:359
  16.4 0.0 collective-permute-done.inside_ref
  16.5 0.0 copy-done.4
  16.5 0.0 copy-done.6
  16.5 0.0 copy-done.1
  16.5 0.0 copy-done.3
  16.5 0.0 copy-done.7
  16.5 0.0 copy-start
  16.5 1.0 %copy-done = f32[16,64,128]{2,1,0:T(8,128)S(1)} copy-done((f32[16,64,128]{2,1,0:T(8,128)S(1)}, f32[16,64,128]{2,1,0:T(8,128)}, u32[]{:S(2)}) %copy-start) | copy-done | bytes 524312
  17.5 5.2 %first.1 = (f32[16,64,128]{2,1,0:T(8,128)S(1)}, f32[31,64,128]{2,1,0:T(8,128)S(1)}) custom-call(f32[3]{0:T(128)S(1)} %add_convert_fusion.keep_ref, f32[16,64,128]{2,1,0:T(8,128)S(1)} %collective-permute-done.inside_ref, f32[16,64,128]{2,1,0:T(8,128)S(1)} %copy-done, f32[16,64,128]{2,1,0:T(8,128)S(1)} %collective-permute-done.1.across_ref, ...), custom_call_target="tpu_custom_call" | custom-call | tf_op jit(solution)/shard_map/first/pallas_call | solution.py:388
  22.7 3.6 %collective-permute-start.3 = (f32[16,64,128]{2,1,0:T(8,128)S(1)}, f32[16,64,128]{2,1,0:T(8,128)S(1)}, u32[]{:S(2)}, u32[]{:S(2)}) collective-permute-start(f32[16,64,128]{2,1,0:T(8,128)S(1)} %get-tuple-element.8.here_ref), channel_id=1, source_target_pairs={{0,0},{1,2},{2,1},{3,4},{4,3},{5,6},{6,5},{7,8},{8,7},{9,10},{10,9... | collective-permute-start | bytes 1572872 | tf_op jit(solution)/shard_map/ppermute | solution.py:359
  26.4 0.1 collective-permute-start.2
  26.5 6.7 %collective-permute-done.3.across_ref = f32[16,64,128]{2,1,0:T(8,128)S(1)} collective-permute-done((f32[16,64,128]{2,1,0:T(8,128)S(1)}, f32[16,64,128]{2,1,0:T(8,128)S(1)}, u32[]{:S(2)}, u32[]{:S(2)}) %collective-permute-start.3) | collective-permute-done | bytes 524320 | tf_op jit(solution)/shard_map/ppermute | solution.py:359
  33.2 0.0 collective-permute-done.2.inside_ref
  33.2 5.4 %second.1 = f32[8,49,8,128]{3,2,1,0:T(8,128)S(1)} custom-call(f32[3]{0:T(128)S(1)} %add_convert_fusion.keep_ref, f32[16,64,128]{2,1,0:T(8,128)S(1)} %collective-permute-done.2.inside_ref, f32[16,64,128]{2,1,0:T(8,128)S(1)} %get-tuple-element.8.here_ref, f32[16,64,128]{2,1,0:T(8,128)S(1)} %collective-permute-done.3.across_ref, ...), custom_call_target="tpu_custom_call" | custom-call | tf_op jit(solution)/shard_map/second/pallas_call | solution.py:399
  38.6 29.7 %all_to_all.13.moved_ref = f32[8,49,8,128]{3,2,1,0:T(8,128)S(1)} all-to-all(f32[8,49,8,128]{3,2,1,0:T(8,128)S(1)} %second.1), channel_id=1, replica_groups=mesh['tm'=32,'chan'=8] {'chan'}, dimensions={0} | all-to-all | bytes 3211264 | tf_op jit(solution)/shard_map/all_to_all | solution.py:362
  68.3 7.2 %collective-permute-start.4 = (f32[16,8,128]{2,1,0:T(8,128)S(1)}, f32[16,8,128]{2,1,0:T(8,128)S(1)}, u32[]{:S(2)}, u32[]{:S(2)}) collective-permute-start(f32[16,8,128]{2,1,0:T(8,128)S(1)} %slice_bitcast_fusion), channel_id=1, source_target_pairs={{8,0},{16,8},{24,16},{32,24},{40,32},{48,40},{56,48},{64,56},{72,6... | collective-permute-start | bytes 196616 | tf_op jit(solution)/shard_map/ppermute | solution.py:413
  75.5 0.6 broadcast_in_dim.3
  76.1 10.3 %all-to-all-start.1 = ((f32[32,1,128]{2,1,0:T(1,128)}), f32[32,1,128]{2,1,0:T(1,128)S(1)}, u32[]{:S(2)}, u32[]{:S(2)}) async-start(f32[32,1,128]{2,1,0:T(1,128)} %broadcast_in_dim.3), calls=%async_computation.1 | async-start | bytes 32768 | tf_op jit(solution)/shard_map/all_to_all | solution.py:362
  86.5 8.5 %all-to-all-done.1 = f32[32,1,128]{2,1,0:T(1,128)S(1)} async-done(((f32[32,1,128]{2,1,0:T(1,128)}), f32[32,1,128]{2,1,0:T(1,128)S(1)}, u32[]{:S(2)}, u32[]{:S(2)}) %all-to-all-start.1) | async-done | bytes 16416 | tf_op jit(solution)/shard_map/all_to_all | solution.py:362
  95.0 0.0 collective-permute-done.4.after_ref
  95.0 2.0 %last.1 = (f32[128,1024]{1,0:T(8,128)}, f32[128,1024]{1,0:T(8,128)}) custom-call(s32[1]{0:T(128)} %bitcast.place_ref, f32[1]{0:T(128)} %bitcast.1.keep_ref, f32[8,49,8,128]{3,2,1,0:T(8,128)S(1)} %all_to_all.13.moved_ref, f32[16,8,128]{2,1,0:T(8,128)S(1)} %collective-permute-done.4.after_ref, f32[32,128]{1,0:T(8,128)S(1)} %bitcast.12, f32[16,64,128]{2,1,0:T(8,128)S(1)} %bitcast.11), custom_call_target="tpu_custom_call" | custom-call | tf_op jit(solution)/shard_map/last/pallas_call | solution.py:418
  (2 shorter events, 0.0 us)
Async XLA Ops:
  0.6 15.8 %copy-start.4 = (f32[2,64,128]{2,1,0:T(8,128)S(1)}, f32[2,64,128]{2,1,0:T(8,128)}, u32[]{:S(2)}) copy-start(f32[2,64,128]{2,1,0:T(8,128)} %constant.44.clone.refs_5_.twist_ref) | copy-start | bytes 196612
  0.6 15.8 %copy-start.6 = (bf16[64,384]{1,0:T(8,128)(2,1)S(1)}, bf16[64,384]{1,0:T(8,128)(2,1)}, u32[]{:S(2)}) copy-start(bf16[64,384]{1,0:T(8,128)(2,1)} %constant.43.clone.refs_4_.back_rows_ref) | copy-start | bytes 147460
  0.7 15.8 %copy-start.1 = (bf16[384,256]{1,0:T(8,128)(2,1)S(1)}, bf16[384,256]{1,0:T(8,128)(2,1)}, u32[]{:S(2)}) copy-start(bf16[384,256]{1,0:T(8,128)(2,1)} %constant.42.clone.refs_3_.back_lanes_ref) | copy-start | bytes 589828
  0.7 15.8 %copy-start.3 = (bf16[768,128]{1,0:T(8,128)(2,1)S(1)}, bf16[768,128]{1,0:T(8,128)(2,1)}, u32[]{:S(2)}) copy-start(bf16[768,128]{1,0:T(8,128)(2,1)} %constant.46.clone.ahead_lanes_ref) | copy-start | bytes 589828
  0.7 15.8 %copy-start.7 = (bf16[128,192]{1,0:T(8,128)(2,1)S(1)}, bf16[128,192]{1,0:T(8,128)(2,1)}, u32[]{:S(2)}) copy-start(bf16[128,192]{1,0:T(8,128)(2,1)} %constant.45.clone.ahead_rows_ref) | copy-start | bytes 147460
  0.7 9.1 %copy-start.2 = (f32[16,4096]{1,0:T(8,128)S(1)}, f32[16,4096]{1,0:T(8,128)}, u32[]{:S(2)}) copy-start(f32[16,4096]{1,0:T(8,128)} %weights_ref.1) | copy-start | bytes 786436
  0.7 9.1 %copy-start.5 = (f32[16,8192]{1,0:T(8,128)S(1)}, f32[16,8192]{1,0:T(8,128)}, u32[]{:S(2)}) copy-start(f32[16,8192]{1,0:T(8,128)} %taps_ref.1) | copy-start | bytes 1572868
  4.9 11.6 %collective-permute-start.1 = (f32[16,64,128]{2,1,0:T(8,128)}, f32[16,64,128]{2,1,0:T(8,128)S(1)}, u32[]{:S(2)}, u32[]{:S(2)}) collective-permute-start(f32[16,64,128]{2,1,0:T(8,128)} %seed.1.here_ref), channel_id=1, source_target_pairs={{0,0},{1,2},{2,1},{3,4},{4,3},{5,6},{6,5},{7,8},{8,7},{9,10},{10,9... | collective-permute-start | bytes 1572872 | tf_op jit(solution)/shard_map/ppermute | solution.py:359
  9.4 7.1 %collective-permute-start = (f32[16,64,128]{2,1,0:T(8,128)}, f32[16,64,128]{2,1,0:T(8,128)S(1)}, u32[]{:S(2)}, u32[]{:S(2)}) collective-permute-start(f32[16,64,128]{2,1,0:T(8,128)} %seed.1.here_ref), channel_id=1, source_target_pairs={{0,1},{1,0},{2,3},{3,2},{4,5},{5,4},{6,7},{7,6},{8,9},{9,8},{10,11... | collective-permute-start | bytes 1572872 | tf_op jit(solution)/shard_map/ppermute | solution.py:359
  16.5 1.0 %copy-start = (f32[16,64,128]{2,1,0:T(8,128)S(1)}, f32[16,64,128]{2,1,0:T(8,128)}, u32[]{:S(2)}) copy-start(f32[16,64,128]{2,1,0:T(8,128)} %seed.1.here_ref) | copy-start | bytes 1572868
  22.7 10.5 %collective-permute-start.3 = (f32[16,64,128]{2,1,0:T(8,128)S(1)}, f32[16,64,128]{2,1,0:T(8,128)S(1)}, u32[]{:S(2)}, u32[]{:S(2)}) collective-permute-start(f32[16,64,128]{2,1,0:T(8,128)S(1)} %get-tuple-element.8.here_ref), channel_id=1, source_target_pairs={{0,0},{1,2},{2,1},{3,4},{4,3},{5,6},{6,5},{7,8},{8,7},{9,10},{10,9... | collective-permute-start | bytes 1572872 | tf_op jit(solution)/shard_map/ppermute | solution.py:359
  26.4 6.9 %collective-permute-start.2 = (f32[16,64,128]{2,1,0:T(8,128)S(1)}, f32[16,64,128]{2,1,0:T(8,128)S(1)}, u32[]{:S(2)}, u32[]{:S(2)}) collective-permute-start(f32[16,64,128]{2,1,0:T(8,128)S(1)} %get-tuple-element.8.here_ref), channel_id=1, source_target_pairs={{0,1},{1,0},{2,3},{3,2},{4,5},{5,4},{6,7},{7,6},{8,9},{9,8},{10,11... | collective-permute-start | bytes 1572872 | tf_op jit(solution)/shard_map/ppermute | solution.py:359
  68.3 26.7 %collective-permute-start.4 = (f32[16,8,128]{2,1,0:T(8,128)S(1)}, f32[16,8,128]{2,1,0:T(8,128)S(1)}, u32[]{:S(2)}, u32[]{:S(2)}) collective-permute-start(f32[16,8,128]{2,1,0:T(8,128)S(1)} %slice_bitcast_fusion), channel_id=1, source_target_pairs={{8,0},{16,8},{24,16},{32,24},{40,32},{48,40},{56,48},{64,56},{72,6... | collective-permute-start | bytes 196616 | tf_op jit(solution)/shard_map/ppermute | solution.py:413
  76.1 18.9 %all-to-all-start.1 = ((f32[32,1,128]{2,1,0:T(1,128)}), f32[32,1,128]{2,1,0:T(1,128)S(1)}, u32[]{:S(2)}, u32[]{:S(2)}) async-start(f32[32,1,128]{2,1,0:T(1,128)} %broadcast_in_dim.3), calls=%async_computation.1 | async-start | bytes 32768 | tf_op jit(solution)/shard_map/all_to_all | solution.py:362

commit v4 on v3

--- a/solution.py
+++ b/solution.py
@@ -16,7 +16,7 @@
 F32 = jnp.float32
 BF16 = jnp.bfloat16
 AXES = ("tm", "chan")
-VMEM_BYTES = 40 * 1024 * 1024
+VMEM_BYTES = 16 * 1024 * 1024
 
 
 def params(limit=VMEM_BYTES):
@@ -101,7 +101,7 @@
 
 
 def seed_kernel(*refs):
-    sources, out_ref, places, held, semaphore = refs[:6], refs[6], refs[7:13], refs[13], refs[14]
+    sources, out_ref, sent_ref, places, held, semaphore = refs[:6], refs[6], refs[7], refs[8:14], refs[14], refs[15]
     copies = [
         pltpu.make_async_copy(source, place, semaphore.at[at])
         for at, (source, place) in enumerate(zip(sources, places))
@@ -127,7 +127,10 @@
             jnp.concatenate(spectra, 0), back_lanes_ref[...], back_rows_ref[...], cos, sin
         )
         for f in range(CHUNK):
-            out_ref[start + f] = frames[:, f * LANES : (f + 1) * LANES]
+            frame = frames[:, f * LANES : (f + 1) * LANES]
+            out_ref[start + f] = frame
+            for group in range(ROWS // 8):
+                sent_ref[group, start + f] = frame[group * 8 : (group + 1) * 8]
 
 
 def arrange_kernel(weights_ref, taps_ref, weights_out, taps_out, held):
@@ -182,7 +185,7 @@
 def first_kernel(
     keep_ref, inside_ref, here_ref, across_ref, taps_ref, weights_ref,
     ahead_rows_ref, ahead_lanes_ref, back_lanes_ref, back_rows_ref, twist_ref,
-    out_ref, side_ref, filtered,
+    out_ref, sent_ref, side_ref, filtered,
 ):
     count = here_ref.shape[0]
     keep = (keep_ref[0], keep_ref[1], keep_ref[2])
@@ -206,7 +209,10 @@
         weights = weights_ref[start : start + CHUNK].reshape(CHUNK * ROWS, LANES)
         frames = backward_chunk(spectra * weights, back_lanes_ref[...], back_rows_ref[...], cos, sin)
         for f in range(CHUNK):
-            out_ref[start + f] = frames[:, f * LANES : (f + 1) * LANES]
+            frame = frames[:, f * LANES : (f + 1) * LANES]
+            out_ref[start + f] = frame
+            for group in range(ROWS // 8):
+                sent_ref[group, start + f] = frame[group * 8 : (group + 1) * 8]
 
 
 def quarters():
@@ -245,8 +251,6 @@
         for at in range(count):
             base = side[reach + at]
             value = image[reach + at]
-            out_ref[group, at] = base
-            out_ref[group, count + at] = value
             first = first + base * base
             second = second + base * value
             third = third + value * value
@@ -267,22 +271,60 @@
         frames = backward_chunk(weighted, back_lanes_ref[...], back_rows_ref[...], cos, sin)
         for f in range(CHUNK):
             for group in range(ROWS // 8):
-                out_ref[group, 2 * count + start + f] = frames[
+                out_ref[group, start + f] = frames[
                     group * 8 : (group + 1) * 8, f * LANES : (f + 1) * LANES
                 ]
     totals = pack([sums[0], sums[1], sums[2], power])
     for group in range(ROWS // 8):
-        out_ref[group, 3 * count] = totals
+        out_ref[group, count] = totals
+
+
+def local_taps(place_ref, taps_ref):
+    rows = pl.ds(pl.multiple_of(place_ref[0] * 8, 8), 8)
+    return [taps_ref[p, rows, :] for p in range(taps_ref.shape[0])]
+
+
+def by_part(moved_ref, after_ref, keep, count, reach, finish):
+    parts = moved_ref.shape[0]
+
+    def frames(part):
+        return [moved_ref[part, t] for t in range(count)]
+
+    @pl.loop(0, parts - 1)
+    def _(part):
+        finish(part, frames(part) + [moved_ref[part + 1, t] for t in range(reach)])
+
+    finish(parts - 1, frames(parts - 1) + [after_ref[t] * keep for t in range(reach)])
+
+
+def rebuild_kernel(
+    place_ref, keep_ref, first_ref, first_after_ref, second_ref, second_after_ref, taps_ref, base_ref, image_ref
+):
+    count = first_ref.shape[1]
+    taps = local_taps(place_ref, taps_ref)
+    reach = len(taps) - 1
+
+    def base(part, frames):
+        for at in range(count):
+            base_ref[part, at] = weighted_sum(taps, frames[at : at + reach + 1])
+
+    def image(part, frames):
+        for at in range(count):
+            image_ref[part, at] = (
+                weighted_sum(taps, frames[at : at + reach + 1]) + RIDGE * base_ref[part, at]
+            )
+
+    by_part(first_ref, first_after_ref, keep_ref[0], count, reach, base)
+    by_part(second_ref, second_after_ref, keep_ref[0], count, reach, image)
 
 
 def last_kernel(
-    place_ref, keep_ref, moved_ref, after_ref, sums_ref, taps_ref,
+    place_ref, keep_ref, base_ref, image_ref, moved_ref, after_ref, sums_ref, taps_ref,
     solution_ref, residual_ref, kept, left,
 ):
-    parts = moved_ref.shape[0]
-    count = (moved_ref.shape[1] - 1) // 3
-    reach = taps_ref.shape[0] - 1
-    rows = pl.ds(pl.multiple_of(place_ref[0] * 8, 8), 8)
+    parts, count = base_ref.shape[:2]
+    taps = local_taps(place_ref, taps_ref)
+    reach = len(taps) - 1
     sums = sums_ref[0:8]
     for at in range(8, sums_ref.shape[0], 8):
         sums = sums + sums_ref[at : at + 8]
@@ -302,23 +344,17 @@
     to_base, to_image, image_rate, cube_rate = (
         jnp.broadcast_to(value, (8, LANES)) for value in (to_base, to_image, image_rate, cube_rate)
     )
-    taps = [taps_ref[p, rows, :] for p in range(reach + 1)]
-
-    def finish(part, tail):
-        frames = [moved_ref[part, 2 * count + t] for t in range(count)] + tail
+
+    def finish(part, frames):
         for at in range(count):
-            base = moved_ref[part, at]
-            image = moved_ref[part, count + at]
+            base = base_ref[part, at]
+            image = image_ref[part, at]
             again = weighted_sum(taps, frames[at : at + reach + 1]) + RIDGE * image
             here = pl.ds(pl.multiple_of((part * count + at) * 8, 8), 8)
             kept[here, :] = to_base * base + to_image * image
             left[here, :] = base + image_rate * image + cube_rate * again
 
-    @pl.loop(0, parts - 1)
-    def _(part):
-        finish(part, [moved_ref[part + 1, 2 * count + t] for t in range(reach)])
-
-    finish(parts - 1, [after_ref[t] * keep_ref[0] for t in range(reach)])
+    by_part(moved_ref, after_ref, keep_ref[0], count, reach, finish)
 
     for block in range(parts * count // 8):
         for n1 in range(8):
@@ -361,18 +397,23 @@
     def exchange(value, axis):
         return lax.all_to_all(value, axis, split_axis=0, concat_axis=0, tiled=True)
 
+    def from_later_group(moved):
+        return lax.ppermute(moved[0, :count], "tm", [((i + 1) % groups, i) for i in range(groups)])
+
     seed_inputs = (observed_real, observed_imag, weights, back_lanes, back_rows, twist)
-    seeds = pl.pallas_call(
+    sent = shape(parts, count, 8, LANES)
+    seeds, outgoing = pl.pallas_call(
         seed_kernel,
-        out_shape=blocks,
+        out_shape=(blocks, sent),
         in_specs=[pl.BlockSpec(memory_space=pltpu.HBM)] * 6,
-        out_specs=vmem(1)[0],
+        out_specs=tuple(vmem(2)),
         scratch_shapes=[pltpu.VMEM(value.shape, value.dtype) for value in seed_inputs]
         + [pltpu.VMEM((count * ROWS, LANES), F32), pltpu.SemaphoreType.DMA((6,))],
         compiler_params=params(62 * 1024 * 1024),
         name="seed",
     )(*seed_inputs)
     inside, across = neighbours(seeds)
+    first_moved = exchange(outgoing, "chan")
     weights, taps = pl.pallas_call(
         arrange_kernel,
         out_shape=(blocks, shape((reach + 1) * ROWS, LANES)),
@@ -385,20 +426,26 @@
     )(weights, taps)
     taps = taps.reshape(reach + 1, ROWS, LANES)
 
-    images, side = pl.pallas_call(
+    inside, across, first_moved = lax.optimization_barrier((inside, across, first_moved))
+    images, outgoing, side = pl.pallas_call(
         first_kernel,
-        out_shape=(blocks, shape(reach + count, ROWS, LANES)),
+        out_shape=(blocks, sent, shape(reach + count, ROWS, LANES)),
         in_specs=[SMEM] + vmem(10),
-        out_specs=tuple(vmem(2)),
+        out_specs=tuple(vmem(3)),
         scratch_shapes=[pltpu.VMEM((count, ROWS, LANES), F32)],
         compiler_params=params(),
         name="first",
     )(keep, inside, seeds, across, taps, weights, *tables)
     inside, across = neighbours(images)
+    second_moved = exchange(outgoing, "chan")
+    first_after = from_later_group(first_moved)
+    inside, across, second_moved, first_after = lax.optimization_barrier(
+        (inside, across, second_moved, first_after)
+    )
 
     outgoing = pl.pallas_call(
         second_kernel,
-        out_shape=shape(parts, 3 * count + 1, 8, LANES),
+        out_shape=shape(parts, count + 1, 8, LANES),
         in_specs=[SMEM] + vmem(11),
         out_specs=vmem(1)[0],
         scratch_shapes=[
@@ -410,15 +457,23 @@
     )(keep, inside, images, across, side, taps, weights, *tables)
 
     moved = exchange(outgoing, "chan")
-    after = lax.ppermute(
-        moved[0, 2 * count : 3 * count], "tm", [((i + 1) % groups, i) for i in range(groups)]
-    )
-    sums = jnp.sum(moved[:, 3 * count], (0, 1))
+    after = from_later_group(moved)
+    sums = jnp.sum(moved[:, count], (0, 1))
     sums = exchange(jnp.broadcast_to(sums, (groups, LANES)), "tm")
+    second_after = from_later_group(second_moved)
+    base, image = pl.pallas_call(
+        rebuild_kernel,
+        out_shape=(sent, sent),
+        in_specs=[SMEM, SMEM] + vmem(5),
+        out_specs=tuple(vmem(2)),
+        compiler_params=params(),
+        cost_estimate=pl.CostEstimate(flops=10**7, bytes_accessed=2 * 10**6, transcendentals=0),
+        name="rebuild",
+    )(place, keep_group, first_moved, first_after, second_moved, second_after, taps)
     return pl.pallas_call(
         last_kernel,
         out_shape=(shape(parts * count, 8 * LANES), shape(parts * count, 8 * LANES)),
-        in_specs=[SMEM, SMEM] + vmem(4),
+        in_specs=[SMEM, SMEM] + vmem(6),
         out_specs=tuple(vmem(2)),
         scratch_shapes=[
             pltpu.VMEM((parts * count * 8, LANES), F32),
@@ -426,7 +481,7 @@
         ],
         compiler_params=params(),
         name="last",
-    )(place, keep_group, moved, after, sums, taps)
+    )(place, keep_group, base, image, moved, after, sums, taps)
 
 
 def solution(mesh):

time: 97.3 us -> 100 us (1.028)
  blocking collectives: 29.7 us -> 0 us
  starting transfers between devices: 26.2 us -> 49.6 us
  Pallas kernels: 17.9 us -> 22.4 us
  local copies, waits for them, and re-layouts: 1.7 us -> 4.83 us
    all_to_all x1 -> x0, blocking collectives: 29.7 us -> none  [exchange(): return lax.all_to_all(value, axis, split_axis=0, concat_axis=0, tiled=True)]
    ppermute x1 -> x3, starting transfers between devices: 7.15 us -> 19.6 us  [from_later_group(): lax.ppermute(moved[0, :count], 'tm', [((i + 1) % groups, i) for i in rang...]
    ppermute x2, waiting for transfers between devices: 12.1 us -> 0.01 us  [neighbours(): lax.ppermute(block, AXES, across)]
    all_to_all x1 -> x4, waiting for transfers between devices: 8.5 us -> 19.9 us  [exchange(): return lax.all_to_all(value, axis, split_axis=0, concat_axis=0, tiled=True)]
    ppermute x2, starting transfers between devices: 0.52 us -> 7.37 us  [neighbours(): lax.ppermute(block, AXES, inside)]
    all_to_all x1 -> x4, starting transfers between devices: 10.3 us -> 15.2 us  [exchange(): return lax.all_to_all(value, axis, split_axis=0, concat_axis=0, tiled=True)]
    pallas_call x3 -> x4, Pallas kernels: 14.7 us -> 19.2 us  [the longest x1 7.03 us: local(): pl.pallas_call(second_kernel, out_shape=shape(parts, count + 1, 8, LANES)...]
    unnamed x16 -> x28, local copies, waits for them, and re-layouts: 1.08 us -> 4.19 us
  transfers between devices with their start and end apart: 6 -> 11, of which waited for: 3 -> 5; matrix products, arithmetic and copies ran while one was open for 1% -> 1% of each run, Pallas kernels for 1% -> 2%
where the time goes in v4:
time: 100 us; the launch traced here: 99.2 us
  starting transfers between devices  49.6 us (50%)
  Pallas kernels  22.4 us (22%)
  waiting for transfers between devices  21.5 us (22%)
  local copies, waits for them, and re-layouts  4.83 us (5%)
    all_to_all x4, waiting for transfers between devices, exchange(): return lax.all_to_all(value, axis, split_axis=0, concat_axis=0, tiled=True)  19.9 us
    ppermute x3, starting transfers between devices, from_later_group(): lax.ppermute(moved[0, :count], 'tm', [((i + 1) % groups, i) for i in rang...  19.6 us
    all_to_all x4, starting transfers between devices, exchange(): return lax.all_to_all(value, axis, split_axis=0, concat_axis=0, tiled=True)  15.2 us
    ppermute x2, starting transfers between devices, neighbours(): lax.ppermute(block, AXES, across)  7.47 us
    ppermute x2, starting transfers between devices, neighbours(): lax.ppermute(block, AXES, inside)  7.37 us
    pallas_call x1, Pallas kernels, local(): pl.pallas_call(second_kernel, out_shape=shape(parts, count + 1, 8, LANES)...  7.03 us
    pallas_call x1, Pallas kernels, local(): pl.pallas_call(first_kernel, out_shape=(blocks, sent, shape(reach + count...  6.66 us
    pallas_call x1, Pallas kernels, local(): pl.pallas_call(seed_kernel, out_shape=(blocks, sent), in_specs=[pl.BlockS...  4.23 us
  transfers between devices with their start and end apart: 11, of which 5 were waited for; matrix products, arithmetic and copies ran while one was open for 1% of the time, Pallas kernels for 2%

profile of v4, /device:TPU:1, one launch (start us, length us, event | category | flops | bytes accessed | tf_op | source)
XLA Modules:
  0.0 99.2 jit_solution(16666096895772280194)
XLA Ops:
  0.6 4.2 %seed.1 = (f32[16,64,128]{2,1,0:T(8,128)}, f32[8,16,8,128]{3,2,1,0:T(8,128)}) custom-call(f32[16,4096]{1,0:T(8,128)} %refs_0_.1, f32[16,4096]{1,0:T(8,128)} %refs_1_.1, f32[16,4096]{1,0:T(8,128)} %weights_ref.1, bf16[384,256]{1,0:T(8,128)(2,1)} %constant.42.clone.refs_3_.back_lanes_ref, bf16[64,384]{1,0:T(8,128)(2,1)} %constant.43.clone.refs_4_.back_rows_ref, ...), custom_call_target="tpu_custom_call" | custom-call | tf_op jit(solution)/shard_map/seed/pallas_call | solution.py:405
  4.9 4.5 %collective-permute-start.1 = (f32[16,64,128]{2,1,0:T(8,128)}, f32[16,64,128]{2,1,0:T(8,128)}, u32[]{:S(2)}, u32[]{:S(2)}) collective-permute-start(f32[16,64,128]{2,1,0:T(8,128)} %get-tuple-element.18.here_ref), channel_id=1, source_target_pairs={{0,0},{1,2},{2,1},{3,4},{4,3},{5,6},{6,5},{7,8},{8,7},{9,10},{10,9... | collective-permute-start | bytes 1572872 | tf_op jit(solution)/shard_map/ppermute | solution.py:395
  9.4 4.1 %collective-permute-start = (f32[16,64,128]{2,1,0:T(8,128)}, f32[16,64,128]{2,1,0:T(8,128)}, u32[]{:S(2)}, u32[]{:S(2)}) collective-permute-start(f32[16,64,128]{2,1,0:T(8,128)} %get-tuple-element.18.here_ref), channel_id=1, source_target_pairs={{0,1},{1,0},{2,3},{3,2},{4,5},{5,4},{6,7},{7,6},{8,9},{9,8},{10,11... | collective-permute-start | bytes 1572872 | tf_op jit(solution)/shard_map/ppermute | solution.py:395
  13.5 0.0 copy-start.1
  13.5 0.0 copy-start.5
  13.5 3.6 %all-to-all-start = ((f32[8,16,8,128]{3,2,1,0:T(8,128)}), f32[8,16,8,128]{3,2,1,0:T(8,128)S(1)}, u32[]{:S(2)}, u32[]{:S(2)}) async-start(f32[8,16,8,128]{3,2,1,0:T(8,128)} %get-tuple-element.19), calls=%async_computation | async-start | bytes 1048576 | tf_op jit(solution)/shard_map/all_to_all | solution.py:398
  17.1 0.0 copy-done.1
  17.1 0.0 copy-done.5
  17.1 0.0 copy-start
  17.1 0.0 copy-start.2
  17.1 0.0 copy-start.3
  17.1 0.0 copy-start.8
  17.2 0.0 copy-start.10
  17.2 1.2 %arrange.1 = (f32[16,64,128]{2,1,0:T(8,128)S(1)}, f32[1024,128]{1,0:T(8,128)S(1)}) custom-call(f32[16,4096]{1,0:T(8,128)S(1)} %copy-done.1, f32[16,8192]{1,0:T(8,128)S(1)} %copy-done.5), custom_call_target="tpu_custom_call" | custom-call | flops 10000000 | bytes 2000000 | tf_op jit(solution)/shard_map/arrange/pallas_call | solution.py:417
  18.4 0.1 add_convert_fusion.keep_ref
  18.4 8.1 %all-to-all-done.first_ref = f32[8,16,8,128]{3,2,1,0:T(8,128)S(1)} async-done(((f32[8,16,8,128]{3,2,1,0:T(8,128)}), f32[8,16,8,128]{3,2,1,0:T(8,128)S(1)}, u32[]{:S(2)}, u32[]{:S(2)}) %all-to-all-start) | async-done | bytes 524320 | tf_op jit(solution)/shard_map/all_to_all | solution.py:398
  26.5 0.0 collective-permute-done.1.across_ref
  26.5 0.0 collective-permute-done.inside_ref
  26.5 0.0 copy-done
  26.5 0.0 copy-done.2
  26.6 0.0 copy-done.3
  26.6 0.0 copy-done.8
  26.6 0.0 copy-done.10
  26.6 0.0 copy-start.7
  26.6 1.0 %copy-done.7 = f32[16,64,128]{2,1,0:T(8,128)S(1)} copy-done((f32[16,64,128]{2,1,0:T(8,128)S(1)}, f32[16,64,128]{2,1,0:T(8,128)}, u32[]{:S(2)}) %copy-start.7) | copy-done | bytes 524312
  27.6 6.7 %first.1 = (f32[16,64,128]{2,1,0:T(8,128)}, f32[8,16,8,128]{3,2,1,0:T(8,128)S(1)}, f32[31,64,128]{2,1,0:T(8,128)S(1)}) custom-call(f32[3]{0:T(128)S(1)} %add_convert_fusion.keep_ref, f32[16,64,128]{2,1,0:T(8,128)} %collective-permute-done.inside_ref, f32[16,64,128]{2,1,0:T(8,128)S(1)} %copy-done.7, f32[16,64,128]{2,1,0:T(8,128)} %collective-permute-done.1.across_ref, ...), custom_call_target="tpu_custom_call" | custom-call | tf_op jit(solution)/shard_map/first/pallas_call | solution.py:430
  34.3 0.0 copy-start.6
  34.3 3.0 %collective-permute-start.3 = (f32[16,64,128]{2,1,0:T(8,128)}, f32[16,64,128]{2,1,0:T(8,128)}, u32[]{:S(2)}, u32[]{:S(2)}) collective-permute-start(f32[16,64,128]{2,1,0:T(8,128)} %get-tuple-element.25.here_ref), channel_id=1, source_target_pairs={{0,0},{1,2},{2,1},{3,4},{4,3},{5,6},{6,5},{7,8},{8,7},{9,10},{10,9... | collective-permute-start | bytes 1572872 | tf_op jit(solution)/shard_map/ppermute | solution.py:395
  37.3 3.3 %collective-permute-start.2 = (f32[16,64,128]{2,1,0:T(8,128)}, f32[16,64,128]{2,1,0:T(8,128)}, u32[]{:S(2)}, u32[]{:S(2)}) collective-permute-start(f32[16,64,128]{2,1,0:T(8,128)} %get-tuple-element.25.here_ref), channel_id=1, source_target_pairs={{0,1},{1,0},{2,3},{3,2},{4,5},{5,4},{6,7},{7,6},{8,9},{9,8},{10,11... | collective-permute-start | bytes 1572872 | tf_op jit(solution)/shard_map/ppermute | solution.py:395
  40.5 0.0 copy-done.6
  40.5 3.4 %all-to-all-start.1 = ((f32[8,16,8,128]{3,2,1,0:T(8,128)}), f32[8,16,8,128]{3,2,1,0:T(8,128)S(1)}, u32[]{:S(2)}, u32[]{:S(2)}) async-start(f32[8,16,8,128]{3,2,1,0:T(8,128)} %copy-done.6), calls=%async_computation.1 | async-start | bytes 1048576 | tf_op jit(solution)/shard_map/all_to_all | solution.py:398
  44.0 5.4 %collective-permute-start.4 = (f32[16,8,128]{2,1,0:T(8,128)S(1)}, f32[16,8,128]{2,1,0:T(8,128)S(1)}, u32[]{:S(2)}, u32[]{:S(2)}) collective-permute-start(f32[16,8,128]{2,1,0:T(8,128)S(1)} %slice_bitcast_fusion.2), channel_id=1, source_target_pairs={{8,0},{16,8},{24,16},{32,24},{40,32},{48,40},{56,48},{64,56},{72,6... | collective-permute-start | bytes 196616 | tf_op jit(solution)/shard_map/ppermute | solution.py:401
  49.4 1.5 %collective-permute-done.4.first_after_ref = f32[16,8,128]{2,1,0:T(8,128)S(1)} collective-permute-done((f32[16,8,128]{2,1,0:T(8,128)S(1)}, f32[16,8,128]{2,1,0:T(8,128)S(1)}, u32[]{:S(2)}, u32[]{:S(2)}) %collective-permute-start.4) | collective-permute-done | bytes 65568 | tf_op jit(solution)/shard_map/ppermute | solution.py:401
  50.9 0.0 copy-start.12
  50.9 0.6 copy-done.12
  51.6 1.9 %all-to-all-done.1.second_ref = f32[8,16,8,128]{3,2,1,0:T(8,128)S(1)} async-done(((f32[8,16,8,128]{3,2,1,0:T(8,128)}), f32[8,16,8,128]{3,2,1,0:T(8,128)S(1)}, u32[]{:S(2)}, u32[]{:S(2)}) %all-to-all-start.1) | async-done | bytes 524320 | tf_op jit(solution)/shard_map/all_to_all | solution.py:398
  53.4 0.0 collective-permute-done.3.across_ref
  53.4 0.0 collective-permute-done.2.inside_ref
  53.4 0.0 copy-start.4
  53.4 0.8 copy-done.4
  54.3 0.0 copy-start.9
  54.3 0.8 copy-done.9
  55.1 0.0 copy-start.11
  55.1 0.8 copy-done.11
  55.9 7.0 %second.1 = f32[8,17,8,128]{3,2,1,0:T(8,128)} custom-call(f32[3]{0:T(128)S(1)} %add_convert_fusion.keep_ref, f32[16,64,128]{2,1,0:T(8,128)} %collective-permute-done.2.inside_ref, f32[16,64,128]{2,1,0:T(8,128)} %get-tuple-element.25.here_ref, f32[16,64,128]{2,1,0:T(8,128)} %collective-permute-done.3.across_ref, ...), custom_call_target="tpu_custom_call" | custom-call | tf_op jit(solution)/shard_map/second/pallas_call | solution.py:446
  62.9 4.3 %all-to-all-start.2 = ((f32[8,17,8,128]{3,2,1,0:T(8,128)}), f32[8,17,8,128]{3,2,1,0:T(8,128)S(1)}, u32[]{:S(2)}, u32[]{:S(2)}) async-start(f32[8,17,8,128]{3,2,1,0:T(8,128)} %second.1), calls=%async_computation.2 | async-start | bytes 1114112 | tf_op jit(solution)/shard_map/all_to_all | solution.py:398
  67.3 7.1 %collective-permute-start.5 = (f32[16,8,128]{2,1,0:T(8,128)S(1)}, f32[16,8,128]{2,1,0:T(8,128)S(1)}, u32[]{:S(2)}, u32[]{:S(2)}) collective-permute-start(f32[16,8,128]{2,1,0:T(8,128)S(1)} %slice_bitcast_fusion.1), channel_id=1, source_target_pairs={{8,0},{16,8},{24,16},{32,24},{40,32},{48,40},{56,48},{64,56},{72,6... | collective-permute-start | bytes 196616 | tf_op jit(solution)/shard_map/ppermute | solution.py:401
  74.4 2.7 %all-to-all-done.2.moved_ref = f32[8,17,8,128]{3,2,1,0:T(8,128)S(1)} async-done(((f32[8,17,8,128]{3,2,1,0:T(8,128)}), f32[8,17,8,128]{3,2,1,0:T(8,128)S(1)}, u32[]{:S(2)}, u32[]{:S(2)}) %all-to-all-start.2) | async-done | bytes 557088 | tf_op jit(solution)/shard_map/all_to_all | solution.py:398
  77.1 0.0 copy-start.13
  77.1 7.1 %collective-permute-start.6 = (f32[16,8,128]{2,1,0:T(8,128)S(1)}, f32[16,8,128]{2,1,0:T(8,128)S(1)}, u32[]{:S(2)}, u32[]{:S(2)}) collective-permute-start(f32[16,8,128]{2,1,0:T(8,128)S(1)} %slice_bitcast_fusion), channel_id=1, source_target_pairs={{8,0},{16,8},{24,16},{32,24},{40,32},{48,40},{56,48},{64,56},{72,6... | collective-permute-start | bytes 196616 | tf_op jit(solution)/shard_map/ppermute | solution.py:401
  84.2 0.6 broadcast_in_dim.3
  84.8 3.8 %all-to-all-start.3 = ((f32[32,1,128]{2,1,0:T(1,128)}), f32[32,1,128]{2,1,0:T(1,128)S(1)}, u32[]{:S(2)}, u32[]{:S(2)}) async-start(f32[32,1,128]{2,1,0:T(1,128)} %broadcast_in_dim.3), calls=%async_computation.3 | async-start | bytes 32768 | tf_op jit(solution)/shard_map/all_to_all | solution.py:398
  88.7 0.0 collective-permute-done.5.second_after_ref
  88.7 0.0 copy-done.13
  88.7 1.2 %rebuild.1 = (f32[8,16,8,128]{3,2,1,0:T(8,128)S(1)}, f32[8,16,8,128]{3,2,1,0:T(8,128)S(1)}) custom-call(s32[1]{0:T(128)} %bitcast.place_ref, f32[1]{0:T(128)} %bitcast.1.keep_ref, f32[8,16,8,128]{3,2,1,0:T(8,128)S(1)} %all-to-all-done.first_ref, f32[16,8,128]{2,1,0:T(8,128)S(1)} %copy-done.13, f32[8,16,8,128]{3,2,1,0:T(8,128)S(1)} %all-to-all-done.1.second_ref, ...), custom_call_target="tpu_custom_call" | custom-call | flops 10000000 | bytes 2000000 | tf_op jit(solution)/shard_map/rebuild/pallas_call | solution.py:464
  89.9 7.2 %all-to-all-done.3 = f32[32,1,128]{2,1,0:T(1,128)S(1)} async-done(((f32[32,1,128]{2,1,0:T(1,128)}), f32[32,1,128]{2,1,0:T(1,128)S(1)}, u32[]{:S(2)}, u32[]{:S(2)}) %all-to-all-start.3) | async-done | bytes 16416 | tf_op jit(solution)/shard_map/all_to_all | solution.py:398
  97.2 0.0 collective-permute-done.6.after_ref
  97.2 2.0 %last.1 = (f32[128,1024]{1,0:T(8,128)}, f32[128,1024]{1,0:T(8,128)}) custom-call(s32[1]{0:T(128)} %bitcast.place_ref, f32[1]{0:T(128)} %bitcast.1.keep_ref, f32[8,16,8,128]{3,2,1,0:T(8,128)S(1)} %get-tuple-element.29.base_ref, f32[8,16,8,128]{3,2,1,0:T(8,128)S(1)} %get-tuple-element.30.image_ref, f32[8,17,8,128]{3,2,1,0:T(8,128)S(1)} %all-to-all-done.2.moved_ref, ...), custom_call_target="tpu_custom_call" | custom-call | tf_op jit(solution)/shard_map/last/pallas_call | solution.py:473
  (4 shorter events, 0.0 us)
Async XLA Ops:
  4.9 21.7 %collective-permute-start.1 = (f32[16,64,128]{2,1,0:T(8,128)}, f32[16,64,128]{2,1,0:T(8,128)}, u32[]{:S(2)}, u32[]{:S(2)}) collective-permute-start(f32[16,64,128]{2,1,0:T(8,128)} %get-tuple-element.18.here_ref), channel_id=1, source_target_pairs={{0,0},{1,2},{2,1},{3,4},{4,3},{5,6},{6,5},{7,8},{8,7},{9,10},{10,9... | collective-permute-start | bytes 1572872 | tf_op jit(solution)/shard_map/ppermute | solution.py:395
  9.4 17.2 %collective-permute-start = (f32[16,64,128]{2,1,0:T(8,128)}, f32[16,64,128]{2,1,0:T(8,128)}, u32[]{:S(2)}, u32[]{:S(2)}) collective-permute-start(f32[16,64,128]{2,1,0:T(8,128)} %get-tuple-element.18.here_ref), channel_id=1, source_target_pairs={{0,1},{1,0},{2,3},{3,2},{4,5},{5,4},{6,7},{7,6},{8,9},{9,8},{10,11... | collective-permute-start | bytes 1572872 | tf_op jit(solution)/shard_map/ppermute | solution.py:395
  13.5 3.6 %copy-start.1 = (f32[16,4096]{1,0:T(8,128)S(1)}, f32[16,4096]{1,0:T(8,128)}, u32[]{:S(2)}) copy-start(f32[16,4096]{1,0:T(8,128)} %weights_ref.1) | copy-start | bytes 786436
  13.5 3.6 %copy-start.5 = (f32[16,8192]{1,0:T(8,128)S(1)}, f32[16,8192]{1,0:T(8,128)}, u32[]{:S(2)}) copy-start(f32[16,8192]{1,0:T(8,128)} %taps_ref.1) | copy-start | bytes 1572868
  13.5 13.0 %all-to-all-start = ((f32[8,16,8,128]{3,2,1,0:T(8,128)}), f32[8,16,8,128]{3,2,1,0:T(8,128)S(1)}, u32[]{:S(2)}, u32[]{:S(2)}) async-start(f32[8,16,8,128]{3,2,1,0:T(8,128)} %get-tuple-element.19), calls=%async_computation | async-start | bytes 1048576 | tf_op jit(solution)/shard_map/all_to_all | solution.py:398
  17.1 9.4 %copy-start = (bf16[384,256]{1,0:T(8,128)(2,1)S(1)}, bf16[384,256]{1,0:T(8,128)(2,1)}, u32[]{:S(2)}) copy-start(bf16[384,256]{1,0:T(8,128)(2,1)} %constant.42.clone.refs_3_.back_lanes_ref) | copy-start | bytes 589828
  17.1 9.4 %copy-start.2 = (bf16[768,128]{1,0:T(8,128)(2,1)S(1)}, bf16[768,128]{1,0:T(8,128)(2,1)}, u32[]{:S(2)}) copy-start(bf16[768,128]{1,0:T(8,128)(2,1)} %constant.46.clone.ahead_lanes_ref) | copy-start | bytes 589828
  17.1 9.4 %copy-start.3 = (f32[2,64,128]{2,1,0:T(8,128)S(1)}, f32[2,64,128]{2,1,0:T(8,128)}, u32[]{:S(2)}) copy-start(f32[2,64,128]{2,1,0:T(8,128)} %constant.44.clone.refs_5_.twist_ref) | copy-start | bytes 196612
  17.1 9.4 %copy-start.8 = (bf16[64,384]{1,0:T(8,128)(2,1)S(1)}, bf16[64,384]{1,0:T(8,128)(2,1)}, u32[]{:S(2)}) copy-start(bf16[64,384]{1,0:T(8,128)(2,1)} %constant.43.clone.refs_4_.back_rows_ref) | copy-start | bytes 147460
  17.2 9.4 %copy-start.10 = (bf16[128,192]{1,0:T(8,128)(2,1)S(1)}, bf16[128,192]{1,0:T(8,128)(2,1)}, u32[]{:S(2)}) copy-start(bf16[128,192]{1,0:T(8,128)(2,1)} %constant.45.clone.ahead_rows_ref) | copy-start | bytes 147460
  26.6 1.0 %copy-start.7 = (f32[16,64,128]{2,1,0:T(8,128)S(1)}, f32[16,64,128]{2,1,0:T(8,128)}, u32[]{:S(2)}) copy-start(f32[16,64,128]{2,1,0:T(8,128)} %get-tuple-element.18.here_ref) | copy-start | bytes 1572868
  34.3 6.2 %copy-start.6 = (f32[8,16,8,128]{3,2,1,0:T(8,128)}, f32[8,16,8,128]{3,2,1,0:T(8,128)S(1)}, u32[]{:S(2)}) copy-start(f32[8,16,8,128]{3,2,1,0:T(8,128)S(1)} %get-tuple-element.26) | copy-start | bytes 1572868
  34.3 19.1 %collective-permute-start.3 = (f32[16,64,128]{2,1,0:T(8,128)}, f32[16,64,128]{2,1,0:T(8,128)}, u32[]{:S(2)}, u32[]{:S(2)}) collective-permute-start(f32[16,64,128]{2,1,0:T(8,128)} %get-tuple-element.25.here_ref), channel_id=1, source_target_pairs={{0,0},{1,2},{2,1},{3,4},{4,3},{5,6},{6,5},{7,8},{8,7},{9,10},{10,9... | collective-permute-start | bytes 1572872 | tf_op jit(solution)/shard_map/ppermute | solution.py:395
  37.3 16.2 %collective-permute-start.2 = (f32[16,64,128]{2,1,0:T(8,128)}, f32[16,64,128]{2,1,0:T(8,128)}, u32[]{:S(2)}, u32[]{:S(2)}) collective-permute-start(f32[16,64,128]{2,1,0:T(8,128)} %get-tuple-element.25.here_ref), channel_id=1, source_target_pairs={{0,1},{1,0},{2,3},{3,2},{4,5},{5,4},{6,7},{7,6},{8,9},{9,8},{10,11... | collective-permute-start | bytes 1572872 | tf_op jit(solution)/shard_map/ppermute | solution.py:395
  40.5 12.9 %all-to-all-start.1 = ((f32[8,16,8,128]{3,2,1,0:T(8,128)}), f32[8,16,8,128]{3,2,1,0:T(8,128)S(1)}, u32[]{:S(2)}, u32[]{:S(2)}) async-start(f32[8,16,8,128]{3,2,1,0:T(8,128)} %copy-done.6), calls=%async_computation.1 | async-start | bytes 1048576 | tf_op jit(solution)/shard_map/all_to_all | solution.py:398
  44.0 6.9 %collective-permute-start.4 = (f32[16,8,128]{2,1,0:T(8,128)S(1)}, f32[16,8,128]{2,1,0:T(8,128)S(1)}, u32[]{:S(2)}, u32[]{:S(2)}) collective-permute-start(f32[16,8,128]{2,1,0:T(8,128)S(1)} %slice_bitcast_fusion.2), channel_id=1, source_target_pairs={{8,0},{16,8},{24,16},{32,24},{40,32},{48,40},{56,48},{64,56},{72,6... | collective-permute-start | bytes 196616 | tf_op jit(solution)/shard_map/ppermute | solution.py:401
  50.9 0.6 copy-start.12
  53.4 0.8 copy-start.4
  54.3 0.8 copy-start.9
  55.1 0.8 copy-start.11
  62.9 14.2 %all-to-all-start.2 = ((f32[8,17,8,128]{3,2,1,0:T(8,128)}), f32[8,17,8,128]{3,2,1,0:T(8,128)S(1)}, u32[]{:S(2)}, u32[]{:S(2)}) async-start(f32[8,17,8,128]{3,2,1,0:T(8,128)} %second.1), calls=%async_computation.2 | async-start | bytes 1114112 | tf_op jit(solution)/shard_map/all_to_all | solution.py:398
  67.3 21.4 %collective-permute-start.5 = (f32[16,8,128]{2,1,0:T(8,128)S(1)}, f32[16,8,128]{2,1,0:T(8,128)S(1)}, u32[]{:S(2)}, u32[]{:S(2)}) collective-permute-start(f32[16,8,128]{2,1,0:T(8,128)S(1)} %slice_bitcast_fusion.1), channel_id=1, source_target_pairs={{8,0},{16,8},{24,16},{32,24},{40,32},{48,40},{56,48},{64,56},{72,6... | collective-permute-start | bytes 196616 | tf_op jit(solution)/shard_map/ppermute | solution.py:401
  77.1 11.6 %copy-start.13 = (f32[16,8,128]{2,1,0:T(8,128)S(1)}, f32[16,8,128]{2,1,0:T(8,128)}, u32[]{:S(2)}) copy-start(f32[16,8,128]{2,1,0:T(8,128)} %copy-done.12) | copy-start | bytes 196612
  77.1 20.1 %collective-permute-start.6 = (f32[16,8,128]{2,1,0:T(8,128)S(1)}, f32[16,8,128]{2,1,0:T(8,128)S(1)}, u32[]{:S(2)}, u32[]{:S(2)}) collective-permute-start(f32[16,8,128]{2,1,0:T(8,128)S(1)} %slice_bitcast_fusion), channel_id=1, source_target_pairs={{8,0},{16,8},{24,16},{32,24},{40,32},{48,40},{56,48},{64,56},{72,6... | collective-permute-start | bytes 196616 | tf_op jit(solution)/shard_map/ppermute | solution.py:401
  84.8 12.4 %all-to-all-start.3 = ((f32[32,1,128]{2,1,0:T(1,128)}), f32[32,1,128]{2,1,0:T(1,128)S(1)}, u32[]{:S(2)}, u32[]{:S(2)}) async-start(f32[32,1,128]{2,1,0:T(1,128)} %broadcast_in_dim.3), calls=%async_computation.3 | async-start | bytes 32768 | tf_op jit(solution)/shard_map/all_to_all | solution.py:398

commit v5 on v4

--- a/solution.py
+++ b/solution.py
@@ -184,7 +184,7 @@
 
 def first_kernel(
     keep_ref, inside_ref, here_ref, across_ref, taps_ref, weights_ref,
-    ahead_rows_ref, ahead_lanes_ref, back_lanes_ref, back_rows_ref, twist_ref,
+    ahead_rows_ref, ahead_lanes_ref, back_lanes_ref, back_rows_ref, twist_ref, _,
     out_ref, sent_ref, side_ref, filtered,
 ):
     count = here_ref.shape[0]
@@ -230,7 +230,7 @@
 
 def second_kernel(
     keep_ref, inside_ref, here_ref, across_ref, side_ref, taps_ref, weights_ref,
-    ahead_rows_ref, ahead_lanes_ref, back_lanes_ref, back_rows_ref, twist_ref,
+    ahead_rows_ref, ahead_lanes_ref, back_lanes_ref, back_rows_ref, twist_ref, _, __,
     out_ref, filtered, sums,
 ):
     count = here_ref.shape[0]
@@ -373,6 +373,7 @@
 
 
 SMEM = pl.BlockSpec(memory_space=pltpu.SMEM)
+ANY = pl.BlockSpec(memory_space=pl.ANY)
 
 
 def local(observed_real, observed_imag, weights, taps):
@@ -398,9 +399,10 @@
         return lax.all_to_all(value, axis, split_axis=0, concat_axis=0, tiled=True)
 
     def from_later_group(moved):
-        return lax.ppermute(moved[0, :count], "tm", [((i + 1) % groups, i) for i in range(groups)])
+        return lax.ppermute(moved[0, :count], "tm", [(i + 1, i) for i in range(groups - 1)])
 
     seed_inputs = (observed_real, observed_imag, weights, back_lanes, back_rows, twist)
+    seed_inputs = tuple(pltpu.with_memory_space_constraint(v, pltpu.HBM) for v in seed_inputs)
     sent = shape(parts, count, 8, LANES)
     seeds, outgoing = pl.pallas_call(
         seed_kernel,
@@ -409,7 +411,7 @@
         out_specs=tuple(vmem(2)),
         scratch_shapes=[pltpu.VMEM(value.shape, value.dtype) for value in seed_inputs]
         + [pltpu.VMEM((count * ROWS, LANES), F32), pltpu.SemaphoreType.DMA((6,))],
-        compiler_params=params(62 * 1024 * 1024),
+        compiler_params=params(),
         name="seed",
     )(*seed_inputs)
     inside, across = neighbours(seeds)
@@ -426,27 +428,23 @@
     )(weights, taps)
     taps = taps.reshape(reach + 1, ROWS, LANES)
 
-    inside, across, first_moved = lax.optimization_barrier((inside, across, first_moved))
     images, outgoing, side = pl.pallas_call(
         first_kernel,
         out_shape=(blocks, sent, shape(reach + count, ROWS, LANES)),
-        in_specs=[SMEM] + vmem(10),
+        in_specs=[SMEM] + vmem(10) + [ANY],
         out_specs=tuple(vmem(3)),
         scratch_shapes=[pltpu.VMEM((count, ROWS, LANES), F32)],
         compiler_params=params(),
         name="first",
-    )(keep, inside, seeds, across, taps, weights, *tables)
+    )(keep, inside, seeds, across, taps, weights, *tables, first_moved)
     inside, across = neighbours(images)
     second_moved = exchange(outgoing, "chan")
     first_after = from_later_group(first_moved)
-    inside, across, second_moved, first_after = lax.optimization_barrier(
-        (inside, across, second_moved, first_after)
-    )
 
     outgoing = pl.pallas_call(
         second_kernel,
         out_shape=shape(parts, count + 1, 8, LANES),
-        in_specs=[SMEM] + vmem(11),
+        in_specs=[SMEM] + vmem(11) + [ANY, ANY],
         out_specs=vmem(1)[0],
         scratch_shapes=[
             pltpu.VMEM((count, ROWS, LANES), F32),
@@ -454,7 +452,7 @@
         ],
         compiler_params=params(),
         name="second",
-    )(keep, inside, images, across, side, taps, weights, *tables)
+    )(keep, inside, images, across, side, taps, weights, *tables, second_moved, first_after)
 
     moved = exchange(outgoing, "chan")
     after = from_later_group(moved)

time: 100 us -> 103 us (1.030)
  waiting for transfers between devices: 21.5 us -> 31.7 us
  starting transfers between devices: 49.6 us -> 42.1 us
    ppermute x3, starting transfers between devices: 19.6 us -> 4.01 us  [from_later_group(): lax.ppermute(moved[0, :count], 'tm', [(i + 1, i) for i in range(groups -...]
    all_to_all x4, starting transfers between devices: 15.2 us -> 30 us  [exchange(): return lax.all_to_all(value, axis, split_axis=0, concat_axis=0, tiled=True)]
    all_to_all x4, waiting for transfers between devices: 19.9 us -> 27.4 us  [exchange(): return lax.all_to_all(value, axis, split_axis=0, concat_axis=0, tiled=True)]
    ppermute x2, starting transfers between devices: 7.47 us -> 4 us  [neighbours(): lax.ppermute(block, AXES, across)]
    ppermute x2, starting transfers between devices: 7.37 us -> 4.02 us  [neighbours(): lax.ppermute(block, AXES, inside)]
    ppermute x3, waiting for transfers between devices: 1.53 us -> 4.27 us  [from_later_group(): lax.ppermute(moved[0, :count], 'tm', [(i + 1, i) for i in range(groups -...]
    unnamed x28 -> x30, local copies, waits for them, and re-layouts: 4.19 us -> 3.85 us
where the time goes in v5:
time: 103 us; the launch traced here: 102 us
  starting transfers between devices  42.1 us (41%)
  waiting for transfers between devices  31.7 us (31%)
  Pallas kernels  22.5 us (22%)
  local copies, waits for them, and re-layouts  4.49 us (4%)
    all_to_all x4, starting transfers between devices, exchange(): return lax.all_to_all(value, axis, split_axis=0, concat_axis=0, tiled=True)  30 us
    all_to_all x4, waiting for transfers between devices, exchange(): return lax.all_to_all(value, axis, split_axis=0, concat_axis=0, tiled=True)  27.4 us
    pallas_call x1, Pallas kernels, local(): pl.pallas_call(second_kernel, out_shape=shape(parts, count + 1, 8, LANES)...  7.01 us
    pallas_call x1, Pallas kernels, local(): pl.pallas_call(first_kernel, out_shape=(blocks, sent, shape(reach + count...  6.82 us
    ppermute x3, waiting for transfers between devices, from_later_group(): lax.ppermute(moved[0, :count], 'tm', [(i + 1, i) for i in range(groups -...  4.27 us
    pallas_call x1, Pallas kernels, local(): pl.pallas_call(seed_kernel, out_shape=(blocks, sent), in_specs=[pl.BlockS...  4.23 us
    ppermute x2, starting transfers between devices, neighbours(): lax.ppermute(block, AXES, inside)  4.02 us
    ppermute x3, starting transfers between devices, from_later_group(): lax.ppermute(moved[0, :count], 'tm', [(i + 1, i) for i in range(groups -...  4.01 us
  transfers between devices with their start and end apart: 11, of which 5 were waited for; matrix products, arithmetic and copies ran while one was open for 1% of the time, Pallas kernels for 2%

profile of v5, /device:TPU:1, one launch (start us, length us, event | category | flops | bytes accessed | tf_op | source)
XLA Modules:
  0.0 101.7 jit_solution(12302039412132135125)
XLA Ops:
  0.6 4.2 %seed.1 = (f32[16,64,128]{2,1,0:T(8,128)}, f32[8,16,8,128]{3,2,1,0:T(8,128)}) custom-call(f32[16,4096]{1,0:T(8,128)} %refs_0_.1, f32[16,4096]{1,0:T(8,128)} %refs_1_.1, f32[16,4096]{1,0:T(8,128)} %weights_ref.1, bf16[384,256]{1,0:T(8,128)(2,1)} %constant.42.clone.refs_3_.back_lanes_ref, bf16[64,384]{1,0:T(8,128)(2,1)} %constant.43.clone.refs_4_.back_rows_ref, ...), custom_call_target="tpu_custom_call" | custom-call | tf_op jit(solution)/shard_map/seed/pallas_call | solution.py:407
  4.9 3.3 %collective-permute-start.1 = (f32[16,64,128]{2,1,0:T(8,128)}, f32[16,64,128]{2,1,0:T(8,128)}, u32[]{:S(2)}, u32[]{:S(2)}) collective-permute-start(f32[16,64,128]{2,1,0:T(8,128)} %get-tuple-element.12.here_ref), channel_id=1, source_target_pairs={{0,1},{1,0},{2,3},{3,2},{4,5},{5,4},{6,7},{7,6},{8,9},{9,8},{10,11... | collective-permute-start | bytes 1572872 | tf_op jit(solution)/shard_map/ppermute | solution.py:396
  8.2 1.9 %collective-permute-start.2 = (f32[16,64,128]{2,1,0:T(8,128)}, f32[16,64,128]{2,1,0:T(8,128)}, u32[]{:S(2)}, u32[]{:S(2)}) collective-permute-start(f32[16,64,128]{2,1,0:T(8,128)} %get-tuple-element.12.here_ref), channel_id=1, source_target_pairs={{0,0},{1,2},{2,1},{3,4},{4,3},{5,6},{6,5},{7,8},{8,7},{9,10},{10,9... | collective-permute-start | bytes 1572872 | tf_op jit(solution)/shard_map/ppermute | solution.py:396
  10.1 0.0 copy-start.1
  10.1 0.0 copy-start.5
  10.1 7.0 %all-to-all-start = ((f32[8,16,8,128]{3,2,1,0:T(8,128)}), f32[8,16,8,128]{3,2,1,0:T(8,128)S(1)}, u32[]{:S(2)}, u32[]{:S(2)}) async-start(f32[8,16,8,128]{3,2,1,0:T(8,128)} %get-tuple-element.11), calls=%async_computation | async-start | bytes 1048576 | tf_op jit(solution)/shard_map/all_to_all | solution.py:399
  17.1 0.0 copy-done.1
  17.1 0.0 copy-done.5
  17.1 0.0 copy-start
  17.1 0.0 copy-start.2
  17.1 0.0 copy-start.3
  17.1 0.0 copy-start.7
  17.2 0.0 copy-start.8
  17.2 1.2 %arrange.1 = (f32[16,64,128]{2,1,0:T(8,128)S(1)}, f32[1024,128]{1,0:T(8,128)S(1)}) custom-call(f32[16,4096]{1,0:T(8,128)S(1)} %copy-done.1, f32[16,8192]{1,0:T(8,128)S(1)} %copy-done.5), custom_call_target="tpu_custom_call" | custom-call | flops 10000000 | bytes 2000000 | tf_op jit(solution)/shard_map/arrange/pallas_call | solution.py:419
  18.4 0.1 add_convert_fusion.keep_ref
  18.4 0.0 copy-start.13
  18.4 8.3 %all-to-all-done._.first_ref = f32[8,16,8,128]{3,2,1,0:T(8,128)S(1)} async-done(((f32[8,16,8,128]{3,2,1,0:T(8,128)}), f32[8,16,8,128]{3,2,1,0:T(8,128)S(1)}, u32[]{:S(2)}, u32[]{:S(2)}) %all-to-all-start) | async-done | bytes 524320 | tf_op jit(solution)/shard_map/all_to_all | solution.py:399
  26.8 0.0 collective-permute-done.1.inside_ref
  26.8 0.0 collective-permute-done.2.across_ref
  26.8 0.0 copy-done.13
  26.8 0.0 copy-done
  26.8 0.0 copy-done.2
  26.8 0.0 copy-done.3
  26.8 0.0 copy-done.7
  26.8 0.0 copy-done.8
  26.8 6.8 %first.1 = (f32[16,64,128]{2,1,0:T(8,128)}, f32[8,16,8,128]{3,2,1,0:T(8,128)S(1)}, f32[31,64,128]{2,1,0:T(8,128)S(1)}) custom-call(f32[3]{0:T(128)S(1)} %add_convert_fusion.keep_ref, f32[16,64,128]{2,1,0:T(8,128)} %collective-permute-done.1.inside_ref, f32[16,64,128]{2,1,0:T(8,128)} %get-tuple-element.12.here_ref, ...), custom_call_target="tpu_custom_call" | custom-call | tf_op jit(solution)/shard_map/first/pallas_call | solution.py:431
  33.7 0.0 copy-start.6
  33.7 0.7 collective-permute-start.4
  34.4 2.1 %collective-permute-start.5 = (f32[16,64,128]{2,1,0:T(8,128)}, f32[16,64,128]{2,1,0:T(8,128)}, u32[]{:S(2)}, u32[]{:S(2)}) collective-permute-start(f32[16,64,128]{2,1,0:T(8,128)} %get-tuple-element.18.here_ref), channel_id=1, source_target_pairs={{0,0},{1,2},{2,1},{3,4},{4,3},{5,6},{6,5},{7,8},{8,7},{9,10},{10,9... | collective-permute-start | bytes 1572872 | tf_op jit(solution)/shard_map/ppermute | solution.py:396
  36.5 0.0 copy-done.6
  36.5 6.6 %all-to-all-start.1 = ((f32[8,16,8,128]{3,2,1,0:T(8,128)}), f32[8,16,8,128]{3,2,1,0:T(8,128)S(1)}, u32[]{:S(2)}, u32[]{:S(2)}) async-start(f32[8,16,8,128]{3,2,1,0:T(8,128)} %copy-done.6), calls=%async_computation.1 | async-start | bytes 1048576 | tf_op jit(solution)/shard_map/all_to_all | solution.py:399
  43.1 1.3 %collective-permute-start = (f32[16,8,128]{2,1,0:T(8,128)S(1)}, f32[16,8,128]{2,1,0:T(8,128)S(1)}, u32[]{:S(2)}, u32[]{:S(2)}) collective-permute-start(f32[16,8,128]{2,1,0:T(8,128)S(1)} %slice_bitcast_fusion.2), channel_id=1, source_target_pairs={{8,0},{16,8},{24,16},{32,24},{40,32},{48,40},{56,48},{64,56},{72,6... | collective-permute-start | bytes 196616 | tf_op jit(solution)/shard_map/ppermute | solution.py:402
  44.4 4.3 %collective-permute-done.first_after_ref.__ = f32[16,8,128]{2,1,0:T(8,128)S(1)} collective-permute-done((f32[16,8,128]{2,1,0:T(8,128)S(1)}, f32[16,8,128]{2,1,0:T(8,128)S(1)}, u32[]{:S(2)}, u32[]{:S(2)}) %collective-permute-start) | collective-permute-done | bytes 65568 | tf_op jit(solution)/shard_map/ppermute | solution.py:402
  48.7 0.0 copy-start.10
  48.7 0.6 copy-done.10
  49.3 3.3 %all-to-all-done.1.second_ref._ = f32[8,16,8,128]{3,2,1,0:T(8,128)S(1)} async-done(((f32[8,16,8,128]{3,2,1,0:T(8,128)}), f32[8,16,8,128]{3,2,1,0:T(8,128)S(1)}, u32[]{:S(2)}, u32[]{:S(2)}) %all-to-all-start.1) | async-done | bytes 524320 | tf_op jit(solution)/shard_map/all_to_all | solution.py:399
  52.6 0.0 copy-start.14
  52.6 0.0 collective-permute-done.4.inside_ref
  52.6 0.0 collective-permute-done.5.across_ref
  52.6 0.7 copy-done.14
  53.3 0.0 copy-start.4
  53.3 0.8 copy-done.4
  54.1 0.0 copy-start.9
  54.1 0.8 copy-done.9
  54.9 0.0 copy-start.11
  54.9 0.8 copy-done.11
  55.8 7.0 %second.1 = f32[8,17,8,128]{3,2,1,0:T(8,128)} custom-call(f32[3]{0:T(128)S(1)} %copy-done.14, f32[16,64,128]{2,1,0:T(8,128)} %collective-permute-done.4.inside_ref, f32[16,64,128]{2,1,0:T(8,128)} %get-tuple-element.18.here_ref, f32[16,64,128]{2,1,0:T(8,128)} %collective-permute-done.5.across_ref, f32[31,64,128]{2,1,0:T(8,128)S(1)} %get-tuple-element.19.side_ref, ...), custom_call_target="tpu_custom_call" | custom-call | tf_op jit(solution)/shard_map/second/pallas_call | solution.py:444
  62.8 4.7 %all-to-all-start.2 = ((f32[8,17,8,128]{3,2,1,0:T(8,128)}), f32[8,17,8,128]{3,2,1,0:T(8,128)S(1)}, u32[]{:S(2)}, u32[]{:S(2)}) async-start(f32[8,17,8,128]{3,2,1,0:T(8,128)} %second.1), calls=%async_computation.2 | async-start | bytes 1114112 | tf_op jit(solution)/shard_map/all_to_all | solution.py:399
  67.5 1.3 %collective-permute-start.3 = (f32[16,8,128]{2,1,0:T(8,128)S(1)}, f32[16,8,128]{2,1,0:T(8,128)S(1)}, u32[]{:S(2)}, u32[]{:S(2)}) collective-permute-start(f32[16,8,128]{2,1,0:T(8,128)S(1)} %slice_bitcast_fusion.1), channel_id=1, source_target_pairs={{8,0},{16,8},{24,16},{32,24},{40,32},{48,40},{56,48},{64,56},{72,6... | collective-permute-start | bytes 196616 | tf_op jit(solution)/shard_map/ppermute | solution.py:402
  68.8 8.5 %all-to-all-done.2.moved_ref = f32[8,17,8,128]{3,2,1,0:T(8,128)S(1)} async-done(((f32[8,17,8,128]{3,2,1,0:T(8,128)}), f32[8,17,8,128]{3,2,1,0:T(8,128)S(1)}, u32[]{:S(2)}, u32[]{:S(2)}) %all-to-all-start.2) | async-done | bytes 557088 | tf_op jit(solution)/shard_map/all_to_all | solution.py:399
  77.4 0.0 copy-start.12
  77.4 1.4 %collective-permute-start.6 = (f32[16,8,128]{2,1,0:T(8,128)S(1)}, f32[16,8,128]{2,1,0:T(8,128)S(1)}, u32[]{:S(2)}, u32[]{:S(2)}) collective-permute-start(f32[16,8,128]{2,1,0:T(8,128)S(1)} %slice_bitcast_fusion), channel_id=1, source_target_pairs={{8,0},{16,8},{24,16},{32,24},{40,32},{48,40},{56,48},{64,56},{72,6... | collective-permute-start | bytes 196616 | tf_op jit(solution)/shard_map/ppermute | solution.py:402
  78.8 0.6 broadcast_in_dim.3
  79.5 11.7 %all-to-all-start.3 = ((f32[32,1,128]{2,1,0:T(1,128)}), f32[32,1,128]{2,1,0:T(1,128)S(1)}, u32[]{:S(2)}, u32[]{:S(2)}) async-start(f32[32,1,128]{2,1,0:T(1,128)} %broadcast_in_dim.3), calls=%async_computation.3 | async-start | bytes 32768 | tf_op jit(solution)/shard_map/all_to_all | solution.py:399
  91.2 0.0 collective-permute-done.3.second_after_ref
  91.2 0.0 copy-done.12
  91.2 1.2 %rebuild.1 = (f32[8,16,8,128]{3,2,1,0:T(8,128)S(1)}, f32[8,16,8,128]{3,2,1,0:T(8,128)S(1)}) custom-call(s32[1]{0:T(128)} %bitcast.place_ref, f32[1]{0:T(128)} %bitcast.1.keep_ref, f32[8,16,8,128]{3,2,1,0:T(8,128)S(1)} %all-to-all-done._.first_ref, f32[16,8,128]{2,1,0:T(8,128)S(1)} %copy-done.12, f32[8,16,8,128]{3,2,1,0:T(8,128)S(1)} %all-to-all-done.1.second_ref._, ...), custom_call_target="tpu_custom_call" | custom-call | flops 10000000 | bytes 2000000 | tf_op jit(solution)/shard_map/rebuild/pallas_call | solution.py:462
  92.4 7.2 %all-to-all-done.3 = f32[32,1,128]{2,1,0:T(1,128)S(1)} async-done(((f32[32,1,128]{2,1,0:T(1,128)}), f32[32,1,128]{2,1,0:T(1,128)S(1)}, u32[]{:S(2)}, u32[]{:S(2)}) %all-to-all-start.3) | async-done | bytes 16416 | tf_op jit(solution)/shard_map/all_to_all | solution.py:399
  99.7 0.0 collective-permute-done.6.after_ref
  99.7 2.0 %last.1 = (f32[128,1024]{1,0:T(8,128)}, f32[128,1024]{1,0:T(8,128)}) custom-call(s32[1]{0:T(128)} %bitcast.place_ref, f32[1]{0:T(128)} %bitcast.1.keep_ref, f32[8,16,8,128]{3,2,1,0:T(8,128)S(1)} %get-tuple-element.16.base_ref, f32[8,16,8,128]{3,2,1,0:T(8,128)S(1)} %get-tuple-element.17.image_ref, f32[8,17,8,128]{3,2,1,0:T(8,128)S(1)} %all-to-all-done.2.moved_ref, ...), custom_call_target="tpu_custom_call" | custom-call | tf_op jit(solution)/shard_map/last/pallas_call | solution.py:471
  (4 shorter events, 0.0 us)
Async XLA Ops:
  4.9 21.9 %collective-permute-start.1 = (f32[16,64,128]{2,1,0:T(8,128)}, f32[16,64,128]{2,1,0:T(8,128)}, u32[]{:S(2)}, u32[]{:S(2)}) collective-permute-start(f32[16,64,128]{2,1,0:T(8,128)} %get-tuple-element.12.here_ref), channel_id=1, source_target_pairs={{0,1},{1,0},{2,3},{3,2},{4,5},{5,4},{6,7},{7,6},{8,9},{9,8},{10,11... | collective-permute-start | bytes 1572872 | tf_op jit(solution)/shard_map/ppermute | solution.py:396
  8.2 18.6 %collective-permute-start.2 = (f32[16,64,128]{2,1,0:T(8,128)}, f32[16,64,128]{2,1,0:T(8,128)}, u32[]{:S(2)}, u32[]{:S(2)}) collective-permute-start(f32[16,64,128]{2,1,0:T(8,128)} %get-tuple-element.12.here_ref), channel_id=1, source_target_pairs={{0,0},{1,2},{2,1},{3,4},{4,3},{5,6},{6,5},{7,8},{8,7},{9,10},{10,9... | collective-permute-start | bytes 1572872 | tf_op jit(solution)/shard_map/ppermute | solution.py:396
  10.1 7.0 %copy-start.1 = (f32[16,4096]{1,0:T(8,128)S(1)}, f32[16,4096]{1,0:T(8,128)}, u32[]{:S(2)}) copy-start(f32[16,4096]{1,0:T(8,128)} %weights_ref.1) | copy-start | bytes 786436
  10.1 7.0 %copy-start.5 = (f32[16,8192]{1,0:T(8,128)S(1)}, f32[16,8192]{1,0:T(8,128)}, u32[]{:S(2)}) copy-start(f32[16,8192]{1,0:T(8,128)} %taps_ref.1) | copy-start | bytes 1572868
  10.1 16.6 %all-to-all-start = ((f32[8,16,8,128]{3,2,1,0:T(8,128)}), f32[8,16,8,128]{3,2,1,0:T(8,128)S(1)}, u32[]{:S(2)}, u32[]{:S(2)}) async-start(f32[8,16,8,128]{3,2,1,0:T(8,128)} %get-tuple-element.11), calls=%async_computation | async-start | bytes 1048576 | tf_op jit(solution)/shard_map/all_to_all | solution.py:399
  17.1 9.7 %copy-start = (bf16[384,256]{1,0:T(8,128)(2,1)S(1)}, bf16[384,256]{1,0:T(8,128)(2,1)}, u32[]{:S(2)}) copy-start(bf16[384,256]{1,0:T(8,128)(2,1)} %constant.42.clone.refs_3_.back_lanes_ref) | copy-start | bytes 589828
  17.1 9.7 %copy-start.2 = (bf16[768,128]{1,0:T(8,128)(2,1)S(1)}, bf16[768,128]{1,0:T(8,128)(2,1)}, u32[]{:S(2)}) copy-start(bf16[768,128]{1,0:T(8,128)(2,1)} %constant.46.clone.ahead_lanes_ref) | copy-start | bytes 589828
  17.1 9.7 %copy-start.3 = (f32[2,64,128]{2,1,0:T(8,128)S(1)}, f32[2,64,128]{2,1,0:T(8,128)}, u32[]{:S(2)}) copy-start(f32[2,64,128]{2,1,0:T(8,128)} %constant.44.clone.refs_5_.twist_ref) | copy-start | bytes 196612
  17.1 9.7 %copy-start.7 = (bf16[64,384]{1,0:T(8,128)(2,1)S(1)}, bf16[64,384]{1,0:T(8,128)(2,1)}, u32[]{:S(2)}) copy-start(bf16[64,384]{1,0:T(8,128)(2,1)} %constant.43.clone.refs_4_.back_rows_ref) | copy-start | bytes 147460
  17.2 9.7 %copy-start.8 = (bf16[128,192]{1,0:T(8,128)(2,1)S(1)}, bf16[128,192]{1,0:T(8,128)(2,1)}, u32[]{:S(2)}) copy-start(bf16[128,192]{1,0:T(8,128)(2,1)} %constant.45.clone.ahead_rows_ref) | copy-start | bytes 147460
  18.4 8.3 %copy-start.13 = (f32[3]{0:T(128)}, f32[3]{0:T(128)S(1)}, u32[]{:S(2)}) copy-start(f32[3]{0:T(128)S(1)} %add_convert_fusion.keep_ref) | copy-start | bytes 40
  33.7 2.8 %copy-start.6 = (f32[8,16,8,128]{3,2,1,0:T(8,128)}, f32[8,16,8,128]{3,2,1,0:T(8,128)S(1)}, u32[]{:S(2)}) copy-start(f32[8,16,8,128]{3,2,1,0:T(8,128)S(1)} %get-tuple-element.15) | copy-start | bytes 1572868
  33.7 18.9 %collective-permute-start.4 = (f32[16,64,128]{2,1,0:T(8,128)}, f32[16,64,128]{2,1,0:T(8,128)}, u32[]{:S(2)}, u32[]{:S(2)}) collective-permute-start(f32[16,64,128]{2,1,0:T(8,128)} %get-tuple-element.18.here_ref), channel_id=1, source_target_pairs={{0,1},{1,0},{2,3},{3,2},{4,5},{5,4},{6,7},{7,6},{8,9},{9,8},{10,11... | collective-permute-start | bytes 1572872 | tf_op jit(solution)/shard_map/ppermute | solution.py:396
  34.4 18.3 %collective-permute-start.5 = (f32[16,64,128]{2,1,0:T(8,128)}, f32[16,64,128]{2,1,0:T(8,128)}, u32[]{:S(2)}, u32[]{:S(2)}) collective-permute-start(f32[16,64,128]{2,1,0:T(8,128)} %get-tuple-element.18.here_ref), channel_id=1, source_target_pairs={{0,0},{1,2},{2,1},{3,4},{4,3},{5,6},{6,5},{7,8},{8,7},{9,10},{10,9... | collective-permute-start | bytes 1572872 | tf_op jit(solution)/shard_map/ppermute | solution.py:396
  36.5 16.1 %all-to-all-start.1 = ((f32[8,16,8,128]{3,2,1,0:T(8,128)}), f32[8,16,8,128]{3,2,1,0:T(8,128)S(1)}, u32[]{:S(2)}, u32[]{:S(2)}) async-start(f32[8,16,8,128]{3,2,1,0:T(8,128)} %copy-done.6), calls=%async_computation.1 | async-start | bytes 1048576 | tf_op jit(solution)/shard_map/all_to_all | solution.py:399
  43.1 5.6 %collective-permute-start = (f32[16,8,128]{2,1,0:T(8,128)S(1)}, f32[16,8,128]{2,1,0:T(8,128)S(1)}, u32[]{:S(2)}, u32[]{:S(2)}) collective-permute-start(f32[16,8,128]{2,1,0:T(8,128)S(1)} %slice_bitcast_fusion.2), channel_id=1, source_target_pairs={{8,0},{16,8},{24,16},{32,24},{40,32},{48,40},{56,48},{64,56},{72,6... | collective-permute-start | bytes 196616 | tf_op jit(solution)/shard_map/ppermute | solution.py:402
  48.7 0.6 copy-start.10
  52.6 0.7 copy-start.14
  53.3 0.8 copy-start.4
  54.1 0.8 copy-start.9
  54.9 0.8 copy-start.11
  62.8 14.6 %all-to-all-start.2 = ((f32[8,17,8,128]{3,2,1,0:T(8,128)}), f32[8,17,8,128]{3,2,1,0:T(8,128)S(1)}, u32[]{:S(2)}, u32[]{:S(2)}) async-start(f32[8,17,8,128]{3,2,1,0:T(8,128)} %second.1), calls=%async_computation.2 | async-start | bytes 1114112 | tf_op jit(solution)/shard_map/all_to_all | solution.py:399
  67.5 23.6 %collective-permute-start.3 = (f32[16,8,128]{2,1,0:T(8,128)S(1)}, f32[16,8,128]{2,1,0:T(8,128)S(1)}, u32[]{:S(2)}, u32[]{:S(2)}) collective-permute-start(f32[16,8,128]{2,1,0:T(8,128)S(1)} %slice_bitcast_fusion.1), channel_id=1, source_target_pairs={{8,0},{16,8},{24,16},{32,24},{40,32},{48,40},{56,48},{64,56},{72,6... | collective-permute-start | bytes 196616 | tf_op jit(solution)/shard_map/ppermute | solution.py:402
  77.4 13.8 %copy-start.12 = (f32[16,8,128]{2,1,0:T(8,128)S(1)}, f32[16,8,128]{2,1,0:T(8,128)}, u32[]{:S(2)}) copy-start(f32[16,8,128]{2,1,0:T(8,128)} %copy-done.10) | copy-start | bytes 196612
  77.4 22.3 %collective-permute-start.6 = (f32[16,8,128]{2,1,0:T(8,128)S(1)}, f32[16,8,128]{2,1,0:T(8,128)S(1)}, u32[]{:S(2)}, u32[]{:S(2)}) collective-permute-start(f32[16,8,128]{2,1,0:T(8,128)S(1)} %slice_bitcast_fusion), channel_id=1, source_target_pairs={{8,0},{16,8},{24,16},{32,24},{40,32},{48,40},{56,48},{64,56},{72,6... | collective-permute-start | bytes 196616 | tf_op jit(solution)/shard_map/ppermute | solution.py:402
  79.5 20.2 %all-to-all-start.3 = ((f32[32,1,128]{2,1,0:T(1,128)}), f32[32,1,128]{2,1,0:T(1,128)S(1)}, u32[]{:S(2)}, u32[]{:S(2)}) async-start(f32[32,1,128]{2,1,0:T(1,128)} %broadcast_in_dim.3), calls=%async_computation.3 | async-start | bytes 32768 | tf_op jit(solution)/shard_map/all_to_all | solution.py:399

commit v6 on v3

--- a/solution.py
+++ b/solution.py
@@ -16,7 +16,7 @@
 F32 = jnp.float32
 BF16 = jnp.bfloat16
 AXES = ("tm", "chan")
-VMEM_BYTES = 40 * 1024 * 1024
+VMEM_BYTES = 16 * 1024 * 1024
 
 
 def params(limit=VMEM_BYTES):
@@ -362,6 +362,7 @@
         return lax.all_to_all(value, axis, split_axis=0, concat_axis=0, tiled=True)
 
     seed_inputs = (observed_real, observed_imag, weights, back_lanes, back_rows, twist)
+    seed_inputs = tuple(pltpu.with_memory_space_constraint(v, pltpu.HBM) for v in seed_inputs)
     seeds = pl.pallas_call(
         seed_kernel,
         out_shape=blocks,
@@ -369,7 +370,7 @@
         out_specs=vmem(1)[0],
         scratch_shapes=[pltpu.VMEM(value.shape, value.dtype) for value in seed_inputs]
         + [pltpu.VMEM((count * ROWS, LANES), F32), pltpu.SemaphoreType.DMA((6,))],
-        compiler_params=params(62 * 1024 * 1024),
+        compiler_params=params(),
         name="seed",
     )(*seed_inputs)
     inside, across = neighbours(seeds)
@@ -411,7 +412,7 @@
 
     moved = exchange(outgoing, "chan")
     after = lax.ppermute(
-        moved[0, 2 * count : 3 * count], "tm", [((i + 1) % groups, i) for i in range(groups)]
+        moved[0, 2 * count : 3 * count], "tm", [(i + 1, i) for i in range(groups - 1)]
     )
     sums = jnp.sum(moved[:, 3 * count], (0, 1))
     sums = exchange(jnp.broadcast_to(sums, (groups, LANES)), "tm")

time: 97.3 us -> 97.7 us (level)
  starting transfers between devices: 26.2 us -> 27.7 us
  local copies, waits for them, and re-layouts: 1.7 us -> 0.67 us
    all_to_all x1, starting transfers between devices: 10.3 us -> 18.1 us  [exchange(): return lax.all_to_all(value, axis, split_axis=0, concat_axis=0, tiled=True)]
    ppermute x1, starting transfers between devices: 7.15 us -> 1.28 us  [local(): lax.ppermute(moved[0, 2 * count:3 * count], 'tm', [(i + 1, i) for i in ra...]
    unnamed x16 -> x14, local copies, waits for them, and re-layouts: 1.08 us -> 0.04 us
where the time goes in v6:
time: 97.7 us; the launch traced here: 97.4 us
  blocking collectives  29.7 us (30%)
  starting transfers between devices  27.7 us (28%)
  waiting for transfers between devices  20.7 us (21%)
  Pallas kernels  17.6 us (18%)
    all_to_all x1, blocking collectives, exchange(): return lax.all_to_all(value, axis, split_axis=0, concat_axis=0, tiled=True)  29.7 us
    all_to_all x1, starting transfers between devices, exchange(): return lax.all_to_all(value, axis, split_axis=0, concat_axis=0, tiled=True)  18.1 us
    ppermute x2, waiting for transfers between devices, neighbours(): lax.ppermute(block, AXES, across)  12.2 us
    all_to_all x1, waiting for transfers between devices, exchange(): return lax.all_to_all(value, axis, split_axis=0, concat_axis=0, tiled=True)  8.5 us
    ppermute x2, starting transfers between devices, neighbours(): lax.ppermute(block, AXES, across)  8.15 us
    pallas_call x1, Pallas kernels, local(): pl.pallas_call(first_kernel, out_shape=(blocks, shape(reach + count, ROWS...  5.7 us
    pallas_call x1, Pallas kernels, local(): pl.pallas_call(second_kernel, out_shape=shape(parts, 3 * count + 1, 8, LA...  5.37 us
    pallas_call x1, Pallas kernels, local(): pl.pallas_call(seed_kernel, out_shape=blocks, in_specs=[pl.BlockSpec(memo...  3.36 us
  transfers between devices with their start and end apart: 6, of which 3 were waited for; matrix products, arithmetic and copies ran while one was open for 1% of the time, Pallas kernels for 1%

profile of v6, /device:TPU:1, one launch (start us, length us, event | category | flops | bytes accessed | tf_op | source)
XLA Modules:
  0.0 97.4 jit_solution(3572796556951091423)
XLA Ops:
  0.6 0.0 copy-start.3
  0.6 0.0 copy-start.5
  0.7 0.0 copy-start
  0.7 0.0 copy-start.2
  0.7 0.0 copy-start.6
  0.7 0.0 copy-start.1
  0.7 0.0 copy-start.4
  0.7 3.4 %seed.1.here_ref = f32[16,64,128]{2,1,0:T(8,128)S(1)} custom-call(f32[16,4096]{1,0:T(8,128)} %refs_0_.1, f32[16,4096]{1,0:T(8,128)} %refs_1_.1, f32[16,4096]{1,0:T(8,128)} %weights_ref.1, bf16[384,256]{1,0:T(8,128)(2,1)} %constant.42.clone.refs_3_.back_lanes_ref, bf16[64,384]{1,0:T(8,128)(2,1)} %constant.43.clone.refs_4_.back_rows_ref, ...), custom_call_target="tpu_custom_call" | custom-call | tf_op jit(solution)/shard_map/seed/pallas_call | solution.py:366
  4.1 4.5 %collective-permute-start.1 = (f32[16,64,128]{2,1,0:T(8,128)S(1)}, f32[16,64,128]{2,1,0:T(8,128)S(1)}, u32[]{:S(2)}, u32[]{:S(2)}) collective-permute-start(f32[16,64,128]{2,1,0:T(8,128)S(1)} %seed.1.here_ref), channel_id=1, source_target_pairs={{0,0},{1,2},{2,1},{3,4},{4,3},{5,6},{6,5},{7,8},{8,7},{9,10},{10,9... | collective-permute-start | bytes 1572872 | tf_op jit(solution)/shard_map/ppermute | solution.py:359
  8.6 0.1 collective-permute-start
  8.7 0.0 copy-done.1
  8.7 0.0 copy-done.4
  8.7 1.2 %arrange.1 = (f32[16,64,128]{2,1,0:T(8,128)S(1)}, f32[1024,128]{1,0:T(8,128)S(1)}) custom-call(f32[16,4096]{1,0:T(8,128)S(1)} %copy-done.1, f32[16,8192]{1,0:T(8,128)S(1)} %copy-done.4), custom_call_target="tpu_custom_call" | custom-call | flops 10000000 | bytes 2000000 | tf_op jit(solution)/shard_map/arrange/pallas_call | solution.py:377
  9.9 0.1 add_convert_fusion.keep_ref
  10.0 5.4 %collective-permute-done.1.across_ref = f32[16,64,128]{2,1,0:T(8,128)S(1)} collective-permute-done((f32[16,64,128]{2,1,0:T(8,128)S(1)}, f32[16,64,128]{2,1,0:T(8,128)S(1)}, u32[]{:S(2)}, u32[]{:S(2)}) %collective-permute-start.1) | collective-permute-done | bytes 524320 | tf_op jit(solution)/shard_map/ppermute | solution.py:359
  15.4 0.0 collective-permute-done.inside_ref
  15.5 0.0 copy-done.3
  15.5 0.0 copy-done.5
  15.5 0.0 copy-done
  15.5 0.0 copy-done.2
  15.5 0.0 copy-done.6
  15.5 5.7 %first.1 = (f32[16,64,128]{2,1,0:T(8,128)S(1)}, f32[31,64,128]{2,1,0:T(8,128)S(1)}) custom-call(f32[3]{0:T(128)S(1)} %add_convert_fusion.keep_ref, f32[16,64,128]{2,1,0:T(8,128)} %collective-permute-done.inside_ref, f32[16,64,128]{2,1,0:T(8,128)S(1)} %seed.1.here_ref, f32[16,64,128]{2,1,0:T(8,128)S(1)} %collective-permute-done.1.across_ref, ...), custom_call_target="tpu_custom_call" | custom-call | tf_op jit(solution)/shard_map/first/pallas_call | solution.py:389
  21.2 3.6 %collective-permute-start.3 = (f32[16,64,128]{2,1,0:T(8,128)S(1)}, f32[16,64,128]{2,1,0:T(8,128)S(1)}, u32[]{:S(2)}, u32[]{:S(2)}) collective-permute-start(f32[16,64,128]{2,1,0:T(8,128)S(1)} %get-tuple-element.8.here_ref), channel_id=1, source_target_pairs={{0,0},{1,2},{2,1},{3,4},{4,3},{5,6},{6,5},{7,8},{8,7},{9,10},{10,9... | collective-permute-start | bytes 1572872 | tf_op jit(solution)/shard_map/ppermute | solution.py:359
  24.8 0.1 collective-permute-start.2
  24.9 6.7 %collective-permute-done.3.across_ref = f32[16,64,128]{2,1,0:T(8,128)S(1)} collective-permute-done((f32[16,64,128]{2,1,0:T(8,128)S(1)}, f32[16,64,128]{2,1,0:T(8,128)S(1)}, u32[]{:S(2)}, u32[]{:S(2)}) %collective-permute-start.3) | collective-permute-done | bytes 524320 | tf_op jit(solution)/shard_map/ppermute | solution.py:359
  31.7 0.0 collective-permute-done.2.inside_ref
  31.7 5.4 %second.1 = f32[8,49,8,128]{3,2,1,0:T(8,128)S(1)} custom-call(f32[3]{0:T(128)S(1)} %add_convert_fusion.keep_ref, f32[16,64,128]{2,1,0:T(8,128)S(1)} %collective-permute-done.2.inside_ref, f32[16,64,128]{2,1,0:T(8,128)S(1)} %get-tuple-element.8.here_ref, f32[16,64,128]{2,1,0:T(8,128)S(1)} %collective-permute-done.3.across_ref, ...), custom_call_target="tpu_custom_call" | custom-call | tf_op jit(solution)/shard_map/second/pallas_call | solution.py:400
  37.1 29.7 %all_to_all.13.moved_ref = f32[8,49,8,128]{3,2,1,0:T(8,128)S(1)} all-to-all(f32[8,49,8,128]{3,2,1,0:T(8,128)S(1)} %second.1), channel_id=1, replica_groups=mesh['tm'=32,'chan'=8] {'chan'}, dimensions={0} | all-to-all | bytes 3211264 | tf_op jit(solution)/shard_map/all_to_all | solution.py:362
  66.8 1.3 %collective-permute-start.4 = (f32[16,8,128]{2,1,0:T(8,128)S(1)}, f32[16,8,128]{2,1,0:T(8,128)S(1)}, u32[]{:S(2)}, u32[]{:S(2)}) collective-permute-start(f32[16,8,128]{2,1,0:T(8,128)S(1)} %slice_bitcast_fusion), channel_id=1, source_target_pairs={{8,0},{16,8},{24,16},{32,24},{40,32},{48,40},{56,48},{64,56},{72,6... | collective-permute-start | bytes 196616 | tf_op jit(solution)/shard_map/ppermute | solution.py:414
  68.1 0.6 broadcast_in_dim.3
  68.7 18.1 %all-to-all-start.1 = ((f32[32,1,128]{2,1,0:T(1,128)}), f32[32,1,128]{2,1,0:T(1,128)S(1)}, u32[]{:S(2)}, u32[]{:S(2)}) async-start(f32[32,1,128]{2,1,0:T(1,128)} %broadcast_in_dim.3), calls=%async_computation.1 | async-start | bytes 32768 | tf_op jit(solution)/shard_map/all_to_all | solution.py:362
  86.9 8.5 %all-to-all-done.1 = f32[32,1,128]{2,1,0:T(1,128)S(1)} async-done(((f32[32,1,128]{2,1,0:T(1,128)}), f32[32,1,128]{2,1,0:T(1,128)S(1)}, u32[]{:S(2)}, u32[]{:S(2)}) %all-to-all-start.1) | async-done | bytes 16416 | tf_op jit(solution)/shard_map/all_to_all | solution.py:362
  95.4 0.0 collective-permute-done.4.after_ref
  95.4 2.0 %last.1 = (f32[128,1024]{1,0:T(8,128)}, f32[128,1024]{1,0:T(8,128)}) custom-call(s32[1]{0:T(128)} %bitcast.place_ref, f32[1]{0:T(128)} %bitcast.1.keep_ref, f32[8,49,8,128]{3,2,1,0:T(8,128)S(1)} %all_to_all.13.moved_ref, f32[16,8,128]{2,1,0:T(8,128)S(1)} %collective-permute-done.4.after_ref, f32[32,128]{1,0:T(8,128)S(1)} %bitcast.12, f32[16,64,128]{2,1,0:T(8,128)S(1)} %bitcast.11), custom_call_target="tpu_custom_call" | custom-call | tf_op jit(solution)/shard_map/last/pallas_call | solution.py:419
  (2 shorter events, 0.0 us)
Async XLA Ops:
  0.6 14.8 %copy-start.3 = (f32[2,64,128]{2,1,0:T(8,128)S(1)}, f32[2,64,128]{2,1,0:T(8,128)}, u32[]{:S(2)}) copy-start(f32[2,64,128]{2,1,0:T(8,128)} %constant.44.clone.refs_5_.twist_ref) | copy-start | bytes 196612
  0.6 14.8 %copy-start.5 = (bf16[64,384]{1,0:T(8,128)(2,1)S(1)}, bf16[64,384]{1,0:T(8,128)(2,1)}, u32[]{:S(2)}) copy-start(bf16[64,384]{1,0:T(8,128)(2,1)} %constant.43.clone.refs_4_.back_rows_ref) | copy-start | bytes 147460
  0.7 14.8 %copy-start = (bf16[384,256]{1,0:T(8,128)(2,1)S(1)}, bf16[384,256]{1,0:T(8,128)(2,1)}, u32[]{:S(2)}) copy-start(bf16[384,256]{1,0:T(8,128)(2,1)} %constant.42.clone.refs_3_.back_lanes_ref) | copy-start | bytes 589828
  0.7 14.8 %copy-start.2 = (bf16[768,128]{1,0:T(8,128)(2,1)S(1)}, bf16[768,128]{1,0:T(8,128)(2,1)}, u32[]{:S(2)}) copy-start(bf16[768,128]{1,0:T(8,128)(2,1)} %constant.46.clone.ahead_lanes_ref) | copy-start | bytes 589828
  0.7 14.8 %copy-start.6 = (bf16[128,192]{1,0:T(8,128)(2,1)S(1)}, bf16[128,192]{1,0:T(8,128)(2,1)}, u32[]{:S(2)}) copy-start(bf16[128,192]{1,0:T(8,128)(2,1)} %constant.45.clone.ahead_rows_ref) | copy-start | bytes 147460
  0.7 8.0 %copy-start.1 = (f32[16,4096]{1,0:T(8,128)S(1)}, f32[16,4096]{1,0:T(8,128)}, u32[]{:S(2)}) copy-start(f32[16,4096]{1,0:T(8,128)} %weights_ref.1) | copy-start | bytes 786436
  0.7 8.0 %copy-start.4 = (f32[16,8192]{1,0:T(8,128)S(1)}, f32[16,8192]{1,0:T(8,128)}, u32[]{:S(2)}) copy-start(f32[16,8192]{1,0:T(8,128)} %taps_ref.1) | copy-start | bytes 1572868
  4.1 11.4 %collective-permute-start.1 = (f32[16,64,128]{2,1,0:T(8,128)S(1)}, f32[16,64,128]{2,1,0:T(8,128)S(1)}, u32[]{:S(2)}, u32[]{:S(2)}) collective-permute-start(f32[16,64,128]{2,1,0:T(8,128)S(1)} %seed.1.here_ref), channel_id=1, source_target_pairs={{0,0},{1,2},{2,1},{3,4},{4,3},{5,6},{6,5},{7,8},{8,7},{9,10},{10,9... | collective-permute-start | bytes 1572872 | tf_op jit(solution)/shard_map/ppermute | solution.py:359
  8.6 6.9 %collective-permute-start = (f32[16,64,128]{2,1,0:T(8,128)S(1)}, f32[16,64,128]{2,1,0:T(8,128)}, u32[]{:S(2)}, u32[]{:S(2)}) collective-permute-start(f32[16,64,128]{2,1,0:T(8,128)S(1)} %seed.1.here_ref), channel_id=1, source_target_pairs={{0,1},{1,0},{2,3},{3,2},{4,5},{5,4},{6,7},{7,6},{8,9},{9,8},{10,11... | collective-permute-start | bytes 1572872 | tf_op jit(solution)/shard_map/ppermute | solution.py:359
  21.2 10.5 %collective-permute-start.3 = (f32[16,64,128]{2,1,0:T(8,128)S(1)}, f32[16,64,128]{2,1,0:T(8,128)S(1)}, u32[]{:S(2)}, u32[]{:S(2)}) collective-permute-start(f32[16,64,128]{2,1,0:T(8,128)S(1)} %get-tuple-element.8.here_ref), channel_id=1, source_target_pairs={{0,0},{1,2},{2,1},{3,4},{4,3},{5,6},{6,5},{7,8},{8,7},{9,10},{10,9... | collective-permute-start | bytes 1572872 | tf_op jit(solution)/shard_map/ppermute | solution.py:359
  24.8 6.9 %collective-permute-start.2 = (f32[16,64,128]{2,1,0:T(8,128)S(1)}, f32[16,64,128]{2,1,0:T(8,128)S(1)}, u32[]{:S(2)}, u32[]{:S(2)}) collective-permute-start(f32[16,64,128]{2,1,0:T(8,128)S(1)} %get-tuple-element.8.here_ref), channel_id=1, source_target_pairs={{0,1},{1,0},{2,3},{3,2},{4,5},{5,4},{6,7},{7,6},{8,9},{9,8},{10,11... | collective-permute-start | bytes 1572872 | tf_op jit(solution)/shard_map/ppermute | solution.py:359
  66.8 28.6 %collective-permute-start.4 = (f32[16,8,128]{2,1,0:T(8,128)S(1)}, f32[16,8,128]{2,1,0:T(8,128)S(1)}, u32[]{:S(2)}, u32[]{:S(2)}) collective-permute-start(f32[16,8,128]{2,1,0:T(8,128)S(1)} %slice_bitcast_fusion), channel_id=1, source_target_pairs={{8,0},{16,8},{24,16},{32,24},{40,32},{48,40},{56,48},{64,56},{72,6... | collective-permute-start | bytes 196616 | tf_op jit(solution)/shard_map/ppermute | solution.py:414
  68.7 26.6 %all-to-all-start.1 = ((f32[32,1,128]{2,1,0:T(1,128)}), f32[32,1,128]{2,1,0:T(1,128)S(1)}, u32[]{:S(2)}, u32[]{:S(2)}) async-start(f32[32,1,128]{2,1,0:T(1,128)} %broadcast_in_dim.3), calls=%async_computation.1 | async-start | bytes 32768 | tf_op jit(solution)/shard_map/all_to_all | solution.py:362

commit v7 on v6

--- a/solution.py
+++ b/solution.py
@@ -12,7 +12,7 @@
 RIDGE = 0.25
 ROWS = 64
 LANES = 128
-CHUNK = 4
+CHUNK = 16
 F32 = jnp.float32
 BF16 = jnp.bfloat16
 AXES = ("tm", "chan")
@@ -48,9 +48,9 @@
     twist = 2.0 * np.pi * k1[:, None] * n2[None, :] / (ROWS * LANES)
     return (
         np.concatenate([rows_high.T, rows_high.T, rows_low.T], 1),
-        np.concatenate([lanes_high.T, lanes_high.T, lanes_low.T], 0),
+        np.concatenate([lanes_high.T, lanes_low.T], 1),
         np.concatenate([lanes_high, lanes_high, lanes_low], 0),
-        np.concatenate([rows_high, rows_high, rows_low], 1),
+        np.block([[rows_high, rows_high], [rows_low, np.zeros_like(rows_low)]]),
         np.stack([np.cos(twist), np.sin(twist)]).astype(np.float32),
     )
 
@@ -74,7 +74,8 @@
         imag = mixed[ROWS:, f * LANES : (f + 1) * LANES]
         turned.append(jnp.concatenate([real * cos + imag * sin, imag * cos - real * sin], 1))
     high, low = split(jnp.concatenate(turned, 0))
-    return dot(jnp.concatenate([high, low, high], 1), ahead_lanes)
+    wide = dot(high, ahead_lanes)
+    return wide[:, :LANES] + wide[:, LANES:] + dot(low, ahead_lanes[:, :LANES])
 
 
 def backward_chunk(spectra, back_lanes, back_rows, cos, sin):
@@ -86,7 +87,8 @@
         imag = mixed[f * ROWS : (f + 1) * ROWS, LANES:]
         turned.append(jnp.concatenate([real * cos - imag * sin, real * sin + imag * cos], 0))
     high, low = split(jnp.concatenate(turned, 1))
-    return dot(back_rows, jnp.concatenate([high, low, high], 0))
+    tall = dot(back_rows, jnp.concatenate([high, low], 0))
+    return tall[:ROWS] + tall[ROWS:]
 
 
 def turn_pair(block):
@@ -209,8 +211,8 @@
             out_ref[start + f] = frames[:, f * LANES : (f + 1) * LANES]
 
 
-def quarters():
-    return lax.broadcasted_iota(jnp.int32, (8, LANES), 1) // 32
+def quarters(rows):
+    return lax.broadcasted_iota(jnp.int32, (rows, LANES), 1) // 32
 
 
 def pack(values):
@@ -218,7 +220,7 @@
     for at, value in enumerate(values):
         value = value + pltpu.roll(value, 64, 1)
         value = value + pltpu.roll(value, 32, 1)
-        packed = jnp.where(quarters() == at, value, packed)
+        packed = jnp.where(quarters(8) == at, value, packed)
     return packed
 
 
@@ -275,6 +277,15 @@
         out_ref[group, 3 * count] = totals
 
 
+def tail_kernel(moved_ref, frames_ref, sums_ref):
+    count = frames_ref.shape[0]
+    frames_ref[...] = moved_ref[0, 2 * count : 3 * count]
+    total = moved_ref[0, 3 * count]
+    for part in range(1, moved_ref.shape[0]):
+        total = total + moved_ref[part, 3 * count]
+    sums_ref[...] = jnp.broadcast_to((total[:4] + total[4:])[None], sums_ref.shape)
+
+
 def last_kernel(
     place_ref, keep_ref, moved_ref, after_ref, sums_ref, taps_ref,
     solution_ref, residual_ref, kept, left,
@@ -283,11 +294,9 @@
     count = (moved_ref.shape[1] - 1) // 3
     reach = taps_ref.shape[0] - 1
     rows = pl.ds(pl.multiple_of(place_ref[0] * 8, 8), 8)
-    sums = sums_ref[0:8]
-    for at in range(8, sums_ref.shape[0], 8):
-        sums = sums + sums_ref[at : at + 8]
+    sums = jnp.sum(sums_ref[...], 0)
     norm, curve, square, power = (
-        jnp.sum(jnp.sum(jnp.where(quarters() == at, sums, 0.0), 1, keepdims=True), 0, keepdims=True)
+        jnp.sum(jnp.sum(jnp.where(quarters(4) == at, sums, 0.0), 1, keepdims=True), 0, keepdims=True)
         for at in range(4)
     )
     cube = power + RIDGE * square
@@ -411,11 +420,16 @@
     )(keep, inside, images, across, side, taps, weights, *tables)
 
     moved = exchange(outgoing, "chan")
-    after = lax.ppermute(
-        moved[0, 2 * count : 3 * count], "tm", [(i + 1, i) for i in range(groups - 1)]
-    )
-    sums = jnp.sum(moved[:, 3 * count], (0, 1))
-    sums = exchange(jnp.broadcast_to(sums, (groups, LANES)), "tm")
+    after, sums = pl.pallas_call(
+        tail_kernel,
+        out_shape=(shape(count, 8, LANES), shape(groups, 4, LANES)),
+        in_specs=vmem(1),
+        out_specs=tuple(vmem(2)),
+        compiler_params=params(),
+        name="tail",
+    )(moved)
+    after = lax.ppermute(after, "tm", [(i + 1, i) for i in range(groups - 1)])
+    sums = exchange(sums, "tm")
     return pl.pallas_call(
         last_kernel,
         out_shape=(shape(parts * count, 8 * LANES), shape(parts * count, 8 * LANES)),

time: 97.7 us -> 90.4 us (0.925)
  starting transfers between devices: 27.7 us -> 24.9 us
  Pallas kernels: 17.6 us -> 14.9 us
  waiting for transfers between devices: 20.7 us -> 19.7 us
    all_to_all x1, waiting for transfers between devices: 8.5 us -> 3.37 us  [exchange(): return lax.all_to_all(value, axis, split_axis=0, concat_axis=0, tiled=True)]
    ppermute x1, waiting for transfers between devices: 0.01 us -> 4.14 us  [local(): after = lax.ppermute(after, 'tm', [(i + 1, i) for i in range(groups - 1)])]
    all_to_all x1, starting transfers between devices: 18.1 us -> 15.2 us  [exchange(): return lax.all_to_all(value, axis, split_axis=0, concat_axis=0, tiled=True)]
    pallas_call x1, Pallas kernels: 5.37 us -> 3.91 us  [local(): pl.pallas_call(second_kernel, out_shape=shape(parts, 3 * count + 1, 8, LA...]
    pallas_call x1, Pallas kernels: 5.7 us -> 4.25 us  [local(): pl.pallas_call(first_kernel, out_shape=(blocks, shape(reach + count, ROWS...]
  transfers between devices with their start and end apart: 6 -> 6, of which waited for: 3 -> 4; matrix products, arithmetic and copies ran while one was open for 1% -> 0% of each run, Pallas kernels for 1% -> 1%
where the time goes in v7:
time: 90.4 us; the launch traced here: 90.1 us
  blocking collectives  29.7 us (33%)
  starting transfers between devices  24.9 us (28%)
  waiting for transfers between devices  19.7 us (22%)
  Pallas kernels  14.9 us (16%)
    all_to_all x1, blocking collectives, exchange(): return lax.all_to_all(value, axis, split_axis=0, concat_axis=0, tiled=True)  29.7 us
    all_to_all x1, starting transfers between devices, exchange(): return lax.all_to_all(value, axis, split_axis=0, concat_axis=0, tiled=True)  15.2 us
    ppermute x2, waiting for transfers between devices, neighbours(): lax.ppermute(block, AXES, across)  12.2 us
    ppermute x2, starting transfers between devices, neighbours(): lax.ppermute(block, AXES, across)  8.15 us
    pallas_call x1, Pallas kernels, local(): pl.pallas_call(first_kernel, out_shape=(blocks, shape(reach + count, ROWS...  4.25 us
    ppermute x1, waiting for transfers between devices, local(): after = lax.ppermute(after, 'tm', [(i + 1, i) for i in range(groups - 1)])  4.14 us
    pallas_call x1, Pallas kernels, local(): pl.pallas_call(second_kernel, out_shape=shape(parts, 3 * count + 1, 8, LA...  3.91 us
    all_to_all x1, waiting for transfers between devices, exchange(): return lax.all_to_all(value, axis, split_axis=0, concat_axis=0, tiled=True)  3.37 us
  transfers between devices with their start and end apart: 6, of which 4 were waited for; matrix products, arithmetic and copies ran while one was open for 0% of the time, Pallas kernels for 1%

profile of v7, /device:TPU:1, one launch (start us, length us, event | category | flops | bytes accessed | tf_op | source)
XLA Modules:
  0.0 90.1 jit_solution(2244489109094894714)
XLA Ops:
  0.6 0.0 copy-start.2
  0.6 0.0 copy-start.3
  0.7 0.0 copy-start
  0.7 0.0 copy-start.5
  0.7 0.0 copy-start.6
  0.7 0.0 copy-start.1
  0.7 0.0 copy-start.4
  0.7 2.8 %seed.1.here_ref = f32[16,64,128]{2,1,0:T(8,128)S(1)} custom-call(f32[16,4096]{1,0:T(8,128)} %refs_0_.1, f32[16,4096]{1,0:T(8,128)} %refs_1_.1, f32[16,4096]{1,0:T(8,128)} %weights_ref.1, bf16[384,256]{1,0:T(8,128)(2,1)} %constant.40.clone.refs_3_.back_lanes_ref, bf16[128,256]{1,0:T(8,128)(2,1)} %constant.41.clone.refs_4_.back_rows_ref, ...), custom_call_target="tpu_custom_call" | custom-call | tf_op jit(solution)/shard_map/seed/pallas_call | solution.py:375
  3.5 4.5 %collective-permute-start.1 = (f32[16,64,128]{2,1,0:T(8,128)S(1)}, f32[16,64,128]{2,1,0:T(8,128)S(1)}, u32[]{:S(2)}, u32[]{:S(2)}) collective-permute-start(f32[16,64,128]{2,1,0:T(8,128)S(1)} %seed.1.here_ref), channel_id=1, source_target_pairs={{0,0},{1,2},{2,1},{3,4},{4,3},{5,6},{6,5},{7,8},{8,7},{9,10},{10,9... | collective-permute-start | bytes 1572872 | tf_op jit(solution)/shard_map/ppermute | solution.py:368
  8.1 0.1 collective-permute-start
  8.2 0.0 copy-done.1
  8.2 0.0 copy-done.4
  8.2 1.2 %arrange.1 = (f32[16,64,128]{2,1,0:T(8,128)S(1)}, f32[1024,128]{1,0:T(8,128)S(1)}) custom-call(f32[16,4096]{1,0:T(8,128)S(1)} %copy-done.1, f32[16,8192]{1,0:T(8,128)S(1)} %copy-done.4), custom_call_target="tpu_custom_call" | custom-call | flops 10000000 | bytes 2000000 | tf_op jit(solution)/shard_map/arrange/pallas_call | solution.py:386
  9.4 0.1 add_convert_fusion.keep_ref
  9.5 5.4 %collective-permute-done.1.across_ref = f32[16,64,128]{2,1,0:T(8,128)S(1)} collective-permute-done((f32[16,64,128]{2,1,0:T(8,128)S(1)}, f32[16,64,128]{2,1,0:T(8,128)S(1)}, u32[]{:S(2)}, u32[]{:S(2)}) %collective-permute-start.1) | collective-permute-done | bytes 524320 | tf_op jit(solution)/shard_map/ppermute | solution.py:368
  14.9 0.0 collective-permute-done.inside_ref
  14.9 0.0 copy-done.2
  14.9 0.0 copy-done.3
  14.9 0.0 copy-done
  14.9 0.0 copy-done.5
  14.9 0.0 copy-done.6
  15.0 4.2 %first.1 = (f32[16,64,128]{2,1,0:T(8,128)S(1)}, f32[31,64,128]{2,1,0:T(8,128)S(1)}) custom-call(f32[3]{0:T(128)S(1)} %add_convert_fusion.keep_ref, f32[16,64,128]{2,1,0:T(8,128)} %collective-permute-done.inside_ref, f32[16,64,128]{2,1,0:T(8,128)S(1)} %seed.1.here_ref, f32[16,64,128]{2,1,0:T(8,128)S(1)} %collective-permute-done.1.across_ref, ...), custom_call_target="tpu_custom_call" | custom-call | tf_op jit(solution)/shard_map/first/pallas_call | solution.py:398
  19.2 3.6 %collective-permute-start.3 = (f32[16,64,128]{2,1,0:T(8,128)S(1)}, f32[16,64,128]{2,1,0:T(8,128)S(1)}, u32[]{:S(2)}, u32[]{:S(2)}) collective-permute-start(f32[16,64,128]{2,1,0:T(8,128)S(1)} %get-tuple-element.10.here_ref), channel_id=1, source_target_pairs={{0,0},{1,2},{2,1},{3,4},{4,3},{5,6},{6,5},{7,8},{8,7},{9,10},{10,9... | collective-permute-start | bytes 1572872 | tf_op jit(solution)/shard_map/ppermute | solution.py:368
  22.9 0.1 collective-permute-start.2
  23.0 6.8 %collective-permute-done.3.across_ref = f32[16,64,128]{2,1,0:T(8,128)S(1)} collective-permute-done((f32[16,64,128]{2,1,0:T(8,128)S(1)}, f32[16,64,128]{2,1,0:T(8,128)S(1)}, u32[]{:S(2)}, u32[]{:S(2)}) %collective-permute-start.3) | collective-permute-done | bytes 524320 | tf_op jit(solution)/shard_map/ppermute | solution.py:368
  29.7 0.0 collective-permute-done.2.inside_ref
  29.7 3.9 %second.1 = f32[8,49,8,128]{3,2,1,0:T(8,128)S(1)} custom-call(f32[3]{0:T(128)S(1)} %add_convert_fusion.keep_ref, f32[16,64,128]{2,1,0:T(8,128)S(1)} %collective-permute-done.2.inside_ref, f32[16,64,128]{2,1,0:T(8,128)S(1)} %get-tuple-element.10.here_ref, f32[16,64,128]{2,1,0:T(8,128)S(1)} %collective-permute-done.3.across_ref, ...), custom_call_target="tpu_custom_call" | custom-call | tf_op jit(solution)/shard_map/second/pallas_call | solution.py:409
  33.6 29.7 %all_to_all.10.moved_ref = f32[8,49,8,128]{3,2,1,0:T(8,128)S(1)} all-to-all(f32[8,49,8,128]{3,2,1,0:T(8,128)S(1)} %second.1), channel_id=1, replica_groups=mesh['tm'=32,'chan'=8] {'chan'}, dimensions={0} | all-to-all | bytes 3211264 | tf_op jit(solution)/shard_map/all_to_all | solution.py:371
  63.3 0.6 tail.1
  64.0 15.2 %all-to-all-start.1 = ((f32[32,4,128]{2,1,0:T(4,128)}), f32[32,4,128]{2,1,0:T(4,128)S(1)}, u32[]{:S(2)}, u32[]{:S(2)}) async-start(f32[32,4,128]{2,1,0:T(4,128)} %get-tuple-element.13), calls=%async_computation.1 | async-start | bytes 131072 | tf_op jit(solution)/shard_map/all_to_all | solution.py:371
  79.2 1.3 %collective-permute-start.4 = (f32[16,8,128]{2,1,0:T(8,128)S(1)}, f32[16,8,128]{2,1,0:T(8,128)S(1)}, u32[]{:S(2)}, u32[]{:S(2)}) collective-permute-start(f32[16,8,128]{2,1,0:T(8,128)S(1)} %get-tuple-element.12), channel_id=1, source_target_pairs={{8,0},{16,8},{24,16},{32,24},{40,32},{48,40},{56,48},{64,56},{72,6... | collective-permute-start | bytes 196616 | tf_op jit(solution)/shard_map/ppermute | solution.py:431
  80.6 4.1 %collective-permute-done.4.after_ref = f32[16,8,128]{2,1,0:T(8,128)S(1)} collective-permute-done((f32[16,8,128]{2,1,0:T(8,128)S(1)}, f32[16,8,128]{2,1,0:T(8,128)S(1)}, u32[]{:S(2)}, u32[]{:S(2)}) %collective-permute-start.4) | collective-permute-done | bytes 65568 | tf_op jit(solution)/shard_map/ppermute | solution.py:431
  84.7 3.4 %all-to-all-done.1.sums_ref = f32[32,4,128]{2,1,0:T(4,128)S(1)} async-done(((f32[32,4,128]{2,1,0:T(4,128)}), f32[32,4,128]{2,1,0:T(4,128)S(1)}, u32[]{:S(2)}, u32[]{:S(2)}) %all-to-all-start.1) | async-done | bytes 65568 | tf_op jit(solution)/shard_map/all_to_all | solution.py:371
  88.1 2.0 %last.1 = (f32[128,1024]{1,0:T(8,128)}, f32[128,1024]{1,0:T(8,128)}) custom-call(s32[1]{0:T(128)} %bitcast.place_ref, f32[1]{0:T(128)} %bitcast.1.keep_ref, f32[8,49,8,128]{3,2,1,0:T(8,128)S(1)} %all_to_all.10.moved_ref, f32[16,8,128]{2,1,0:T(8,128)S(1)} %collective-permute-done.4.after_ref, f32[32,4,128]{2,1,0:T(4,128)S(1)} %all-to-all-done.1.sums_ref, ...), custom_call_target="tpu_custom_call" | custom-call | tf_op jit(solution)/shard_map/last/pallas_call | solution.py:433
Async XLA Ops:
  0.6 14.3 %copy-start.2 = (f32[2,64,128]{2,1,0:T(8,128)S(1)}, f32[2,64,128]{2,1,0:T(8,128)}, u32[]{:S(2)}) copy-start(f32[2,64,128]{2,1,0:T(8,128)} %constant.42.clone.refs_5_.twist_ref) | copy-start | bytes 196612
  0.6 14.3 %copy-start.3 = (bf16[128,256]{1,0:T(8,128)(2,1)S(1)}, bf16[128,256]{1,0:T(8,128)(2,1)}, u32[]{:S(2)}) copy-start(bf16[128,256]{1,0:T(8,128)(2,1)} %constant.41.clone.refs_4_.back_rows_ref) | copy-start | bytes 196612
  0.7 14.3 %copy-start = (bf16[384,256]{1,0:T(8,128)(2,1)S(1)}, bf16[384,256]{1,0:T(8,128)(2,1)}, u32[]{:S(2)}) copy-start(bf16[384,256]{1,0:T(8,128)(2,1)} %constant.40.clone.refs_3_.back_lanes_ref) | copy-start | bytes 589828
  0.7 14.3 %copy-start.5 = (bf16[256,256]{1,0:T(8,128)(2,1)S(1)}, bf16[256,256]{1,0:T(8,128)(2,1)}, u32[]{:S(2)}) copy-start(bf16[256,256]{1,0:T(8,128)(2,1)} %constant.44.clone.ahead_lanes_ref) | copy-start | bytes 393220
  0.7 14.3 %copy-start.6 = (bf16[128,192]{1,0:T(8,128)(2,1)S(1)}, bf16[128,192]{1,0:T(8,128)(2,1)}, u32[]{:S(2)}) copy-start(bf16[128,192]{1,0:T(8,128)(2,1)} %constant.43.clone.ahead_rows_ref) | copy-start | bytes 147460
  0.7 7.5 %copy-start.1 = (f32[16,4096]{1,0:T(8,128)S(1)}, f32[16,4096]{1,0:T(8,128)}, u32[]{:S(2)}) copy-start(f32[16,4096]{1,0:T(8,128)} %weights_ref.1) | copy-start | bytes 786436
  0.7 7.5 %copy-start.4 = (f32[16,8192]{1,0:T(8,128)S(1)}, f32[16,8192]{1,0:T(8,128)}, u32[]{:S(2)}) copy-start(f32[16,8192]{1,0:T(8,128)} %taps_ref.1) | copy-start | bytes 1572868
  3.5 11.4 %collective-permute-start.1 = (f32[16,64,128]{2,1,0:T(8,128)S(1)}, f32[16,64,128]{2,1,0:T(8,128)S(1)}, u32[]{:S(2)}, u32[]{:S(2)}) collective-permute-start(f32[16,64,128]{2,1,0:T(8,128)S(1)} %seed.1.here_ref), channel_id=1, source_target_pairs={{0,0},{1,2},{2,1},{3,4},{4,3},{5,6},{6,5},{7,8},{8,7},{9,10},{10,9... | collective-permute-start | bytes 1572872 | tf_op jit(solution)/shard_map/ppermute | solution.py:368
  8.1 6.9 %collective-permute-start = (f32[16,64,128]{2,1,0:T(8,128)S(1)}, f32[16,64,128]{2,1,0:T(8,128)}, u32[]{:S(2)}, u32[]{:S(2)}) collective-permute-start(f32[16,64,128]{2,1,0:T(8,128)S(1)} %seed.1.here_ref), channel_id=1, source_target_pairs={{0,1},{1,0},{2,3},{3,2},{4,5},{5,4},{6,7},{7,6},{8,9},{9,8},{10,11... | collective-permute-start | bytes 1572872 | tf_op jit(solution)/shard_map/ppermute | solution.py:368
  19.2 10.5 %collective-permute-start.3 = (f32[16,64,128]{2,1,0:T(8,128)S(1)}, f32[16,64,128]{2,1,0:T(8,128)S(1)}, u32[]{:S(2)}, u32[]{:S(2)}) collective-permute-start(f32[16,64,128]{2,1,0:T(8,128)S(1)} %get-tuple-element.10.here_ref), channel_id=1, source_target_pairs={{0,0},{1,2},{2,1},{3,4},{4,3},{5,6},{6,5},{7,8},{8,7},{9,10},{10,9... | collective-permute-start | bytes 1572872 | tf_op jit(solution)/shard_map/ppermute | solution.py:368
  22.9 6.9 %collective-permute-start.2 = (f32[16,64,128]{2,1,0:T(8,128)S(1)}, f32[16,64,128]{2,1,0:T(8,128)S(1)}, u32[]{:S(2)}, u32[]{:S(2)}) collective-permute-start(f32[16,64,128]{2,1,0:T(8,128)S(1)} %get-tuple-element.10.here_ref), channel_id=1, source_target_pairs={{0,1},{1,0},{2,3},{3,2},{4,5},{5,4},{6,7},{7,6},{8,9},{9,8},{10,11... | collective-permute-start | bytes 1572872 | tf_op jit(solution)/shard_map/ppermute | solution.py:368
  64.0 24.1 %all-to-all-start.1 = ((f32[32,4,128]{2,1,0:T(4,128)}), f32[32,4,128]{2,1,0:T(4,128)S(1)}, u32[]{:S(2)}, u32[]{:S(2)}) async-start(f32[32,4,128]{2,1,0:T(4,128)} %get-tuple-element.13), calls=%async_computation.1 | async-start | bytes 131072 | tf_op jit(solution)/shard_map/all_to_all | solution.py:371
  79.2 5.4 %collective-permute-start.4 = (f32[16,8,128]{2,1,0:T(8,128)S(1)}, f32[16,8,128]{2,1,0:T(8,128)S(1)}, u32[]{:S(2)}, u32[]{:S(2)}) collective-permute-start(f32[16,8,128]{2,1,0:T(8,128)S(1)} %get-tuple-element.12), channel_id=1, source_target_pairs={{8,0},{16,8},{24,16},{32,24},{40,32},{48,40},{56,48},{64,56},{72,6... | collective-permute-start | bytes 196616 | tf_op jit(solution)/shard_map/ppermute | solution.py:431

commit v8 on v7

--- a/solution.py
+++ b/solution.py
@@ -286,14 +286,60 @@
     sums_ref[...] = jnp.broadcast_to((total[:4] + total[4:])[None], sums_ref.shape)
 
 
-def last_kernel(
-    place_ref, keep_ref, moved_ref, after_ref, sums_ref, taps_ref,
-    solution_ref, residual_ref, kept, left,
-):
+def local_taps(place_ref, taps_ref):
+    rows = pl.ds(pl.multiple_of(place_ref[0] * 8, 8), 8)
+    return [taps_ref[p, rows, :] for p in range(taps_ref.shape[0])]
+
+
+def to_rows(held, out_ref, first, frames):
+    for block in range(frames // 8):
+        for n1 in range(8):
+            places = pl.ds(block * 64 + n1, 8, stride=8)
+            columns = slice(n1 * LANES, (n1 + 1) * LANES)
+            out_ref[first + block * 8 : first + (block + 1) * 8, columns] = held[places, :]
+
+
+def prepare_kernel(place_ref, moved_ref, taps_ref, base_ref, image_ref, again_ref, base_held, image_held, again_held):
     parts = moved_ref.shape[0]
     count = (moved_ref.shape[1] - 1) // 3
-    reach = taps_ref.shape[0] - 1
-    rows = pl.ds(pl.multiple_of(place_ref[0] * 8, 8), 8)
+    taps = local_taps(place_ref, taps_ref)
+    reach = len(taps) - 1
+
+    @pl.loop(0, parts)
+    def _(part):
+        for at in range(count):
+            here = pl.ds(pl.multiple_of((part * count + at) * 8, 8), 8)
+            base_held[here, :] = moved_ref[part, at]
+            image_held[here, :] = moved_ref[part, count + at]
+
+    @pl.loop(0, parts - 1)
+    def _(part):
+        frames = [moved_ref[part, 2 * count + t] for t in range(count)]
+        frames += [moved_ref[part + 1, 2 * count + t] for t in range(reach)]
+        for at in range(count):
+            here = pl.ds(pl.multiple_of((part * count + at) * 8, 8), 8)
+            again_held[here, :] = weighted_sum(taps, frames[at : at + reach + 1])
+
+    to_rows(base_held, base_ref, 0, parts * count)
+    to_rows(image_held, image_ref, 0, parts * count)
+    to_rows(again_held, again_ref, 0, (parts - 1) * count)
+
+
+def last_kernel(
+    place_ref, keep_ref, moved_ref, base_ref, image_ref, again_ref, after_ref, sums_ref, taps_ref,
+    solution_ref, residual_ref, held, rest, fetched, semaphore,
+):
+    copy = pltpu.make_async_copy(again_ref, fetched, semaphore)
+    copy.start()
+    parts = moved_ref.shape[0]
+    count = (moved_ref.shape[1] - 1) // 3
+    taps = local_taps(place_ref, taps_ref)
+    reach = len(taps) - 1
+    frames = [moved_ref[parts - 1, 2 * count + t] for t in range(count)]
+    frames += [after_ref[t] * keep_ref[0] for t in range(reach)]
+    for at in range(count):
+        held[at * 8 : (at + 1) * 8, :] = weighted_sum(taps, frames[at : at + reach + 1])
+    to_rows(held, rest, 0, count)
     sums = jnp.sum(sums_ref[...], 0)
     norm, curve, square, power = (
         jnp.sum(jnp.sum(jnp.where(quarters(4) == at, sums, 0.0), 1, keepdims=True), 0, keepdims=True)
@@ -306,35 +352,26 @@
     next_step = next_norm / (step * (step * cube - grown * square))
     to_base = step + next_step * grown
     to_image = -(next_step * step)
-    image_rate = -(step + next_step * grown)
     cube_rate = next_step * step
+    image_rate = RIDGE * cube_rate - (step + next_step * grown)
     to_base, to_image, image_rate, cube_rate = (
-        jnp.broadcast_to(value, (8, LANES)) for value in (to_base, to_image, image_rate, cube_rate)
+        jnp.broadcast_to(value, (8, 8 * LANES)) for value in (to_base, to_image, image_rate, cube_rate)
     )
-    taps = [taps_ref[p, rows, :] for p in range(reach + 1)]
-
-    def finish(part, tail):
-        frames = [moved_ref[part, 2 * count + t] for t in range(count)] + tail
-        for at in range(count):
-            base = moved_ref[part, at]
-            image = moved_ref[part, count + at]
-            again = weighted_sum(taps, frames[at : at + reach + 1]) + RIDGE * image
-            here = pl.ds(pl.multiple_of((part * count + at) * 8, 8), 8)
-            kept[here, :] = to_base * base + to_image * image
-            left[here, :] = base + image_rate * image + cube_rate * again
-
-    @pl.loop(0, parts - 1)
-    def _(part):
-        finish(part, [moved_ref[part + 1, 2 * count + t] for t in range(reach)])
-
-    finish(parts - 1, [after_ref[t] * keep_ref[0] for t in range(reach)])
-
-    for block in range(parts * count // 8):
-        for n1 in range(8):
-            places = pl.ds(block * 64 + n1, 8, stride=8)
-            columns = slice(n1 * LANES, (n1 + 1) * LANES)
-            solution_ref[block * 8 : (block + 1) * 8, columns] = kept[places, :]
-            residual_ref[block * 8 : (block + 1) * 8, columns] = left[places, :]
+
+    def finish(rows, again):
+        base = base_ref[rows, :]
+        image = image_ref[rows, :]
+        solution_ref[rows, :] = to_base * base + to_image * image
+        residual_ref[rows, :] = base + image_rate * image + cube_rate * again
+
+    for block in range(count // 8):
+        finish(pl.ds((parts - 1) * count + block * 8, 8), rest[block * 8 : (block + 1) * 8, :])
+    copy.wait()
+
+    @pl.loop(0, (parts - 1) * count // 8)
+    def _(block):
+        rows = pl.ds(pl.multiple_of(block * 8, 8), 8)
+        finish(rows, fetched[rows, :])
 
 
 def shape(*dims):
@@ -346,6 +383,7 @@
 
 
 SMEM = pl.BlockSpec(memory_space=pltpu.SMEM)
+HBM = pl.BlockSpec(memory_space=pltpu.HBM)
 
 
 def local(observed_real, observed_imag, weights, taps):
@@ -430,18 +468,32 @@
     )(moved)
     after = lax.ppermute(after, "tm", [(i + 1, i) for i in range(groups - 1)])
     sums = exchange(sums, "tm")
+    whole = shape(parts * count, 8 * LANES)
+    base, image, again = pl.pallas_call(
+        prepare_kernel,
+        out_shape=(whole, whole, shape((parts - 1) * count, 8 * LANES)),
+        in_specs=[SMEM] + vmem(2),
+        out_specs=tuple(vmem(3)),
+        scratch_shapes=[pltpu.VMEM((parts * count * 8, LANES), F32)] * 3,
+        compiler_params=params(),
+        cost_estimate=pl.CostEstimate(flops=10**7, bytes_accessed=3 * 10**6, transcendentals=0),
+        name="prepare",
+    )(place, moved, taps)
+    again = pltpu.with_memory_space_constraint(again, pltpu.HBM)
     return pl.pallas_call(
         last_kernel,
-        out_shape=(shape(parts * count, 8 * LANES), shape(parts * count, 8 * LANES)),
-        in_specs=[SMEM, SMEM] + vmem(4),
+        out_shape=(whole, whole),
+        in_specs=[SMEM, SMEM] + vmem(3) + [HBM] + vmem(3),
         out_specs=tuple(vmem(2)),
         scratch_shapes=[
-            pltpu.VMEM((parts * count * 8, LANES), F32),
-            pltpu.VMEM((parts * count * 8, LANES), F32),
+            pltpu.VMEM((count * 8, LANES), F32),
+            pltpu.VMEM((count, 8 * LANES), F32),
+            pltpu.VMEM(again.shape, F32),
+            pltpu.SemaphoreType.DMA,
         ],
         compiler_params=params(),
         name="last",
-    )(place, keep_group, moved, after, sums, taps)
+    )(place, keep_group, moved, base, image, again, after, sums, taps)
 
 
 def solution(mesh):

time: 90.4 us -> 90.6 us (level)
  waiting for transfers between devices: 19.7 us -> 18 us
  Pallas kernels: 14.9 us -> 15.9 us
    ppermute x1, waiting for transfers between devices: 4.14 us -> 2.45 us  [local(): after = lax.ppermute(after, 'tm', [(i + 1, i) for i in range(groups - 1)])]
    pallas_call x1 -> x2, Pallas kernels: 2.05 us -> 3.08 us  [the longest x1 2.17 us: local(): pl.pallas_call(last_kernel, out_shape=(whole, whole), in_specs=[SMEM, SME...]
  transfers between devices with their start and end apart: 6 -> 6, of which waited for: 4 -> 4; matrix products, arithmetic and copies ran while one was open for 0% -> 0% of each run, Pallas kernels for 1% -> 2%
where the time goes in v8:
time: 90.6 us; the launch traced here: 90.2 us
  blocking collectives  29.7 us (33%)
  starting transfers between devices  24.9 us (27%)
  waiting for transfers between devices  18 us (20%)
  Pallas kernels  15.9 us (18%)
    all_to_all x1, blocking collectives, exchange(): return lax.all_to_all(value, axis, split_axis=0, concat_axis=0, tiled=True)  29.7 us
    all_to_all x1, starting transfers between devices, exchange(): return lax.all_to_all(value, axis, split_axis=0, concat_axis=0, tiled=True)  15.2 us
    ppermute x2, waiting for transfers between devices, neighbours(): lax.ppermute(block, AXES, across)  12.2 us
    ppermute x2, starting transfers between devices, neighbours(): lax.ppermute(block, AXES, across)  8.15 us
    pallas_call x1, Pallas kernels, local(): pl.pallas_call(first_kernel, out_shape=(blocks, shape(reach + count, ROWS...  4.25 us
    pallas_call x1, Pallas kernels, local(): pl.pallas_call(second_kernel, out_shape=shape(parts, 3 * count + 1, 8, LA...  3.91 us
    all_to_all x1, waiting for transfers between devices, exchange(): return lax.all_to_all(value, axis, split_axis=0, concat_axis=0, tiled=True)  3.37 us
    pallas_call x1, Pallas kernels, local(): pl.pallas_call(seed_kernel, out_shape=blocks, in_specs=[pl.BlockSpec(memo...  2.82 us
  transfers between devices with their start and end apart: 6, of which 4 were waited for; matrix products, arithmetic and copies ran while one was open for 0% of the time, Pallas kernels for 2%

profile of v8, /device:TPU:1, one launch (start us, length us, event | category | flops | bytes accessed | tf_op | source)
XLA Modules:
  0.0 90.2 jit_solution(2352993757327803564)
XLA Ops:
  0.6 0.0 copy-start.2
  0.6 0.0 copy-start.3
  0.7 0.0 copy-start
  0.7 0.0 copy-start.5
  0.7 0.0 copy-start.7
  0.7 0.0 copy-start.1
  0.7 0.0 copy-start.4
  0.7 2.8 %seed.1.here_ref = f32[16,64,128]{2,1,0:T(8,128)S(1)} custom-call(f32[16,4096]{1,0:T(8,128)} %refs_0_.1, f32[16,4096]{1,0:T(8,128)} %refs_1_.1, f32[16,4096]{1,0:T(8,128)} %weights_ref.1, bf16[384,256]{1,0:T(8,128)(2,1)} %constant.40.clone.refs_3_.back_lanes_ref, bf16[128,256]{1,0:T(8,128)(2,1)} %constant.41.clone.refs_4_.back_rows_ref, ...), custom_call_target="tpu_custom_call" | custom-call | tf_op jit(solution)/shard_map/seed/pallas_call | solution.py:413
  3.5 4.5 %collective-permute-start.1 = (f32[16,64,128]{2,1,0:T(8,128)S(1)}, f32[16,64,128]{2,1,0:T(8,128)S(1)}, u32[]{:S(2)}, u32[]{:S(2)}) collective-permute-start(f32[16,64,128]{2,1,0:T(8,128)S(1)} %seed.1.here_ref), channel_id=1, source_target_pairs={{0,0},{1,2},{2,1},{3,4},{4,3},{5,6},{6,5},{7,8},{8,7},{9,10},{10,9... | collective-permute-start | bytes 1572872 | tf_op jit(solution)/shard_map/ppermute | solution.py:406
  8.1 0.1 collective-permute-start
  8.2 0.0 copy-done.1
  8.2 0.0 copy-done.4
  8.2 1.2 %arrange.1 = (f32[16,64,128]{2,1,0:T(8,128)S(1)}, f32[1024,128]{1,0:T(8,128)S(1)}) custom-call(f32[16,4096]{1,0:T(8,128)S(1)} %copy-done.1, f32[16,8192]{1,0:T(8,128)S(1)} %copy-done.4), custom_call_target="tpu_custom_call" | custom-call | flops 10000000 | bytes 2000000 | tf_op jit(solution)/shard_map/arrange/pallas_call | solution.py:424
  9.4 0.1 add_convert_fusion.keep_ref
  9.5 5.4 %collective-permute-done.1.across_ref = f32[16,64,128]{2,1,0:T(8,128)S(1)} collective-permute-done((f32[16,64,128]{2,1,0:T(8,128)S(1)}, f32[16,64,128]{2,1,0:T(8,128)S(1)}, u32[]{:S(2)}, u32[]{:S(2)}) %collective-permute-start.1) | collective-permute-done | bytes 524320 | tf_op jit(solution)/shard_map/ppermute | solution.py:406
  14.9 0.0 collective-permute-done.inside_ref
  14.9 0.0 copy-done.2
  14.9 0.0 copy-done.3
  14.9 0.0 copy-done
  14.9 0.0 copy-done.5
  14.9 0.0 copy-done.7
  15.0 4.2 %first.1 = (f32[16,64,128]{2,1,0:T(8,128)S(1)}, f32[31,64,128]{2,1,0:T(8,128)S(1)}) custom-call(f32[3]{0:T(128)S(1)} %add_convert_fusion.keep_ref, f32[16,64,128]{2,1,0:T(8,128)} %collective-permute-done.inside_ref, f32[16,64,128]{2,1,0:T(8,128)S(1)} %seed.1.here_ref, f32[16,64,128]{2,1,0:T(8,128)S(1)} %collective-permute-done.1.across_ref, ...), custom_call_target="tpu_custom_call" | custom-call | tf_op jit(solution)/shard_map/first/pallas_call | solution.py:436
  19.2 3.6 %collective-permute-start.3 = (f32[16,64,128]{2,1,0:T(8,128)S(1)}, f32[16,64,128]{2,1,0:T(8,128)S(1)}, u32[]{:S(2)}, u32[]{:S(2)}) collective-permute-start(f32[16,64,128]{2,1,0:T(8,128)S(1)} %get-tuple-element.13.here_ref), channel_id=1, source_target_pairs={{0,0},{1,2},{2,1},{3,4},{4,3},{5,6},{6,5},{7,8},{8,7},{9,10},{10,9... | collective-permute-start | bytes 1572872 | tf_op jit(solution)/shard_map/ppermute | solution.py:406
  22.9 0.1 collective-permute-start.2
  23.0 6.8 %collective-permute-done.3.across_ref = f32[16,64,128]{2,1,0:T(8,128)S(1)} collective-permute-done((f32[16,64,128]{2,1,0:T(8,128)S(1)}, f32[16,64,128]{2,1,0:T(8,128)S(1)}, u32[]{:S(2)}, u32[]{:S(2)}) %collective-permute-start.3) | collective-permute-done | bytes 524320 | tf_op jit(solution)/shard_map/ppermute | solution.py:406
  29.7 0.0 collective-permute-done.2.inside_ref
  29.7 3.9 %second.1 = f32[8,49,8,128]{3,2,1,0:T(8,128)S(1)} custom-call(f32[3]{0:T(128)S(1)} %add_convert_fusion.keep_ref, f32[16,64,128]{2,1,0:T(8,128)S(1)} %collective-permute-done.2.inside_ref, f32[16,64,128]{2,1,0:T(8,128)S(1)} %get-tuple-element.13.here_ref, f32[16,64,128]{2,1,0:T(8,128)S(1)} %collective-permute-done.3.across_ref, ...), custom_call_target="tpu_custom_call" | custom-call | tf_op jit(solution)/shard_map/second/pallas_call | solution.py:447
  33.6 29.7 %all_to_all.10.moved_ref = f32[8,49,8,128]{3,2,1,0:T(8,128)S(1)} all-to-all(f32[8,49,8,128]{3,2,1,0:T(8,128)S(1)} %second.1), channel_id=1, replica_groups=mesh['tm'=32,'chan'=8] {'chan'}, dimensions={0} | all-to-all | bytes 3211264 | tf_op jit(solution)/shard_map/all_to_all | solution.py:409
  63.3 0.6 tail.1
  64.0 15.2 %all-to-all-start.1 = ((f32[32,4,128]{2,1,0:T(4,128)}), f32[32,4,128]{2,1,0:T(4,128)S(1)}, u32[]{:S(2)}, u32[]{:S(2)}) async-start(f32[32,4,128]{2,1,0:T(4,128)} %get-tuple-element.19), calls=%async_computation.1 | async-start | bytes 131072 | tf_op jit(solution)/shard_map/all_to_all | solution.py:409
  79.2 1.3 %collective-permute-start.4 = (f32[16,8,128]{2,1,0:T(8,128)S(1)}, f32[16,8,128]{2,1,0:T(8,128)S(1)}, u32[]{:S(2)}, u32[]{:S(2)}) collective-permute-start(f32[16,8,128]{2,1,0:T(8,128)S(1)} %get-tuple-element.18), channel_id=1, source_target_pairs={{8,0},{16,8},{24,16},{32,24},{40,32},{48,40},{56,48},{64,56},{72,6... | collective-permute-start | bytes 196616 | tf_op jit(solution)/shard_map/ppermute | solution.py:469
  80.6 0.9 %prepare.1 = (f32[128,1024]{1,0:T(8,128)S(1)}, f32[128,1024]{1,0:T(8,128)S(1)}, f32[112,1024]{1,0:T(8,128)S(1)}) custom-call(s32[1]{0:T(128)} %bitcast.place_ref, f32[8,49,8,128]{3,2,1,0:T(8,128)S(1)} %all_to_all.10.moved_ref, f32[16,64,128]{2,1,0:T(8,128)S(1)} %bitcast.8), custom_call_target="tpu_custom_call" | custom-call | flops 10000000 | bytes 3000000 | tf_op jit(solution)/shard_map/prepare/pallas_call | solution.py:472
  81.5 0.0 copy-start.6
  81.5 0.8 copy-done.6
  82.2 2.4 %collective-permute-done.4.after_ref = f32[16,8,128]{2,1,0:T(8,128)S(1)} collective-permute-done((f32[16,8,128]{2,1,0:T(8,128)S(1)}, f32[16,8,128]{2,1,0:T(8,128)S(1)}, u32[]{:S(2)}, u32[]{:S(2)}) %collective-permute-start.4) | collective-permute-done | bytes 65568 | tf_op jit(solution)/shard_map/ppermute | solution.py:469
  84.7 3.4 %all-to-all-done.1.sums_ref = f32[32,4,128]{2,1,0:T(4,128)S(1)} async-done(((f32[32,4,128]{2,1,0:T(4,128)}), f32[32,4,128]{2,1,0:T(4,128)S(1)}, u32[]{:S(2)}, u32[]{:S(2)}) %all-to-all-start.1) | async-done | bytes 65568 | tf_op jit(solution)/shard_map/all_to_all | solution.py:409
  88.1 2.2 %last.1 = (f32[128,1024]{1,0:T(8,128)}, f32[128,1024]{1,0:T(8,128)}) custom-call(s32[1]{0:T(128)} %bitcast.place_ref, f32[1]{0:T(128)} %bitcast.1.keep_ref, f32[8,49,8,128]{3,2,1,0:T(8,128)S(1)} %all_to_all.10.moved_ref, f32[128,1024]{1,0:T(8,128)S(1)} %get-tuple-element.15.base_ref, f32[128,1024]{1,0:T(8,128)S(1)} %get-tuple-element.16.image_ref, ...), custom_call_target="tpu_custom_call" | custom-call | tf_op jit(solution)/shard_map/last/pallas_call | solution.py:483
Async XLA Ops:
  0.6 14.3 %copy-start.2 = (f32[2,64,128]{2,1,0:T(8,128)S(1)}, f32[2,64,128]{2,1,0:T(8,128)}, u32[]{:S(2)}) copy-start(f32[2,64,128]{2,1,0:T(8,128)} %constant.42.clone.refs_5_.twist_ref) | copy-start | bytes 196612
  0.6 14.3 %copy-start.3 = (bf16[128,256]{1,0:T(8,128)(2,1)S(1)}, bf16[128,256]{1,0:T(8,128)(2,1)}, u32[]{:S(2)}) copy-start(bf16[128,256]{1,0:T(8,128)(2,1)} %constant.41.clone.refs_4_.back_rows_ref) | copy-start | bytes 196612
  0.7 14.3 %copy-start = (bf16[384,256]{1,0:T(8,128)(2,1)S(1)}, bf16[384,256]{1,0:T(8,128)(2,1)}, u32[]{:S(2)}) copy-start(bf16[384,256]{1,0:T(8,128)(2,1)} %constant.40.clone.refs_3_.back_lanes_ref) | copy-start | bytes 589828
  0.7 14.3 %copy-start.5 = (bf16[256,256]{1,0:T(8,128)(2,1)S(1)}, bf16[256,256]{1,0:T(8,128)(2,1)}, u32[]{:S(2)}) copy-start(bf16[256,256]{1,0:T(8,128)(2,1)} %constant.44.clone.ahead_lanes_ref) | copy-start | bytes 393220
  0.7 14.3 %copy-start.7 = (bf16[128,192]{1,0:T(8,128)(2,1)S(1)}, bf16[128,192]{1,0:T(8,128)(2,1)}, u32[]{:S(2)}) copy-start(bf16[128,192]{1,0:T(8,128)(2,1)} %constant.43.clone.ahead_rows_ref) | copy-start | bytes 147460
  0.7 7.5 %copy-start.1 = (f32[16,4096]{1,0:T(8,128)S(1)}, f32[16,4096]{1,0:T(8,128)}, u32[]{:S(2)}) copy-start(f32[16,4096]{1,0:T(8,128)} %weights_ref.1) | copy-start | bytes 786436
  0.7 7.5 %copy-start.4 = (f32[16,8192]{1,0:T(8,128)S(1)}, f32[16,8192]{1,0:T(8,128)}, u32[]{:S(2)}) copy-start(f32[16,8192]{1,0:T(8,128)} %taps_ref.1) | copy-start | bytes 1572868
  3.5 11.4 %collective-permute-start.1 = (f32[16,64,128]{2,1,0:T(8,128)S(1)}, f32[16,64,128]{2,1,0:T(8,128)S(1)}, u32[]{:S(2)}, u32[]{:S(2)}) collective-permute-start(f32[16,64,128]{2,1,0:T(8,128)S(1)} %seed.1.here_ref), channel_id=1, source_target_pairs={{0,0},{1,2},{2,1},{3,4},{4,3},{5,6},{6,5},{7,8},{8,7},{9,10},{10,9... | collective-permute-start | bytes 1572872 | tf_op jit(solution)/shard_map/ppermute | solution.py:406
  8.1 6.9 %collective-permute-start = (f32[16,64,128]{2,1,0:T(8,128)S(1)}, f32[16,64,128]{2,1,0:T(8,128)}, u32[]{:S(2)}, u32[]{:S(2)}) collective-permute-start(f32[16,64,128]{2,1,0:T(8,128)S(1)} %seed.1.here_ref), channel_id=1, source_target_pairs={{0,1},{1,0},{2,3},{3,2},{4,5},{5,4},{6,7},{7,6},{8,9},{9,8},{10,11... | collective-permute-start | bytes 1572872 | tf_op jit(solution)/shard_map/ppermute | solution.py:406
  19.2 10.5 %collective-permute-start.3 = (f32[16,64,128]{2,1,0:T(8,128)S(1)}, f32[16,64,128]{2,1,0:T(8,128)S(1)}, u32[]{:S(2)}, u32[]{:S(2)}) collective-permute-start(f32[16,64,128]{2,1,0:T(8,128)S(1)} %get-tuple-element.13.here_ref), channel_id=1, source_target_pairs={{0,0},{1,2},{2,1},{3,4},{4,3},{5,6},{6,5},{7,8},{8,7},{9,10},{10,9... | collective-permute-start | bytes 1572872 | tf_op jit(solution)/shard_map/ppermute | solution.py:406
  22.9 6.9 %collective-permute-start.2 = (f32[16,64,128]{2,1,0:T(8,128)S(1)}, f32[16,64,128]{2,1,0:T(8,128)S(1)}, u32[]{:S(2)}, u32[]{:S(2)}) collective-permute-start(f32[16,64,128]{2,1,0:T(8,128)S(1)} %get-tuple-element.13.here_ref), channel_id=1, source_target_pairs={{0,1},{1,0},{2,3},{3,2},{4,5},{5,4},{6,7},{7,6},{8,9},{9,8},{10,11... | collective-permute-start | bytes 1572872 | tf_op jit(solution)/shard_map/ppermute | solution.py:406
  64.0 24.1 %all-to-all-start.1 = ((f32[32,4,128]{2,1,0:T(4,128)}), f32[32,4,128]{2,1,0:T(4,128)S(1)}, u32[]{:S(2)}, u32[]{:S(2)}) async-start(f32[32,4,128]{2,1,0:T(4,128)} %get-tuple-element.19), calls=%async_computation.1 | async-start | bytes 131072 | tf_op jit(solution)/shard_map/all_to_all | solution.py:409
  79.2 5.4 %collective-permute-start.4 = (f32[16,8,128]{2,1,0:T(8,128)S(1)}, f32[16,8,128]{2,1,0:T(8,128)S(1)}, u32[]{:S(2)}, u32[]{:S(2)}) collective-permute-start(f32[16,8,128]{2,1,0:T(8,128)S(1)} %get-tuple-element.18), channel_id=1, source_target_pairs={{8,0},{16,8},{24,16},{32,24},{40,32},{48,40},{56,48},{64,56},{72,6... | collective-permute-start | bytes 196616 | tf_op jit(solution)/shard_map/ppermute | solution.py:469
  81.5 0.8 copy-start.6

commit v9 on v7

--- a/solution.py
+++ b/solution.py
@@ -225,10 +225,14 @@
 
 
 def second_kernel(
-    keep_ref, inside_ref, here_ref, across_ref, side_ref, taps_ref, weights_ref,
+    place_ref, keep_ref, inside_ref, here_ref, across_ref, side_ref, taps_ref, weights_ref,
     ahead_rows_ref, ahead_lanes_ref, back_lanes_ref, back_rows_ref, twist_ref,
-    out_ref, filtered, sums,
+    out_ref, *rest,
 ):
+    lanes, (filtered, sums, staged, semaphore) = rest[:8], rest[8:]
+    copies = [
+        pltpu.make_async_copy(staged.at[d], lane, semaphore.at[d]) for d, lane in enumerate(lanes)
+    ]
     count = here_ref.shape[0]
     keep = (keep_ref[0], keep_ref[1], keep_ref[2])
     reach = taps_ref.shape[0] - 1
@@ -247,8 +251,8 @@
         for at in range(count):
             base = side[reach + at]
             value = image[reach + at]
-            out_ref[group, at] = base
-            out_ref[group, count + at] = value
+            staged[group ^ place_ref[0], at] = base
+            staged[group ^ place_ref[0], count + at] = value
             first = first + base * base
             second = second + base * value
             third = third + value * value
@@ -256,6 +260,8 @@
         sums[1] = second
         sums[2] = third
 
+    for copy in copies:
+        copy.start()
     cos = twist_ref[0]
     sin = twist_ref[1]
     power = jnp.zeros((8, LANES), F32)
@@ -269,31 +275,32 @@
         frames = backward_chunk(weighted, back_lanes_ref[...], back_rows_ref[...], cos, sin)
         for f in range(CHUNK):
             for group in range(ROWS // 8):
-                out_ref[group, 2 * count + start + f] = frames[
+                out_ref[group, start + f] = frames[
                     group * 8 : (group + 1) * 8, f * LANES : (f + 1) * LANES
                 ]
     totals = pack([sums[0], sums[1], sums[2], power])
     for group in range(ROWS // 8):
-        out_ref[group, 3 * count] = totals
+        out_ref[group, count] = totals
+    for copy in copies:
+        copy.wait()
 
 
 def tail_kernel(moved_ref, frames_ref, sums_ref):
     count = frames_ref.shape[0]
-    frames_ref[...] = moved_ref[0, 2 * count : 3 * count]
-    total = moved_ref[0, 3 * count]
+    frames_ref[...] = moved_ref[0, :count]
+    total = moved_ref[0, count]
     for part in range(1, moved_ref.shape[0]):
-        total = total + moved_ref[part, 3 * count]
+        total = total + moved_ref[part, count]
     sums_ref[...] = jnp.broadcast_to((total[:4] + total[4:])[None], sums_ref.shape)
 
 
-def last_kernel(
-    place_ref, keep_ref, moved_ref, after_ref, sums_ref, taps_ref,
-    solution_ref, residual_ref, kept, left,
-):
-    parts = moved_ref.shape[0]
-    count = (moved_ref.shape[1] - 1) // 3
+def last_kernel(place_ref, keep_ref, moved_ref, after_ref, sums_ref, taps_ref, *rest):
+    lanes, (solution_ref, residual_ref, kept, left, pairs) = rest[:8], rest[8:]
+    parts, count = moved_ref.shape[0], moved_ref.shape[1] - 1
     reach = taps_ref.shape[0] - 1
     rows = pl.ds(pl.multiple_of(place_ref[0] * 8, 8), 8)
+    for d, lane in enumerate(lanes):
+        pairs[place_ref[0] ^ d] = lane[...]
     sums = jnp.sum(sums_ref[...], 0)
     norm, curve, square, power = (
         jnp.sum(jnp.sum(jnp.where(quarters(4) == at, sums, 0.0), 1, keepdims=True), 0, keepdims=True)
@@ -314,10 +321,10 @@
     taps = [taps_ref[p, rows, :] for p in range(reach + 1)]
 
     def finish(part, tail):
-        frames = [moved_ref[part, 2 * count + t] for t in range(count)] + tail
+        frames = [moved_ref[part, t] for t in range(count)] + tail
         for at in range(count):
-            base = moved_ref[part, at]
-            image = moved_ref[part, count + at]
+            base = pairs[part, at]
+            image = pairs[part, count + at]
             again = weighted_sum(taps, frames[at : at + reach + 1]) + RIDGE * image
             here = pl.ds(pl.multiple_of((part * count + at) * 8, 8), 8)
             kept[here, :] = to_base * base + to_image * image
@@ -325,7 +332,7 @@
 
     @pl.loop(0, parts - 1)
     def _(part):
-        finish(part, [moved_ref[part + 1, 2 * count + t] for t in range(reach)])
+        finish(part, [moved_ref[part + 1, t] for t in range(reach)])
 
     finish(parts - 1, [after_ref[t] * keep_ref[0] for t in range(reach)])
 
@@ -406,20 +413,26 @@
     )(keep, inside, seeds, across, taps, weights, *tables)
     inside, across = neighbours(images)
 
-    outgoing = pl.pallas_call(
+    outgoing, *lanes = pl.pallas_call(
         second_kernel,
-        out_shape=shape(parts, 3 * count + 1, 8, LANES),
-        in_specs=[SMEM] + vmem(11),
-        out_specs=vmem(1)[0],
+        out_shape=(shape(parts, count + 1, 8, LANES),) + (shape(2 * count, 8, LANES),) * 8,
+        in_specs=[SMEM, SMEM] + vmem(11),
+        out_specs=tuple(vmem(9)),
         scratch_shapes=[
             pltpu.VMEM((count, ROWS, LANES), F32),
             pltpu.VMEM((3, 8, LANES), F32),
+            pltpu.VMEM((parts, 2 * count, 8, LANES), F32),
+            pltpu.SemaphoreType.DMA((8,)),
         ],
         compiler_params=params(),
         name="second",
-    )(keep, inside, images, across, side, taps, weights, *tables)
+    )(place, keep, inside, images, across, side, taps, weights, *tables)
 
     moved = exchange(outgoing, "chan")
+    moved, lanes = lax.optimization_barrier((moved, lanes))
+    lanes = lanes[:1] + [
+        lax.ppermute(lanes[d], AXES, [(i, i ^ d) for i in range(devices)]) for d in range(1, 8)
+    ]
     after, sums = pl.pallas_call(
         tail_kernel,
         out_shape=(shape(count, 8, LANES), shape(groups, 4, LANES)),
@@ -433,15 +446,16 @@
     return pl.pallas_call(
         last_kernel,
         out_shape=(shape(parts * count, 8 * LANES), shape(parts * count, 8 * LANES)),
-        in_specs=[SMEM, SMEM] + vmem(4),
+        in_specs=[SMEM, SMEM] + vmem(12),
         out_specs=tuple(vmem(2)),
         scratch_shapes=[
             pltpu.VMEM((parts * count * 8, LANES), F32),
             pltpu.VMEM((parts * count * 8, LANES), F32),
+            pltpu.VMEM((parts, 2 * count, 8, LANES), F32),
         ],
         compiler_params=params(),
         name="last",
-    )(place, keep_group, moved, after, sums, taps)
+    )(place, keep_group, moved, after, sums, taps, *lanes)
 
 
 def solution(mesh):

time: 90.4 us -> 94.4 us (1.044)
  blocking collectives: 29.7 us -> 18.3 us
  starting transfers between devices: 24.9 us -> 35.9 us
  waiting for transfers between devices: 19.7 us -> 22.8 us
    all_to_all x1, blocking collectives: 29.7 us -> 18.3 us  [exchange(): return lax.all_to_all(value, axis, split_axis=0, concat_axis=0, tiled=True)]
    ppermute x0 -> x7, starting transfers between devices: none -> 8.11 us  [local(): lax.ppermute(lanes[d], AXES, [(i, i ^ d) for i in range(devices)])]
    all_to_all x1, waiting for transfers between devices: 3.37 us -> 8.87 us  [exchange(): return lax.all_to_all(value, axis, split_axis=0, concat_axis=0, tiled=True)]
    all_to_all x1, starting transfers between devices: 15.2 us -> 18.1 us  [exchange(): return lax.all_to_all(value, axis, split_axis=0, concat_axis=0, tiled=True)]
    ppermute x1, waiting for transfers between devices: 4.14 us -> 1.77 us  [local(): after = lax.ppermute(after, 'tm', [(i + 1, i) for i in range(groups - 1)])]
    pallas_call x1, Pallas kernels: 3.91 us -> 5.39 us  [local(): pl.pallas_call(second_kernel, out_shape=(shape(parts, count + 1, 8, LANES...]
  transfers between devices with their start and end apart: 6 -> 13, of which waited for: 4 -> 4; matrix products, arithmetic and copies ran while one was open for 0% -> 0% of each run, Pallas kernels for 1% -> 2%
where the time goes in v9:
time: 94.4 us; the launch traced here: 93.7 us
  starting transfers between devices  35.9 us (38%)
  waiting for transfers between devices  22.8 us (24%)
  blocking collectives  18.3 us (19%)
  Pallas kernels  15.8 us (17%)
    all_to_all x1, blocking collectives, exchange(): return lax.all_to_all(value, axis, split_axis=0, concat_axis=0, tiled=True)  18.3 us
    all_to_all x1, starting transfers between devices, exchange(): return lax.all_to_all(value, axis, split_axis=0, concat_axis=0, tiled=True)  18.1 us
    ppermute x2, waiting for transfers between devices, neighbours(): lax.ppermute(block, AXES, across)  12.1 us
    all_to_all x1, waiting for transfers between devices, exchange(): return lax.all_to_all(value, axis, split_axis=0, concat_axis=0, tiled=True)  8.87 us
    ppermute x2, starting transfers between devices, neighbours(): lax.ppermute(block, AXES, across)  8.15 us
    ppermute x7, starting transfers between devices, local(): lax.ppermute(lanes[d], AXES, [(i, i ^ d) for i in range(devices)])  8.11 us
    pallas_call x1, Pallas kernels, local(): pl.pallas_call(second_kernel, out_shape=(shape(parts, count + 1, 8, LANES...  5.39 us
    pallas_call x1, Pallas kernels, local(): pl.pallas_call(first_kernel, out_shape=(blocks, shape(reach + count, ROWS...  3.73 us
  transfers between devices with their start and end apart: 13, of which 4 were waited for; matrix products, arithmetic and copies ran while one was open for 0% of the time, Pallas kernels for 2%

profile of v9, /device:TPU:1, one launch (start us, length us, event | category | flops | bytes accessed | tf_op | source)
XLA Modules:
  0.0 93.7 jit_solution(3756858853684665478)
XLA Ops:
  0.6 0.0 copy-start.1
  0.6 0.0 copy-start.4
  0.7 2.8 %seed.1.here_ref = f32[16,64,128]{2,1,0:T(8,128)S(1)} custom-call(f32[16,4096]{1,0:T(8,128)} %refs_0_.1, f32[16,4096]{1,0:T(8,128)} %refs_1_.1, f32[16,4096]{1,0:T(8,128)} %weights_ref.1, bf16[384,256]{1,0:T(8,128)(2,1)} %constant.40.clone.refs_3_.back_lanes_ref, bf16[128,256]{1,0:T(8,128)(2,1)} %constant.41.clone.refs_4_.back_rows_ref, ...), custom_call_target="tpu_custom_call" | custom-call | tf_op jit(solution)/shard_map/seed/pallas_call | solution.py:382
  3.5 4.5 %collective-permute-start.1 = (f32[16,64,128]{2,1,0:T(8,128)S(1)}, f32[16,64,128]{2,1,0:T(8,128)S(1)}, u32[]{:S(2)}, u32[]{:S(2)}) collective-permute-start(f32[16,64,128]{2,1,0:T(8,128)S(1)} %seed.1.here_ref), channel_id=1, source_target_pairs={{0,0},{1,2},{2,1},{3,4},{4,3},{5,6},{6,5},{7,8},{8,7},{9,10},{10,9... | collective-permute-start | bytes 1572872 | tf_op jit(solution)/shard_map/ppermute | solution.py:375
  8.0 0.1 collective-permute-start
  8.1 0.0 copy-done.1
  8.1 0.0 copy-done.4
  8.1 0.0 copy-start
  8.1 0.0 copy-start.2
  8.1 0.0 copy-start.3
  8.2 0.0 copy-start.5
  8.2 0.0 copy-start.6
  8.2 1.2 %arrange.1 = (f32[16,64,128]{2,1,0:T(8,128)S(1)}, f32[1024,128]{1,0:T(8,128)S(1)}) custom-call(f32[16,4096]{1,0:T(8,128)S(1)} %copy-done.1, f32[16,8192]{1,0:T(8,128)S(1)} %copy-done.4), custom_call_target="tpu_custom_call" | custom-call | flops 10000000 | bytes 2000000 | tf_op jit(solution)/shard_map/arrange/pallas_call | solution.py:393
  9.4 0.1 add_convert_fusion.keep_ref
  9.5 5.4 %collective-permute-done.1.across_ref = f32[16,64,128]{2,1,0:T(8,128)S(1)} collective-permute-done((f32[16,64,128]{2,1,0:T(8,128)S(1)}, f32[16,64,128]{2,1,0:T(8,128)S(1)}, u32[]{:S(2)}, u32[]{:S(2)}) %collective-permute-start.1) | collective-permute-done | bytes 524320 | tf_op jit(solution)/shard_map/ppermute | solution.py:375
  14.8 0.0 collective-permute-done.inside_ref
  14.8 0.0 copy-done
  14.8 0.0 copy-done.2
  14.8 0.0 copy-done.3
  14.9 0.0 copy-done.5
  14.9 0.0 copy-done.6
  14.9 3.7 %first.1 = (f32[16,64,128]{2,1,0:T(8,128)S(1)}, f32[31,64,128]{2,1,0:T(8,128)S(1)}) custom-call(f32[3]{0:T(128)S(1)} %add_convert_fusion.keep_ref, f32[16,64,128]{2,1,0:T(8,128)S(1)} %collective-permute-done.inside_ref, f32[16,64,128]{2,1,0:T(8,128)S(1)} %seed.1.here_ref, f32[16,64,128]{2,1,0:T(8,128)S(1)} %collective-permute-done.1.across_ref, ...), custom_call_target="tpu_custom_call" | custom-call | tf_op jit(solution)/shard_map/first/pallas_call | solution.py:405
  18.6 3.6 %collective-permute-start.3 = (f32[16,64,128]{2,1,0:T(8,128)S(1)}, f32[16,64,128]{2,1,0:T(8,128)S(1)}, u32[]{:S(2)}, u32[]{:S(2)}) collective-permute-start(f32[16,64,128]{2,1,0:T(8,128)S(1)} %get-tuple-element.28.here_ref), channel_id=1, source_target_pairs={{0,0},{1,2},{2,1},{3,4},{4,3},{5,6},{6,5},{7,8},{8,7},{9,10},{10,9... | collective-permute-start | bytes 1572872 | tf_op jit(solution)/shard_map/ppermute | solution.py:375
  22.3 0.1 collective-permute-start.2
  22.4 6.8 %collective-permute-done.3.across_ref = f32[16,64,128]{2,1,0:T(8,128)S(1)} collective-permute-done((f32[16,64,128]{2,1,0:T(8,128)S(1)}, f32[16,64,128]{2,1,0:T(8,128)S(1)}, u32[]{:S(2)}, u32[]{:S(2)}) %collective-permute-start.3) | collective-permute-done | bytes 524320 | tf_op jit(solution)/shard_map/ppermute | solution.py:375
  29.1 0.0 collective-permute-done.2.inside_ref
  29.1 5.4 %second.1 = (f32[8,17,8,128]{3,2,1,0:T(8,128)S(1)}, f32[32,8,128]{2,1,0:T(8,128)S(1)}, f32[32,8,128]{2,1,0:T(8,128)S(1)}, f32[32,8,128]{2,1,0:T(8,128)S(1)}, f32...) custom-call(s32[1]{0:T(128)} %bitcast.place_ref, ...), custom_call_target="tpu_custom_call" | custom-call | tf_op jit(solution)/shard_map/second/pallas_call | solution.py:416
  34.5 18.3 %all_to_all.10.moved_ref = f32[8,17,8,128]{3,2,1,0:T(8,128)S(1)} all-to-all(f32[8,17,8,128]{3,2,1,0:T(8,128)S(1)} %get-tuple-element.30), channel_id=1, replica_groups=mesh['tm'=32,'chan'=8] {'chan'}, dimensions={0} | all-to-all | bytes 1114112 | tf_op jit(solution)/shard_map/all_to_all | solution.py:378
  52.8 0.6 collective-permute-start.5
  53.4 0.3 collective-permute-start.6
  53.7 0.6 tail.1
  54.3 1.3 %collective-permute-start.4 = (f32[16,8,128]{2,1,0:T(8,128)S(1)}, f32[16,8,128]{2,1,0:T(8,128)S(1)}, u32[]{:S(2)}, u32[]{:S(2)}) collective-permute-start(f32[16,8,128]{2,1,0:T(8,128)S(1)} %get-tuple-element.40), channel_id=1, source_target_pairs={{8,0},{16,8},{24,16},{32,24},{40,32},{48,40},{56,48},{64,56},{72,6... | collective-permute-start | bytes 196616 | tf_op jit(solution)/shard_map/ppermute | solution.py:444
  55.6 1.4 %collective-permute-start.7 = (f32[32,8,128]{2,1,0:T(8,128)S(1)}, f32[32,8,128]{2,1,0:T(8,128)S(1)}, u32[]{:S(2)}, u32[]{:S(2)}) collective-permute-start(f32[32,8,128]{2,1,0:T(8,128)S(1)} %get-tuple-element.45), channel_id=1, source_target_pairs={{0,3},{1,2},{2,1},{3,0},{4,7},{5,6},{6,5},{7,4},{8,11},{9,10},{10,... | collective-permute-start | bytes 393224 | tf_op jit(solution)/shard_map/ppermute | solution.py:434
  57.0 0.8 collective-permute-start.8
  57.8 1.8 %collective-permute-done.4.after_ref = f32[16,8,128]{2,1,0:T(8,128)S(1)} collective-permute-done((f32[16,8,128]{2,1,0:T(8,128)S(1)}, f32[16,8,128]{2,1,0:T(8,128)S(1)}, u32[]{:S(2)}, u32[]{:S(2)}) %collective-permute-start.4) | collective-permute-done | bytes 65568 | tf_op jit(solution)/shard_map/ppermute | solution.py:444
  59.6 2.8 %collective-permute-start.9 = (f32[32,8,128]{2,1,0:T(8,128)S(1)}, f32[32,8,128]{2,1,0:T(8,128)S(1)}, u32[]{:S(2)}, u32[]{:S(2)}) collective-permute-start(f32[32,8,128]{2,1,0:T(8,128)S(1)} %get-tuple-element.47), channel_id=1, source_target_pairs={{0,5},{1,4},{2,7},{3,6},{4,1},{5,0},{6,3},{7,2},{8,13},{9,12},{10,... | collective-permute-start | bytes 393224 | tf_op jit(solution)/shard_map/ppermute | solution.py:434
  62.4 0.0 collective-permute-done.5.rest_1_
  62.4 1.8 %collective-permute-start.10 = (f32[32,8,128]{2,1,0:T(8,128)S(1)}, f32[32,8,128]{2,1,0:T(8,128)S(1)}, u32[]{:S(2)}, u32[]{:S(2)}) collective-permute-start(f32[32,8,128]{2,1,0:T(8,128)S(1)} %get-tuple-element.48), channel_id=1, source_target_pairs={{0,6},{1,7},{2,4},{3,5},{4,2},{5,3},{6,0},{7,1},{8,14},{9,15},{10,... | collective-permute-start | bytes 393224 | tf_op jit(solution)/shard_map/ppermute | solution.py:434
  64.2 0.0 collective-permute-done.6.rest_2_
  64.2 0.4 collective-permute-start.11
  64.6 18.1 %all-to-all-start.1 = ((f32[32,4,128]{2,1,0:T(4,128)}), f32[32,4,128]{2,1,0:T(4,128)S(1)}, u32[]{:S(2)}, u32[]{:S(2)}) async-start(f32[32,4,128]{2,1,0:T(4,128)} %get-tuple-element.41), calls=%async_computation.1 | async-start | bytes 131072 | tf_op jit(solution)/shard_map/all_to_all | solution.py:378
  82.8 8.9 %all-to-all-done.1.sums_ref = f32[32,4,128]{2,1,0:T(4,128)S(1)} async-done(((f32[32,4,128]{2,1,0:T(4,128)}), f32[32,4,128]{2,1,0:T(4,128)S(1)}, u32[]{:S(2)}, u32[]{:S(2)}) %all-to-all-start.1) | async-done | bytes 65568 | tf_op jit(solution)/shard_map/all_to_all | solution.py:378
  91.7 0.0 collective-permute-done.7.rest_3_
  91.7 0.0 collective-permute-done.8.rest_4_
  91.7 0.0 collective-permute-done.9.rest_5_
  91.7 0.0 collective-permute-done.10.rest_6_
  91.7 0.0 collective-permute-done.11.rest_7_
  91.7 2.1 %last.1 = (f32[128,1024]{1,0:T(8,128)}, f32[128,1024]{1,0:T(8,128)}) custom-call(s32[1]{0:T(128)} %bitcast.place_ref, f32[1]{0:T(128)} %bitcast.1.keep_ref, f32[8,17,8,128]{3,2,1,0:T(8,128)S(1)} %all_to_all.10.moved_ref, f32[16,8,128]{2,1,0:T(8,128)S(1)} %collective-permute-done.4.after_ref, f32[32,4,128]{2,1,0:T(4,128)S(1)} %all-to-all-done.1.sums_ref, ...), custom_call_target="tpu_custom_call" | custom-call | tf_op jit(solution)/shard_map/last/pallas_call | solution.py:446
Async XLA Ops:
  0.6 7.5 %copy-start.1 = (f32[16,4096]{1,0:T(8,128)S(1)}, f32[16,4096]{1,0:T(8,128)}, u32[]{:S(2)}) copy-start(f32[16,4096]{1,0:T(8,128)} %weights_ref.1) | copy-start | bytes 786436
  0.6 7.5 %copy-start.4 = (f32[16,8192]{1,0:T(8,128)S(1)}, f32[16,8192]{1,0:T(8,128)}, u32[]{:S(2)}) copy-start(f32[16,8192]{1,0:T(8,128)} %taps_ref.1) | copy-start | bytes 1572868
  3.5 11.4 %collective-permute-start.1 = (f32[16,64,128]{2,1,0:T(8,128)S(1)}, f32[16,64,128]{2,1,0:T(8,128)S(1)}, u32[]{:S(2)}, u32[]{:S(2)}) collective-permute-start(f32[16,64,128]{2,1,0:T(8,128)S(1)} %seed.1.here_ref), channel_id=1, source_target_pairs={{0,0},{1,2},{2,1},{3,4},{4,3},{5,6},{6,5},{7,8},{8,7},{9,10},{10,9... | collective-permute-start | bytes 1572872 | tf_op jit(solution)/shard_map/ppermute | solution.py:375
  8.0 6.9 %collective-permute-start = (f32[16,64,128]{2,1,0:T(8,128)S(1)}, f32[16,64,128]{2,1,0:T(8,128)S(1)}, u32[]{:S(2)}, u32[]{:S(2)}) collective-permute-start(f32[16,64,128]{2,1,0:T(8,128)S(1)} %seed.1.here_ref), channel_id=1, source_target_pairs={{0,1},{1,0},{2,3},{3,2},{4,5},{5,4},{6,7},{7,6},{8,9},{9,8},{10,11... | collective-permute-start | bytes 1572872 | tf_op jit(solution)/shard_map/ppermute | solution.py:375
  8.1 6.7 %copy-start = (bf16[384,256]{1,0:T(8,128)(2,1)S(1)}, bf16[384,256]{1,0:T(8,128)(2,1)}, u32[]{:S(2)}) copy-start(bf16[384,256]{1,0:T(8,128)(2,1)} %constant.40.clone.refs_3_.back_lanes_ref) | copy-start | bytes 589828
  8.1 6.7 %copy-start.2 = (f32[2,64,128]{2,1,0:T(8,128)S(1)}, f32[2,64,128]{2,1,0:T(8,128)}, u32[]{:S(2)}) copy-start(f32[2,64,128]{2,1,0:T(8,128)} %constant.42.clone.refs_5_.twist_ref) | copy-start | bytes 196612
  8.1 6.7 %copy-start.3 = (bf16[128,256]{1,0:T(8,128)(2,1)S(1)}, bf16[128,256]{1,0:T(8,128)(2,1)}, u32[]{:S(2)}) copy-start(bf16[128,256]{1,0:T(8,128)(2,1)} %constant.41.clone.refs_4_.back_rows_ref) | copy-start | bytes 196612
  8.2 6.7 %copy-start.5 = (bf16[256,256]{1,0:T(8,128)(2,1)S(1)}, bf16[256,256]{1,0:T(8,128)(2,1)}, u32[]{:S(2)}) copy-start(bf16[256,256]{1,0:T(8,128)(2,1)} %constant.44.clone.ahead_lanes_ref) | copy-start | bytes 393220
  8.2 6.7 %copy-start.6 = (bf16[128,192]{1,0:T(8,128)(2,1)S(1)}, bf16[128,192]{1,0:T(8,128)(2,1)}, u32[]{:S(2)}) copy-start(bf16[128,192]{1,0:T(8,128)(2,1)} %constant.43.clone.ahead_rows_ref) | copy-start | bytes 147460
  18.6 10.5 %collective-permute-start.3 = (f32[16,64,128]{2,1,0:T(8,128)S(1)}, f32[16,64,128]{2,1,0:T(8,128)S(1)}, u32[]{:S(2)}, u32[]{:S(2)}) collective-permute-start(f32[16,64,128]{2,1,0:T(8,128)S(1)} %get-tuple-element.28.here_ref), channel_id=1, source_target_pairs={{0,0},{1,2},{2,1},{3,4},{4,3},{5,6},{6,5},{7,8},{8,7},{9,10},{10,9... | collective-permute-start | bytes 1572872 | tf_op jit(solution)/shard_map/ppermute | solution.py:375
  22.3 6.9 %collective-permute-start.2 = (f32[16,64,128]{2,1,0:T(8,128)S(1)}, f32[16,64,128]{2,1,0:T(8,128)S(1)}, u32[]{:S(2)}, u32[]{:S(2)}) collective-permute-start(f32[16,64,128]{2,1,0:T(8,128)S(1)} %get-tuple-element.28.here_ref), channel_id=1, source_target_pairs={{0,1},{1,0},{2,3},{3,2},{4,5},{5,4},{6,7},{7,6},{8,9},{9,8},{10,11... | collective-permute-start | bytes 1572872 | tf_op jit(solution)/shard_map/ppermute | solution.py:375
  52.8 9.6 %collective-permute-start.5 = (f32[32,8,128]{2,1,0:T(8,128)S(1)}, f32[32,8,128]{2,1,0:T(8,128)S(1)}, u32[]{:S(2)}, u32[]{:S(2)}) collective-permute-start(f32[32,8,128]{2,1,0:T(8,128)S(1)} %get-tuple-element.43), channel_id=1, source_target_pairs={{0,1},{1,0},{2,3},{3,2},{4,5},{5,4},{6,7},{7,6},{8,9},{9,8},{10,11... | collective-permute-start | bytes 393224 | tf_op jit(solution)/shard_map/ppermute | solution.py:434
  53.4 10.8 %collective-permute-start.6 = (f32[32,8,128]{2,1,0:T(8,128)S(1)}, f32[32,8,128]{2,1,0:T(8,128)S(1)}, u32[]{:S(2)}, u32[]{:S(2)}) collective-permute-start(f32[32,8,128]{2,1,0:T(8,128)S(1)} %get-tuple-element.44), channel_id=1, source_target_pairs={{0,2},{1,3},{2,0},{3,1},{4,6},{5,7},{6,4},{7,5},{8,10},{9,11},{10,... | collective-permute-start | bytes 393224 | tf_op jit(solution)/shard_map/ppermute | solution.py:434
  54.3 5.3 %collective-permute-start.4 = (f32[16,8,128]{2,1,0:T(8,128)S(1)}, f32[16,8,128]{2,1,0:T(8,128)S(1)}, u32[]{:S(2)}, u32[]{:S(2)}) collective-permute-start(f32[16,8,128]{2,1,0:T(8,128)S(1)} %get-tuple-element.40), channel_id=1, source_target_pairs={{8,0},{16,8},{24,16},{32,24},{40,32},{48,40},{56,48},{64,56},{72,6... | collective-permute-start | bytes 196616 | tf_op jit(solution)/shard_map/ppermute | solution.py:444
  55.6 36.1 %collective-permute-start.7 = (f32[32,8,128]{2,1,0:T(8,128)S(1)}, f32[32,8,128]{2,1,0:T(8,128)S(1)}, u32[]{:S(2)}, u32[]{:S(2)}) collective-permute-start(f32[32,8,128]{2,1,0:T(8,128)S(1)} %get-tuple-element.45), channel_id=1, source_target_pairs={{0,3},{1,2},{2,1},{3,0},{4,7},{5,6},{6,5},{7,4},{8,11},{9,10},{10,... | collective-permute-start | bytes 393224 | tf_op jit(solution)/shard_map/ppermute | solution.py:434
  57.0 34.6 %collective-permute-start.8 = (f32[32,8,128]{2,1,0:T(8,128)S(1)}, f32[32,8,128]{2,1,0:T(8,128)S(1)}, u32[]{:S(2)}, u32[]{:S(2)}) collective-permute-start(f32[32,8,128]{2,1,0:T(8,128)S(1)} %get-tuple-element.46), channel_id=1, source_target_pairs={{0,4},{1,5},{2,6},{3,7},{4,0},{5,1},{6,2},{7,3},{8,12},{9,13},{10,... | collective-permute-start | bytes 393224 | tf_op jit(solution)/shard_map/ppermute | solution.py:434
  59.6 32.1 %collective-permute-start.9 = (f32[32,8,128]{2,1,0:T(8,128)S(1)}, f32[32,8,128]{2,1,0:T(8,128)S(1)}, u32[]{:S(2)}, u32[]{:S(2)}) collective-permute-start(f32[32,8,128]{2,1,0:T(8,128)S(1)} %get-tuple-element.47), channel_id=1, source_target_pairs={{0,5},{1,4},{2,7},{3,6},{4,1},{5,0},{6,3},{7,2},{8,13},{9,12},{10,... | collective-permute-start | bytes 393224 | tf_op jit(solution)/shard_map/ppermute | solution.py:434
  62.4 29.2 %collective-permute-start.10 = (f32[32,8,128]{2,1,0:T(8,128)S(1)}, f32[32,8,128]{2,1,0:T(8,128)S(1)}, u32[]{:S(2)}, u32[]{:S(2)}) collective-permute-start(f32[32,8,128]{2,1,0:T(8,128)S(1)} %get-tuple-element.48), channel_id=1, source_target_pairs={{0,6},{1,7},{2,4},{3,5},{4,2},{5,3},{6,0},{7,1},{8,14},{9,15},{10,... | collective-permute-start | bytes 393224 | tf_op jit(solution)/shard_map/ppermute | solution.py:434
  64.2 27.5 %collective-permute-start.11 = (f32[32,8,128]{2,1,0:T(8,128)S(1)}, f32[32,8,128]{2,1,0:T(8,128)S(1)}, u32[]{:S(2)}, u32[]{:S(2)}) collective-permute-start(f32[32,8,128]{2,1,0:T(8,128)S(1)} %get-tuple-element.49), channel_id=1, source_target_pairs={{0,7},{1,6},{2,5},{3,4},{4,3},{5,2},{6,1},{7,0},{8,15},{9,14},{10,... | collective-permute-start | bytes 393224 | tf_op jit(solution)/shard_map/ppermute | solution.py:434
  64.6 27.0 %all-to-all-start.1 = ((f32[32,4,128]{2,1,0:T(4,128)}), f32[32,4,128]{2,1,0:T(4,128)S(1)}, u32[]{:S(2)}, u32[]{:S(2)}) async-start(f32[32,4,128]{2,1,0:T(4,128)} %get-tuple-element.41), calls=%async_computation.1 | async-start | bytes 131072 | tf_op jit(solution)/shard_map/all_to_all | solution.py:378

commit v10 on v9

--- a/solution.py
+++ b/solution.py
@@ -229,10 +229,7 @@
     ahead_rows_ref, ahead_lanes_ref, back_lanes_ref, back_rows_ref, twist_ref,
     out_ref, *rest,
 ):
-    lanes, (filtered, sums, staged, semaphore) = rest[:8], rest[8:]
-    copies = [
-        pltpu.make_async_copy(staged.at[d], lane, semaphore.at[d]) for d, lane in enumerate(lanes)
-    ]
+    lanes, (filtered, sums, staged) = rest[:8], rest[8:]
     count = here_ref.shape[0]
     keep = (keep_ref[0], keep_ref[1], keep_ref[2])
     reach = taps_ref.shape[0] - 1
@@ -260,8 +257,8 @@
         sums[1] = second
         sums[2] = third
 
-    for copy in copies:
-        copy.start()
+    for d, lane in enumerate(lanes):
+        lane[...] = staged[d]
     cos = twist_ref[0]
     sin = twist_ref[1]
     power = jnp.zeros((8, LANES), F32)
@@ -281,8 +278,6 @@
     totals = pack([sums[0], sums[1], sums[2], power])
     for group in range(ROWS // 8):
         out_ref[group, count] = totals
-    for copy in copies:
-        copy.wait()
 
 
 def tail_kernel(moved_ref, frames_ref, sums_ref):
@@ -291,7 +286,7 @@
     total = moved_ref[0, count]
     for part in range(1, moved_ref.shape[0]):
         total = total + moved_ref[part, count]
-    sums_ref[...] = jnp.broadcast_to((total[:4] + total[4:])[None], sums_ref.shape)
+    sums_ref[...] = jnp.broadcast_to(total[None], sums_ref.shape)
 
 
 def last_kernel(place_ref, keep_ref, moved_ref, after_ref, sums_ref, taps_ref, *rest):
@@ -303,7 +298,7 @@
         pairs[place_ref[0] ^ d] = lane[...]
     sums = jnp.sum(sums_ref[...], 0)
     norm, curve, square, power = (
-        jnp.sum(jnp.sum(jnp.where(quarters(4) == at, sums, 0.0), 1, keepdims=True), 0, keepdims=True)
+        jnp.sum(jnp.sum(jnp.where(quarters(8) == at, sums, 0.0), 1, keepdims=True), 0, keepdims=True)
         for at in range(4)
     )
     cube = power + RIDGE * square
@@ -422,7 +417,6 @@
             pltpu.VMEM((count, ROWS, LANES), F32),
             pltpu.VMEM((3, 8, LANES), F32),
             pltpu.VMEM((parts, 2 * count, 8, LANES), F32),
-            pltpu.SemaphoreType.DMA((8,)),
         ],
         compiler_params=params(),
         name="second",
@@ -435,7 +429,7 @@
     ]
     after, sums = pl.pallas_call(
         tail_kernel,
-        out_shape=(shape(count, 8, LANES), shape(groups, 4, LANES)),
+        out_shape=(shape(count, 8, LANES), shape(groups, 8, LANES)),
         in_specs=vmem(1),
         out_specs=tuple(vmem(2)),
         compiler_params=params(),

time: 94.4 us -> 91.9 us (0.974)
  the two profiles are of different devices: /device:TPU:1 before, /device:TPU:33 now
where the time goes in v10:
time: 91.9 us; the launch traced here: 91.6 us
  starting transfers between devices  42.8 us (47%)
  blocking collectives  19.5 us (21%)
  Pallas kernels  14.5 us (16%)
  waiting for transfers between devices  13.9 us (15%)
    all_to_all x1, blocking collectives, exchange(): return lax.all_to_all(value, axis, split_axis=0, concat_axis=0, tiled=True)  19.5 us
    all_to_all x1, starting transfers between devices, exchange(): return lax.all_to_all(value, axis, split_axis=0, concat_axis=0, tiled=True)  11.5 us
    ppermute x2, starting transfers between devices, neighbours(): lax.ppermute(block, AXES, inside)  10.6 us
    ppermute x7, waiting for transfers between devices, local(): lax.ppermute(lanes[d], AXES, [(i, i ^ d) for i in range(devices)])  9.77 us
    ppermute x7, starting transfers between devices, local(): lax.ppermute(lanes[d], AXES, [(i, i ^ d) for i in range(devices)])  9.35 us
    ppermute x2, starting transfers between devices, neighbours(): lax.ppermute(block, AXES, across)  7.02 us
    ppermute x1, starting transfers between devices, local(): after = lax.ppermute(after, 'tm', [(i + 1, i) for i in range(groups - 1)])  4.3 us
    pallas_call x1, Pallas kernels, local(): pl.pallas_call(second_kernel, out_shape=(shape(parts, count + 1, 8, LANES...  4.01 us
  transfers between devices with their start and end apart: 13, of which 6 were waited for; matrix products, arithmetic and copies ran while one was open for 0% of the time, Pallas kernels for 2%

profile of v10, /device:TPU:33, one launch (start us, length us, event | category | flops | bytes accessed | tf_op | source)
XLA Modules:
  0.0 91.6 jit_solution(7165151320440792190)
XLA Ops:
  0.6 0.0 copy-start.1
  0.6 0.0 copy-start.4
  0.7 2.8 %seed.1.here_ref = f32[16,64,128]{2,1,0:T(8,128)S(1)} custom-call(f32[16,4096]{1,0:T(8,128)} %refs_0_.1, f32[16,4096]{1,0:T(8,128)} %refs_1_.1, f32[16,4096]{1,0:T(8,128)} %weights_ref.1, bf16[384,256]{1,0:T(8,128)(2,1)} %constant.40.clone.refs_3_.back_lanes_ref, bf16[128,256]{1,0:T(8,128)(2,1)} %constant.41.clone.refs_4_.back_rows_ref, ...), custom_call_target="tpu_custom_call" | custom-call | tf_op jit(solution)/shard_map/seed/pallas_call | solution.py:377
  3.5 3.7 %collective-permute-start.1 = (f32[16,64,128]{2,1,0:T(8,128)S(1)}, f32[16,64,128]{2,1,0:T(8,128)S(1)}, u32[]{:S(2)}, u32[]{:S(2)}) collective-permute-start(f32[16,64,128]{2,1,0:T(8,128)S(1)} %seed.1.here_ref), channel_id=1, source_target_pairs={{0,0},{1,2},{2,1},{3,4},{4,3},{5,6},{6,5},{7,8},{8,7},{9,10},{10,9... | collective-permute-start | bytes 1572872 | tf_op jit(solution)/shard_map/ppermute | solution.py:370
  7.1 3.2 %collective-permute-start = (f32[16,64,128]{2,1,0:T(8,128)S(1)}, f32[16,64,128]{2,1,0:T(8,128)S(1)}, u32[]{:S(2)}, u32[]{:S(2)}) collective-permute-start(f32[16,64,128]{2,1,0:T(8,128)S(1)} %seed.1.here_ref), channel_id=1, source_target_pairs={{0,1},{1,0},{2,3},{3,2},{4,5},{5,4},{6,7},{7,6},{8,9},{9,8},{10,11... | collective-permute-start | bytes 1572872 | tf_op jit(solution)/shard_map/ppermute | solution.py:370
  10.3 0.0 copy-done.1
  10.3 0.0 copy-done.4
  10.3 0.0 copy-start
  10.3 0.0 copy-start.2
  10.4 0.0 copy-start.3
  10.4 0.0 copy-start.5
  10.4 0.0 copy-start.6
  10.4 1.2 %arrange.1 = (f32[16,64,128]{2,1,0:T(8,128)S(1)}, f32[1024,128]{1,0:T(8,128)S(1)}) custom-call(f32[16,4096]{1,0:T(8,128)S(1)} %copy-done.1, f32[16,8192]{1,0:T(8,128)S(1)} %copy-done.4), custom_call_target="tpu_custom_call" | custom-call | flops 10000000 | bytes 2000000 | tf_op jit(solution)/shard_map/arrange/pallas_call | solution.py:388
  11.6 0.1 add_convert_fusion.keep_ref
  11.7 2.6 %collective-permute-done.1.across_ref = f32[16,64,128]{2,1,0:T(8,128)S(1)} collective-permute-done((f32[16,64,128]{2,1,0:T(8,128)S(1)}, f32[16,64,128]{2,1,0:T(8,128)S(1)}, u32[]{:S(2)}, u32[]{:S(2)}) %collective-permute-start.1) | collective-permute-done | bytes 524320 | tf_op jit(solution)/shard_map/ppermute | solution.py:370
  14.3 0.0 collective-permute-done.inside_ref
  14.3 0.0 copy-done
  14.3 0.0 copy-done.2
  14.3 0.0 copy-done.3
  14.3 0.0 copy-done.5
  14.3 0.0 copy-done.6
  14.3 3.7 %first.1 = (f32[16,64,128]{2,1,0:T(8,128)S(1)}, f32[31,64,128]{2,1,0:T(8,128)S(1)}) custom-call(f32[3]{0:T(128)S(1)} %add_convert_fusion.keep_ref, f32[16,64,128]{2,1,0:T(8,128)S(1)} %collective-permute-done.inside_ref, f32[16,64,128]{2,1,0:T(8,128)S(1)} %seed.1.here_ref, f32[16,64,128]{2,1,0:T(8,128)S(1)} %collective-permute-done.1.across_ref, ...), custom_call_target="tpu_custom_call" | custom-call | tf_op jit(solution)/shard_map/first/pallas_call | solution.py:400
  18.1 3.3 %collective-permute-start.3 = (f32[16,64,128]{2,1,0:T(8,128)S(1)}, f32[16,64,128]{2,1,0:T(8,128)S(1)}, u32[]{:S(2)}, u32[]{:S(2)}) collective-permute-start(f32[16,64,128]{2,1,0:T(8,128)S(1)} %get-tuple-element.28.here_ref), channel_id=1, source_target_pairs={{0,0},{1,2},{2,1},{3,4},{4,3},{5,6},{6,5},{7,8},{8,7},{9,10},{10,9... | collective-permute-start | bytes 1572872 | tf_op jit(solution)/shard_map/ppermute | solution.py:370
  21.4 7.4 %collective-permute-start.2 = (f32[16,64,128]{2,1,0:T(8,128)S(1)}, f32[16,64,128]{2,1,0:T(8,128)S(1)}, u32[]{:S(2)}, u32[]{:S(2)}) collective-permute-start(f32[16,64,128]{2,1,0:T(8,128)S(1)} %get-tuple-element.28.here_ref), channel_id=1, source_target_pairs={{0,1},{1,0},{2,3},{3,2},{4,5},{5,4},{6,7},{7,6},{8,9},{9,8},{10,11... | collective-permute-start | bytes 1572872 | tf_op jit(solution)/shard_map/ppermute | solution.py:370
  28.8 0.0 collective-permute-done.3.across_ref
  28.8 1.5 %collective-permute-done.2.inside_ref = f32[16,64,128]{2,1,0:T(8,128)S(1)} collective-permute-done((f32[16,64,128]{2,1,0:T(8,128)S(1)}, f32[16,64,128]{2,1,0:T(8,128)S(1)}, u32[]{:S(2)}, u32[]{:S(2)}) %collective-permute-start.2) | collective-permute-done | bytes 524320 | tf_op jit(solution)/shard_map/ppermute | solution.py:370
  30.4 4.0 %second.1 = (f32[8,17,8,128]{3,2,1,0:T(8,128)S(1)}, f32[32,8,128]{2,1,0:T(8,128)S(1)}, f32[32,8,128]{2,1,0:T(8,128)S(1)}, f32[32,8,128]{2,1,0:T(8,128)S(1)}, f32...) custom-call(s32[1]{0:T(128)} %bitcast.place_ref, ...), custom_call_target="tpu_custom_call" | custom-call | tf_op jit(solution)/shard_map/second/pallas_call | solution.py:411
  34.4 19.5 %all_to_all.10.moved_ref = f32[8,17,8,128]{3,2,1,0:T(8,128)S(1)} all-to-all(f32[8,17,8,128]{3,2,1,0:T(8,128)S(1)} %get-tuple-element.30), channel_id=1, replica_groups=mesh['tm'=32,'chan'=8] {'chan'}, dimensions={0} | all-to-all | bytes 1114112 | tf_op jit(solution)/shard_map/all_to_all | solution.py:373
  53.9 0.6 collective-permute-start.5
  54.5 0.3 collective-permute-start.6
  54.8 0.7 tail.1
  55.5 11.5 %all-to-all-start.1 = ((f32[32,8,128]{2,1,0:T(8,128)}), f32[32,8,128]{2,1,0:T(8,128)S(1)}, u32[]{:S(2)}, u32[]{:S(2)}) async-start(f32[32,8,128]{2,1,0:T(8,128)} %get-tuple-element.41), calls=%async_computation.1 | async-start | bytes 262144 | tf_op jit(solution)/shard_map/all_to_all | solution.py:373
  67.0 4.3 %collective-permute-start.4 = (f32[16,8,128]{2,1,0:T(8,128)S(1)}, f32[16,8,128]{2,1,0:T(8,128)S(1)}, u32[]{:S(2)}, u32[]{:S(2)}) collective-permute-start(f32[16,8,128]{2,1,0:T(8,128)S(1)} %get-tuple-element.40), channel_id=1, source_target_pairs={{8,0},{16,8},{24,16},{32,24},{40,32},{48,40},{56,48},{64,56},{72,6... | collective-permute-start | bytes 196616 | tf_op jit(solution)/shard_map/ppermute | solution.py:438
  71.3 2.3 %collective-permute-start.7 = (f32[32,8,128]{2,1,0:T(8,128)S(1)}, f32[32,8,128]{2,1,0:T(8,128)S(1)}, u32[]{:S(2)}, u32[]{:S(2)}) collective-permute-start(f32[32,8,128]{2,1,0:T(8,128)S(1)} %get-tuple-element.45), channel_id=1, source_target_pairs={{0,3},{1,2},{2,1},{3,0},{4,7},{5,6},{6,5},{7,4},{8,11},{9,10},{10,... | collective-permute-start | bytes 393224 | tf_op jit(solution)/shard_map/ppermute | solution.py:428
  73.6 0.8 collective-permute-start.8
  74.4 0.0 collective-permute-done.4.after_ref
  74.4 1.7 %collective-permute-start.9 = (f32[32,8,128]{2,1,0:T(8,128)S(1)}, f32[32,8,128]{2,1,0:T(8,128)S(1)}, u32[]{:S(2)}, u32[]{:S(2)}) collective-permute-start(f32[32,8,128]{2,1,0:T(8,128)S(1)} %get-tuple-element.47), channel_id=1, source_target_pairs={{0,5},{1,4},{2,7},{3,6},{4,1},{5,0},{6,3},{7,2},{8,13},{9,12},{10,... | collective-permute-start | bytes 393224 | tf_op jit(solution)/shard_map/ppermute | solution.py:428
  76.1 0.0 collective-permute-done.5.rest_1_
  76.1 1.7 %collective-permute-start.10 = (f32[32,8,128]{2,1,0:T(8,128)S(1)}, f32[32,8,128]{2,1,0:T(8,128)S(1)}, u32[]{:S(2)}, u32[]{:S(2)}) collective-permute-start(f32[32,8,128]{2,1,0:T(8,128)S(1)} %get-tuple-element.48), channel_id=1, source_target_pairs={{0,6},{1,7},{2,4},{3,5},{4,2},{5,3},{6,0},{7,1},{8,14},{9,15},{10,... | collective-permute-start | bytes 393224 | tf_op jit(solution)/shard_map/ppermute | solution.py:428
  77.8 0.0 collective-permute-done.6.rest_2_
  77.8 2.0 %collective-permute-start.11 = (f32[32,8,128]{2,1,0:T(8,128)S(1)}, f32[32,8,128]{2,1,0:T(8,128)S(1)}, u32[]{:S(2)}, u32[]{:S(2)}) collective-permute-start(f32[32,8,128]{2,1,0:T(8,128)S(1)} %get-tuple-element.49), channel_id=1, source_target_pairs={{0,7},{1,6},{2,5},{3,4},{4,3},{5,2},{6,1},{7,0},{8,15},{9,14},{10,... | collective-permute-start | bytes 393224 | tf_op jit(solution)/shard_map/ppermute | solution.py:428
  79.8 0.0 collective-permute-done.7.rest_3_
  79.8 1.3 %collective-permute-done.8.rest_4_ = f32[32,8,128]{2,1,0:T(8,128)S(1)} collective-permute-done((f32[32,8,128]{2,1,0:T(8,128)S(1)}, f32[32,8,128]{2,1,0:T(8,128)S(1)}, u32[]{:S(2)}, u32[]{:S(2)}) %collective-permute-start.8) | collective-permute-done | bytes 131104 | tf_op jit(solution)/shard_map/ppermute | solution.py:428
  81.1 2.9 %collective-permute-done.9.rest_5_ = f32[32,8,128]{2,1,0:T(8,128)S(1)} collective-permute-done((f32[32,8,128]{2,1,0:T(8,128)S(1)}, f32[32,8,128]{2,1,0:T(8,128)S(1)}, u32[]{:S(2)}, u32[]{:S(2)}) %collective-permute-start.9) | collective-permute-done | bytes 131104 | tf_op jit(solution)/shard_map/ppermute | solution.py:428
  84.0 2.8 %collective-permute-done.10.rest_6_ = f32[32,8,128]{2,1,0:T(8,128)S(1)} collective-permute-done((f32[32,8,128]{2,1,0:T(8,128)S(1)}, f32[32,8,128]{2,1,0:T(8,128)S(1)}, u32[]{:S(2)}, u32[]{:S(2)}) %collective-permute-start.10) | collective-permute-done | bytes 131104 | tf_op jit(solution)/shard_map/ppermute | solution.py:428
  86.7 2.8 %collective-permute-done.11.rest_7_ = f32[32,8,128]{2,1,0:T(8,128)S(1)} collective-permute-done((f32[32,8,128]{2,1,0:T(8,128)S(1)}, f32[32,8,128]{2,1,0:T(8,128)S(1)}, u32[]{:S(2)}, u32[]{:S(2)}) %collective-permute-start.11) | collective-permute-done | bytes 131104 | tf_op jit(solution)/shard_map/ppermute | solution.py:428
  89.5 0.0 all-to-all-done.1.sums_ref
  89.6 2.0 %last.1 = (f32[128,1024]{1,0:T(8,128)}, f32[128,1024]{1,0:T(8,128)}) custom-call(s32[1]{0:T(128)} %bitcast.place_ref, f32[1]{0:T(128)} %bitcast.1.keep_ref, f32[8,17,8,128]{3,2,1,0:T(8,128)S(1)} %all_to_all.10.moved_ref, f32[16,8,128]{2,1,0:T(8,128)S(1)} %collective-permute-done.4.after_ref, f32[32,8,128]{2,1,0:T(8,128)S(1)} %all-to-all-done.1.sums_ref, ...), custom_call_target="tpu_custom_call" | custom-call | tf_op jit(solution)/shard_map/last/pallas_call | solution.py:440
Async XLA Ops:
  0.6 9.7 %copy-start.1 = (f32[16,4096]{1,0:T(8,128)S(1)}, f32[16,4096]{1,0:T(8,128)}, u32[]{:S(2)}) copy-start(f32[16,4096]{1,0:T(8,128)} %weights_ref.1) | copy-start | bytes 786436
  0.6 9.7 %copy-start.4 = (f32[16,8192]{1,0:T(8,128)S(1)}, f32[16,8192]{1,0:T(8,128)}, u32[]{:S(2)}) copy-start(f32[16,8192]{1,0:T(8,128)} %taps_ref.1) | copy-start | bytes 1572868
  3.5 10.8 %collective-permute-start.1 = (f32[16,64,128]{2,1,0:T(8,128)S(1)}, f32[16,64,128]{2,1,0:T(8,128)S(1)}, u32[]{:S(2)}, u32[]{:S(2)}) collective-permute-start(f32[16,64,128]{2,1,0:T(8,128)S(1)} %seed.1.here_ref), channel_id=1, source_target_pairs={{0,0},{1,2},{2,1},{3,4},{4,3},{5,6},{6,5},{7,8},{8,7},{9,10},{10,9... | collective-permute-start | bytes 1572872 | tf_op jit(solution)/shard_map/ppermute | solution.py:370
  7.1 7.1 %collective-permute-start = (f32[16,64,128]{2,1,0:T(8,128)S(1)}, f32[16,64,128]{2,1,0:T(8,128)S(1)}, u32[]{:S(2)}, u32[]{:S(2)}) collective-permute-start(f32[16,64,128]{2,1,0:T(8,128)S(1)} %seed.1.here_ref), channel_id=1, source_target_pairs={{0,1},{1,0},{2,3},{3,2},{4,5},{5,4},{6,7},{7,6},{8,9},{9,8},{10,11... | collective-permute-start | bytes 1572872 | tf_op jit(solution)/shard_map/ppermute | solution.py:370
  10.3 4.0 %copy-start = (bf16[384,256]{1,0:T(8,128)(2,1)S(1)}, bf16[384,256]{1,0:T(8,128)(2,1)}, u32[]{:S(2)}) copy-start(bf16[384,256]{1,0:T(8,128)(2,1)} %constant.40.clone.refs_3_.back_lanes_ref) | copy-start | bytes 589828
  10.3 4.0 %copy-start.2 = (f32[2,64,128]{2,1,0:T(8,128)S(1)}, f32[2,64,128]{2,1,0:T(8,128)}, u32[]{:S(2)}) copy-start(f32[2,64,128]{2,1,0:T(8,128)} %constant.42.clone.refs_5_.twist_ref) | copy-start | bytes 196612
  10.4 4.0 %copy-start.3 = (bf16[128,256]{1,0:T(8,128)(2,1)S(1)}, bf16[128,256]{1,0:T(8,128)(2,1)}, u32[]{:S(2)}) copy-start(bf16[128,256]{1,0:T(8,128)(2,1)} %constant.41.clone.refs_4_.back_rows_ref) | copy-start | bytes 196612
  10.4 4.0 %copy-start.5 = (bf16[256,256]{1,0:T(8,128)(2,1)S(1)}, bf16[256,256]{1,0:T(8,128)(2,1)}, u32[]{:S(2)}) copy-start(bf16[256,256]{1,0:T(8,128)(2,1)} %constant.44.clone.ahead_lanes_ref) | copy-start | bytes 393220
  10.4 3.9 %copy-start.6 = (bf16[128,192]{1,0:T(8,128)(2,1)S(1)}, bf16[128,192]{1,0:T(8,128)(2,1)}, u32[]{:S(2)}) copy-start(bf16[128,192]{1,0:T(8,128)(2,1)} %constant.43.clone.ahead_rows_ref) | copy-start | bytes 147460
  18.1 10.8 %collective-permute-start.3 = (f32[16,64,128]{2,1,0:T(8,128)S(1)}, f32[16,64,128]{2,1,0:T(8,128)S(1)}, u32[]{:S(2)}, u32[]{:S(2)}) collective-permute-start(f32[16,64,128]{2,1,0:T(8,128)S(1)} %get-tuple-element.28.here_ref), channel_id=1, source_target_pairs={{0,0},{1,2},{2,1},{3,4},{4,3},{5,6},{6,5},{7,8},{8,7},{9,10},{10,9... | collective-permute-start | bytes 1572872 | tf_op jit(solution)/shard_map/ppermute | solution.py:370
  21.4 8.9 %collective-permute-start.2 = (f32[16,64,128]{2,1,0:T(8,128)S(1)}, f32[16,64,128]{2,1,0:T(8,128)S(1)}, u32[]{:S(2)}, u32[]{:S(2)}) collective-permute-start(f32[16,64,128]{2,1,0:T(8,128)S(1)} %get-tuple-element.28.here_ref), channel_id=1, source_target_pairs={{0,1},{1,0},{2,3},{3,2},{4,5},{5,4},{6,7},{7,6},{8,9},{9,8},{10,11... | collective-permute-start | bytes 1572872 | tf_op jit(solution)/shard_map/ppermute | solution.py:370
  53.9 22.2 %collective-permute-start.5 = (f32[32,8,128]{2,1,0:T(8,128)S(1)}, f32[32,8,128]{2,1,0:T(8,128)S(1)}, u32[]{:S(2)}, u32[]{:S(2)}) collective-permute-start(f32[32,8,128]{2,1,0:T(8,128)S(1)} %get-tuple-element.43), channel_id=1, source_target_pairs={{0,1},{1,0},{2,3},{3,2},{4,5},{5,4},{6,7},{7,6},{8,9},{9,8},{10,11... | collective-permute-start | bytes 393224 | tf_op jit(solution)/shard_map/ppermute | solution.py:428
  54.5 23.3 %collective-permute-start.6 = (f32[32,8,128]{2,1,0:T(8,128)S(1)}, f32[32,8,128]{2,1,0:T(8,128)S(1)}, u32[]{:S(2)}, u32[]{:S(2)}) collective-permute-start(f32[32,8,128]{2,1,0:T(8,128)S(1)} %get-tuple-element.44), channel_id=1, source_target_pairs={{0,2},{1,3},{2,0},{3,1},{4,6},{5,7},{6,4},{7,5},{8,10},{9,11},{10,... | collective-permute-start | bytes 393224 | tf_op jit(solution)/shard_map/ppermute | solution.py:428
  55.5 34.1 %all-to-all-start.1 = ((f32[32,8,128]{2,1,0:T(8,128)}), f32[32,8,128]{2,1,0:T(8,128)S(1)}, u32[]{:S(2)}, u32[]{:S(2)}) async-start(f32[32,8,128]{2,1,0:T(8,128)} %get-tuple-element.41), calls=%async_computation.1 | async-start | bytes 262144 | tf_op jit(solution)/shard_map/all_to_all | solution.py:373
  67.0 7.4 %collective-permute-start.4 = (f32[16,8,128]{2,1,0:T(8,128)S(1)}, f32[16,8,128]{2,1,0:T(8,128)S(1)}, u32[]{:S(2)}, u32[]{:S(2)}) collective-permute-start(f32[16,8,128]{2,1,0:T(8,128)S(1)} %get-tuple-element.40), channel_id=1, source_target_pairs={{8,0},{16,8},{24,16},{32,24},{40,32},{48,40},{56,48},{64,56},{72,6... | collective-permute-start | bytes 196616 | tf_op jit(solution)/shard_map/ppermute | solution.py:438
  71.3 8.5 %collective-permute-start.7 = (f32[32,8,128]{2,1,0:T(8,128)S(1)}, f32[32,8,128]{2,1,0:T(8,128)S(1)}, u32[]{:S(2)}, u32[]{:S(2)}) collective-permute-start(f32[32,8,128]{2,1,0:T(8,128)S(1)} %get-tuple-element.45), channel_id=1, source_target_pairs={{0,3},{1,2},{2,1},{3,0},{4,7},{5,6},{6,5},{7,4},{8,11},{9,10},{10,... | collective-permute-start | bytes 393224 | tf_op jit(solution)/shard_map/ppermute | solution.py:428
  73.6 7.6 %collective-permute-start.8 = (f32[32,8,128]{2,1,0:T(8,128)S(1)}, f32[32,8,128]{2,1,0:T(8,128)S(1)}, u32[]{:S(2)}, u32[]{:S(2)}) collective-permute-start(f32[32,8,128]{2,1,0:T(8,128)S(1)} %get-tuple-element.46), channel_id=1, source_target_pairs={{0,4},{1,5},{2,6},{3,7},{4,0},{5,1},{6,2},{7,3},{8,12},{9,13},{10,... | collective-permute-start | bytes 393224 | tf_op jit(solution)/shard_map/ppermute | solution.py:428
  74.4 9.6 %collective-permute-start.9 = (f32[32,8,128]{2,1,0:T(8,128)S(1)}, f32[32,8,128]{2,1,0:T(8,128)S(1)}, u32[]{:S(2)}, u32[]{:S(2)}) collective-permute-start(f32[32,8,128]{2,1,0:T(8,128)S(1)} %get-tuple-element.47), channel_id=1, source_target_pairs={{0,5},{1,4},{2,7},{3,6},{4,1},{5,0},{6,3},{7,2},{8,13},{9,12},{10,... | collective-permute-start | bytes 393224 | tf_op jit(solution)/shard_map/ppermute | solution.py:428
  76.1 10.7 %collective-permute-start.10 = (f32[32,8,128]{2,1,0:T(8,128)S(1)}, f32[32,8,128]{2,1,0:T(8,128)S(1)}, u32[]{:S(2)}, u32[]{:S(2)}) collective-permute-start(f32[32,8,128]{2,1,0:T(8,128)S(1)} %get-tuple-element.48), channel_id=1, source_target_pairs={{0,6},{1,7},{2,4},{3,5},{4,2},{5,3},{6,0},{7,1},{8,14},{9,15},{10,... | collective-permute-start | bytes 393224 | tf_op jit(solution)/shard_map/ppermute | solution.py:428
  77.8 11.8 %collective-permute-start.11 = (f32[32,8,128]{2,1,0:T(8,128)S(1)}, f32[32,8,128]{2,1,0:T(8,128)S(1)}, u32[]{:S(2)}, u32[]{:S(2)}) collective-permute-start(f32[32,8,128]{2,1,0:T(8,128)S(1)} %get-tuple-element.49), channel_id=1, source_target_pairs={{0,7},{1,6},{2,5},{3,4},{4,3},{5,2},{6,1},{7,0},{8,15},{9,14},{10,... | collective-permute-start | bytes 393224 | tf_op jit(solution)/shard_map/ppermute | solution.py:428

commit v11 on v10

--- a/solution.py
+++ b/solution.py
@@ -280,13 +280,13 @@
         out_ref[group, count] = totals
 
 
-def tail_kernel(moved_ref, frames_ref, sums_ref):
+def tail_kernel(moved_ref, _, __, frames_ref, sums_ref):
     count = frames_ref.shape[0]
     frames_ref[...] = moved_ref[0, :count]
     total = moved_ref[0, count]
     for part in range(1, moved_ref.shape[0]):
         total = total + moved_ref[part, count]
-    sums_ref[...] = jnp.broadcast_to(total[None], sums_ref.shape)
+    sums_ref[...] = jnp.broadcast_to((total[:4] + total[4:])[None], sums_ref.shape)
 
 
 def last_kernel(place_ref, keep_ref, moved_ref, after_ref, sums_ref, taps_ref, *rest):
@@ -298,7 +298,7 @@
         pairs[place_ref[0] ^ d] = lane[...]
     sums = jnp.sum(sums_ref[...], 0)
     norm, curve, square, power = (
-        jnp.sum(jnp.sum(jnp.where(quarters(8) == at, sums, 0.0), 1, keepdims=True), 0, keepdims=True)
+        jnp.sum(jnp.sum(jnp.where(quarters(4) == at, sums, 0.0), 1, keepdims=True), 0, keepdims=True)
         for at in range(4)
     )
     cube = power + RIDGE * square
@@ -348,6 +348,7 @@
 
 
 SMEM = pl.BlockSpec(memory_space=pltpu.SMEM)
+ANY = pl.BlockSpec(memory_space=pl.ANY)
 
 
 def local(observed_real, observed_imag, weights, taps):
@@ -429,12 +430,12 @@
     ]
     after, sums = pl.pallas_call(
         tail_kernel,
-        out_shape=(shape(count, 8, LANES), shape(groups, 8, LANES)),
-        in_specs=vmem(1),
+        out_shape=(shape(count, 8, LANES), shape(groups, 4, LANES)),
+        in_specs=vmem(1) + [ANY, ANY],
         out_specs=tuple(vmem(2)),
         compiler_params=params(),
         name="tail",
-    )(moved)
+    )(moved, lanes[1], lanes[2])
     after = lax.ppermute(after, "tm", [(i + 1, i) for i in range(groups - 1)])
     sums = exchange(sums, "tm")
     return pl.pallas_call(

time: 91.9 us -> 86.9 us (0.946)
  the two profiles are of different devices: /device:TPU:33 before, /device:TPU:1 now
where the time goes in v11:
time: 86.9 us; the launch traced here: 86.6 us
  starting transfers between devices  33.3 us (38%)
  waiting for transfers between devices  19.6 us (23%)
  blocking collectives  18.3 us (21%)
  Pallas kernels  14.4 us (17%)
  between operations  0.88 us (1%)
    all_to_all x1, blocking collectives, exchange(): return lax.all_to_all(value, axis, split_axis=0, concat_axis=0, tiled=True)  18.3 us
    all_to_all x1, starting transfers between devices, exchange(): return lax.all_to_all(value, axis, split_axis=0, concat_axis=0, tiled=True)  15.2 us
    ppermute x2, waiting for transfers between devices, neighbours(): lax.ppermute(block, AXES, across)  12.1 us
    ppermute x7, starting transfers between devices, local(): lax.ppermute(lanes[d], AXES, [(i, i ^ d) for i in range(devices)])  8.41 us
    ppermute x2, starting transfers between devices, neighbours(): lax.ppermute(block, AXES, across)  8.15 us
    ppermute x1, waiting for transfers between devices, local(): after = lax.ppermute(after, 'tm', [(i + 1, i) for i in range(groups - 1)])  4.1 us
    pallas_call x1, Pallas kernels, local(): pl.pallas_call(second_kernel, out_shape=(shape(parts, count + 1, 8, LANES...  4.01 us
    pallas_call x1, Pallas kernels, local(): pl.pallas_call(first_kernel, out_shape=(blocks, shape(reach + count, ROWS...  3.73 us
  transfers between devices with their start and end apart: 13, of which 4 were waited for; matrix products, arithmetic and copies ran while one was open for 0% of the time, Pallas kernels for 2%

profile of v11, /device:TPU:1, one launch (start us, length us, event | category | flops | bytes accessed | tf_op | source)
XLA Modules:
  0.0 86.6 jit_solution(13260142314619830598)
XLA Ops:
  0.6 0.0 copy-start.1
  0.6 0.0 copy-start.4
  0.7 2.8 %seed.1.here_ref = f32[16,64,128]{2,1,0:T(8,128)S(1)} custom-call(f32[16,4096]{1,0:T(8,128)} %refs_0_.1, f32[16,4096]{1,0:T(8,128)} %refs_1_.1, f32[16,4096]{1,0:T(8,128)} %weights_ref.1, bf16[384,256]{1,0:T(8,128)(2,1)} %constant.40.clone.refs_3_.back_lanes_ref, bf16[128,256]{1,0:T(8,128)(2,1)} %constant.41.clone.refs_4_.back_rows_ref, ...), custom_call_target="tpu_custom_call" | custom-call | tf_op jit(solution)/shard_map/seed/pallas_call | solution.py:378
  3.5 4.5 %collective-permute-start.1 = (f32[16,64,128]{2,1,0:T(8,128)S(1)}, f32[16,64,128]{2,1,0:T(8,128)S(1)}, u32[]{:S(2)}, u32[]{:S(2)}) collective-permute-start(f32[16,64,128]{2,1,0:T(8,128)S(1)} %seed.1.here_ref), channel_id=1, source_target_pairs={{0,0},{1,2},{2,1},{3,4},{4,3},{5,6},{6,5},{7,8},{8,7},{9,10},{10,9... | collective-permute-start | bytes 1572872 | tf_op jit(solution)/shard_map/ppermute | solution.py:371
  8.0 0.1 collective-permute-start
  8.1 0.0 copy-done.1
  8.1 0.0 copy-done.4
  8.1 0.0 copy-start
  8.1 0.0 copy-start.2
  8.1 0.0 copy-start.3
  8.2 0.0 copy-start.5
  8.2 0.0 copy-start.6
  8.2 1.2 %arrange.1 = (f32[16,64,128]{2,1,0:T(8,128)S(1)}, f32[1024,128]{1,0:T(8,128)S(1)}) custom-call(f32[16,4096]{1,0:T(8,128)S(1)} %copy-done.1, f32[16,8192]{1,0:T(8,128)S(1)} %copy-done.4), custom_call_target="tpu_custom_call" | custom-call | flops 10000000 | bytes 2000000 | tf_op jit(solution)/shard_map/arrange/pallas_call | solution.py:389
  9.4 0.1 add_convert_fusion.keep_ref
  9.5 5.4 %collective-permute-done.1.across_ref = f32[16,64,128]{2,1,0:T(8,128)S(1)} collective-permute-done((f32[16,64,128]{2,1,0:T(8,128)S(1)}, f32[16,64,128]{2,1,0:T(8,128)S(1)}, u32[]{:S(2)}, u32[]{:S(2)}) %collective-permute-start.1) | collective-permute-done | bytes 524320 | tf_op jit(solution)/shard_map/ppermute | solution.py:371
  14.8 0.0 collective-permute-done.inside_ref
  14.8 0.0 copy-done
  14.8 0.0 copy-done.2
  14.8 0.0 copy-done.3
  14.9 0.0 copy-done.5
  14.9 0.0 copy-done.6
  14.9 3.7 %first.1 = (f32[16,64,128]{2,1,0:T(8,128)S(1)}, f32[31,64,128]{2,1,0:T(8,128)S(1)}) custom-call(f32[3]{0:T(128)S(1)} %add_convert_fusion.keep_ref, f32[16,64,128]{2,1,0:T(8,128)S(1)} %collective-permute-done.inside_ref, f32[16,64,128]{2,1,0:T(8,128)S(1)} %seed.1.here_ref, f32[16,64,128]{2,1,0:T(8,128)S(1)} %collective-permute-done.1.across_ref, ...), custom_call_target="tpu_custom_call" | custom-call | tf_op jit(solution)/shard_map/first/pallas_call | solution.py:401
  18.6 3.6 %collective-permute-start.3 = (f32[16,64,128]{2,1,0:T(8,128)S(1)}, f32[16,64,128]{2,1,0:T(8,128)S(1)}, u32[]{:S(2)}, u32[]{:S(2)}) collective-permute-start(f32[16,64,128]{2,1,0:T(8,128)S(1)} %get-tuple-element.28.here_ref), channel_id=1, source_target_pairs={{0,0},{1,2},{2,1},{3,4},{4,3},{5,6},{6,5},{7,8},{8,7},{9,10},{10,9... | collective-permute-start | bytes 1572872 | tf_op jit(solution)/shard_map/ppermute | solution.py:371
  22.3 0.1 collective-permute-start.2
  22.4 6.8 %collective-permute-done.3.across_ref = f32[16,64,128]{2,1,0:T(8,128)S(1)} collective-permute-done((f32[16,64,128]{2,1,0:T(8,128)S(1)}, f32[16,64,128]{2,1,0:T(8,128)S(1)}, u32[]{:S(2)}, u32[]{:S(2)}) %collective-permute-start.3) | collective-permute-done | bytes 524320 | tf_op jit(solution)/shard_map/ppermute | solution.py:371
  29.1 0.0 collective-permute-done.2.inside_ref
  29.1 4.0 %second.1 = (f32[8,17,8,128]{3,2,1,0:T(8,128)S(1)}, f32[32,8,128]{2,1,0:T(8,128)S(1)}, f32[32,8,128]{2,1,0:T(8,128)S(1)}, f32[32,8,128]{2,1,0:T(8,128)S(1)}, f32...) custom-call(s32[1]{0:T(128)} %bitcast.place_ref, ...), custom_call_target="tpu_custom_call" | custom-call | tf_op jit(solution)/shard_map/second/pallas_call | solution.py:412
  33.1 18.3 %all_to_all.10.moved_ref = f32[8,17,8,128]{3,2,1,0:T(8,128)S(1)} all-to-all(f32[8,17,8,128]{3,2,1,0:T(8,128)S(1)} %get-tuple-element.30), channel_id=1, replica_groups=mesh['tm'=32,'chan'=8] {'chan'}, dimensions={0} | all-to-all | bytes 1114112 | tf_op jit(solution)/shard_map/all_to_all | solution.py:374
  51.4 0.6 collective-permute-start.4
  52.0 0.3 collective-permute-start.5
  52.3 1.4 %collective-permute-start.7 = (f32[32,8,128]{2,1,0:T(8,128)S(1)}, f32[32,8,128]{2,1,0:T(8,128)S(1)}, u32[]{:S(2)}, u32[]{:S(2)}) collective-permute-start(f32[32,8,128]{2,1,0:T(8,128)S(1)} %get-tuple-element.45), channel_id=1, source_target_pairs={{0,3},{1,2},{2,1},{3,0},{4,7},{5,6},{6,5},{7,4},{8,11},{9,10},{10,... | collective-permute-start | bytes 393224 | tf_op jit(solution)/shard_map/ppermute | solution.py:429
  53.6 0.8 collective-permute-start.8
  54.4 2.6 %collective-permute-start.9 = (f32[32,8,128]{2,1,0:T(8,128)S(1)}, f32[32,8,128]{2,1,0:T(8,128)S(1)}, u32[]{:S(2)}, u32[]{:S(2)}) collective-permute-start(f32[32,8,128]{2,1,0:T(8,128)S(1)} %get-tuple-element.47), channel_id=1, source_target_pairs={{0,5},{1,4},{2,7},{3,6},{4,1},{5,0},{6,3},{7,2},{8,13},{9,12},{10,... | collective-permute-start | bytes 393224 | tf_op jit(solution)/shard_map/ppermute | solution.py:429
  57.0 0.0 collective-permute-done.4._.rest_1_
  57.0 0.9 %collective-permute-start.10 = (f32[32,8,128]{2,1,0:T(8,128)S(1)}, f32[32,8,128]{2,1,0:T(8,128)S(1)}, u32[]{:S(2)}, u32[]{:S(2)}) collective-permute-start(f32[32,8,128]{2,1,0:T(8,128)S(1)} %get-tuple-element.48), channel_id=1, source_target_pairs={{0,6},{1,7},{2,4},{3,5},{4,2},{5,3},{6,0},{7,1},{8,14},{9,15},{10,... | collective-permute-start | bytes 393224 | tf_op jit(solution)/shard_map/ppermute | solution.py:429
  57.9 0.0 collective-permute-done.5.__.rest_2_
  57.9 2.0 %collective-permute-start.11 = (f32[32,8,128]{2,1,0:T(8,128)S(1)}, f32[32,8,128]{2,1,0:T(8,128)S(1)}, u32[]{:S(2)}, u32[]{:S(2)}) collective-permute-start(f32[32,8,128]{2,1,0:T(8,128)S(1)} %get-tuple-element.49), channel_id=1, source_target_pairs={{0,7},{1,6},{2,5},{3,4},{4,3},{5,2},{6,1},{7,0},{8,15},{9,14},{10,... | collective-permute-start | bytes 393224 | tf_op jit(solution)/shard_map/ppermute | solution.py:429
  59.9 0.6 tail.1
  60.5 15.2 %all-to-all-start.1 = ((f32[32,4,128]{2,1,0:T(4,128)}), f32[32,4,128]{2,1,0:T(4,128)S(1)}, u32[]{:S(2)}, u32[]{:S(2)}) async-start(f32[32,4,128]{2,1,0:T(4,128)} %get-tuple-element.43), calls=%async_computation.1 | async-start | bytes 131072 | tf_op jit(solution)/shard_map/all_to_all | solution.py:374
  75.8 0.0 collective-permute-done.7.rest_3_
  75.8 1.3 %collective-permute-start.6 = (f32[16,8,128]{2,1,0:T(8,128)S(1)}, f32[16,8,128]{2,1,0:T(8,128)S(1)}, u32[]{:S(2)}, u32[]{:S(2)}) collective-permute-start(f32[16,8,128]{2,1,0:T(8,128)S(1)} %get-tuple-element.42), channel_id=1, source_target_pairs={{8,0},{16,8},{24,16},{32,24},{40,32},{48,40},{56,48},{64,56},{72,6... | collective-permute-start | bytes 196616 | tf_op jit(solution)/shard_map/ppermute | solution.py:439
  77.1 0.0 collective-permute-done.8.rest_4_
  77.1 0.0 collective-permute-done.9.rest_5_
  77.1 0.0 collective-permute-done.10.rest_6_
  77.1 0.0 collective-permute-done.11.rest_7_
  77.1 4.1 %collective-permute-done.6.after_ref = f32[16,8,128]{2,1,0:T(8,128)S(1)} collective-permute-done((f32[16,8,128]{2,1,0:T(8,128)S(1)}, f32[16,8,128]{2,1,0:T(8,128)S(1)}, u32[]{:S(2)}, u32[]{:S(2)}) %collective-permute-start.6) | collective-permute-done | bytes 65568 | tf_op jit(solution)/shard_map/ppermute | solution.py:439
  81.2 3.4 %all-to-all-done.1.sums_ref = f32[32,4,128]{2,1,0:T(4,128)S(1)} async-done(((f32[32,4,128]{2,1,0:T(4,128)}), f32[32,4,128]{2,1,0:T(4,128)S(1)}, u32[]{:S(2)}, u32[]{:S(2)}) %all-to-all-start.1) | async-done | bytes 65568 | tf_op jit(solution)/shard_map/all_to_all | solution.py:374
  84.6 2.1 %last.1 = (f32[128,1024]{1,0:T(8,128)}, f32[128,1024]{1,0:T(8,128)}) custom-call(s32[1]{0:T(128)} %bitcast.place_ref, f32[1]{0:T(128)} %bitcast.1.keep_ref, f32[8,17,8,128]{3,2,1,0:T(8,128)S(1)} %all_to_all.10.moved_ref, f32[16,8,128]{2,1,0:T(8,128)S(1)} %collective-permute-done.6.after_ref, f32[32,4,128]{2,1,0:T(4,128)S(1)} %all-to-all-done.1.sums_ref, ...), custom_call_target="tpu_custom_call" | custom-call | tf_op jit(solution)/shard_map/last/pallas_call | solution.py:441
Async XLA Ops:
  0.6 7.5 %copy-start.1 = (f32[16,4096]{1,0:T(8,128)S(1)}, f32[16,4096]{1,0:T(8,128)}, u32[]{:S(2)}) copy-start(f32[16,4096]{1,0:T(8,128)} %weights_ref.1) | copy-start | bytes 786436
  0.6 7.5 %copy-start.4 = (f32[16,8192]{1,0:T(8,128)S(1)}, f32[16,8192]{1,0:T(8,128)}, u32[]{:S(2)}) copy-start(f32[16,8192]{1,0:T(8,128)} %taps_ref.1) | copy-start | bytes 1572868
  3.5 11.4 %collective-permute-start.1 = (f32[16,64,128]{2,1,0:T(8,128)S(1)}, f32[16,64,128]{2,1,0:T(8,128)S(1)}, u32[]{:S(2)}, u32[]{:S(2)}) collective-permute-start(f32[16,64,128]{2,1,0:T(8,128)S(1)} %seed.1.here_ref), channel_id=1, source_target_pairs={{0,0},{1,2},{2,1},{3,4},{4,3},{5,6},{6,5},{7,8},{8,7},{9,10},{10,9... | collective-permute-start | bytes 1572872 | tf_op jit(solution)/shard_map/ppermute | solution.py:371
  8.0 6.9 %collective-permute-start = (f32[16,64,128]{2,1,0:T(8,128)S(1)}, f32[16,64,128]{2,1,0:T(8,128)S(1)}, u32[]{:S(2)}, u32[]{:S(2)}) collective-permute-start(f32[16,64,128]{2,1,0:T(8,128)S(1)} %seed.1.here_ref), channel_id=1, source_target_pairs={{0,1},{1,0},{2,3},{3,2},{4,5},{5,4},{6,7},{7,6},{8,9},{9,8},{10,11... | collective-permute-start | bytes 1572872 | tf_op jit(solution)/shard_map/ppermute | solution.py:371
  8.1 6.7 %copy-start = (bf16[384,256]{1,0:T(8,128)(2,1)S(1)}, bf16[384,256]{1,0:T(8,128)(2,1)}, u32[]{:S(2)}) copy-start(bf16[384,256]{1,0:T(8,128)(2,1)} %constant.40.clone.refs_3_.back_lanes_ref) | copy-start | bytes 589828
  8.1 6.7 %copy-start.2 = (f32[2,64,128]{2,1,0:T(8,128)S(1)}, f32[2,64,128]{2,1,0:T(8,128)}, u32[]{:S(2)}) copy-start(f32[2,64,128]{2,1,0:T(8,128)} %constant.42.clone.refs_5_.twist_ref) | copy-start | bytes 196612
  8.1 6.7 %copy-start.3 = (bf16[128,256]{1,0:T(8,128)(2,1)S(1)}, bf16[128,256]{1,0:T(8,128)(2,1)}, u32[]{:S(2)}) copy-start(bf16[128,256]{1,0:T(8,128)(2,1)} %constant.41.clone.refs_4_.back_rows_ref) | copy-start | bytes 196612
  8.2 6.7 %copy-start.5 = (bf16[256,256]{1,0:T(8,128)(2,1)S(1)}, bf16[256,256]{1,0:T(8,128)(2,1)}, u32[]{:S(2)}) copy-start(bf16[256,256]{1,0:T(8,128)(2,1)} %constant.44.clone.ahead_lanes_ref) | copy-start | bytes 393220
  8.2 6.7 %copy-start.6 = (bf16[128,192]{1,0:T(8,128)(2,1)S(1)}, bf16[128,192]{1,0:T(8,128)(2,1)}, u32[]{:S(2)}) copy-start(bf16[128,192]{1,0:T(8,128)(2,1)} %constant.43.clone.ahead_rows_ref) | copy-start | bytes 147460
  18.6 10.5 %collective-permute-start.3 = (f32[16,64,128]{2,1,0:T(8,128)S(1)}, f32[16,64,128]{2,1,0:T(8,128)S(1)}, u32[]{:S(2)}, u32[]{:S(2)}) collective-permute-start(f32[16,64,128]{2,1,0:T(8,128)S(1)} %get-tuple-element.28.here_ref), channel_id=1, source_target_pairs={{0,0},{1,2},{2,1},{3,4},{4,3},{5,6},{6,5},{7,8},{8,7},{9,10},{10,9... | collective-permute-start | bytes 1572872 | tf_op jit(solution)/shard_map/ppermute | solution.py:371
  22.3 6.9 %collective-permute-start.2 = (f32[16,64,128]{2,1,0:T(8,128)S(1)}, f32[16,64,128]{2,1,0:T(8,128)S(1)}, u32[]{:S(2)}, u32[]{:S(2)}) collective-permute-start(f32[16,64,128]{2,1,0:T(8,128)S(1)} %get-tuple-element.28.here_ref), channel_id=1, source_target_pairs={{0,1},{1,0},{2,3},{3,2},{4,5},{5,4},{6,7},{7,6},{8,9},{9,8},{10,11... | collective-permute-start | bytes 1572872 | tf_op jit(solution)/shard_map/ppermute | solution.py:371
  51.4 5.6 %collective-permute-start.4 = (f32[32,8,128]{2,1,0:T(8,128)S(1)}, f32[32,8,128]{2,1,0:T(8,128)S(1)}, u32[]{:S(2)}, u32[]{:S(2)}) collective-permute-start(f32[32,8,128]{2,1,0:T(8,128)S(1)} %get-tuple-element.40), channel_id=1, source_target_pairs={{0,1},{1,0},{2,3},{3,2},{4,5},{5,4},{6,7},{7,6},{8,9},{9,8},{10,11... | collective-permute-start | bytes 393224 | tf_op jit(solution)/shard_map/ppermute | solution.py:429
  52.0 5.9 %collective-permute-start.5 = (f32[32,8,128]{2,1,0:T(8,128)S(1)}, f32[32,8,128]{2,1,0:T(8,128)S(1)}, u32[]{:S(2)}, u32[]{:S(2)}) collective-permute-start(f32[32,8,128]{2,1,0:T(8,128)S(1)} %get-tuple-element.41), channel_id=1, source_target_pairs={{0,2},{1,3},{2,0},{3,1},{4,6},{5,7},{6,4},{7,5},{8,10},{9,11},{10,... | collective-permute-start | bytes 393224 | tf_op jit(solution)/shard_map/ppermute | solution.py:429
  52.3 23.5 %collective-permute-start.7 = (f32[32,8,128]{2,1,0:T(8,128)S(1)}, f32[32,8,128]{2,1,0:T(8,128)S(1)}, u32[]{:S(2)}, u32[]{:S(2)}) collective-permute-start(f32[32,8,128]{2,1,0:T(8,128)S(1)} %get-tuple-element.45), channel_id=1, source_target_pairs={{0,3},{1,2},{2,1},{3,0},{4,7},{5,6},{6,5},{7,4},{8,11},{9,10},{10,... | collective-permute-start | bytes 393224 | tf_op jit(solution)/shard_map/ppermute | solution.py:429
  53.6 23.4 %collective-permute-start.8 = (f32[32,8,128]{2,1,0:T(8,128)S(1)}, f32[32,8,128]{2,1,0:T(8,128)S(1)}, u32[]{:S(2)}, u32[]{:S(2)}) collective-permute-start(f32[32,8,128]{2,1,0:T(8,128)S(1)} %get-tuple-element.46), channel_id=1, source_target_pairs={{0,4},{1,5},{2,6},{3,7},{4,0},{5,1},{6,2},{7,3},{8,12},{9,13},{10,... | collective-permute-start | bytes 393224 | tf_op jit(solution)/shard_map/ppermute | solution.py:429
  54.4 22.6 %collective-permute-start.9 = (f32[32,8,128]{2,1,0:T(8,128)S(1)}, f32[32,8,128]{2,1,0:T(8,128)S(1)}, u32[]{:S(2)}, u32[]{:S(2)}) collective-permute-start(f32[32,8,128]{2,1,0:T(8,128)S(1)} %get-tuple-element.47), channel_id=1, source_target_pairs={{0,5},{1,4},{2,7},{3,6},{4,1},{5,0},{6,3},{7,2},{8,13},{9,12},{10,... | collective-permute-start | bytes 393224 | tf_op jit(solution)/shard_map/ppermute | solution.py:429
  57.0 20.1 %collective-permute-start.10 = (f32[32,8,128]{2,1,0:T(8,128)S(1)}, f32[32,8,128]{2,1,0:T(8,128)S(1)}, u32[]{:S(2)}, u32[]{:S(2)}) collective-permute-start(f32[32,8,128]{2,1,0:T(8,128)S(1)} %get-tuple-element.48), channel_id=1, source_target_pairs={{0,6},{1,7},{2,4},{3,5},{4,2},{5,3},{6,0},{7,1},{8,14},{9,15},{10,... | collective-permute-start | bytes 393224 | tf_op jit(solution)/shard_map/ppermute | solution.py:429
  57.9 19.2 %collective-permute-start.11 = (f32[32,8,128]{2,1,0:T(8,128)S(1)}, f32[32,8,128]{2,1,0:T(8,128)S(1)}, u32[]{:S(2)}, u32[]{:S(2)}) collective-permute-start(f32[32,8,128]{2,1,0:T(8,128)S(1)} %get-tuple-element.49), channel_id=1, source_target_pairs={{0,7},{1,6},{2,5},{3,4},{4,3},{5,2},{6,1},{7,0},{8,15},{9,14},{10,... | collective-permute-start | bytes 393224 | tf_op jit(solution)/shard_map/ppermute | solution.py:429
  60.5 24.1 %all-to-all-start.1 = ((f32[32,4,128]{2,1,0:T(4,128)}), f32[32,4,128]{2,1,0:T(4,128)S(1)}, u32[]{:S(2)}, u32[]{:S(2)}) async-start(f32[32,4,128]{2,1,0:T(4,128)} %get-tuple-element.43), calls=%async_computation.1 | async-start | bytes 131072 | tf_op jit(solution)/shard_map/all_to_all | solution.py:374
  75.8 5.4 %collective-permute-start.6 = (f32[16,8,128]{2,1,0:T(8,128)S(1)}, f32[16,8,128]{2,1,0:T(8,128)S(1)}, u32[]{:S(2)}, u32[]{:S(2)}) collective-permute-start(f32[16,8,128]{2,1,0:T(8,128)S(1)} %get-tuple-element.42), channel_id=1, source_target_pairs={{8,0},{16,8},{24,16},{32,24},{40,32},{48,40},{56,48},{64,56},{72,6... | collective-permute-start | bytes 196616 | tf_op jit(solution)/shard_map/ppermute | solution.py:439

commit v12 on v11

--- a/solution.py
+++ b/solution.py
@@ -103,22 +103,39 @@
 
 
 def seed_kernel(*refs):
-    sources, out_ref, places, held, semaphore = refs[:6], refs[6], refs[7:13], refs[13], refs[14]
-    copies = [
-        pltpu.make_async_copy(source, place, semaphore.at[at])
-        for at, (source, place) in enumerate(zip(sources, places))
-    ]
-    for copy in copies:
-        copy.start()
+    sources, out_ref, edge_ref, places, held, semaphore = (
+        refs[:6], refs[6], refs[7], refs[8:14], refs[14], refs[15]
+    )
     real_ref, imag_ref, weights_ref, back_lanes_ref, back_rows_ref, twist_ref = places
     count = real_ref.shape[0]
-    for copy in copies:
+    half = count // 2
+    pieces = [
+        [
+            pltpu.make_async_copy(
+                source.at[pl.ds(at * half, half)], place.at[pl.ds(at * half, half)], semaphore.at[at * 3 + which]
+            )
+            for which, (source, place) in enumerate(zip(sources[:3], places[:3]))
+        ]
+        for at in range(2)
+    ]
+    tables = [
+        pltpu.make_async_copy(source, place, semaphore.at[6 + which])
+        for which, (source, place) in enumerate(zip(sources[3:], places[3:]))
+    ]
+    for copy in pieces[0] + pieces[1] + tables:
+        copy.start()
+    for at in range(2):
+        for copy in pieces[at]:
+            copy.wait()
+        rows = slice(at * half, (at + 1) * half)
+        for j in range(32):
+            columns = slice(j * LANES, (j + 1) * LANES)
+            weights = weights_ref[rows, columns]
+            first = at * half * ROWS + j
+            held[pl.ds(first, half, stride=ROWS), :] = weights * real_ref[rows, columns]
+            held[pl.ds(first + 32, half, stride=ROWS), :] = weights * imag_ref[rows, columns]
+    for copy in tables:
         copy.wait()
-    for j in range(32):
-        columns = slice(j * LANES, (j + 1) * LANES)
-        weights = weights_ref[:, columns]
-        held[pl.ds(j, count, stride=ROWS), :] = weights * real_ref[:, columns]
-        held[pl.ds(32 + j, count, stride=ROWS), :] = weights * imag_ref[:, columns]
     cos = twist_ref[0]
     sin = twist_ref[1]
     for start in range(0, count, CHUNK):
@@ -128,8 +145,7 @@
         frames = backward_chunk(
             jnp.concatenate(spectra, 0), back_lanes_ref[...], back_rows_ref[...], cos, sin
         )
-        for f in range(CHUNK):
-            out_ref[start + f] = frames[:, f * LANES : (f + 1) * LANES]
+        keep_frames(frames, out_ref, edge_ref)
 
 
 def arrange_kernel(weights_ref, taps_ref, weights_out, taps_out, held):
@@ -148,6 +164,16 @@
         ]
 
 
+def keep_frames(frames, out_ref, edge_ref):
+    count = out_ref.shape[0]
+    odd = jnp.full((ROWS, LANES), lax.axis_index("chan") % 2) > 0
+    frames = [frames[:, f * LANES : (f + 1) * LANES] for f in range(count)]
+    for f in range(count):
+        out_ref[f] = frames[f]
+    for f in range(count - 1):
+        edge_ref[f] = jnp.where(odd, frames[f + 1], frames[f])
+
+
 def weighted_sum(taps, values):
     total = taps[0] * values[0]
     for tap, value in zip(taps[1:], values[1:]):
@@ -160,7 +186,7 @@
     count = here_ref.shape[0]
     odd = jnp.full((8, LANES), keep[2]) > 0.5
     frames = [
-        jnp.where(odd, inside_ref[t, rows, :], across_ref[t, rows, :]) for t in range(count - reach, count)
+        jnp.where(odd, inside_ref[t, rows, :], across_ref[t - 1, rows, :]) for t in range(1, count)
     ]
     frames += [here_ref[t, rows, :] for t in range(count)]
     frames += [
@@ -184,7 +210,7 @@
 def first_kernel(
     keep_ref, inside_ref, here_ref, across_ref, taps_ref, weights_ref,
     ahead_rows_ref, ahead_lanes_ref, back_lanes_ref, back_rows_ref, twist_ref,
-    out_ref, side_ref, filtered,
+    out_ref, edge_ref, side_ref, filtered,
 ):
     count = here_ref.shape[0]
     keep = (keep_ref[0], keep_ref[1], keep_ref[2])
@@ -207,8 +233,7 @@
         )
         weights = weights_ref[start : start + CHUNK].reshape(CHUNK * ROWS, LANES)
         frames = backward_chunk(spectra * weights, back_lanes_ref[...], back_rows_ref[...], cos, sin)
-        for f in range(CHUNK):
-            out_ref[start + f] = frames[:, f * LANES : (f + 1) * LANES]
+        keep_frames(frames, out_ref, edge_ref)
 
 
 def quarters(rows):
@@ -290,7 +315,7 @@
 
 
 def last_kernel(place_ref, keep_ref, moved_ref, after_ref, sums_ref, taps_ref, *rest):
-    lanes, (solution_ref, residual_ref, kept, left, pairs) = rest[:8], rest[8:]
+    lanes, (*outputs, kept, left, pairs, kept_rows, left_rows, semaphore) = rest[:8], rest[8:]
     parts, count = moved_ref.shape[0], moved_ref.shape[1] - 1
     reach = taps_ref.shape[0] - 1
     rows = pl.ds(pl.multiple_of(place_ref[0] * 8, 8), 8)
@@ -321,22 +346,34 @@
             base = pairs[part, at]
             image = pairs[part, count + at]
             again = weighted_sum(taps, frames[at : at + reach + 1]) + RIDGE * image
-            here = pl.ds(pl.multiple_of((part * count + at) * 8, 8), 8)
+            here = slice(at * 8, (at + 1) * 8)
             kept[here, :] = to_base * base + to_image * image
             left[here, :] = base + image_rate * image + cube_rate * again
+        for block in range(count // 8):
+            ready = pl.ds(pl.multiple_of(part * count + block * 8, 8), 8)
+            for n1 in range(8):
+                places = pl.ds(block * 64 + n1, 8, stride=8)
+                columns = slice(n1 * LANES, (n1 + 1) * LANES)
+                kept_rows[ready, columns] = kept[places, :]
+                left_rows[ready, columns] = left[places, :]
+        for copy in copies(part):
+            copy.start()
+
+    def copies(part):
+        ready = pl.ds(pl.multiple_of(part * count, 8), count)
+        return [
+            pltpu.make_async_copy(held.at[ready], output.at[ready], semaphore.at[which, part])
+            for which, (held, output) in enumerate(zip((kept_rows, left_rows), outputs))
+        ]
 
     @pl.loop(0, parts - 1)
     def _(part):
         finish(part, [moved_ref[part + 1, t] for t in range(reach)])
 
     finish(parts - 1, [after_ref[t] * keep_ref[0] for t in range(reach)])
-
-    for block in range(parts * count // 8):
-        for n1 in range(8):
-            places = pl.ds(block * 64 + n1, 8, stride=8)
-            columns = slice(n1 * LANES, (n1 + 1) * LANES)
-            solution_ref[block * 8 : (block + 1) * 8, columns] = kept[places, :]
-            residual_ref[block * 8 : (block + 1) * 8, columns] = left[places, :]
+    for part in range(parts):
+        for copy in copies(part):
+            copy.wait()
 
 
 def shape(*dims):
@@ -365,27 +402,28 @@
     keep_group = (lax.axis_index("tm") < groups - 1).astype(F32).reshape(1)
     tables = (ahead_rows, ahead_lanes, back_lanes, back_rows, twist)
 
-    def neighbours(block):
+    def neighbours(block, edge):
         inside = [(i, i ^ 1) for i in range(devices)]
         across = [(i, min(max(((i + 1) ^ 1) - 1, 0), devices - 1)) for i in range(devices)]
-        return lax.ppermute(block, AXES, inside), lax.ppermute(block, AXES, across)
+        return lax.ppermute(block, AXES, inside), lax.ppermute(edge, AXES, across)
 
     def exchange(value, axis):
         return lax.all_to_all(value, axis, split_axis=0, concat_axis=0, tiled=True)
 
     seed_inputs = (observed_real, observed_imag, weights, back_lanes, back_rows, twist)
     seed_inputs = tuple(pltpu.with_memory_space_constraint(v, pltpu.HBM) for v in seed_inputs)
-    seeds = pl.pallas_call(
+    edge = shape(count - 1, ROWS, LANES)
+    seeds, edges = pl.pallas_call(
         seed_kernel,
-        out_shape=blocks,
+        out_shape=(blocks, edge),
         in_specs=[pl.BlockSpec(memory_space=pltpu.HBM)] * 6,
-        out_specs=vmem(1)[0],
+        out_specs=tuple(vmem(2)),
         scratch_shapes=[pltpu.VMEM(value.shape, value.dtype) for value in seed_inputs]
-        + [pltpu.VMEM((count * ROWS, LANES), F32), pltpu.SemaphoreType.DMA((6,))],
+        + [pltpu.VMEM((count * ROWS, LANES), F32), pltpu.SemaphoreType.DMA((9,))],
         compiler_params=params(),
         name="seed",
     )(*seed_inputs)
-    inside, across = neighbours(seeds)
+    inside, across = neighbours(seeds, edges)
     weights, taps = pl.pallas_call(
         arrange_kernel,
         out_shape=(blocks, shape((reach + 1) * ROWS, LANES)),
@@ -398,16 +436,16 @@
     )(weights, taps)
     taps = taps.reshape(reach + 1, ROWS, LANES)
 
-    images, side = pl.pallas_call(
+    images, edges, side = pl.pallas_call(
         first_kernel,
-        out_shape=(blocks, shape(reach + count, ROWS, LANES)),
+        out_shape=(blocks, edge, shape(reach + count, ROWS, LANES)),
         in_specs=[SMEM] + vmem(10),
-        out_specs=tuple(vmem(2)),
+        out_specs=tuple(vmem(3)),
         scratch_shapes=[pltpu.VMEM((count, ROWS, LANES), F32)],
         compiler_params=params(),
         name="first",
     )(keep, inside, seeds, across, taps, weights, *tables)
-    inside, across = neighbours(images)
+    inside, across = neighbours(images, edges)
 
     outgoing, *lanes = pl.pallas_call(
         second_kernel,
@@ -442,11 +480,14 @@
         last_kernel,
         out_shape=(shape(parts * count, 8 * LANES), shape(parts * count, 8 * LANES)),
         in_specs=[SMEM, SMEM] + vmem(12),
-        out_specs=tuple(vmem(2)),
+        out_specs=(pl.BlockSpec(memory_space=pltpu.HBM),) * 2,
         scratch_shapes=[
-            pltpu.VMEM((parts * count * 8, LANES), F32),
-            pltpu.VMEM((parts * count * 8, LANES), F32),
+            pltpu.VMEM((count * 8, LANES), F32),
+            pltpu.VMEM((count * 8, LANES), F32),
             pltpu.VMEM((parts, 2 * count, 8, LANES), F32),
+            pltpu.VMEM((parts * count, 8 * LANES), F32),
+            pltpu.VMEM((parts * count, 8 * LANES), F32),
+            pltpu.SemaphoreType.DMA((2, parts)),
         ],
         compiler_params=params(),
         name="last",

time: 86.9 us -> 87.9 us (1.012)
  waiting for transfers between devices: 19.6 us -> 22.7 us
  blocking collectives: 18.3 us -> 16.6 us
  starting transfers between devices: 33.3 us -> 32.3 us
    ppermute x4, waiting for transfers between devices: 12.1 us -> 15.2 us  [neighbours(): return (lax.ppermute(block, AXES, inside), lax.ppermute(edge, AXES, across))]
    all_to_all x1, blocking collectives: 18.3 us -> 16.6 us  [exchange(): return lax.all_to_all(value, axis, split_axis=0, concat_axis=0, tiled=True)]
    ppermute x4, starting transfers between devices: 8.34 us -> 7.34 us  [neighbours(): return (lax.ppermute(block, AXES, inside), lax.ppermute(edge, AXES, across))]
    pallas_call x2, Pallas kernels: 6.54 us -> 7.42 us  [the longest x1 3.71 us: local(): pl.pallas_call(first_kernel, out_shape=(blocks, edge, shape(reach + count...]
where the time goes in v12:
time: 87.9 us; the launch traced here: 87.6 us
  starting transfers between devices  32.3 us (37%)
  waiting for transfers between devices  22.7 us (26%)
  blocking collectives  16.6 us (19%)
  Pallas kernels  15 us (17%)
    all_to_all x1, blocking collectives, exchange(): return lax.all_to_all(value, axis, split_axis=0, concat_axis=0, tiled=True)  16.6 us
    all_to_all x1, starting transfers between devices, exchange(): return lax.all_to_all(value, axis, split_axis=0, concat_axis=0, tiled=True)  15.2 us
    ppermute x4, waiting for transfers between devices, neighbours(): return (lax.ppermute(block, AXES, inside), lax.ppermute(edge, AXES, across))  15.2 us
    ppermute x7, starting transfers between devices, local(): lax.ppermute(lanes[d], AXES, [(i, i ^ d) for i in range(devices)])  8.41 us
    ppermute x4, starting transfers between devices, neighbours(): return (lax.ppermute(block, AXES, inside), lax.ppermute(edge, AXES, across))  7.34 us
    ppermute x1, waiting for transfers between devices, local(): after = lax.ppermute(after, 'tm', [(i + 1, i) for i in range(groups - 1)])  4.1 us
    pallas_call x1, Pallas kernels, local(): pl.pallas_call(second_kernel, out_shape=(shape(parts, count + 1, 8, LANES...  3.99 us
    pallas_call x1, Pallas kernels, local(): pl.pallas_call(first_kernel, out_shape=(blocks, edge, shape(reach + count...  3.71 us
  transfers between devices with their start and end apart: 13, of which 4 were waited for; matrix products, arithmetic and copies ran while one was open for 0% of the time, Pallas kernels for 2%

profile of v12, /device:TPU:1, one launch (start us, length us, event | category | flops | bytes accessed | tf_op | source)
XLA Modules:
  0.0 87.6 jit_solution(8907446896739670886)
XLA Ops:
  0.6 0.0 copy-start.1
  0.6 0.0 copy-start.5
  0.7 3.7 %seed.1 = (f32[16,64,128]{2,1,0:T(8,128)S(1)}, f32[15,64,128]{2,1,0:T(8,128)}) custom-call(f32[16,4096]{1,0:T(8,128)} %refs_0_.1, f32[16,4096]{1,0:T(8,128)} %refs_1_.1, f32[16,4096]{1,0:T(8,128)} %weights_ref.1, bf16[384,256]{1,0:T(8,128)(2,1)} %constant.40.clone.refs_3_.back_lanes_ref, bf16[128,256]{1,0:T(8,128)(2,1)} %constant.41.clone.refs_4_.back_rows_ref, ...), custom_call_target="tpu_custom_call" | custom-call | tf_op jit(solution)/shard_map/seed/pallas_call | solution.py:416
  4.4 3.3 %collective-permute-start = (f32[16,64,128]{2,1,0:T(8,128)S(1)}, f32[16,64,128]{2,1,0:T(8,128)S(1)}, u32[]{:S(2)}, u32[]{:S(2)}) collective-permute-start(f32[16,64,128]{2,1,0:T(8,128)S(1)} %get-tuple-element.29.here_ref), channel_id=1, source_target_pairs={{0,1},{1,0},{2,3},{3,2},{4,5},{5,4},{6,7},{7,6},{8,9},{9,8},{10,11... | collective-permute-start | bytes 1572872 | tf_op jit(solution)/shard_map/ppermute | solution.py:408
  7.7 1.9 %collective-permute-start.1 = (f32[15,64,128]{2,1,0:T(8,128)}, f32[15,64,128]{2,1,0:T(8,128)S(1)}, u32[]{:S(2)}, u32[]{:S(2)}) collective-permute-start(f32[15,64,128]{2,1,0:T(8,128)} %get-tuple-element.30), channel_id=1, source_target_pairs={{0,0},{1,2},{2,1},{3,4},{4,3},{5,6},{6,5},{7,8},{8,7},{9,10},{10,9... | collective-permute-start | bytes 1474568 | tf_op jit(solution)/shard_map/ppermute | solution.py:408
  9.6 0.0 copy-done.1
  9.6 0.0 copy-done.5
  9.7 0.0 copy-start
  9.7 0.0 copy-start.2
  9.7 0.0 copy-start.3
  9.7 0.0 copy-start.4
  9.7 0.0 copy-start.6
  9.7 1.2 %arrange.1 = (f32[16,64,128]{2,1,0:T(8,128)S(1)}, f32[1024,128]{1,0:T(8,128)S(1)}) custom-call(f32[16,4096]{1,0:T(8,128)S(1)} %copy-done.1, f32[16,8192]{1,0:T(8,128)S(1)} %copy-done.5), custom_call_target="tpu_custom_call" | custom-call | flops 10000000 | bytes 2000000 | tf_op jit(solution)/shard_map/arrange/pallas_call | solution.py:427
  10.9 0.1 add_convert_fusion.keep_ref
  11.0 7.1 %collective-permute-done.1.across_ref = f32[15,64,128]{2,1,0:T(8,128)S(1)} collective-permute-done((f32[15,64,128]{2,1,0:T(8,128)}, f32[15,64,128]{2,1,0:T(8,128)S(1)}, u32[]{:S(2)}, u32[]{:S(2)}) %collective-permute-start.1) | collective-permute-done | bytes 491552 | tf_op jit(solution)/shard_map/ppermute | solution.py:408
  18.0 0.0 collective-permute-done.inside_ref
  18.0 0.0 copy-done
  18.0 0.0 copy-done.2
  18.1 0.0 copy-done.3
  18.1 0.0 copy-done.4
  18.1 0.0 copy-done.6
  18.1 3.7 %first.1 = (f32[16,64,128]{2,1,0:T(8,128)S(1)}, f32[15,64,128]{2,1,0:T(8,128)S(1)}, f32[31,64,128]{2,1,0:T(8,128)S(1)}) custom-call(f32[3]{0:T(128)S(1)} %add_convert_fusion.keep_ref, f32[16,64,128]{2,1,0:T(8,128)S(1)} %collective-permute-done.inside_ref, f32[16,64,128]{2,1,0:T(8,128)S(1)} %get-tuple-element.29.here_ref, ...), custom_call_target="tpu_custom_call" | custom-call | tf_op jit(solution)/shard_map/first/pallas_call | solution.py:439
  21.8 0.1 collective-permute-start.2
  21.9 2.0 %collective-permute-start.3 = (f32[15,64,128]{2,1,0:T(8,128)S(1)}, f32[15,64,128]{2,1,0:T(8,128)S(1)}, u32[]{:S(2)}, u32[]{:S(2)}) collective-permute-start(f32[15,64,128]{2,1,0:T(8,128)S(1)} %get-tuple-element.34), channel_id=1, source_target_pairs={{0,0},{1,2},{2,1},{3,4},{4,3},{5,6},{6,5},{7,8},{8,7},{9,10},{10,9... | collective-permute-start | bytes 1474568 | tf_op jit(solution)/shard_map/ppermute | solution.py:408
  23.9 8.1 %collective-permute-done.3.across_ref = f32[15,64,128]{2,1,0:T(8,128)S(1)} collective-permute-done((f32[15,64,128]{2,1,0:T(8,128)S(1)}, f32[15,64,128]{2,1,0:T(8,128)S(1)}, u32[]{:S(2)}, u32[]{:S(2)}) %collective-permute-start.3) | collective-permute-done | bytes 491552 | tf_op jit(solution)/shard_map/ppermute | solution.py:408
  32.1 0.0 collective-permute-done.2.inside_ref
  32.1 4.0 %second.1 = (f32[8,17,8,128]{3,2,1,0:T(8,128)S(1)}, f32[32,8,128]{2,1,0:T(8,128)S(1)}, f32[32,8,128]{2,1,0:T(8,128)S(1)}, f32[32,8,128]{2,1,0:T(8,128)S(1)}, f32...) custom-call(s32[1]{0:T(128)} %bitcast.place_ref, ...), custom_call_target="tpu_custom_call" | custom-call | tf_op jit(solution)/shard_map/second/pallas_call | solution.py:450
  36.0 16.6 %all_to_all.10.moved_ref = f32[8,17,8,128]{3,2,1,0:T(8,128)S(1)} all-to-all(f32[8,17,8,128]{3,2,1,0:T(8,128)S(1)} %get-tuple-element.36), channel_id=1, replica_groups=mesh['tm'=32,'chan'=8] {'chan'}, dimensions={0} | all-to-all | bytes 1114112 | tf_op jit(solution)/shard_map/all_to_all | solution.py:411
  52.7 0.6 collective-permute-start.4
  53.2 0.3 collective-permute-start.5
  53.5 1.4 %collective-permute-start.7 = (f32[32,8,128]{2,1,0:T(8,128)S(1)}, f32[32,8,128]{2,1,0:T(8,128)S(1)}, u32[]{:S(2)}, u32[]{:S(2)}) collective-permute-start(f32[32,8,128]{2,1,0:T(8,128)S(1)} %get-tuple-element.51), channel_id=1, source_target_pairs={{0,3},{1,2},{2,1},{3,0},{4,7},{5,6},{6,5},{7,4},{8,11},{9,10},{10,... | collective-permute-start | bytes 393224 | tf_op jit(solution)/shard_map/ppermute | solution.py:467
  54.9 0.8 collective-permute-start.8
  55.7 2.6 %collective-permute-start.9 = (f32[32,8,128]{2,1,0:T(8,128)S(1)}, f32[32,8,128]{2,1,0:T(8,128)S(1)}, u32[]{:S(2)}, u32[]{:S(2)}) collective-permute-start(f32[32,8,128]{2,1,0:T(8,128)S(1)} %get-tuple-element.53), channel_id=1, source_target_pairs={{0,5},{1,4},{2,7},{3,6},{4,1},{5,0},{6,3},{7,2},{8,13},{9,12},{10,... | collective-permute-start | bytes 393224 | tf_op jit(solution)/shard_map/ppermute | solution.py:467
  58.2 0.0 collective-permute-done.4._.rest_1_
  58.2 0.9 %collective-permute-start.10 = (f32[32,8,128]{2,1,0:T(8,128)S(1)}, f32[32,8,128]{2,1,0:T(8,128)S(1)}, u32[]{:S(2)}, u32[]{:S(2)}) collective-permute-start(f32[32,8,128]{2,1,0:T(8,128)S(1)} %get-tuple-element.54), channel_id=1, source_target_pairs={{0,6},{1,7},{2,4},{3,5},{4,2},{5,3},{6,0},{7,1},{8,14},{9,15},{10,... | collective-permute-start | bytes 393224 | tf_op jit(solution)/shard_map/ppermute | solution.py:467
  59.1 0.0 collective-permute-done.5.__.rest_2_
  59.1 2.0 %collective-permute-start.11 = (f32[32,8,128]{2,1,0:T(8,128)S(1)}, f32[32,8,128]{2,1,0:T(8,128)S(1)}, u32[]{:S(2)}, u32[]{:S(2)}) collective-permute-start(f32[32,8,128]{2,1,0:T(8,128)S(1)} %get-tuple-element.55), channel_id=1, source_target_pairs={{0,7},{1,6},{2,5},{3,4},{4,3},{5,2},{6,1},{7,0},{8,15},{9,14},{10,... | collective-permute-start | bytes 393224 | tf_op jit(solution)/shard_map/ppermute | solution.py:467
  61.1 0.6 tail.1
  61.7 15.2 %all-to-all-start.1 = ((f32[32,4,128]{2,1,0:T(4,128)}), f32[32,4,128]{2,1,0:T(4,128)S(1)}, u32[]{:S(2)}, u32[]{:S(2)}) async-start(f32[32,4,128]{2,1,0:T(4,128)} %get-tuple-element.49), calls=%async_computation.1 | async-start | bytes 131072 | tf_op jit(solution)/shard_map/all_to_all | solution.py:411
  77.0 0.0 collective-permute-done.7.rest_3_
  77.0 1.3 %collective-permute-start.6 = (f32[16,8,128]{2,1,0:T(8,128)S(1)}, f32[16,8,128]{2,1,0:T(8,128)S(1)}, u32[]{:S(2)}, u32[]{:S(2)}) collective-permute-start(f32[16,8,128]{2,1,0:T(8,128)S(1)} %get-tuple-element.48), channel_id=1, source_target_pairs={{8,0},{16,8},{24,16},{32,24},{40,32},{48,40},{56,48},{64,56},{72,6... | collective-permute-start | bytes 196616 | tf_op jit(solution)/shard_map/ppermute | solution.py:477
  78.3 0.0 collective-permute-done.8.rest_4_
  78.3 0.0 collective-permute-done.9.rest_5_
  78.3 0.0 collective-permute-done.10.rest_6_
  78.3 0.0 collective-permute-done.11.rest_7_
  78.3 4.1 %collective-permute-done.6.after_ref = f32[16,8,128]{2,1,0:T(8,128)S(1)} collective-permute-done((f32[16,8,128]{2,1,0:T(8,128)S(1)}, f32[16,8,128]{2,1,0:T(8,128)S(1)}, u32[]{:S(2)}, u32[]{:S(2)}) %collective-permute-start.6) | collective-permute-done | bytes 65568 | tf_op jit(solution)/shard_map/ppermute | solution.py:477
  82.4 3.4 %all-to-all-done.1.sums_ref = f32[32,4,128]{2,1,0:T(4,128)S(1)} async-done(((f32[32,4,128]{2,1,0:T(4,128)}), f32[32,4,128]{2,1,0:T(4,128)S(1)}, u32[]{:S(2)}, u32[]{:S(2)}) %all-to-all-start.1) | async-done | bytes 65568 | tf_op jit(solution)/shard_map/all_to_all | solution.py:411
  85.8 1.8 %last.1 = (f32[128,1024]{1,0:T(8,128)}, f32[128,1024]{1,0:T(8,128)}) custom-call(s32[1]{0:T(128)} %bitcast.place_ref, f32[1]{0:T(128)} %bitcast.1.keep_ref, f32[8,17,8,128]{3,2,1,0:T(8,128)S(1)} %all_to_all.10.moved_ref, f32[16,8,128]{2,1,0:T(8,128)S(1)} %collective-permute-done.6.after_ref, f32[32,4,128]{2,1,0:T(4,128)S(1)} %all-to-all-done.1.sums_ref, ...), custom_call_target="tpu_custom_call" | custom-call | tf_op jit(solution)/shard_map/last/pallas_call | solution.py:479
Async XLA Ops:
  0.6 9.0 %copy-start.1 = (f32[16,4096]{1,0:T(8,128)S(1)}, f32[16,4096]{1,0:T(8,128)}, u32[]{:S(2)}) copy-start(f32[16,4096]{1,0:T(8,128)} %weights_ref.1) | copy-start | bytes 786436
  0.6 9.0 %copy-start.5 = (f32[16,8192]{1,0:T(8,128)S(1)}, f32[16,8192]{1,0:T(8,128)}, u32[]{:S(2)}) copy-start(f32[16,8192]{1,0:T(8,128)} %taps_ref.1) | copy-start | bytes 1572868
  4.4 13.7 %collective-permute-start = (f32[16,64,128]{2,1,0:T(8,128)S(1)}, f32[16,64,128]{2,1,0:T(8,128)S(1)}, u32[]{:S(2)}, u32[]{:S(2)}) collective-permute-start(f32[16,64,128]{2,1,0:T(8,128)S(1)} %get-tuple-element.29.here_ref), channel_id=1, source_target_pairs={{0,1},{1,0},{2,3},{3,2},{4,5},{5,4},{6,7},{7,6},{8,9},{9,8},{10,11... | collective-permute-start | bytes 1572872 | tf_op jit(solution)/shard_map/ppermute | solution.py:408
  7.7 10.3 %collective-permute-start.1 = (f32[15,64,128]{2,1,0:T(8,128)}, f32[15,64,128]{2,1,0:T(8,128)S(1)}, u32[]{:S(2)}, u32[]{:S(2)}) collective-permute-start(f32[15,64,128]{2,1,0:T(8,128)} %get-tuple-element.30), channel_id=1, source_target_pairs={{0,0},{1,2},{2,1},{3,4},{4,3},{5,6},{6,5},{7,8},{8,7},{9,10},{10,9... | collective-permute-start | bytes 1474568 | tf_op jit(solution)/shard_map/ppermute | solution.py:408
  9.7 8.4 %copy-start = (bf16[384,256]{1,0:T(8,128)(2,1)S(1)}, bf16[384,256]{1,0:T(8,128)(2,1)}, u32[]{:S(2)}) copy-start(bf16[384,256]{1,0:T(8,128)(2,1)} %constant.40.clone.refs_3_.back_lanes_ref) | copy-start | bytes 589828
  9.7 8.4 %copy-start.2 = (f32[2,64,128]{2,1,0:T(8,128)S(1)}, f32[2,64,128]{2,1,0:T(8,128)}, u32[]{:S(2)}) copy-start(f32[2,64,128]{2,1,0:T(8,128)} %constant.42.clone.refs_5_.twist_ref) | copy-start | bytes 196612
  9.7 8.4 %copy-start.3 = (bf16[128,256]{1,0:T(8,128)(2,1)S(1)}, bf16[128,256]{1,0:T(8,128)(2,1)}, u32[]{:S(2)}) copy-start(bf16[128,256]{1,0:T(8,128)(2,1)} %constant.41.clone.refs_4_.back_rows_ref) | copy-start | bytes 196612
  9.7 8.4 %copy-start.4 = (bf16[256,256]{1,0:T(8,128)(2,1)S(1)}, bf16[256,256]{1,0:T(8,128)(2,1)}, u32[]{:S(2)}) copy-start(bf16[256,256]{1,0:T(8,128)(2,1)} %constant.44.clone.ahead_lanes_ref) | copy-start | bytes 393220
  9.7 8.4 %copy-start.6 = (bf16[128,192]{1,0:T(8,128)(2,1)S(1)}, bf16[128,192]{1,0:T(8,128)(2,1)}, u32[]{:S(2)}) copy-start(bf16[128,192]{1,0:T(8,128)(2,1)} %constant.43.clone.ahead_rows_ref) | copy-start | bytes 147460
  21.8 10.3 %collective-permute-start.2 = (f32[16,64,128]{2,1,0:T(8,128)S(1)}, f32[16,64,128]{2,1,0:T(8,128)S(1)}, u32[]{:S(2)}, u32[]{:S(2)}) collective-permute-start(f32[16,64,128]{2,1,0:T(8,128)S(1)} %get-tuple-element.33.here_ref), channel_id=1, source_target_pairs={{0,1},{1,0},{2,3},{3,2},{4,5},{5,4},{6,7},{7,6},{8,9},{9,8},{10,11... | collective-permute-start | bytes 1572872 | tf_op jit(solution)/shard_map/ppermute | solution.py:408
  21.9 10.1 %collective-permute-start.3 = (f32[15,64,128]{2,1,0:T(8,128)S(1)}, f32[15,64,128]{2,1,0:T(8,128)S(1)}, u32[]{:S(2)}, u32[]{:S(2)}) collective-permute-start(f32[15,64,128]{2,1,0:T(8,128)S(1)} %get-tuple-element.34), channel_id=1, source_target_pairs={{0,0},{1,2},{2,1},{3,4},{4,3},{5,6},{6,5},{7,8},{8,7},{9,10},{10,9... | collective-permute-start | bytes 1474568 | tf_op jit(solution)/shard_map/ppermute | solution.py:408
  52.7 5.6 %collective-permute-start.4 = (f32[32,8,128]{2,1,0:T(8,128)S(1)}, f32[32,8,128]{2,1,0:T(8,128)S(1)}, u32[]{:S(2)}, u32[]{:S(2)}) collective-permute-start(f32[32,8,128]{2,1,0:T(8,128)S(1)} %get-tuple-element.46), channel_id=1, source_target_pairs={{0,1},{1,0},{2,3},{3,2},{4,5},{5,4},{6,7},{7,6},{8,9},{9,8},{10,11... | collective-permute-start | bytes 393224 | tf_op jit(solution)/shard_map/ppermute | solution.py:467
  53.2 5.9 %collective-permute-start.5 = (f32[32,8,128]{2,1,0:T(8,128)S(1)}, f32[32,8,128]{2,1,0:T(8,128)S(1)}, u32[]{:S(2)}, u32[]{:S(2)}) collective-permute-start(f32[32,8,128]{2,1,0:T(8,128)S(1)} %get-tuple-element.47), channel_id=1, source_target_pairs={{0,2},{1,3},{2,0},{3,1},{4,6},{5,7},{6,4},{7,5},{8,10},{9,11},{10,... | collective-permute-start | bytes 393224 | tf_op jit(solution)/shard_map/ppermute | solution.py:467
  53.5 23.5 %collective-permute-start.7 = (f32[32,8,128]{2,1,0:T(8,128)S(1)}, f32[32,8,128]{2,1,0:T(8,128)S(1)}, u32[]{:S(2)}, u32[]{:S(2)}) collective-permute-start(f32[32,8,128]{2,1,0:T(8,128)S(1)} %get-tuple-element.51), channel_id=1, source_target_pairs={{0,3},{1,2},{2,1},{3,0},{4,7},{5,6},{6,5},{7,4},{8,11},{9,10},{10,... | collective-permute-start | bytes 393224 | tf_op jit(solution)/shard_map/ppermute | solution.py:467
  54.9 23.4 %collective-permute-start.8 = (f32[32,8,128]{2,1,0:T(8,128)S(1)}, f32[32,8,128]{2,1,0:T(8,128)S(1)}, u32[]{:S(2)}, u32[]{:S(2)}) collective-permute-start(f32[32,8,128]{2,1,0:T(8,128)S(1)} %get-tuple-element.52), channel_id=1, source_target_pairs={{0,4},{1,5},{2,6},{3,7},{4,0},{5,1},{6,2},{7,3},{8,12},{9,13},{10,... | collective-permute-start | bytes 393224 | tf_op jit(solution)/shard_map/ppermute | solution.py:467
  55.7 22.6 %collective-permute-start.9 = (f32[32,8,128]{2,1,0:T(8,128)S(1)}, f32[32,8,128]{2,1,0:T(8,128)S(1)}, u32[]{:S(2)}, u32[]{:S(2)}) collective-permute-start(f32[32,8,128]{2,1,0:T(8,128)S(1)} %get-tuple-element.53), channel_id=1, source_target_pairs={{0,5},{1,4},{2,7},{3,6},{4,1},{5,0},{6,3},{7,2},{8,13},{9,12},{10,... | collective-permute-start | bytes 393224 | tf_op jit(solution)/shard_map/ppermute | solution.py:467
  58.2 20.1 %collective-permute-start.10 = (f32[32,8,128]{2,1,0:T(8,128)S(1)}, f32[32,8,128]{2,1,0:T(8,128)S(1)}, u32[]{:S(2)}, u32[]{:S(2)}) collective-permute-start(f32[32,8,128]{2,1,0:T(8,128)S(1)} %get-tuple-element.54), channel_id=1, source_target_pairs={{0,6},{1,7},{2,4},{3,5},{4,2},{5,3},{6,0},{7,1},{8,14},{9,15},{10,... | collective-permute-start | bytes 393224 | tf_op jit(solution)/shard_map/ppermute | solution.py:467
  59.1 19.2 %collective-permute-start.11 = (f32[32,8,128]{2,1,0:T(8,128)S(1)}, f32[32,8,128]{2,1,0:T(8,128)S(1)}, u32[]{:S(2)}, u32[]{:S(2)}) collective-permute-start(f32[32,8,128]{2,1,0:T(8,128)S(1)} %get-tuple-element.55), channel_id=1, source_target_pairs={{0,7},{1,6},{2,5},{3,4},{4,3},{5,2},{6,1},{7,0},{8,15},{9,14},{10,... | collective-permute-start | bytes 393224 | tf_op jit(solution)/shard_map/ppermute | solution.py:467
  61.7 24.1 %all-to-all-start.1 = ((f32[32,4,128]{2,1,0:T(4,128)}), f32[32,4,128]{2,1,0:T(4,128)S(1)}, u32[]{:S(2)}, u32[]{:S(2)}) async-start(f32[32,4,128]{2,1,0:T(4,128)} %get-tuple-element.49), calls=%async_computation.1 | async-start | bytes 131072 | tf_op jit(solution)/shard_map/all_to_all | solution.py:411
  77.0 5.4 %collective-permute-start.6 = (f32[16,8,128]{2,1,0:T(8,128)S(1)}, f32[16,8,128]{2,1,0:T(8,128)S(1)}, u32[]{:S(2)}, u32[]{:S(2)}) collective-permute-start(f32[16,8,128]{2,1,0:T(8,128)S(1)} %get-tuple-element.48), channel_id=1, source_target_pairs={{8,0},{16,8},{24,16},{32,24},{40,32},{48,40},{56,48},{64,56},{72,6... | collective-permute-start | bytes 196616 | tf_op jit(solution)/shard_map/ppermute | solution.py:477

commit v13 on v11

--- a/solution.py
+++ b/solution.py
@@ -229,7 +229,7 @@
     ahead_rows_ref, ahead_lanes_ref, back_lanes_ref, back_rows_ref, twist_ref,
     out_ref, *rest,
 ):
-    lanes, (filtered, sums, staged) = rest[:8], rest[8:]
+    own_ref, other_ref, filtered, sums, staged = rest
     count = here_ref.shape[0]
     keep = (keep_ref[0], keep_ref[1], keep_ref[2])
     reach = taps_ref.shape[0] - 1
@@ -257,8 +257,9 @@
         sums[1] = second
         sums[2] = third
 
-    for d, lane in enumerate(lanes):
-        lane[...] = staged[d]
+    for e in range(4):
+        own_ref[e] = staged[2 * e]
+        other_ref[e] = staged[2 * e + 1]
     cos = twist_ref[0]
     sin = twist_ref[1]
     power = jnp.zeros((8, LANES), F32)
@@ -280,7 +281,14 @@
         out_ref[group, count] = totals
 
 
-def tail_kernel(moved_ref, _, __, frames_ref, sums_ref):
+def join_kernel(own_ref, other_ref, *outputs):
+    slots = own_ref.shape[1]
+    for e, output in enumerate(outputs):
+        output[:slots] = own_ref[e + 1]
+        output[slots:] = other_ref[e + 1]
+
+
+def tail_kernel(moved_ref, _, frames_ref, sums_ref):
     count = frames_ref.shape[0]
     frames_ref[...] = moved_ref[0, :count]
     total = moved_ref[0, count]
@@ -290,12 +298,16 @@
 
 
 def last_kernel(place_ref, keep_ref, moved_ref, after_ref, sums_ref, taps_ref, *rest):
-    lanes, (solution_ref, residual_ref, kept, left, pairs) = rest[:8], rest[8:]
+    own_ref, other_ref, *lanes = rest[:5]
+    solution_ref, residual_ref, kept, left, pairs = rest[5:]
     parts, count = moved_ref.shape[0], moved_ref.shape[1] - 1
     reach = taps_ref.shape[0] - 1
     rows = pl.ds(pl.multiple_of(place_ref[0] * 8, 8), 8)
-    for d, lane in enumerate(lanes):
-        pairs[place_ref[0] ^ d] = lane[...]
+    pairs[place_ref[0]] = own_ref[0]
+    pairs[place_ref[0] ^ 1] = other_ref[0]
+    for e, lane in enumerate(lanes):
+        pairs[place_ref[0] ^ (2 * e + 2)] = lane[: 2 * count]
+        pairs[place_ref[0] ^ (2 * e + 3)] = lane[2 * count :]
     sums = jnp.sum(sums_ref[...], 0)
     norm, curve, square, power = (
         jnp.sum(jnp.sum(jnp.where(quarters(4) == at, sums, 0.0), 1, keepdims=True), 0, keepdims=True)
@@ -409,11 +421,11 @@
     )(keep, inside, seeds, across, taps, weights, *tables)
     inside, across = neighbours(images)
 
-    outgoing, *lanes = pl.pallas_call(
+    outgoing, own, other = pl.pallas_call(
         second_kernel,
-        out_shape=(shape(parts, count + 1, 8, LANES),) + (shape(2 * count, 8, LANES),) * 8,
+        out_shape=(shape(parts, count + 1, 8, LANES),) + (shape(4, 2 * count, 8, LANES),) * 2,
         in_specs=[SMEM, SMEM] + vmem(11),
-        out_specs=tuple(vmem(9)),
+        out_specs=tuple(vmem(3)),
         scratch_shapes=[
             pltpu.VMEM((count, ROWS, LANES), F32),
             pltpu.VMEM((3, 8, LANES), F32),
@@ -424,24 +436,34 @@
     )(place, keep, inside, images, across, side, taps, weights, *tables)
 
     moved = exchange(outgoing, "chan")
-    moved, lanes = lax.optimization_barrier((moved, lanes))
-    lanes = lanes[:1] + [
-        lax.ppermute(lanes[d], AXES, [(i, i ^ d) for i in range(devices)]) for d in range(1, 8)
+    other = lax.ppermute(other, AXES, [(i, i ^ 1) for i in range(devices)])
+    moved, own, other = lax.optimization_barrier((moved, own, other))
+    lanes = pl.pallas_call(
+        join_kernel,
+        out_shape=(shape(4 * count, 8, LANES),) * 3,
+        in_specs=vmem(2),
+        out_specs=tuple(vmem(3)),
+        compiler_params=params(),
+        name="join",
+    )(own, other)
+    lanes = [
+        lax.ppermute(lane, AXES, [(i, i ^ (2 * e + 2)) for i in range(devices)])
+        for e, lane in enumerate(lanes)
     ]
     after, sums = pl.pallas_call(
         tail_kernel,
         out_shape=(shape(count, 8, LANES), shape(groups, 4, LANES)),
-        in_specs=vmem(1) + [ANY, ANY],
+        in_specs=vmem(1) + [ANY],
         out_specs=tuple(vmem(2)),
         compiler_params=params(),
         name="tail",
-    )(moved, lanes[1], lanes[2])
+    )(moved, lanes[0])
     after = lax.ppermute(after, "tm", [(i + 1, i) for i in range(groups - 1)])
     sums = exchange(sums, "tm")
     return pl.pallas_call(
         last_kernel,
         out_shape=(shape(parts * count, 8 * LANES), shape(parts * count, 8 * LANES)),
-        in_specs=[SMEM, SMEM] + vmem(12),
+        in_specs=[SMEM, SMEM] + vmem(9),
         out_specs=tuple(vmem(2)),
         scratch_shapes=[
             pltpu.VMEM((parts * count * 8, LANES), F32),
@@ -450,7 +472,7 @@
         ],
         compiler_params=params(),
         name="last",
-    )(place, keep_group, moved, after, sums, taps, *lanes)
+    )(place, keep_group, moved, after, sums, taps, own, other, *lanes)
 
 
 def solution(mesh):

time: 86.9 us -> 88.4 us (1.017); the launches traced: 86.6 us -> 86.7 us
  starting transfers between devices: 33.3 us -> 28.8 us
  waiting for transfers between devices: 19.6 us -> 23.1 us
    ppermute x7 -> x4, starting transfers between devices: 8.41 us -> 3.95 us  [the longest x3 3.86 us: local(): lax.ppermute(lane, AXES, [(i, i ^ 2 * e + 2) for i in range(devices)])]
    ppermute x7 -> x4, waiting for transfers between devices: 0.02 us -> 3.44 us  [the longest x3 3.44 us: local(): lax.ppermute(lane, AXES, [(i, i ^ 2 * e + 2) for i in range(devices)])]
  transfers between devices with their start and end apart: 13 -> 10, of which waited for: 4 -> 5; matrix products, arithmetic and copies ran while one was open for 0% -> 0% of each run, Pallas kernels for 2% -> 2%
where the time goes in v13:
time: 88.4 us; the launch traced here: 86.7 us
  starting transfers between devices  28.8 us (33%)
  waiting for transfers between devices  23.1 us (26%)
  blocking collectives  18.7 us (21%)
  Pallas kernels  15.2 us (17%)
    all_to_all x1, blocking collectives, exchange(): return lax.all_to_all(value, axis, split_axis=0, concat_axis=0, tiled=True)  18.7 us
    all_to_all x1, starting transfers between devices, exchange(): return lax.all_to_all(value, axis, split_axis=0, concat_axis=0, tiled=True)  15.2 us
    ppermute x2, waiting for transfers between devices, neighbours(): lax.ppermute(block, AXES, across)  12.1 us
    ppermute x2, starting transfers between devices, neighbours(): lax.ppermute(block, AXES, across)  8.15 us
    pallas_call x1, Pallas kernels, local(): pl.pallas_call(second_kernel, out_shape=(shape(parts, count + 1, 8, LANES...  4 us
    ppermute x3, starting transfers between devices, local(): lax.ppermute(lane, AXES, [(i, i ^ 2 * e + 2) for i in range(devices)])  3.86 us
    ppermute x1, waiting for transfers between devices, local(): after = lax.ppermute(after, 'tm', [(i + 1, i) for i in range(groups - 1)])  3.78 us
    pallas_call x1, Pallas kernels, local(): pl.pallas_call(first_kernel, out_shape=(blocks, shape(reach + count, ROWS...  3.73 us
  transfers between devices with their start and end apart: 10, of which 5 were waited for; matrix products, arithmetic and copies ran while one was open for 0% of the time, Pallas kernels for 2%

profile of v13, /device:TPU:1, one launch (start us, length us, event | category | flops | bytes accessed | tf_op | source)
XLA Modules:
  0.0 86.7 jit_solution(15947044559923426225)
XLA Ops:
  0.6 0.0 copy-start.1
  0.6 0.0 copy-start.4
  0.7 2.8 %seed.1.here_ref = f32[16,64,128]{2,1,0:T(8,128)S(1)} custom-call(f32[16,4096]{1,0:T(8,128)} %refs_0_.1, f32[16,4096]{1,0:T(8,128)} %refs_1_.1, f32[16,4096]{1,0:T(8,128)} %weights_ref.1, bf16[384,256]{1,0:T(8,128)(2,1)} %constant.40.clone.refs_3_.back_lanes_ref, bf16[128,256]{1,0:T(8,128)(2,1)} %constant.41.clone.refs_4_.back_rows_ref, ...), custom_call_target="tpu_custom_call" | custom-call | tf_op jit(solution)/shard_map/seed/pallas_call | solution.py:390
  3.5 4.5 %collective-permute-start.1 = (f32[16,64,128]{2,1,0:T(8,128)S(1)}, f32[16,64,128]{2,1,0:T(8,128)S(1)}, u32[]{:S(2)}, u32[]{:S(2)}) collective-permute-start(f32[16,64,128]{2,1,0:T(8,128)S(1)} %seed.1.here_ref), channel_id=1, source_target_pairs={{0,0},{1,2},{2,1},{3,4},{4,3},{5,6},{6,5},{7,8},{8,7},{9,10},{10,9... | collective-permute-start | bytes 1572872 | tf_op jit(solution)/shard_map/ppermute | solution.py:383
  8.0 0.1 collective-permute-start
  8.1 0.0 copy-done.1
  8.1 0.0 copy-done.4
  8.1 0.0 copy-start
  8.1 0.0 copy-start.2
  8.1 0.0 copy-start.3
  8.2 0.0 copy-start.5
  8.2 0.0 copy-start.6
  8.2 1.2 %arrange.1 = (f32[16,64,128]{2,1,0:T(8,128)S(1)}, f32[1024,128]{1,0:T(8,128)S(1)}) custom-call(f32[16,4096]{1,0:T(8,128)S(1)} %copy-done.1, f32[16,8192]{1,0:T(8,128)S(1)} %copy-done.4), custom_call_target="tpu_custom_call" | custom-call | flops 10000000 | bytes 2000000 | tf_op jit(solution)/shard_map/arrange/pallas_call | solution.py:401
  9.4 0.1 add_convert_fusion.keep_ref
  9.5 5.4 %collective-permute-done.1.across_ref = f32[16,64,128]{2,1,0:T(8,128)S(1)} collective-permute-done((f32[16,64,128]{2,1,0:T(8,128)S(1)}, f32[16,64,128]{2,1,0:T(8,128)S(1)}, u32[]{:S(2)}, u32[]{:S(2)}) %collective-permute-start.1) | collective-permute-done | bytes 524320 | tf_op jit(solution)/shard_map/ppermute | solution.py:383
  14.8 0.0 collective-permute-done.inside_ref
  14.8 0.0 copy-done
  14.8 0.0 copy-done.2
  14.8 0.0 copy-done.3
  14.9 0.0 copy-done.5
  14.9 0.0 copy-done.6
  14.9 3.7 %first.1 = (f32[16,64,128]{2,1,0:T(8,128)S(1)}, f32[31,64,128]{2,1,0:T(8,128)S(1)}) custom-call(f32[3]{0:T(128)S(1)} %add_convert_fusion.keep_ref, f32[16,64,128]{2,1,0:T(8,128)S(1)} %collective-permute-done.inside_ref, f32[16,64,128]{2,1,0:T(8,128)S(1)} %seed.1.here_ref, f32[16,64,128]{2,1,0:T(8,128)S(1)} %collective-permute-done.1.across_ref, ...), custom_call_target="tpu_custom_call" | custom-call | tf_op jit(solution)/shard_map/first/pallas_call | solution.py:413
  18.6 3.6 %collective-permute-start.3 = (f32[16,64,128]{2,1,0:T(8,128)S(1)}, f32[16,64,128]{2,1,0:T(8,128)S(1)}, u32[]{:S(2)}, u32[]{:S(2)}) collective-permute-start(f32[16,64,128]{2,1,0:T(8,128)S(1)} %get-tuple-element.19.here_ref), channel_id=1, source_target_pairs={{0,0},{1,2},{2,1},{3,4},{4,3},{5,6},{6,5},{7,8},{8,7},{9,10},{10,9... | collective-permute-start | bytes 1572872 | tf_op jit(solution)/shard_map/ppermute | solution.py:383
  22.3 0.1 collective-permute-start.2
  22.4 6.8 %collective-permute-done.3.across_ref = f32[16,64,128]{2,1,0:T(8,128)S(1)} collective-permute-done((f32[16,64,128]{2,1,0:T(8,128)S(1)}, f32[16,64,128]{2,1,0:T(8,128)S(1)}, u32[]{:S(2)}, u32[]{:S(2)}) %collective-permute-start.3) | collective-permute-done | bytes 524320 | tf_op jit(solution)/shard_map/ppermute | solution.py:383
  29.1 0.0 collective-permute-done.2.inside_ref
  29.1 4.0 %second.1 = (f32[8,17,8,128]{3,2,1,0:T(8,128)S(1)}, f32[4,32,8,128]{3,2,1,0:T(8,128)S(1)}, f32[4,32,8,128]{3,2,1,0:T(8,128)S(1)}) custom-call(s32[1]{0:T(128)} %bitcast.place_ref, f32[3]{0:T(128)S(1)} %add_convert_fusion.keep_ref, f32[16,64,128]{2,1,0:T(8,128)S(1)} %collective-permute-done.2.inside_ref, f32[16,64,128]{2,1,0:T(8,128)S(1)} %get-tuple-element.19.here_ref, ...), custom_call_target="tpu_custom_call" | custom-call | tf_op jit(solution)/shard_map/second/pallas_call | solution.py:424
  33.1 0.1 collective-permute-start.4
  33.2 18.7 %all_to_all.10.moved_ref = f32[8,17,8,128]{3,2,1,0:T(8,128)S(1)} all-to-all(f32[8,17,8,128]{3,2,1,0:T(8,128)S(1)} %get-tuple-element.21), channel_id=1, replica_groups=mesh['tm'=32,'chan'=8] {'chan'}, dimensions={0} | all-to-all | bytes 1114112 | tf_op jit(solution)/shard_map/all_to_all | solution.py:386
  51.9 0.0 collective-permute-done.4.other_ref.rest_1_
  51.9 0.8 join.1
  52.6 0.3 collective-permute-start.5
  52.9 1.8 %collective-permute-start.7 = (f32[64,8,128]{2,1,0:T(8,128)}, f32[64,8,128]{2,1,0:T(8,128)S(1)}, u32[]{:S(2)}, u32[]{:S(2)}) collective-permute-start(f32[64,8,128]{2,1,0:T(8,128)} %get-tuple-element.30), channel_id=1, source_target_pairs={{0,4},{1,5},{2,6},{3,7},{4,0},{5,1},{6,2},{7,3},{8,12},{9,13},{10,... | collective-permute-start | bytes 786440 | tf_op jit(solution)/shard_map/ppermute | solution.py:450
  54.7 1.8 %collective-permute-start.8 = (f32[64,8,128]{2,1,0:T(8,128)S(1)}, f32[64,8,128]{2,1,0:T(8,128)S(1)}, u32[]{:S(2)}, u32[]{:S(2)}) collective-permute-start(f32[64,8,128]{2,1,0:T(8,128)S(1)} %get-tuple-element.31), channel_id=1, source_target_pairs={{0,6},{1,7},{2,4},{3,5},{4,2},{5,3},{6,0},{7,1},{8,14},{9,15},{10,... | collective-permute-start | bytes 786440 | tf_op jit(solution)/shard_map/ppermute | solution.py:450
  56.5 3.4 %collective-permute-done.5._.rest_2_ = f32[64,8,128]{2,1,0:T(8,128)S(1)} collective-permute-done((f32[64,8,128]{2,1,0:T(8,128)S(1)}, f32[64,8,128]{2,1,0:T(8,128)S(1)}, u32[]{:S(2)}, u32[]{:S(2)}) %collective-permute-start.5) | collective-permute-done | bytes 262176 | tf_op jit(solution)/shard_map/ppermute | solution.py:450
  59.9 0.6 tail.1
  60.6 15.2 %all-to-all-start.1 = ((f32[32,4,128]{2,1,0:T(4,128)}), f32[32,4,128]{2,1,0:T(4,128)S(1)}, u32[]{:S(2)}, u32[]{:S(2)}) async-start(f32[32,4,128]{2,1,0:T(4,128)} %get-tuple-element.29), calls=%async_computation.1 | async-start | bytes 131072 | tf_op jit(solution)/shard_map/all_to_all | solution.py:386
  75.8 1.3 %collective-permute-start.6 = (f32[16,8,128]{2,1,0:T(8,128)S(1)}, f32[16,8,128]{2,1,0:T(8,128)S(1)}, u32[]{:S(2)}, u32[]{:S(2)}) collective-permute-start(f32[16,8,128]{2,1,0:T(8,128)S(1)} %get-tuple-element.28), channel_id=1, source_target_pairs={{8,0},{16,8},{24,16},{32,24},{40,32},{48,40},{56,48},{64,56},{72,6... | collective-permute-start | bytes 196616 | tf_op jit(solution)/shard_map/ppermute | solution.py:461
  77.2 0.0 collective-permute-done.7.rest_3_
  77.2 0.0 collective-permute-done.8.rest_4_
  77.2 3.8 %collective-permute-done.6.after_ref = f32[16,8,128]{2,1,0:T(8,128)S(1)} collective-permute-done((f32[16,8,128]{2,1,0:T(8,128)S(1)}, f32[16,8,128]{2,1,0:T(8,128)S(1)}, u32[]{:S(2)}, u32[]{:S(2)}) %collective-permute-start.6) | collective-permute-done | bytes 65568 | tf_op jit(solution)/shard_map/ppermute | solution.py:461
  81.0 3.7 %all-to-all-done.1.sums_ref = f32[32,4,128]{2,1,0:T(4,128)S(1)} async-done(((f32[32,4,128]{2,1,0:T(4,128)}), f32[32,4,128]{2,1,0:T(4,128)S(1)}, u32[]{:S(2)}, u32[]{:S(2)}) %all-to-all-start.1) | async-done | bytes 65568 | tf_op jit(solution)/shard_map/all_to_all | solution.py:386
  84.7 2.1 %last.1 = (f32[128,1024]{1,0:T(8,128)}, f32[128,1024]{1,0:T(8,128)}) custom-call(s32[1]{0:T(128)} %bitcast.place_ref, f32[1]{0:T(128)} %bitcast.1.keep_ref, f32[8,17,8,128]{3,2,1,0:T(8,128)S(1)} %all_to_all.10.moved_ref, f32[16,8,128]{2,1,0:T(8,128)S(1)} %collective-permute-done.6.after_ref, f32[32,4,128]{2,1,0:T(4,128)S(1)} %all-to-all-done.1.sums_ref, ...), custom_call_target="tpu_custom_call" | custom-call | tf_op jit(solution)/shard_map/last/pallas_call | solution.py:463
Async XLA Ops:
  0.6 7.5 %copy-start.1 = (f32[16,4096]{1,0:T(8,128)S(1)}, f32[16,4096]{1,0:T(8,128)}, u32[]{:S(2)}) copy-start(f32[16,4096]{1,0:T(8,128)} %weights_ref.1) | copy-start | bytes 786436
  0.6 7.5 %copy-start.4 = (f32[16,8192]{1,0:T(8,128)S(1)}, f32[16,8192]{1,0:T(8,128)}, u32[]{:S(2)}) copy-start(f32[16,8192]{1,0:T(8,128)} %taps_ref.1) | copy-start | bytes 1572868
  3.5 11.4 %collective-permute-start.1 = (f32[16,64,128]{2,1,0:T(8,128)S(1)}, f32[16,64,128]{2,1,0:T(8,128)S(1)}, u32[]{:S(2)}, u32[]{:S(2)}) collective-permute-start(f32[16,64,128]{2,1,0:T(8,128)S(1)} %seed.1.here_ref), channel_id=1, source_target_pairs={{0,0},{1,2},{2,1},{3,4},{4,3},{5,6},{6,5},{7,8},{8,7},{9,10},{10,9... | collective-permute-start | bytes 1572872 | tf_op jit(solution)/shard_map/ppermute | solution.py:383
  8.0 6.9 %collective-permute-start = (f32[16,64,128]{2,1,0:T(8,128)S(1)}, f32[16,64,128]{2,1,0:T(8,128)S(1)}, u32[]{:S(2)}, u32[]{:S(2)}) collective-permute-start(f32[16,64,128]{2,1,0:T(8,128)S(1)} %seed.1.here_ref), channel_id=1, source_target_pairs={{0,1},{1,0},{2,3},{3,2},{4,5},{5,4},{6,7},{7,6},{8,9},{9,8},{10,11... | collective-permute-start | bytes 1572872 | tf_op jit(solution)/shard_map/ppermute | solution.py:383
  8.1 6.7 %copy-start = (bf16[384,256]{1,0:T(8,128)(2,1)S(1)}, bf16[384,256]{1,0:T(8,128)(2,1)}, u32[]{:S(2)}) copy-start(bf16[384,256]{1,0:T(8,128)(2,1)} %constant.40.clone.refs_3_.back_lanes_ref) | copy-start | bytes 589828
  8.1 6.7 %copy-start.2 = (f32[2,64,128]{2,1,0:T(8,128)S(1)}, f32[2,64,128]{2,1,0:T(8,128)}, u32[]{:S(2)}) copy-start(f32[2,64,128]{2,1,0:T(8,128)} %constant.42.clone.refs_5_.twist_ref) | copy-start | bytes 196612
  8.1 6.7 %copy-start.3 = (bf16[128,256]{1,0:T(8,128)(2,1)S(1)}, bf16[128,256]{1,0:T(8,128)(2,1)}, u32[]{:S(2)}) copy-start(bf16[128,256]{1,0:T(8,128)(2,1)} %constant.41.clone.refs_4_.back_rows_ref) | copy-start | bytes 196612
  8.2 6.7 %copy-start.5 = (bf16[256,256]{1,0:T(8,128)(2,1)S(1)}, bf16[256,256]{1,0:T(8,128)(2,1)}, u32[]{:S(2)}) copy-start(bf16[256,256]{1,0:T(8,128)(2,1)} %constant.44.clone.ahead_lanes_ref) | copy-start | bytes 393220
  8.2 6.7 %copy-start.6 = (bf16[128,192]{1,0:T(8,128)(2,1)S(1)}, bf16[128,192]{1,0:T(8,128)(2,1)}, u32[]{:S(2)}) copy-start(bf16[128,192]{1,0:T(8,128)(2,1)} %constant.43.clone.ahead_rows_ref) | copy-start | bytes 147460
  18.6 10.5 %collective-permute-start.3 = (f32[16,64,128]{2,1,0:T(8,128)S(1)}, f32[16,64,128]{2,1,0:T(8,128)S(1)}, u32[]{:S(2)}, u32[]{:S(2)}) collective-permute-start(f32[16,64,128]{2,1,0:T(8,128)S(1)} %get-tuple-element.19.here_ref), channel_id=1, source_target_pairs={{0,0},{1,2},{2,1},{3,4},{4,3},{5,6},{6,5},{7,8},{8,7},{9,10},{10,9... | collective-permute-start | bytes 1572872 | tf_op jit(solution)/shard_map/ppermute | solution.py:383
  22.3 6.9 %collective-permute-start.2 = (f32[16,64,128]{2,1,0:T(8,128)S(1)}, f32[16,64,128]{2,1,0:T(8,128)S(1)}, u32[]{:S(2)}, u32[]{:S(2)}) collective-permute-start(f32[16,64,128]{2,1,0:T(8,128)S(1)} %get-tuple-element.19.here_ref), channel_id=1, source_target_pairs={{0,1},{1,0},{2,3},{3,2},{4,5},{5,4},{6,7},{7,6},{8,9},{9,8},{10,11... | collective-permute-start | bytes 1572872 | tf_op jit(solution)/shard_map/ppermute | solution.py:383
  33.1 18.8 %collective-permute-start.4 = (f32[4,32,8,128]{3,2,1,0:T(8,128)S(1)}, f32[4,32,8,128]{3,2,1,0:T(8,128)S(1)}, u32[]{:S(2)}, u32[]{:S(2)}) collective-permute-start(f32[4,32,8,128]{3,2,1,0:T(8,128)S(1)} %get-tuple-element.23), channel_id=1, source_target_pairs={{0,1},{1,0},{2,3},{3,2},{4,5},{5,4},{6,7},{7,6},{8,9},{9,8},{10,11... | collective-permute-start | bytes 1572872 | tf_op jit(solution)/shard_map/ppermute | solution.py:439
  52.6 7.3 %collective-permute-start.5 = (f32[64,8,128]{2,1,0:T(8,128)S(1)}, f32[64,8,128]{2,1,0:T(8,128)S(1)}, u32[]{:S(2)}, u32[]{:S(2)}) collective-permute-start(f32[64,8,128]{2,1,0:T(8,128)S(1)} %get-tuple-element.27), channel_id=1, source_target_pairs={{0,2},{1,3},{2,0},{3,1},{4,6},{5,7},{6,4},{7,5},{8,10},{9,11},{10,... | collective-permute-start | bytes 786440 | tf_op jit(solution)/shard_map/ppermute | solution.py:450
  52.9 24.2 %collective-permute-start.7 = (f32[64,8,128]{2,1,0:T(8,128)}, f32[64,8,128]{2,1,0:T(8,128)S(1)}, u32[]{:S(2)}, u32[]{:S(2)}) collective-permute-start(f32[64,8,128]{2,1,0:T(8,128)} %get-tuple-element.30), channel_id=1, source_target_pairs={{0,4},{1,5},{2,6},{3,7},{4,0},{5,1},{6,2},{7,3},{8,12},{9,13},{10,... | collective-permute-start | bytes 786440 | tf_op jit(solution)/shard_map/ppermute | solution.py:450
  54.7 22.4 %collective-permute-start.8 = (f32[64,8,128]{2,1,0:T(8,128)S(1)}, f32[64,8,128]{2,1,0:T(8,128)S(1)}, u32[]{:S(2)}, u32[]{:S(2)}) collective-permute-start(f32[64,8,128]{2,1,0:T(8,128)S(1)} %get-tuple-element.31), channel_id=1, source_target_pairs={{0,6},{1,7},{2,4},{3,5},{4,2},{5,3},{6,0},{7,1},{8,14},{9,15},{10,... | collective-permute-start | bytes 786440 | tf_op jit(solution)/shard_map/ppermute | solution.py:450
  60.6 24.1 %all-to-all-start.1 = ((f32[32,4,128]{2,1,0:T(4,128)}), f32[32,4,128]{2,1,0:T(4,128)S(1)}, u32[]{:S(2)}, u32[]{:S(2)}) async-start(f32[32,4,128]{2,1,0:T(4,128)} %get-tuple-element.29), calls=%async_computation.1 | async-start | bytes 131072 | tf_op jit(solution)/shard_map/all_to_all | solution.py:386
  75.8 5.1 %collective-permute-start.6 = (f32[16,8,128]{2,1,0:T(8,128)S(1)}, f32[16,8,128]{2,1,0:T(8,128)S(1)}, u32[]{:S(2)}, u32[]{:S(2)}) collective-permute-start(f32[16,8,128]{2,1,0:T(8,128)S(1)} %get-tuple-element.28), channel_id=1, source_target_pairs={{8,0},{16,8},{24,16},{32,24},{40,32},{48,40},{56,48},{64,56},{72,6... | collective-permute-start | bytes 196616 | tf_op jit(solution)/shard_map/ppermute | solution.py:461

commit v14 on v13

--- a/solution.py
+++ b/solution.py
@@ -446,6 +446,7 @@
         compiler_params=params(),
         name="join",
     )(own, other)
+    joined = lanes[0]
     lanes = [
         lax.ppermute(lane, AXES, [(i, i ^ (2 * e + 2)) for i in range(devices)])
         for e, lane in enumerate(lanes)
@@ -457,7 +458,7 @@
         out_specs=tuple(vmem(2)),
         compiler_params=params(),
         name="tail",
-    )(moved, lanes[0])
+    )(moved, joined)
     after = lax.ppermute(after, "tm", [(i + 1, i) for i in range(groups - 1)])
     sums = exchange(sums, "tm")
     return pl.pallas_call(

time: 88.4 us -> 84.1 us (0.951)
  the two profiles are of different devices: /device:TPU:1 before, /device:TPU:2 now
where the time goes in v14:
time: 84.1 us; the launch traced here: 83.8 us
  starting transfers between devices  28.9 us (34%)
  waiting for transfers between devices  21.1 us (25%)
  blocking collectives  17.6 us (21%)
  Pallas kernels  15.3 us (18%)
    all_to_all x1, blocking collectives, exchange(): return lax.all_to_all(value, axis, split_axis=0, concat_axis=0, tiled=True)  17.6 us
    all_to_all x1, starting transfers between devices, exchange(): return lax.all_to_all(value, axis, split_axis=0, concat_axis=0, tiled=True)  15.5 us
    ppermute x2, waiting for transfers between devices, neighbours(): lax.ppermute(block, AXES, across)  12.4 us
    ppermute x1, waiting for transfers between devices, local(): after = lax.ppermute(after, 'tm', [(i + 1, i) for i in range(groups - 1)])  4.95 us
    ppermute x3, starting transfers between devices, local(): lax.ppermute(lane, AXES, [(i, i ^ 2 * e + 2) for i in range(devices)])  4.7 us
    pallas_call x1, Pallas kernels, local(): pl.pallas_call(second_kernel, out_shape=(shape(parts, count + 1, 8, LANES...  4 us
    ppermute x2, starting transfers between devices, neighbours(): lax.ppermute(block, AXES, across)  3.84 us
    all_to_all x1, waiting for transfers between devices, exchange(): return lax.all_to_all(value, axis, split_axis=0, concat_axis=0, tiled=True)  3.73 us
  transfers between devices with their start and end apart: 10, of which 4 were waited for; matrix products, arithmetic and copies ran while one was open for 0% of the time, Pallas kernels for 2%

profile of v14, /device:TPU:2, one launch (start us, length us, event | category | flops | bytes accessed | tf_op | source)
XLA Modules:
  0.0 83.8 jit_solution(7226183971309672844)
XLA Ops:
  0.6 0.0 copy-start.1
  0.6 0.0 copy-start.4
  0.7 2.8 %seed.1.here_ref = f32[16,64,128]{2,1,0:T(8,128)S(1)} custom-call(f32[16,4096]{1,0:T(8,128)} %refs_0_.1, f32[16,4096]{1,0:T(8,128)} %refs_1_.1, f32[16,4096]{1,0:T(8,128)} %weights_ref.1, bf16[384,256]{1,0:T(8,128)(2,1)} %constant.40.clone.refs_3_.back_lanes_ref, bf16[128,256]{1,0:T(8,128)(2,1)} %constant.41.clone.refs_4_.back_rows_ref, ...), custom_call_target="tpu_custom_call" | custom-call | tf_op jit(solution)/shard_map/seed/pallas_call | solution.py:390
  3.5 1.9 %collective-permute-start.1 = (f32[16,64,128]{2,1,0:T(8,128)S(1)}, f32[16,64,128]{2,1,0:T(8,128)S(1)}, u32[]{:S(2)}, u32[]{:S(2)}) collective-permute-start(f32[16,64,128]{2,1,0:T(8,128)S(1)} %seed.1.here_ref), channel_id=1, source_target_pairs={{0,0},{1,2},{2,1},{3,4},{4,3},{5,6},{6,5},{7,8},{8,7},{9,10},{10,9... | collective-permute-start | bytes 1572872 | tf_op jit(solution)/shard_map/ppermute | solution.py:383
  5.4 1.7 %collective-permute-start = (f32[16,64,128]{2,1,0:T(8,128)S(1)}, f32[16,64,128]{2,1,0:T(8,128)S(1)}, u32[]{:S(2)}, u32[]{:S(2)}) collective-permute-start(f32[16,64,128]{2,1,0:T(8,128)S(1)} %seed.1.here_ref), channel_id=1, source_target_pairs={{0,1},{1,0},{2,3},{3,2},{4,5},{5,4},{6,7},{7,6},{8,9},{9,8},{10,11... | collective-permute-start | bytes 1572872 | tf_op jit(solution)/shard_map/ppermute | solution.py:383
  7.1 0.0 copy-done.1
  7.1 0.0 copy-done.4
  7.1 0.0 copy-start
  7.1 0.0 copy-start.2
  7.1 0.0 copy-start.3
  7.1 0.0 copy-start.5
  7.1 0.0 copy-start.6
  7.1 1.2 %arrange.1 = (f32[16,64,128]{2,1,0:T(8,128)S(1)}, f32[1024,128]{1,0:T(8,128)S(1)}) custom-call(f32[16,4096]{1,0:T(8,128)S(1)} %copy-done.1, f32[16,8192]{1,0:T(8,128)S(1)} %copy-done.4), custom_call_target="tpu_custom_call" | custom-call | flops 10000000 | bytes 2000000 | tf_op jit(solution)/shard_map/arrange/pallas_call | solution.py:401
  8.3 0.1 add_convert_fusion.keep_ref
  8.4 5.6 %collective-permute-done.1.across_ref = f32[16,64,128]{2,1,0:T(8,128)S(1)} collective-permute-done((f32[16,64,128]{2,1,0:T(8,128)S(1)}, f32[16,64,128]{2,1,0:T(8,128)S(1)}, u32[]{:S(2)}, u32[]{:S(2)}) %collective-permute-start.1) | collective-permute-done | bytes 524320 | tf_op jit(solution)/shard_map/ppermute | solution.py:383
  14.0 0.0 collective-permute-done.inside_ref
  14.0 0.0 copy-done
  14.0 0.0 copy-done.2
  14.0 0.0 copy-done.3
  14.0 0.0 copy-done.5
  14.0 0.0 copy-done.6
  14.0 3.7 %first.1 = (f32[16,64,128]{2,1,0:T(8,128)S(1)}, f32[31,64,128]{2,1,0:T(8,128)S(1)}) custom-call(f32[3]{0:T(128)S(1)} %add_convert_fusion.keep_ref, f32[16,64,128]{2,1,0:T(8,128)S(1)} %collective-permute-done.inside_ref, f32[16,64,128]{2,1,0:T(8,128)S(1)} %seed.1.here_ref, f32[16,64,128]{2,1,0:T(8,128)S(1)} %collective-permute-done.1.across_ref, ...), custom_call_target="tpu_custom_call" | custom-call | tf_op jit(solution)/shard_map/first/pallas_call | solution.py:413
  17.7 1.9 %collective-permute-start.3 = (f32[16,64,128]{2,1,0:T(8,128)S(1)}, f32[16,64,128]{2,1,0:T(8,128)S(1)}, u32[]{:S(2)}, u32[]{:S(2)}) collective-permute-start(f32[16,64,128]{2,1,0:T(8,128)S(1)} %get-tuple-element.19.here_ref), channel_id=1, source_target_pairs={{0,0},{1,2},{2,1},{3,4},{4,3},{5,6},{6,5},{7,8},{8,7},{9,10},{10,9... | collective-permute-start | bytes 1572872 | tf_op jit(solution)/shard_map/ppermute | solution.py:383
  19.7 1.7 %collective-permute-start.2 = (f32[16,64,128]{2,1,0:T(8,128)S(1)}, f32[16,64,128]{2,1,0:T(8,128)S(1)}, u32[]{:S(2)}, u32[]{:S(2)}) collective-permute-start(f32[16,64,128]{2,1,0:T(8,128)S(1)} %get-tuple-element.19.here_ref), channel_id=1, source_target_pairs={{0,1},{1,0},{2,3},{3,2},{4,5},{5,4},{6,7},{7,6},{8,9},{9,8},{10,11... | collective-permute-start | bytes 1572872 | tf_op jit(solution)/shard_map/ppermute | solution.py:383
  21.4 6.9 %collective-permute-done.3.across_ref = f32[16,64,128]{2,1,0:T(8,128)S(1)} collective-permute-done((f32[16,64,128]{2,1,0:T(8,128)S(1)}, f32[16,64,128]{2,1,0:T(8,128)S(1)}, u32[]{:S(2)}, u32[]{:S(2)}) %collective-permute-start.3) | collective-permute-done | bytes 524320 | tf_op jit(solution)/shard_map/ppermute | solution.py:383
  28.2 0.0 collective-permute-done.2.inside_ref
  28.2 4.0 %second.1 = (f32[8,17,8,128]{3,2,1,0:T(8,128)S(1)}, f32[4,32,8,128]{3,2,1,0:T(8,128)S(1)}, f32[4,32,8,128]{3,2,1,0:T(8,128)S(1)}) custom-call(s32[1]{0:T(128)} %bitcast.place_ref, f32[3]{0:T(128)S(1)} %add_convert_fusion.keep_ref, f32[16,64,128]{2,1,0:T(8,128)S(1)} %collective-permute-done.2.inside_ref, f32[16,64,128]{2,1,0:T(8,128)S(1)} %get-tuple-element.19.here_ref, ...), custom_call_target="tpu_custom_call" | custom-call | tf_op jit(solution)/shard_map/second/pallas_call | solution.py:424
  32.3 0.2 collective-permute-start.4
  32.5 17.6 %all_to_all.10.moved_ref = f32[8,17,8,128]{3,2,1,0:T(8,128)S(1)} all-to-all(f32[8,17,8,128]{3,2,1,0:T(8,128)S(1)} %get-tuple-element.21), channel_id=1, replica_groups=mesh['tm'=32,'chan'=8] {'chan'}, dimensions={0} | all-to-all | bytes 1114112 | tf_op jit(solution)/shard_map/all_to_all | solution.py:386
  50.0 0.0 collective-permute-done.4.other_ref.rest_1_
  50.0 0.8 %join.1 = (f32[64,8,128]{2,1,0:T(8,128)S(1)}, f32[64,8,128]{2,1,0:T(8,128)}, f32[64,8,128]{2,1,0:T(8,128)}) custom-call(f32[4,32,8,128]{3,2,1,0:T(8,128)S(1)} %get-tuple-element.25.own_ref.rest_0_, f32[4,32,8,128]{3,2,1,0:T(8,128)S(1)} %collective-permute-done.4.other_ref.rest_1_), custom_call_target="tpu_custom_call" | custom-call | tf_op jit(solution)/shard_map/join/pallas_call | solution.py:441
  50.9 1.5 %collective-permute-start.7 = (f32[64,8,128]{2,1,0:T(8,128)}, f32[64,8,128]{2,1,0:T(8,128)S(1)}, u32[]{:S(2)}, u32[]{:S(2)}) collective-permute-start(f32[64,8,128]{2,1,0:T(8,128)} %get-tuple-element.30), channel_id=1, source_target_pairs={{0,4},{1,5},{2,6},{3,7},{4,0},{5,1},{6,2},{7,3},{8,12},{9,13},{10,... | collective-permute-start | bytes 786440 | tf_op jit(solution)/shard_map/ppermute | solution.py:451
  52.3 1.5 %collective-permute-start.8 = (f32[64,8,128]{2,1,0:T(8,128)}, f32[64,8,128]{2,1,0:T(8,128)S(1)}, u32[]{:S(2)}, u32[]{:S(2)}) collective-permute-start(f32[64,8,128]{2,1,0:T(8,128)} %get-tuple-element.31), channel_id=1, source_target_pairs={{0,6},{1,7},{2,4},{3,5},{4,2},{5,3},{6,0},{7,1},{8,14},{9,15},{10,... | collective-permute-start | bytes 786440 | tf_op jit(solution)/shard_map/ppermute | solution.py:451
  53.8 1.8 %collective-permute-start.6 = (f32[64,8,128]{2,1,0:T(8,128)S(1)}, f32[64,8,128]{2,1,0:T(8,128)S(1)}, u32[]{:S(2)}, u32[]{:S(2)}) collective-permute-start(f32[64,8,128]{2,1,0:T(8,128)S(1)} %get-tuple-element.27._), channel_id=1, source_target_pairs={{0,2},{1,3},{2,0},{3,1},{4,6},{5,7},{6,4},{7,5},{8,10},{9,11},{10,... | collective-permute-start | bytes 786440 | tf_op jit(solution)/shard_map/ppermute | solution.py:451
  55.6 0.6 tail.1
  56.2 15.5 %all-to-all-start.1 = ((f32[32,4,128]{2,1,0:T(4,128)}), f32[32,4,128]{2,1,0:T(4,128)S(1)}, u32[]{:S(2)}, u32[]{:S(2)}) async-start(f32[32,4,128]{2,1,0:T(4,128)} %get-tuple-element.29), calls=%async_computation.1 | async-start | bytes 131072 | tf_op jit(solution)/shard_map/all_to_all | solution.py:386
  71.7 1.3 %collective-permute-start.5 = (f32[16,8,128]{2,1,0:T(8,128)S(1)}, f32[16,8,128]{2,1,0:T(8,128)S(1)}, u32[]{:S(2)}, u32[]{:S(2)}) collective-permute-start(f32[16,8,128]{2,1,0:T(8,128)S(1)} %get-tuple-element.28), channel_id=1, source_target_pairs={{8,0},{16,8},{24,16},{32,24},{40,32},{48,40},{56,48},{64,56},{72,6... | collective-permute-start | bytes 196616 | tf_op jit(solution)/shard_map/ppermute | solution.py:462
  73.1 5.0 %collective-permute-done.5.after_ref = f32[16,8,128]{2,1,0:T(8,128)S(1)} collective-permute-done((f32[16,8,128]{2,1,0:T(8,128)S(1)}, f32[16,8,128]{2,1,0:T(8,128)S(1)}, u32[]{:S(2)}, u32[]{:S(2)}) %collective-permute-start.5) | collective-permute-done | bytes 65568 | tf_op jit(solution)/shard_map/ppermute | solution.py:462
  78.0 3.7 %all-to-all-done.1.sums_ref = f32[32,4,128]{2,1,0:T(4,128)S(1)} async-done(((f32[32,4,128]{2,1,0:T(4,128)}), f32[32,4,128]{2,1,0:T(4,128)S(1)}, u32[]{:S(2)}, u32[]{:S(2)}) %all-to-all-start.1) | async-done | bytes 65568 | tf_op jit(solution)/shard_map/all_to_all | solution.py:386
  81.7 0.0 collective-permute-done.7.rest_3_
  81.7 0.0 collective-permute-done.8.rest_4_
  81.7 0.0 collective-permute-done.6.rest_2_
  81.7 2.1 %last.1 = (f32[128,1024]{1,0:T(8,128)}, f32[128,1024]{1,0:T(8,128)}) custom-call(s32[1]{0:T(128)} %bitcast.place_ref, f32[1]{0:T(128)} %bitcast.1.keep_ref, f32[8,17,8,128]{3,2,1,0:T(8,128)S(1)} %all_to_all.10.moved_ref, f32[16,8,128]{2,1,0:T(8,128)S(1)} %collective-permute-done.5.after_ref, f32[32,4,128]{2,1,0:T(4,128)S(1)} %all-to-all-done.1.sums_ref, ...), custom_call_target="tpu_custom_call" | custom-call | tf_op jit(solution)/shard_map/last/pallas_call | solution.py:464
Async XLA Ops:
  0.6 6.4 %copy-start.1 = (f32[16,4096]{1,0:T(8,128)S(1)}, f32[16,4096]{1,0:T(8,128)}, u32[]{:S(2)}) copy-start(f32[16,4096]{1,0:T(8,128)} %weights_ref.1) | copy-start | bytes 786436
  0.6 6.4 %copy-start.4 = (f32[16,8192]{1,0:T(8,128)S(1)}, f32[16,8192]{1,0:T(8,128)}, u32[]{:S(2)}) copy-start(f32[16,8192]{1,0:T(8,128)} %taps_ref.1) | copy-start | bytes 1572868
  3.5 10.5 %collective-permute-start.1 = (f32[16,64,128]{2,1,0:T(8,128)S(1)}, f32[16,64,128]{2,1,0:T(8,128)S(1)}, u32[]{:S(2)}, u32[]{:S(2)}) collective-permute-start(f32[16,64,128]{2,1,0:T(8,128)S(1)} %seed.1.here_ref), channel_id=1, source_target_pairs={{0,0},{1,2},{2,1},{3,4},{4,3},{5,6},{6,5},{7,8},{8,7},{9,10},{10,9... | collective-permute-start | bytes 1572872 | tf_op jit(solution)/shard_map/ppermute | solution.py:383
  5.4 8.6 %collective-permute-start = (f32[16,64,128]{2,1,0:T(8,128)S(1)}, f32[16,64,128]{2,1,0:T(8,128)S(1)}, u32[]{:S(2)}, u32[]{:S(2)}) collective-permute-start(f32[16,64,128]{2,1,0:T(8,128)S(1)} %seed.1.here_ref), channel_id=1, source_target_pairs={{0,1},{1,0},{2,3},{3,2},{4,5},{5,4},{6,7},{7,6},{8,9},{9,8},{10,11... | collective-permute-start | bytes 1572872 | tf_op jit(solution)/shard_map/ppermute | solution.py:383
  7.1 6.9 %copy-start = (bf16[384,256]{1,0:T(8,128)(2,1)S(1)}, bf16[384,256]{1,0:T(8,128)(2,1)}, u32[]{:S(2)}) copy-start(bf16[384,256]{1,0:T(8,128)(2,1)} %constant.40.clone.refs_3_.back_lanes_ref) | copy-start | bytes 589828
  7.1 6.9 %copy-start.2 = (f32[2,64,128]{2,1,0:T(8,128)S(1)}, f32[2,64,128]{2,1,0:T(8,128)}, u32[]{:S(2)}) copy-start(f32[2,64,128]{2,1,0:T(8,128)} %constant.42.clone.refs_5_.twist_ref) | copy-start | bytes 196612
  7.1 6.9 %copy-start.3 = (bf16[128,256]{1,0:T(8,128)(2,1)S(1)}, bf16[128,256]{1,0:T(8,128)(2,1)}, u32[]{:S(2)}) copy-start(bf16[128,256]{1,0:T(8,128)(2,1)} %constant.41.clone.refs_4_.back_rows_ref) | copy-start | bytes 196612
  7.1 6.9 %copy-start.5 = (bf16[256,256]{1,0:T(8,128)(2,1)S(1)}, bf16[256,256]{1,0:T(8,128)(2,1)}, u32[]{:S(2)}) copy-start(bf16[256,256]{1,0:T(8,128)(2,1)} %constant.44.clone.ahead_lanes_ref) | copy-start | bytes 393220
  7.1 6.9 %copy-start.6 = (bf16[128,192]{1,0:T(8,128)(2,1)S(1)}, bf16[128,192]{1,0:T(8,128)(2,1)}, u32[]{:S(2)}) copy-start(bf16[128,192]{1,0:T(8,128)(2,1)} %constant.43.clone.ahead_rows_ref) | copy-start | bytes 147460
  17.7 10.5 %collective-permute-start.3 = (f32[16,64,128]{2,1,0:T(8,128)S(1)}, f32[16,64,128]{2,1,0:T(8,128)S(1)}, u32[]{:S(2)}, u32[]{:S(2)}) collective-permute-start(f32[16,64,128]{2,1,0:T(8,128)S(1)} %get-tuple-element.19.here_ref), channel_id=1, source_target_pairs={{0,0},{1,2},{2,1},{3,4},{4,3},{5,6},{6,5},{7,8},{8,7},{9,10},{10,9... | collective-permute-start | bytes 1572872 | tf_op jit(solution)/shard_map/ppermute | solution.py:383
  19.7 8.6 %collective-permute-start.2 = (f32[16,64,128]{2,1,0:T(8,128)S(1)}, f32[16,64,128]{2,1,0:T(8,128)S(1)}, u32[]{:S(2)}, u32[]{:S(2)}) collective-permute-start(f32[16,64,128]{2,1,0:T(8,128)S(1)} %get-tuple-element.19.here_ref), channel_id=1, source_target_pairs={{0,1},{1,0},{2,3},{3,2},{4,5},{5,4},{6,7},{7,6},{8,9},{9,8},{10,11... | collective-permute-start | bytes 1572872 | tf_op jit(solution)/shard_map/ppermute | solution.py:383
  32.3 17.8 %collective-permute-start.4 = (f32[4,32,8,128]{3,2,1,0:T(8,128)S(1)}, f32[4,32,8,128]{3,2,1,0:T(8,128)S(1)}, u32[]{:S(2)}, u32[]{:S(2)}) collective-permute-start(f32[4,32,8,128]{3,2,1,0:T(8,128)S(1)} %get-tuple-element.23), channel_id=1, source_target_pairs={{0,1},{1,0},{2,3},{3,2},{4,5},{5,4},{6,7},{7,6},{8,9},{9,8},{10,11... | collective-permute-start | bytes 1572872 | tf_op jit(solution)/shard_map/ppermute | solution.py:439
  50.9 30.9 %collective-permute-start.7 = (f32[64,8,128]{2,1,0:T(8,128)}, f32[64,8,128]{2,1,0:T(8,128)S(1)}, u32[]{:S(2)}, u32[]{:S(2)}) collective-permute-start(f32[64,8,128]{2,1,0:T(8,128)} %get-tuple-element.30), channel_id=1, source_target_pairs={{0,4},{1,5},{2,6},{3,7},{4,0},{5,1},{6,2},{7,3},{8,12},{9,13},{10,... | collective-permute-start | bytes 786440 | tf_op jit(solution)/shard_map/ppermute | solution.py:451
  52.3 29.4 %collective-permute-start.8 = (f32[64,8,128]{2,1,0:T(8,128)}, f32[64,8,128]{2,1,0:T(8,128)S(1)}, u32[]{:S(2)}, u32[]{:S(2)}) collective-permute-start(f32[64,8,128]{2,1,0:T(8,128)} %get-tuple-element.31), channel_id=1, source_target_pairs={{0,6},{1,7},{2,4},{3,5},{4,2},{5,3},{6,0},{7,1},{8,14},{9,15},{10,... | collective-permute-start | bytes 786440 | tf_op jit(solution)/shard_map/ppermute | solution.py:451
  53.8 27.9 %collective-permute-start.6 = (f32[64,8,128]{2,1,0:T(8,128)S(1)}, f32[64,8,128]{2,1,0:T(8,128)S(1)}, u32[]{:S(2)}, u32[]{:S(2)}) collective-permute-start(f32[64,8,128]{2,1,0:T(8,128)S(1)} %get-tuple-element.27._), channel_id=1, source_target_pairs={{0,2},{1,3},{2,0},{3,1},{4,6},{5,7},{6,4},{7,5},{8,10},{9,11},{10,... | collective-permute-start | bytes 786440 | tf_op jit(solution)/shard_map/ppermute | solution.py:451
  56.2 25.5 %all-to-all-start.1 = ((f32[32,4,128]{2,1,0:T(4,128)}), f32[32,4,128]{2,1,0:T(4,128)S(1)}, u32[]{:S(2)}, u32[]{:S(2)}) async-start(f32[32,4,128]{2,1,0:T(4,128)} %get-tuple-element.29), calls=%async_computation.1 | async-start | bytes 131072 | tf_op jit(solution)/shard_map/all_to_all | solution.py:386
  71.7 6.3 %collective-permute-start.5 = (f32[16,8,128]{2,1,0:T(8,128)S(1)}, f32[16,8,128]{2,1,0:T(8,128)S(1)}, u32[]{:S(2)}, u32[]{:S(2)}) collective-permute-start(f32[16,8,128]{2,1,0:T(8,128)S(1)} %get-tuple-element.28), channel_id=1, source_target_pairs={{8,0},{16,8},{24,16},{32,24},{40,32},{48,40},{56,48},{64,56},{72,6... | collective-permute-start | bytes 196616 | tf_op jit(solution)/shard_map/ppermute | solution.py:462

commit v15 on v14

--- a/solution.py
+++ b/solution.py
@@ -299,7 +299,7 @@
 
 def last_kernel(place_ref, keep_ref, moved_ref, after_ref, sums_ref, taps_ref, *rest):
     own_ref, other_ref, *lanes = rest[:5]
-    solution_ref, residual_ref, kept, left, pairs = rest[5:]
+    *outputs, kept, left, pairs, kept_rows, left_rows, semaphore = rest[5:]
     parts, count = moved_ref.shape[0], moved_ref.shape[1] - 1
     reach = taps_ref.shape[0] - 1
     rows = pl.ds(pl.multiple_of(place_ref[0] * 8, 8), 8)
@@ -333,22 +333,34 @@
             base = pairs[part, at]
             image = pairs[part, count + at]
             again = weighted_sum(taps, frames[at : at + reach + 1]) + RIDGE * image
-            here = pl.ds(pl.multiple_of((part * count + at) * 8, 8), 8)
+            here = slice(at * 8, (at + 1) * 8)
             kept[here, :] = to_base * base + to_image * image
             left[here, :] = base + image_rate * image + cube_rate * again
+        for block in range(count // 8):
+            ready = pl.ds(pl.multiple_of(part * count + block * 8, 8), 8)
+            for n1 in range(8):
+                places = pl.ds(block * 64 + n1, 8, stride=8)
+                columns = slice(n1 * LANES, (n1 + 1) * LANES)
+                kept_rows[ready, columns] = kept[places, :]
+                left_rows[ready, columns] = left[places, :]
+        for copy in copies(part):
+            copy.start()
+
+    def copies(part):
+        ready = pl.ds(pl.multiple_of(part * count, 8), count)
+        return [
+            pltpu.make_async_copy(held.at[ready], output.at[ready], semaphore.at[which, part])
+            for which, (held, output) in enumerate(zip((kept_rows, left_rows), outputs))
+        ]
 
     @pl.loop(0, parts - 1)
     def _(part):
         finish(part, [moved_ref[part + 1, t] for t in range(reach)])
 
     finish(parts - 1, [after_ref[t] * keep_ref[0] for t in range(reach)])
-
-    for block in range(parts * count // 8):
-        for n1 in range(8):
-            places = pl.ds(block * 64 + n1, 8, stride=8)
-            columns = slice(n1 * LANES, (n1 + 1) * LANES)
-            solution_ref[block * 8 : (block + 1) * 8, columns] = kept[places, :]
-            residual_ref[block * 8 : (block + 1) * 8, columns] = left[places, :]
+    for part in range(parts):
+        for copy in copies(part):
+            copy.wait()
 
 
 def shape(*dims):
@@ -465,11 +477,14 @@
         last_kernel,
         out_shape=(shape(parts * count, 8 * LANES), shape(parts * count, 8 * LANES)),
         in_specs=[SMEM, SMEM] + vmem(9),
-        out_specs=tuple(vmem(2)),
+        out_specs=(pl.BlockSpec(memory_space=pltpu.HBM),) * 2,
         scratch_shapes=[
-            pltpu.VMEM((parts * count * 8, LANES), F32),
-            pltpu.VMEM((parts * count * 8, LANES), F32),
+            pltpu.VMEM((count * 8, LANES), F32),
+            pltpu.VMEM((count * 8, LANES), F32),
             pltpu.VMEM((parts, 2 * count, 8, LANES), F32),
+            pltpu.VMEM((parts * count, 8 * LANES), F32),
+            pltpu.VMEM((parts * count, 8 * LANES), F32),
+            pltpu.SemaphoreType.DMA((2, parts)),
         ],
         compiler_params=params(),
         name="last",

time: 84.1 us -> 83.8 us (level)
  no operation moved by 1% of the time
where the time goes in v15:
time: 83.8 us; the launch traced here: 83.6 us
  starting transfers between devices  28.9 us (34%)
  waiting for transfers between devices  21.1 us (25%)
  blocking collectives  17.6 us (21%)
  Pallas kernels  15 us (18%)
    all_to_all x1, blocking collectives, exchange(): return lax.all_to_all(value, axis, split_axis=0, concat_axis=0, tiled=True)  17.6 us
    all_to_all x1, starting transfers between devices, exchange(): return lax.all_to_all(value, axis, split_axis=0, concat_axis=0, tiled=True)  15.5 us
    ppermute x2, waiting for transfers between devices, neighbours(): lax.ppermute(block, AXES, across)  12.4 us
    ppermute x1, waiting for transfers between devices, local(): after = lax.ppermute(after, 'tm', [(i + 1, i) for i in range(groups - 1)])  4.95 us
    ppermute x3, starting transfers between devices, local(): lax.ppermute(lane, AXES, [(i, i ^ 2 * e + 2) for i in range(devices)])  4.7 us
    pallas_call x1, Pallas kernels, local(): pl.pallas_call(second_kernel, out_shape=(shape(parts, count + 1, 8, LANES...  4 us
    ppermute x2, starting transfers between devices, neighbours(): lax.ppermute(block, AXES, across)  3.84 us
    all_to_all x1, waiting for transfers between devices, exchange(): return lax.all_to_all(value, axis, split_axis=0, concat_axis=0, tiled=True)  3.73 us
  transfers between devices with their start and end apart: 10, of which 4 were waited for; matrix products, arithmetic and copies ran while one was open for 0% of the time, Pallas kernels for 2%

profile of v15, /device:TPU:2, one launch (start us, length us, event | category | flops | bytes accessed | tf_op | source)
XLA Modules:
  0.0 83.6 jit_solution(5347587964743277295)
XLA Ops:
  0.6 0.0 copy-start.1
  0.6 0.0 copy-start.4
  0.7 2.8 %seed.1.here_ref = f32[16,64,128]{2,1,0:T(8,128)S(1)} custom-call(f32[16,4096]{1,0:T(8,128)} %refs_0_.1, f32[16,4096]{1,0:T(8,128)} %refs_1_.1, f32[16,4096]{1,0:T(8,128)} %weights_ref.1, bf16[384,256]{1,0:T(8,128)(2,1)} %constant.40.clone.refs_3_.back_lanes_ref, bf16[128,256]{1,0:T(8,128)(2,1)} %constant.41.clone.refs_4_.back_rows_ref, ...), custom_call_target="tpu_custom_call" | custom-call | tf_op jit(solution)/shard_map/seed/pallas_call | solution.py:402
  3.5 1.9 %collective-permute-start.1 = (f32[16,64,128]{2,1,0:T(8,128)S(1)}, f32[16,64,128]{2,1,0:T(8,128)S(1)}, u32[]{:S(2)}, u32[]{:S(2)}) collective-permute-start(f32[16,64,128]{2,1,0:T(8,128)S(1)} %seed.1.here_ref), channel_id=1, source_target_pairs={{0,0},{1,2},{2,1},{3,4},{4,3},{5,6},{6,5},{7,8},{8,7},{9,10},{10,9... | collective-permute-start | bytes 1572872 | tf_op jit(solution)/shard_map/ppermute | solution.py:395
  5.4 1.7 %collective-permute-start = (f32[16,64,128]{2,1,0:T(8,128)S(1)}, f32[16,64,128]{2,1,0:T(8,128)S(1)}, u32[]{:S(2)}, u32[]{:S(2)}) collective-permute-start(f32[16,64,128]{2,1,0:T(8,128)S(1)} %seed.1.here_ref), channel_id=1, source_target_pairs={{0,1},{1,0},{2,3},{3,2},{4,5},{5,4},{6,7},{7,6},{8,9},{9,8},{10,11... | collective-permute-start | bytes 1572872 | tf_op jit(solution)/shard_map/ppermute | solution.py:395
  7.1 0.0 copy-done.1
  7.1 0.0 copy-done.4
  7.1 0.0 copy-start
  7.1 0.0 copy-start.2
  7.1 0.0 copy-start.3
  7.1 0.0 copy-start.5
  7.1 0.0 copy-start.6
  7.1 1.2 %arrange.1 = (f32[16,64,128]{2,1,0:T(8,128)S(1)}, f32[1024,128]{1,0:T(8,128)S(1)}) custom-call(f32[16,4096]{1,0:T(8,128)S(1)} %copy-done.1, f32[16,8192]{1,0:T(8,128)S(1)} %copy-done.4), custom_call_target="tpu_custom_call" | custom-call | flops 10000000 | bytes 2000000 | tf_op jit(solution)/shard_map/arrange/pallas_call | solution.py:413
  8.3 0.1 add_convert_fusion.keep_ref
  8.4 5.6 %collective-permute-done.1.across_ref = f32[16,64,128]{2,1,0:T(8,128)S(1)} collective-permute-done((f32[16,64,128]{2,1,0:T(8,128)S(1)}, f32[16,64,128]{2,1,0:T(8,128)S(1)}, u32[]{:S(2)}, u32[]{:S(2)}) %collective-permute-start.1) | collective-permute-done | bytes 524320 | tf_op jit(solution)/shard_map/ppermute | solution.py:395
  14.0 0.0 collective-permute-done.inside_ref
  14.0 0.0 copy-done
  14.0 0.0 copy-done.2
  14.0 0.0 copy-done.3
  14.0 0.0 copy-done.5
  14.0 0.0 copy-done.6
  14.0 3.7 %first.1 = (f32[16,64,128]{2,1,0:T(8,128)S(1)}, f32[31,64,128]{2,1,0:T(8,128)S(1)}) custom-call(f32[3]{0:T(128)S(1)} %add_convert_fusion.keep_ref, f32[16,64,128]{2,1,0:T(8,128)S(1)} %collective-permute-done.inside_ref, f32[16,64,128]{2,1,0:T(8,128)S(1)} %seed.1.here_ref, f32[16,64,128]{2,1,0:T(8,128)S(1)} %collective-permute-done.1.across_ref, ...), custom_call_target="tpu_custom_call" | custom-call | tf_op jit(solution)/shard_map/first/pallas_call | solution.py:425
  17.7 1.9 %collective-permute-start.3 = (f32[16,64,128]{2,1,0:T(8,128)S(1)}, f32[16,64,128]{2,1,0:T(8,128)S(1)}, u32[]{:S(2)}, u32[]{:S(2)}) collective-permute-start(f32[16,64,128]{2,1,0:T(8,128)S(1)} %get-tuple-element.19.here_ref), channel_id=1, source_target_pairs={{0,0},{1,2},{2,1},{3,4},{4,3},{5,6},{6,5},{7,8},{8,7},{9,10},{10,9... | collective-permute-start | bytes 1572872 | tf_op jit(solution)/shard_map/ppermute | solution.py:395
  19.7 1.7 %collective-permute-start.2 = (f32[16,64,128]{2,1,0:T(8,128)S(1)}, f32[16,64,128]{2,1,0:T(8,128)S(1)}, u32[]{:S(2)}, u32[]{:S(2)}) collective-permute-start(f32[16,64,128]{2,1,0:T(8,128)S(1)} %get-tuple-element.19.here_ref), channel_id=1, source_target_pairs={{0,1},{1,0},{2,3},{3,2},{4,5},{5,4},{6,7},{7,6},{8,9},{9,8},{10,11... | collective-permute-start | bytes 1572872 | tf_op jit(solution)/shard_map/ppermute | solution.py:395
  21.4 6.9 %collective-permute-done.3.across_ref = f32[16,64,128]{2,1,0:T(8,128)S(1)} collective-permute-done((f32[16,64,128]{2,1,0:T(8,128)S(1)}, f32[16,64,128]{2,1,0:T(8,128)S(1)}, u32[]{:S(2)}, u32[]{:S(2)}) %collective-permute-start.3) | collective-permute-done | bytes 524320 | tf_op jit(solution)/shard_map/ppermute | solution.py:395
  28.2 0.0 collective-permute-done.2.inside_ref
  28.2 4.0 %second.1 = (f32[8,17,8,128]{3,2,1,0:T(8,128)S(1)}, f32[4,32,8,128]{3,2,1,0:T(8,128)S(1)}, f32[4,32,8,128]{3,2,1,0:T(8,128)S(1)}) custom-call(s32[1]{0:T(128)} %bitcast.place_ref, f32[3]{0:T(128)S(1)} %add_convert_fusion.keep_ref, f32[16,64,128]{2,1,0:T(8,128)S(1)} %collective-permute-done.2.inside_ref, f32[16,64,128]{2,1,0:T(8,128)S(1)} %get-tuple-element.19.here_ref, ...), custom_call_target="tpu_custom_call" | custom-call | tf_op jit(solution)/shard_map/second/pallas_call | solution.py:436
  32.3 0.2 collective-permute-start.4
  32.5 17.6 %all_to_all.10.moved_ref = f32[8,17,8,128]{3,2,1,0:T(8,128)S(1)} all-to-all(f32[8,17,8,128]{3,2,1,0:T(8,128)S(1)} %get-tuple-element.21), channel_id=1, replica_groups=mesh['tm'=32,'chan'=8] {'chan'}, dimensions={0} | all-to-all | bytes 1114112 | tf_op jit(solution)/shard_map/all_to_all | solution.py:398
  50.0 0.0 collective-permute-done.4.other_ref.rest_1_
  50.0 0.8 %join.1 = (f32[64,8,128]{2,1,0:T(8,128)S(1)}, f32[64,8,128]{2,1,0:T(8,128)}, f32[64,8,128]{2,1,0:T(8,128)}) custom-call(f32[4,32,8,128]{3,2,1,0:T(8,128)S(1)} %get-tuple-element.25.own_ref.rest_0_, f32[4,32,8,128]{3,2,1,0:T(8,128)S(1)} %collective-permute-done.4.other_ref.rest_1_), custom_call_target="tpu_custom_call" | custom-call | tf_op jit(solution)/shard_map/join/pallas_call | solution.py:453
  50.9 1.5 %collective-permute-start.7 = (f32[64,8,128]{2,1,0:T(8,128)}, f32[64,8,128]{2,1,0:T(8,128)S(1)}, u32[]{:S(2)}, u32[]{:S(2)}) collective-permute-start(f32[64,8,128]{2,1,0:T(8,128)} %get-tuple-element.30), channel_id=1, source_target_pairs={{0,4},{1,5},{2,6},{3,7},{4,0},{5,1},{6,2},{7,3},{8,12},{9,13},{10,... | collective-permute-start | bytes 786440 | tf_op jit(solution)/shard_map/ppermute | solution.py:463
  52.3 1.5 %collective-permute-start.8 = (f32[64,8,128]{2,1,0:T(8,128)}, f32[64,8,128]{2,1,0:T(8,128)S(1)}, u32[]{:S(2)}, u32[]{:S(2)}) collective-permute-start(f32[64,8,128]{2,1,0:T(8,128)} %get-tuple-element.31), channel_id=1, source_target_pairs={{0,6},{1,7},{2,4},{3,5},{4,2},{5,3},{6,0},{7,1},{8,14},{9,15},{10,... | collective-permute-start | bytes 786440 | tf_op jit(solution)/shard_map/ppermute | solution.py:463
  53.8 1.8 %collective-permute-start.6 = (f32[64,8,128]{2,1,0:T(8,128)S(1)}, f32[64,8,128]{2,1,0:T(8,128)S(1)}, u32[]{:S(2)}, u32[]{:S(2)}) collective-permute-start(f32[64,8,128]{2,1,0:T(8,128)S(1)} %get-tuple-element.27._), channel_id=1, source_target_pairs={{0,2},{1,3},{2,0},{3,1},{4,6},{5,7},{6,4},{7,5},{8,10},{9,11},{10,... | collective-permute-start | bytes 786440 | tf_op jit(solution)/shard_map/ppermute | solution.py:463
  55.6 0.6 tail.1
  56.2 15.5 %all-to-all-start.1 = ((f32[32,4,128]{2,1,0:T(4,128)}), f32[32,4,128]{2,1,0:T(4,128)S(1)}, u32[]{:S(2)}, u32[]{:S(2)}) async-start(f32[32,4,128]{2,1,0:T(4,128)} %get-tuple-element.29), calls=%async_computation.1 | async-start | bytes 131072 | tf_op jit(solution)/shard_map/all_to_all | solution.py:398
  71.7 1.3 %collective-permute-start.5 = (f32[16,8,128]{2,1,0:T(8,128)S(1)}, f32[16,8,128]{2,1,0:T(8,128)S(1)}, u32[]{:S(2)}, u32[]{:S(2)}) collective-permute-start(f32[16,8,128]{2,1,0:T(8,128)S(1)} %get-tuple-element.28), channel_id=1, source_target_pairs={{8,0},{16,8},{24,16},{32,24},{40,32},{48,40},{56,48},{64,56},{72,6... | collective-permute-start | bytes 196616 | tf_op jit(solution)/shard_map/ppermute | solution.py:474
  73.1 5.0 %collective-permute-done.5.after_ref = f32[16,8,128]{2,1,0:T(8,128)S(1)} collective-permute-done((f32[16,8,128]{2,1,0:T(8,128)S(1)}, f32[16,8,128]{2,1,0:T(8,128)S(1)}, u32[]{:S(2)}, u32[]{:S(2)}) %collective-permute-start.5) | collective-permute-done | bytes 65568 | tf_op jit(solution)/shard_map/ppermute | solution.py:474
  78.0 3.7 %all-to-all-done.1.sums_ref = f32[32,4,128]{2,1,0:T(4,128)S(1)} async-done(((f32[32,4,128]{2,1,0:T(4,128)}), f32[32,4,128]{2,1,0:T(4,128)S(1)}, u32[]{:S(2)}, u32[]{:S(2)}) %all-to-all-start.1) | async-done | bytes 65568 | tf_op jit(solution)/shard_map/all_to_all | solution.py:398
  81.7 0.0 collective-permute-done.7.rest_3_
  81.7 0.0 collective-permute-done.8.rest_4_
  81.7 0.0 collective-permute-done.6.rest_2_
  81.7 1.8 %last.1 = (f32[128,1024]{1,0:T(8,128)}, f32[128,1024]{1,0:T(8,128)}) custom-call(s32[1]{0:T(128)} %bitcast.place_ref, f32[1]{0:T(128)} %bitcast.1.keep_ref, f32[8,17,8,128]{3,2,1,0:T(8,128)S(1)} %all_to_all.10.moved_ref, f32[16,8,128]{2,1,0:T(8,128)S(1)} %collective-permute-done.5.after_ref, f32[32,4,128]{2,1,0:T(4,128)S(1)} %all-to-all-done.1.sums_ref, ...), custom_call_target="tpu_custom_call" | custom-call | tf_op jit(solution)/shard_map/last/pallas_call | solution.py:476
Async XLA Ops:
  0.6 6.4 %copy-start.1 = (f32[16,4096]{1,0:T(8,128)S(1)}, f32[16,4096]{1,0:T(8,128)}, u32[]{:S(2)}) copy-start(f32[16,4096]{1,0:T(8,128)} %weights_ref.1) | copy-start | bytes 786436
  0.6 6.4 %copy-start.4 = (f32[16,8192]{1,0:T(8,128)S(1)}, f32[16,8192]{1,0:T(8,128)}, u32[]{:S(2)}) copy-start(f32[16,8192]{1,0:T(8,128)} %taps_ref.1) | copy-start | bytes 1572868
  3.5 10.5 %collective-permute-start.1 = (f32[16,64,128]{2,1,0:T(8,128)S(1)}, f32[16,64,128]{2,1,0:T(8,128)S(1)}, u32[]{:S(2)}, u32[]{:S(2)}) collective-permute-start(f32[16,64,128]{2,1,0:T(8,128)S(1)} %seed.1.here_ref), channel_id=1, source_target_pairs={{0,0},{1,2},{2,1},{3,4},{4,3},{5,6},{6,5},{7,8},{8,7},{9,10},{10,9... | collective-permute-start | bytes 1572872 | tf_op jit(solution)/shard_map/ppermute | solution.py:395
  5.4 8.6 %collective-permute-start = (f32[16,64,128]{2,1,0:T(8,128)S(1)}, f32[16,64,128]{2,1,0:T(8,128)S(1)}, u32[]{:S(2)}, u32[]{:S(2)}) collective-permute-start(f32[16,64,128]{2,1,0:T(8,128)S(1)} %seed.1.here_ref), channel_id=1, source_target_pairs={{0,1},{1,0},{2,3},{3,2},{4,5},{5,4},{6,7},{7,6},{8,9},{9,8},{10,11... | collective-permute-start | bytes 1572872 | tf_op jit(solution)/shard_map/ppermute | solution.py:395
  7.1 6.9 %copy-start = (bf16[384,256]{1,0:T(8,128)(2,1)S(1)}, bf16[384,256]{1,0:T(8,128)(2,1)}, u32[]{:S(2)}) copy-start(bf16[384,256]{1,0:T(8,128)(2,1)} %constant.40.clone.refs_3_.back_lanes_ref) | copy-start | bytes 589828
  7.1 6.9 %copy-start.2 = (f32[2,64,128]{2,1,0:T(8,128)S(1)}, f32[2,64,128]{2,1,0:T(8,128)}, u32[]{:S(2)}) copy-start(f32[2,64,128]{2,1,0:T(8,128)} %constant.42.clone.refs_5_.twist_ref) | copy-start | bytes 196612
  7.1 6.9 %copy-start.3 = (bf16[128,256]{1,0:T(8,128)(2,1)S(1)}, bf16[128,256]{1,0:T(8,128)(2,1)}, u32[]{:S(2)}) copy-start(bf16[128,256]{1,0:T(8,128)(2,1)} %constant.41.clone.refs_4_.back_rows_ref) | copy-start | bytes 196612
  7.1 6.9 %copy-start.5 = (bf16[256,256]{1,0:T(8,128)(2,1)S(1)}, bf16[256,256]{1,0:T(8,128)(2,1)}, u32[]{:S(2)}) copy-start(bf16[256,256]{1,0:T(8,128)(2,1)} %constant.44.clone.ahead_lanes_ref) | copy-start | bytes 393220
  7.1 6.9 %copy-start.6 = (bf16[128,192]{1,0:T(8,128)(2,1)S(1)}, bf16[128,192]{1,0:T(8,128)(2,1)}, u32[]{:S(2)}) copy-start(bf16[128,192]{1,0:T(8,128)(2,1)} %constant.43.clone.ahead_rows_ref) | copy-start | bytes 147460
  17.7 10.5 %collective-permute-start.3 = (f32[16,64,128]{2,1,0:T(8,128)S(1)}, f32[16,64,128]{2,1,0:T(8,128)S(1)}, u32[]{:S(2)}, u32[]{:S(2)}) collective-permute-start(f32[16,64,128]{2,1,0:T(8,128)S(1)} %get-tuple-element.19.here_ref), channel_id=1, source_target_pairs={{0,0},{1,2},{2,1},{3,4},{4,3},{5,6},{6,5},{7,8},{8,7},{9,10},{10,9... | collective-permute-start | bytes 1572872 | tf_op jit(solution)/shard_map/ppermute | solution.py:395
  19.7 8.6 %collective-permute-start.2 = (f32[16,64,128]{2,1,0:T(8,128)S(1)}, f32[16,64,128]{2,1,0:T(8,128)S(1)}, u32[]{:S(2)}, u32[]{:S(2)}) collective-permute-start(f32[16,64,128]{2,1,0:T(8,128)S(1)} %get-tuple-element.19.here_ref), channel_id=1, source_target_pairs={{0,1},{1,0},{2,3},{3,2},{4,5},{5,4},{6,7},{7,6},{8,9},{9,8},{10,11... | collective-permute-start | bytes 1572872 | tf_op jit(solution)/shard_map/ppermute | solution.py:395
  32.3 17.8 %collective-permute-start.4 = (f32[4,32,8,128]{3,2,1,0:T(8,128)S(1)}, f32[4,32,8,128]{3,2,1,0:T(8,128)S(1)}, u32[]{:S(2)}, u32[]{:S(2)}) collective-permute-start(f32[4,32,8,128]{3,2,1,0:T(8,128)S(1)} %get-tuple-element.23), channel_id=1, source_target_pairs={{0,1},{1,0},{2,3},{3,2},{4,5},{5,4},{6,7},{7,6},{8,9},{9,8},{10,11... | collective-permute-start | bytes 1572872 | tf_op jit(solution)/shard_map/ppermute | solution.py:451
  50.9 30.9 %collective-permute-start.7 = (f32[64,8,128]{2,1,0:T(8,128)}, f32[64,8,128]{2,1,0:T(8,128)S(1)}, u32[]{:S(2)}, u32[]{:S(2)}) collective-permute-start(f32[64,8,128]{2,1,0:T(8,128)} %get-tuple-element.30), channel_id=1, source_target_pairs={{0,4},{1,5},{2,6},{3,7},{4,0},{5,1},{6,2},{7,3},{8,12},{9,13},{10,... | collective-permute-start | bytes 786440 | tf_op jit(solution)/shard_map/ppermute | solution.py:463
  52.3 29.4 %collective-permute-start.8 = (f32[64,8,128]{2,1,0:T(8,128)}, f32[64,8,128]{2,1,0:T(8,128)S(1)}, u32[]{:S(2)}, u32[]{:S(2)}) collective-permute-start(f32[64,8,128]{2,1,0:T(8,128)} %get-tuple-element.31), channel_id=1, source_target_pairs={{0,6},{1,7},{2,4},{3,5},{4,2},{5,3},{6,0},{7,1},{8,14},{9,15},{10,... | collective-permute-start | bytes 786440 | tf_op jit(solution)/shard_map/ppermute | solution.py:463
  53.8 27.9 %collective-permute-start.6 = (f32[64,8,128]{2,1,0:T(8,128)S(1)}, f32[64,8,128]{2,1,0:T(8,128)S(1)}, u32[]{:S(2)}, u32[]{:S(2)}) collective-permute-start(f32[64,8,128]{2,1,0:T(8,128)S(1)} %get-tuple-element.27._), channel_id=1, source_target_pairs={{0,2},{1,3},{2,0},{3,1},{4,6},{5,7},{6,4},{7,5},{8,10},{9,11},{10,... | collective-permute-start | bytes 786440 | tf_op jit(solution)/shard_map/ppermute | solution.py:463
  56.2 25.5 %all-to-all-start.1 = ((f32[32,4,128]{2,1,0:T(4,128)}), f32[32,4,128]{2,1,0:T(4,128)S(1)}, u32[]{:S(2)}, u32[]{:S(2)}) async-start(f32[32,4,128]{2,1,0:T(4,128)} %get-tuple-element.29), calls=%async_computation.1 | async-start | bytes 131072 | tf_op jit(solution)/shard_map/all_to_all | solution.py:398
  71.7 6.3 %collective-permute-start.5 = (f32[16,8,128]{2,1,0:T(8,128)S(1)}, f32[16,8,128]{2,1,0:T(8,128)S(1)}, u32[]{:S(2)}, u32[]{:S(2)}) collective-permute-start(f32[16,8,128]{2,1,0:T(8,128)S(1)} %get-tuple-element.28), channel_id=1, source_target_pairs={{8,0},{16,8},{24,16},{32,24},{40,32},{48,40},{56,48},{64,56},{72,6... | collective-permute-start | bytes 196616 | tf_op jit(solution)/shard_map/ppermute | solution.py:474
